TPU v7x, 32 devices: a whole 2x2x4 slice. The times are simulated.
32 devices in a mesh: groups: 2 (over y), row: 4 (over x, core), col: 4 (over z).
Axes of the slice: x: 2, y: 2, z: 4, core: 2. Of those that a mesh axis runs over, the one named last changes fastest.
Arguments:
- pair: bfloat16 [192, 96, 128], P(('groups', 'row'), 'col'), parts along dimension 0, may hold values from -6 to 6
- token_mask: int32 [192], P('groups'), parts along dimension 0, may hold values from 0 to 1, as said below
- in_gain: float32 [2, 128], replicated, may hold values from 0.25 to 1.75
- in_shift: float32 [2, 128], replicated, may hold values from -3 to 3
- w_in: bfloat16 [2, 128, 640], replicated, may hold values from -0.5 to 0.5
- bias_in: float32 [2, 640], replicated, may hold values from -3 to 3
- out_gain: float32 [2, 128], replicated, may hold values from 0.25 to 1.75
- out_shift: float32 [2, 128], replicated, may hold values from -3 to 3
- w_out: bfloat16 [2, 128, 128], replicated, may hold values from -0.5 to 0.5
- bias_out: float32 [2, 128], replicated, may hold values from -3 to 3
Outputs:
- pair_out: bfloat16 [192, 96, 128], P(('groups', 'row'), 'col'), parts along dimension 0
There are 2 independent parts, one for each index of `groups`. A program takes and returns all parts, laid end to end along the dimension named above; an argument that names none is the same for every part. Nothing has to cross between parts.
Inputs may be any that keep to these rules, and one draw needn't show every extreme that they name: token_mask is 1 on the first L tokens and 0 on the rest, with 48 <= L < 96.
All inputs are finite; a program needn't handle non-finite values.
Results may differ from a plain program's by a relative error of at most 0.0085.
Values may be sent and summed in bfloat16 or wider, within the bound.
No kernel may reach another device: no remote copies, remote signals or barrier semaphores. Data moves between devices by JAX's collectives and lax.ppermute only.
A program may use at most 64 MiB of HBM per device.

v0:
```python
import jax
import jax.numpy as jnp
from jax import lax
from jax.sharding import PartitionSpec as P


def from_root(array, axis, root):
    mine = lax.axis_index(axis) == root
    return lax.psum(jnp.where(mine, array, jnp.zeros_like(array)), axis)


def norm_rows(values, gain, shift):
    center = values - jnp.mean(values, axis=-1, keepdims=True)
    spread = jnp.mean(center * center, axis=-1, keepdims=True)
    return center * lax.rsqrt(spread + 1e-05) * gain + shift


def gated(normed, weights, biases, tile_grid, hidden_units):
    product = jnp.dot(normed, weights, preferred_element_type=jnp.float32) + biases
    return (
        jax.nn.sigmoid(product[..., hidden_units:])
        * product[..., :hidden_units]
        * tile_grid[..., None]
    ).astype(jnp.bfloat16)


def finish(pair, mixture, gating, out_gain, out_shift, w_out, bias_out):
    normout = norm_rows(mixture, out_gain, out_shift).astype(jnp.bfloat16)
    update = gating * (jnp.dot(normout, w_out, preferred_element_type=jnp.float32) + bias_out)
    return (pair.astype(jnp.float32) + update).astype(jnp.bfloat16)


def per_device(
    pair, token_mask, in_gain, in_shift, w_in, bias_in, out_gain, out_shift, w_out, bias_out
):
    rows_dev = pair.shape[0]
    hidden_units = w_out.shape[1]
    double = 2 * hidden_units
    present = token_mask.astype(jnp.float32)
    row_mask = lax.dynamic_slice_in_dim(present, lax.axis_index("row") * rows_dev, rows_dev)
    col_mask = lax.dynamic_slice_in_dim(present, lax.axis_index("col") * rows_dev, rows_dev)
    tile_grid = row_mask[:, None] * col_mask[None, :]
    weights = w_in[0]
    biases = bias_in[0]
    normed = norm_rows(pair.astype(jnp.float32), in_gain[0], in_shift[0]).astype(jnp.bfloat16)
    leading = gated(normed, weights[:, :double], biases[:double], tile_grid, hidden_units)
    source = gated(
        normed,
        weights[:, double : 2 * double],
        biases[double : 2 * double],
        tile_grid,
        hidden_units,
    )
    gating = jax.nn.sigmoid(
        jnp.dot(normed, weights[:, 2 * double :], preferred_element_type=jnp.float32)
        + biases[2 * double :]
    )
    lead_panel = lax.all_gather(leading, "col", axis=1, tiled=True)
    source_panel = lax.all_gather(source, "col", axis=1, tiled=True)
    mirrored = from_root(source_panel, "row", lax.axis_index("col"))
    left_panel = lead_panel
    right_panel = mirrored
    mixture = jnp.einsum(
        "ikh,jkh->ijh", left_panel, right_panel, preferred_element_type=jnp.float32
    )
    updated = finish(pair, mixture, gating, out_gain[0], out_shift[0], w_out[0], bias_out[0])
    weights = w_in[1]
    biases = bias_in[1]
    normed = norm_rows(updated.astype(jnp.float32), in_gain[1], in_shift[1]).astype(jnp.bfloat16)
    source = gated(normed, weights[:, :double], biases[:double], tile_grid, hidden_units)
    leading = gated(
        normed,
        weights[:, double : 2 * double],
        biases[double : 2 * double],
        tile_grid,
        hidden_units,
    )
    gating = jax.nn.sigmoid(
        jnp.dot(normed, weights[:, 2 * double :], preferred_element_type=jnp.float32)
        + biases[2 * double :]
    )
    lead_panel = lax.all_gather(leading, "row", axis=0, tiled=True)
    source_panel = lax.all_gather(source, "row", axis=0, tiled=True)
    mirrored = from_root(source_panel, "col", lax.axis_index("row"))
    right_panel = lead_panel
    left_panel = mirrored
    mixture = jnp.einsum(
        "kih,kjh->ijh", left_panel, right_panel, preferred_element_type=jnp.float32
    )
    return finish(updated, mixture, gating, out_gain[1], out_shift[1], w_out[1], bias_out[1])


def solution(mesh):
    placed = (
        P(("groups", "row"), "col", None),
        P("groups"),
        P(),
        P(),
        P(),
        P(),
        P(),
        P(),
        P(),
        P(),
    )
    return jax.shard_map(
        per_device,
        mesh=mesh,
        in_specs=placed,
        out_specs=P(("groups", "row"), "col", None),
        check_vma=False,
    )
```

profile of v0, /device:TPU:0, one launch (start us, length us, event | category | flops | bytes accessed | tf_op | source)
XLA Modules:
  0.0 136.6 jit_solution(1499474321744215619)
XLA Ops:
  6.5 0.7 convert_element_type.43
  7.2 0.8 fusion.56
  8.0 1.1 convert_reduce_fusion
  9.1 1.2 fusion.17
  10.3 1.0 slice_bitcast_fusion
  11.3 0.8 slice_bitcast_fusion.18
  12.1 1.3 convolution_add_fusion.2
  13.4 0.4 convolution_add_fusion.3
  13.7 0.1 fusion.57
  13.8 0.1 broadcast_multiply_fusion
  13.9 0.2 fusion.32
  14.1 0.0 copy-start.4
  14.1 0.0 copy-start.5
  14.1 18.5 %all_gather.12 = bf16[24,96,128]{2,1,0:T(8,128)(2,1)S(1)} all-gather(bf16[24,24,128]{2,1,0:T(8,128)(2,1)S(1)} %get-tuple-element.10), channel_id=1, replica_groups=mesh['groups'=2,'row'=4,'col'=4] {'col'}, dimensions={1}, use_global_device_ids=true | all-gather | bytes 737280 | tf_op jit(solution)/shard_map/all_gather | solution.py:59
  32.6 0.9 broadcast_select_fusion.1
  33.4 0.0 all-reduce.3.cloned.1.call-update
  33.4 0.0 all-reduce.5.cloned.1.call-start
  33.5 0.8 slice_bitcast_fusion.17
  34.3 16.5 %all_gather.13 = bf16[24,96,128]{2,1,0:T(8,128)(2,1)S(1)} all-gather(bf16[24,24,128]{2,1,0:T(8,128)(2,1)S(1)} %get-tuple-element.9), channel_id=1, replica_groups=mesh['groups'=2,'row'=4,'col'=4] {'col'}, dimensions={1}, use_global_device_ids=true | all-gather | bytes 737280 | tf_op jit(solution)/shard_map/all_gather | solution.py:58
  50.8 0.4 copy.46
  51.3 1.1 fusion.11
  52.4 16.3 %all-reduce.3.cloned.1.call-done = bf16[24,96,128]{2,1,0:T(8,128)(2,1)} async-done(((bf16[24,96,128]{2,1,0:T(8,128)(2,1)}), bf16[24,96,128]{2,1,0:T(8,128)(2,1)}) %all-reduce.3.cloned.1.call-update) | async-done | bytes 589840 | tf_op jit(solution)/shard_map/psum | solution.py:9
  68.7 1.5 %copy.45 = bf16[24,96,128]{1,0,2:T(8,128)(2,1)S(1)} copy(bf16[24,96,128]{2,1,0:T(8,128)(2,1)} %all-reduce.3.cloned.1.call-done) | data formatting | bytes 1179648 | tf_op jit(solution)/shard_map/psum | solution.py:9
  70.1 0.5 bitcast_reduce_fusion.1
  70.7 0.0 copy-start.2
  70.7 0.1 copy.49
  70.8 0.5 copy.47
  71.3 0.3 multiply_reduce_fusion.2
  71.6 0.1 copy-done.1
  71.7 0.4 fusion.58
  72.1 0.3 multiply_reduce_fusion.1
  72.4 0.2 add_convert_fusion.1
  72.6 0.2 convolution_add_fusion
  72.9 0.2 convolution_add_fusion.1
  73.1 0.2 fusion.22
  73.3 6.7 %all_gather.15 = bf16[96,24,128]{2,1,0:T(8,128)(2,1)S(1)} all-gather(bf16[24,24,128]{2,1,0:T(8,128)(2,1)S(1)} %get-tuple-element.7), channel_id=1, replica_groups=mesh['groups'=2,'row'=4,'col'=4] {'row'}, dimensions={0}, use_global_device_ids=true | all-gather | bytes 737280 | tf_op jit(solution)/shard_map/all_gather | solution.py:83
  80.0 0.6 copy.52
  80.6 1.0 broadcast_select_fusion
  81.5 0.0 all-reduce.5.cloned.1.call-update
  81.6 7.6 %all_gather.14 = bf16[96,24,128]{2,1,0:T(8,128)(2,1)S(1)} all-gather(bf16[24,24,128]{2,1,0:T(8,128)(2,1)S(1)} %get-tuple-element.8), channel_id=1, replica_groups=mesh['groups'=2,'row'=4,'col'=4] {'row'}, dimensions={0}, use_global_device_ids=true | all-gather | bytes 737280 | tf_op jit(solution)/shard_map/all_gather | solution.py:82
  89.2 0.6 copy.53
  89.8 0.2 fusion.5
  90.1 36.2 %all-reduce.5.cloned.1.call-done = bf16[96,24,128]{0,1,2:T(8,128)(2,1)} async-done(((bf16[96,24,128]{0,1,2:T(8,128)(2,1)}), bf16[96,24,128]{0,1,2:T(8,128)(2,1)}) %all-reduce.5.cloned.1.call-update) | async-done | bytes 589840 | tf_op jit(solution)/shard_map/psum | solution.py:9
  126.2 1.7 %bitcast_reduce_fusion = (f32[24,24]{0,1:T(8,128)S(1)}, f32[128,24,24]{2,1,0:T(8,128)S(1)}) fusion(bf16[96,24,128]{0,1,2:T(8,128)(2,1)S(1)} %copy.53, bf16[96,24,128]{0,1,2:T(8,128)(2,1)} %all-reduce.5.cloned.1.call-done), kind=kOutput, calls=%fused_computation | convolution fusion | flops 14228928 | bytes 1476864 | tf_op jit(solution)/shard_map/kih,kjh->ijh/dot_general | solution.py:87
  127.9 0.1 copy.56
  128.0 0.5 copy.54
  128.5 0.3 multiply_reduce_fusion
  128.8 1.0 fusion.14
  (19 shorter events, 0.1 us)
Async XLA Ops:
  6.5 6.8 %copy-start = (bf16[24,24,128]{2,1,0:T(8,128)(2,1)S(1)}, bf16[24,24,128]{2,1,0:T(8,128)(2,1)}, u32[]{:S(2)}) copy-start(bf16[24,24,128]{2,1,0:T(8,128)(2,1)} %param.10) | copy-start | bytes 442372
  6.5 62.1 %all-reduce.3.cloned.1.call-start = ((), (), s32[]{:S(2)}) async-start(), calls=%async_computation | async-start | bytes 1179648 | tf_op jit(solution)/shard_map/psum | solution.py:9
  14.1 20.2 %copy-start.3 = (f32[2,128]{1,0:T(2,128)S(1)}, f32[2,128]{1,0:T(2,128)}, u32[]{:S(2)}) copy-start(f32[2,128]{1,0:T(2,128)} %param.16) | copy-start | bytes 3076
  14.1 20.2 %copy-start.4 = (f32[2,128]{1,0:T(2,128)S(1)}, f32[2,128]{1,0:T(2,128)}, u32[]{:S(2)}) copy-start(f32[2,128]{1,0:T(2,128)} %param.19) | copy-start | bytes 3076
  14.1 20.2 %copy-start.5 = (f32[2,128]{1,0:T(2,128)S(1)}, f32[2,128]{1,0:T(2,128)}, u32[]{:S(2)}) copy-start(f32[2,128]{1,0:T(2,128)} %param.17) | copy-start | bytes 3076
  33.4 92.8 %all-reduce.5.cloned.1.call-start = ((), (), s32[]{:S(2)}) async-start(), calls=%async_computation.1 | async-start | bytes 1572864 | tf_op jit(solution)/shard_map/psum | solution.py:9
  70.7 1.0 copy-start.1
  70.7 1.0 copy-start.2
Sparse Core Ops, SparseCore 0:
  33.6 35.0 all-reduce.2
  81.7 44.4 all-reduce.4
where the time goes:
time: 137 us
  waiting for transfers between devices  52.5 us (38%)
  blocking collectives  49.3 us (36%)
  between operations  13.7 us (10%)
  local copies, waits for them, and re-layouts  7.72 us (6%)
  matrix products  7.12 us (5%)
  other arithmetic  6.27 us (5%)
    psum x2, waiting for transfers between devices, from_root(): return lax.psum(jnp.where(mine, array, jnp.zeros_like(array)), axis)  52.5 us
    all_gather x1, blocking collectives, per_device(): source_panel = lax.all_gather(source, 'col', axis=1, tiled=True)  18.5 us
    all_gather x1, blocking collectives, per_device(): lead_panel = lax.all_gather(leading, 'col', axis=1, tiled=True)  16.5 us
    all_gather x1, blocking collectives, per_device(): lead_panel = lax.all_gather(leading, 'row', axis=0, tiled=True)  7.65 us
    all_gather x1, blocking collectives, per_device(): source_panel = lax.all_gather(source, 'row', axis=0, tiled=True)  6.69 us
  transfers between devices with their start and end apart: 2, of which 2 were waited for; matrix products, arithmetic and copies ran while one was open for 2% of the time, Pallas kernels for 0%

commit v1 on v0

v1 whole, which is shorter than its diff:
```python
import jax
import jax.numpy as jnp
from jax import lax
from jax.sharding import PartitionSpec as P


def norm_rows(values, gain, shift):
    center = values - jnp.mean(values, axis=-1, keepdims=True)
    spread = jnp.mean(center * center, axis=-1, keepdims=True)
    return center * lax.rsqrt(spread + 1e-05) * gain + shift


def update(pair, grid, in_gain, in_shift, w_in, bias_in, out_gain, out_shift, w_out, bias_out, shape, incoming):
    rows, cols, _ = pair.shape
    peers_r, peers_c = shape
    peers = peers_r * peers_c
    hidden = w_out.shape[0]
    normed = norm_rows(pair.astype(jnp.float32), in_gain, in_shift).astype(jnp.bfloat16)
    product = jnp.dot(normed, w_in, preferred_element_type=jnp.float32) + bias_in
    values = product[..., : 4 * hidden].reshape(rows, cols, 2, 2, hidden)
    sides = (jax.nn.sigmoid(values[..., 1, :]) * values[..., 0, :] * grid[..., None, None]).astype(jnp.bfloat16)
    gating = jax.nn.sigmoid(product[..., 4 * hidden :])
    if hidden % peers == 0:
        part = hidden // peers
        sides = sides.reshape(rows * cols, 2, peers, part).transpose(2, 1, 3, 0).reshape(peers, 2 * part, rows * cols)
        sides = lax.all_to_all(sides, ("row", "col"), 0, 0, tiled=True)
        sides = sides.reshape(peers_r, peers_c, 2, part, rows, cols).transpose(2, 3, 0, 4, 1, 5)
        sides = sides.reshape(2, part, peers_r * rows, peers_c * cols)
        form = "hki,hkj->hij" if incoming else "hik,hjk->hij"
        mixed = jnp.einsum(form, sides[0], sides[1], preferred_element_type=jnp.float32).astype(jnp.bfloat16)
        mixed = mixed.reshape(part, peers_r, rows, peers_c, cols).transpose(1, 3, 0, 2, 4).reshape(peers, part, rows * cols)
        mixed = lax.all_to_all(mixed, ("row", "col"), 0, 0, tiled=True)
    else:
        part = hidden // peers_c
        sides = sides.reshape(rows, cols, 2, peers_c, part).transpose(3, 2, 4, 0, 1)
        sides = lax.all_to_all(sides, "col", 0, 0).transpose(1, 2, 3, 0, 4).reshape(2, part, rows, peers_c * cols)
        panel = lax.all_gather(sides, "row", axis=2, tiled=True)
        here = lax.axis_index("row") * rows
        if incoming:
            own = lax.dynamic_slice_in_dim(panel[0], here, rows, 2)
            mixed = jnp.einsum("hki,hkj->hij", own, panel[1], preferred_element_type=jnp.float32)
        else:
            mixed = jnp.einsum("hik,hjk->hij", sides[0], panel[1], preferred_element_type=jnp.float32)
        mixed = mixed.astype(jnp.bfloat16).reshape(part, rows, peers_c, cols).transpose(2, 0, 1, 3)
        mixed = lax.all_to_all(mixed, "col", 0, 0)
    mixed = mixed.reshape(hidden, rows * cols).T.reshape(rows, cols, hidden).astype(jnp.float32)
    normout = norm_rows(mixed, out_gain, out_shift).astype(jnp.bfloat16)
    result = gating * (jnp.dot(normout, w_out, preferred_element_type=jnp.float32) + bias_out)
    return (pair.astype(jnp.float32) + result).astype(jnp.bfloat16)


def solution(mesh):
    shape = (mesh.shape["row"], mesh.shape["col"])

    def per_device(pair, token_mask, in_gain, in_shift, w_in, bias_in, out_gain, out_shift, w_out, bias_out):
        rows, cols, _ = pair.shape
        present = token_mask.astype(jnp.float32)
        row_mask = lax.dynamic_slice_in_dim(present, lax.axis_index("row") * rows, rows)
        col_mask = lax.dynamic_slice_in_dim(present, lax.axis_index("col") * cols, cols)
        grid = row_mask[:, None] * col_mask[None, :]
        for index in range(2):
            pair = update(
                pair, grid, in_gain[index], in_shift[index], w_in[index], bias_in[index],
                out_gain[index], out_shift[index], w_out[index], bias_out[index], shape, index == 1,
            )
        return pair

    placed = (P(("groups", "row"), "col", None), P("groups")) + (P(),) * 8
    return jax.shard_map(
        per_device, mesh=mesh, in_specs=placed, out_specs=P(("groups", "row"), "col", None), check_vma=False
    )
```

time: 137 us -> 112 us (0.82)
  waiting for transfers between devices: 52.5 us -> 7.33 us
  local copies, waits for them, and re-layouts: 7.72 us -> 37.7 us
  between operations: 13.7 us -> 0.5 us
  other arithmetic: 6.27 us -> 12.5 us
  blocking collectives: 49.3 us -> 44.3 us
  starting transfers between devices: 0.04 us -> 3.7 us
  matrix products: 7.12 us -> 5.61 us
    psum x2 -> x0, waiting for transfers between devices: 52.5 us -> none  [from_root(): return lax.psum(jnp.where(mine, array, jnp.zeros_like(array)), axis)]
    all_gather x4 -> x0, blocking collectives: 49.3 us -> none  [the longest x1 18.5 us: per_device(): source_panel = lax.all_gather(source, 'col', axis=1, tiled=True)]
    all_to_all x0 -> x3, blocking collectives: none -> 44.3 us  [the longest x2 33.6 us: update(): sides = lax.all_to_all(sides, ('row', 'col'), 0, 0, tiled=True)]
    unnamed x12 -> x20, local copies, waits for them, and re-layouts: 0.11 us -> 15.2 us
    mul x1 -> x3, other arithmetic: 0.07 us -> 8.76 us  [the longest x2 8.75 us: update(): jax.nn.sigmoid(values[..., 1, :]) * values[..., 0, :]]
    all_to_all x0 -> x1, waiting for transfers between devices: none -> 7.33 us  [update(): mixed = lax.all_to_all(mixed, ('row', 'col'), 0, 0, tiled=True)]
    slice x1 -> x11, local copies, waits for them, and re-layouts: 0.76 us -> 7.93 us  [the longest x2 3.88 us: update(): values[..., 1, :]]
    reshape x0 -> x10, local copies, waits for them, and re-layouts: none -> 6.69 us  [the longest x2 2.61 us: update(): sides.reshape(peers_r, peers_c, 2, part, rows, cols)]
  transfers between devices with their start and end apart: 2 -> 1, of which waited for: 2 -> 1; matrix products, arithmetic and copies ran while one was open for 2% -> 0% of each run, Pallas kernels for 0% -> 0%
where the time goes in v1:
time: 112 us
  blocking collectives  44.3 us (40%)
  local copies, waits for them, and re-layouts  37.7 us (34%)
  other arithmetic  12.5 us (11%)
  waiting for transfers between devices  7.33 us (7%)
  matrix products  5.61 us (5%)
  starting transfers between devices  3.7 us (3%)
    all_to_all x2, blocking collectives, update(): sides = lax.all_to_all(sides, ('row', 'col'), 0, 0, tiled=True)  33.6 us
    unnamed x20, local copies, waits for them, and re-layouts  15.2 us
    all_to_all x1, blocking collectives, update(): mixed = lax.all_to_all(mixed, ('row', 'col'), 0, 0, tiled=True)  10.8 us
    mul x2, other arithmetic, update(): jax.nn.sigmoid(values[..., 1, :]) * values[..., 0, :]  8.75 us
    all_to_all x1, waiting for transfers between devices, update(): mixed = lax.all_to_all(mixed, ('row', 'col'), 0, 0, tiled=True)  7.33 us
    mul x2, local copies, waits for them, and re-layouts, update(): jax.nn.sigmoid(values[..., 1, :]) * values[..., 0, :]  4.89 us
    slice x2, local copies, waits for them, and re-layouts, update(): values[..., 1, :]  3.88 us
    all_to_all x1, starting transfers between devices, update(): mixed = lax.all_to_all(mixed, ('row', 'col'), 0, 0, tiled=True)  3.7 us
  transfers between devices with their start and end apart: 1, of which 1 were waited for; matrix products, arithmetic and copies ran while one was open for 0% of the time, Pallas kernels for 0%

profile of v1, /device:TPU:0, one launch (start us, length us, event | category | flops | bytes accessed | tf_op | source)
XLA Modules:
  0.0 111.7 jit_solution(2831482869109406955)
XLA Ops:
  0.0 0.7 convert_element_type.71
  0.7 0.8 slice_reduce_fusion
  1.8 1.1 convert_reduce_fusion
  2.9 1.2 %fusion.25 = f32[24,24]{1,0:T(8,128)S(1)} fusion(bf16[24,24,128]{2,1,0:T(8,128)(2,1)} %param.10, f32[24,24]{1,0:T(8,128)S(1)} %broadcast_multiply_fusion.1), kind=kLoop, calls=%fused_computation.45 | loop fusion | flops 294336 | bytes 152064 | tf_op jit(solution)/shard_map/reduce_sum | solution.py:9
  4.1 0.8 slice_bitcast_fusion.3
  4.8 1.5 %convolution_add_fusion.1 = f32[24,24,640]{2,1,0:T(8,128)S(1)} fusion(f32[640]{0:T(1024)S(1)} %get-tuple-element.6, bf16[2,128,640]{2,1,0:T(8,128)(2,1)} %param.14, bf16[24,24,128]{2,1,0:T(8,128)(2,1)} %param.10, f32[128]{0:T(128)S(1)} %get-tuple-element.24, f32[128]{0:T(128)S(1)} %get-tuple-element.29, f32[24,24]{1,0:T(8,128)S(1)} %add_rsqrt_fusion.1, ...), kind=kOutput, calls=%fused_computation.3 | convolution fusion | flops 95182848 | bytes 1794048 | tf_op jit(solution)/shard_map/dot_general | solution.py:19
  6.4 1.1 copy-done
  7.5 0.1 slice.117
  7.6 0.8 reshape.177
  8.4 1.9 %fusion.57 = (f32[24,24,2,1,128]{4,3,2,1,0:T(1,128)}, f32[24,24,2,1,128]{4,3,2,1,0:T(1,128)}) fusion(f32[24,24,2,2,128]{4,3,2,1,0:T(2,128)S(1)} %reshape.177), kind=kLoop, calls=%fused_computation.101 | loop fusion | bytes 2359296 | tf_op jit(solution)/shard_map/slice | solution.py:21
  10.3 2.6 %copy.40 = f32[24,24,2,1,128]{1,0,4,2,3:T(8,128)S(1)} copy(f32[24,24,2,1,128]{4,3,2,1,0:T(1,128)} %get-tuple-element.13) | data formatting | bytes 1179648
  13.0 3.8 %copy.41 = f32[24,24,2,1,128]{1,0,4,2,3:T(8,128)} copy(f32[24,24,2,1,128]{4,3,2,1,0:T(1,128)} %get-tuple-element.14) | data formatting | bytes 1179648
  16.8 4.4 %divide_multiply_fusion.1 = f32[24,24,2,1,128]{1,0,4,2,3:T(8,128)} fusion(f32[24,24,2,1,128]{1,0,4,2,3:T(8,128)} %copy.41, f32[24,24,2,1,128]{1,0,4,2,3:T(8,128)S(1)} %copy.40), kind=kLoop, calls=%fused_computation.1 | loop fusion | flops 589824 | bytes 1769472 | tf_op jit(solution)/shard_map/mul | solution.py:21
  21.2 2.4 %reshape.187 = f32[576,2,16,8]{0,3,2,1:T(8,128)S(1)} reshape(f32[24,24,2,1,128]{1,0,4,2,3:T(8,128)} %divide_multiply_fusion.1) | data formatting | bytes 1179648 | tf_op jit(solution)/shard_map/mul | solution.py:21
  23.7 18.6 %all_to_all.20 = bf16[16,16,576]{2,1,0:T(8,128)(2,1)S(1)} all-to-all(bf16[16,16,576]{2,1,0:T(8,128)(2,1)S(1)} %copy_bitcast_fusion.3), channel_id=1, replica_groups=mesh['groups'=2,'row'=4,'col'=4] {'row','col'}, dimensions={0} | all-to-all | bytes 589824 | tf_op jit(solution)/shard_map/all_to_all | solution.py:26
  42.4 1.3 %reshape.179 = bf16[4,4,2,8,24,24]{5,4,3,2,1,0:T(8,128)(2,1)S(1)} reshape(bf16[16,16,576]{2,1,0:T(8,128)(2,1)S(1)} %all_to_all.20) | data formatting | bytes 589824 | tf_op jit(solution)/shard_map/reshape | solution.py:27
  43.7 0.3 fusion.55
  44.0 0.6 copy.30
  44.6 0.4 squeeze.35
  45.0 0.6 copy.29
  45.6 0.4 squeeze.34
  46.0 0.2 convolution_convert_fusion.1
  46.3 0.3 reshape.180
  46.8 1.1 %reshape.181 = bf16[16,8,576]{2,1,0:T(8,128)(2,1)} reshape(bf16[4,4,8,24,24]{4,3,2,1,0:T(8,128)(2,1)S(1)} %bitcast.120) | data formatting | bytes 294912 | tf_op jit(solution)/shard_map/reshape | solution.py:31
  47.9 3.7 %all-to-all-start.1 = ((bf16[16,8,576]{2,1,0:T(8,128)(2,1)}), bf16[16,8,576]{2,1,0:T(8,128)(2,1)S(1)}, u32[]{:S(2)}, u32[]{:S(2)}) async-start(bf16[16,8,576]{2,1,0:T(8,128)(2,1)} %reshape.181), calls=%async_computation.1 | async-start | bytes 327680 | tf_op jit(solution)/shard_map/all_to_all | solution.py:32
  51.7 7.3 %all-to-all-done.1 = bf16[16,8,576]{2,1,0:T(8,128)(2,1)S(1)} async-done(((bf16[16,8,576]{2,1,0:T(8,128)(2,1)}), bf16[16,8,576]{2,1,0:T(8,128)(2,1)S(1)}, u32[]{:S(2)}, u32[]{:S(2)}) %all-to-all-start.1) | async-done | bytes 147488 | tf_op jit(solution)/shard_map/all_to_all | solution.py:32
  59.4 1.3 %fusion.59 = (f32[24,24]{1,0:T(8,128)S(1)}, f32[24,24,128]{2,1,0:T(8,128)S(1)}) fusion(f32[128]{0:T(128)S(1)} %get-tuple-element.16, bf16[24,24,128]{2,1,0:T(8,128)(2,1)S(1)} %bitcast.122, bf16[2,128,128]{2,1,0:T(8,128)(2,1)S(1)} %copy-done.7, f32[24,24,640]{2,1,0:T(8,128)} %copy-done, bf16[24,24,128]{2,1,0:T(8,128)(2,1)S(1)} %copy-done.2), kind=kOutput, calls=%fused_computation.103 | convolution fusion | flops 19611072 | bytes 920320 | tf_op jit(solution)/shard_map/dot_general | solution.py:48
  60.7 0.3 multiply_reduce_fusion
  61.0 0.5 convolution_add_fusion
  61.6 1.1 copy-done.1
  62.8 0.8 reshape.182
  63.6 1.9 %fusion.56 = (f32[24,24,2,1,128]{4,3,2,1,0:T(1,128)}, f32[24,24,2,1,128]{4,3,2,1,0:T(1,128)}) fusion(f32[24,24,2,2,128]{4,3,2,1,0:T(2,128)S(1)} %reshape.182), kind=kLoop, calls=%fused_computation.100 | loop fusion | bytes 2359296 | tf_op jit(solution)/shard_map/slice | solution.py:21
  65.6 2.6 %copy.42 = f32[24,24,2,1,128]{1,0,4,2,3:T(8,128)S(1)} copy(f32[24,24,2,1,128]{4,3,2,1,0:T(1,128)} %get-tuple-element.11) | data formatting | bytes 1179648
  68.2 3.8 %copy.43 = f32[24,24,2,1,128]{1,0,4,2,3:T(8,128)} copy(f32[24,24,2,1,128]{4,3,2,1,0:T(1,128)} %get-tuple-element.12) | data formatting | bytes 1179648
  72.0 4.4 %divide_multiply_fusion = f32[24,24,2,1,128]{1,0,4,2,3:T(8,128)} fusion(f32[24,24,2,1,128]{1,0,4,2,3:T(8,128)} %copy.43, f32[24,24,2,1,128]{1,0,4,2,3:T(8,128)S(1)} %copy.42), kind=kLoop, calls=%fused_computation | loop fusion | flops 589824 | bytes 1769472 | tf_op jit(solution)/shard_map/mul | solution.py:21
  76.4 2.4 %reshape.188 = f32[576,2,16,8]{0,3,2,1:T(8,128)S(1)} reshape(f32[24,24,2,1,128]{1,0,4,2,3:T(8,128)} %divide_multiply_fusion) | data formatting | bytes 1179648 | tf_op jit(solution)/shard_map/mul | solution.py:21
  78.9 14.9 %all_to_all.21 = bf16[16,16,576]{2,1,0:T(8,128)(2,1)S(1)} all-to-all(bf16[16,16,576]{2,1,0:T(8,128)(2,1)S(1)} %copy_bitcast_fusion.2), channel_id=1, replica_groups=mesh['groups'=2,'row'=4,'col'=4] {'row','col'}, dimensions={0} | all-to-all | bytes 589824 | tf_op jit(solution)/shard_map/all_to_all | solution.py:26
  93.8 1.3 %reshape.184 = bf16[4,4,2,8,24,24]{5,4,3,2,1,0:T(8,128)(2,1)S(1)} reshape(bf16[16,16,576]{2,1,0:T(8,128)(2,1)S(1)} %all_to_all.21) | data formatting | bytes 589824 | tf_op jit(solution)/shard_map/reshape | solution.py:27
  95.2 0.3 fusion.54
  95.4 0.6 copy.37
  96.1 0.4 squeeze.40
  96.5 0.6 copy.36
  97.1 0.4 squeeze.39
  97.5 0.2 convolution_convert_fusion
  97.7 0.3 reshape.185
  98.1 0.5 reshape.186
  98.6 10.8 %all_to_all.22 = bf16[16,8,576]{2,1,0:T(8,128)(2,1)S(1)} all-to-all(bf16[16,8,576]{2,1,0:T(8,128)(2,1)S(1)} %reshape.186), channel_id=1, replica_groups=mesh['groups'=2,'row'=4,'col'=4] {'row','col'}, dimensions={0} | all-to-all | bytes 294912 | tf_op jit(solution)/shard_map/all_to_all | solution.py:32
  109.8 1.9 %fusion.6 = bf16[24,24,128]{2,1,0:T(8,128)(2,1)} fusion(f32[24,24,128]{2,1,0:T(8,128)S(1)} %get-tuple-element.28, bf16[24,24,128]{2,1,0:T(8,128)(2,1)S(1)} %bitcast.123, f32[24,24,640]{2,1,0:T(8,128)} %copy-done.1, f32[128]{0:T(128)S(1)} %get-tuple-element.15, bf16[2,128,128]{2,1,0:T(8,128)(2,1)S(1)} %copy-done.7), kind=kOutput, calls=%fused_computation.14 | convolution fusion | flops 19390464 | bytes 918016 | tf_op jit(solution)/shard_map/dot_general | solution.py:48
  (43 shorter events, 1.7 us)
Async XLA Ops:
  6.4 1.1 copy-start
  45.0 6.7 %copy-start.4 = (f32[2,128]{1,0:T(2,128)S(1)}, f32[2,128]{1,0:T(2,128)}, u32[]{:S(2)}) copy-start(f32[2,128]{1,0:T(2,128)} %param.19) | copy-start | bytes 3076
  45.0 6.7 %copy-start.5 = (f32[2,128]{1,0:T(2,128)S(1)}, f32[2,128]{1,0:T(2,128)}, u32[]{:S(2)}) copy-start(f32[2,128]{1,0:T(2,128)} %param.17) | copy-start | bytes 3076
  45.0 6.7 %copy-start.6 = (f32[2,128]{1,0:T(2,128)S(1)}, f32[2,128]{1,0:T(2,128)}, u32[]{:S(2)}) copy-start(f32[2,128]{1,0:T(2,128)} %param.16) | copy-start | bytes 3076
  45.6 13.8 %copy-start.2 = (bf16[24,24,128]{2,1,0:T(8,128)(2,1)S(1)}, bf16[24,24,128]{2,1,0:T(8,128)(2,1)}, u32[]{:S(2)}) copy-start(bf16[24,24,128]{2,1,0:T(8,128)(2,1)} %param.10) | copy-start | bytes 442372
  45.6 13.8 %copy-start.7 = (bf16[2,128,128]{2,1,0:T(8,128)(2,1)S(1)}, bf16[2,128,128]{2,1,0:T(8,128)(2,1)}, u32[]{:S(2)}) copy-start(bf16[2,128,128]{2,1,0:T(8,128)(2,1)} %param.18) | copy-start | bytes 196612
  46.6 14.4 %copy-start.3 = (bf16[2,128,640]{2,1,0:T(8,128)(2,1)S(1)}, bf16[2,128,640]{2,1,0:T(8,128)(2,1)}, u32[]{:S(2)}) copy-start(bf16[2,128,640]{2,1,0:T(8,128)(2,1)} %param.14) | copy-start | bytes 983044
  47.9 11.1 %all-to-all-start.1 = ((bf16[16,8,576]{2,1,0:T(8,128)(2,1)}), bf16[16,8,576]{2,1,0:T(8,128)(2,1)S(1)}, u32[]{:S(2)}, u32[]{:S(2)}) async-start(bf16[16,8,576]{2,1,0:T(8,128)(2,1)} %reshape.181), calls=%async_computation.1 | async-start | bytes 327680 | tf_op jit(solution)/shard_map/all_to_all | solution.py:32
  61.6 1.1 copy-start.1

commit v2 on v1

v2 whole, which is shorter than its diff:
```python
import jax
import jax.numpy as jnp
from jax import lax
from jax.sharding import PartitionSpec as P


def norm_rows(values, gain, shift):
    center = values - jnp.mean(values, axis=-1, keepdims=True)
    spread = jnp.mean(center * center, axis=-1, keepdims=True)
    return center * lax.rsqrt(spread + 1e-05) * gain + shift


def project(pair, grid, in_gain, in_shift, w_in, bias_in, hidden):
    normed = norm_rows(pair.astype(jnp.float32), in_gain, in_shift).astype(jnp.bfloat16)
    product = jnp.dot(normed, w_in, preferred_element_type=jnp.float32) + bias_in
    gates = jax.nn.sigmoid(product[..., hidden : 2 * hidden]), jax.nn.sigmoid(product[..., 3 * hidden : 4 * hidden])
    left = (gates[0] * product[..., :hidden] * grid[..., None]).astype(jnp.bfloat16)
    right = (gates[1] * product[..., 2 * hidden : 3 * hidden] * grid[..., None]).astype(jnp.bfloat16)
    return left, right, jax.nn.sigmoid(product[..., 4 * hidden :])


def finish(pair, mixed, gating, out_gain, out_shift, w_out, bias_out):
    normout = norm_rows(mixed, out_gain, out_shift).astype(jnp.bfloat16)
    result = gating * (jnp.dot(normout, w_out, preferred_element_type=jnp.float32) + bias_out)
    return (pair.astype(jnp.float32) + result).astype(jnp.bfloat16)


def solution(mesh):
    n = mesh.shape["col"]

    def along(block, axis, step):
        return lax.ppermute(block, axis, [(k, (k + step) % n) for k in range(n)]) if step else block

    def across(block, step):
        pairs = [(a * n + z, z * n + (a + step) % n) for a in range(n) for z in range(n)]
        return lax.ppermute(block, ("row", "col"), pairs)

    def matched(blocks):
        start = lax.rem(lax.axis_index("row") - lax.axis_index("col") + n, n)
        return lax.dynamic_slice_in_dim(jnp.concatenate([jnp.stack(blocks)] * 2), start, n)

    def per_device(pair, token_mask, in_gain, in_shift, w_in, bias_in, out_gain, out_shift, w_out, bias_out):
        rows, cols, _ = pair.shape
        hidden = w_out.shape[1]
        present = token_mask.astype(jnp.float32)
        row_mask = lax.dynamic_slice_in_dim(present, lax.axis_index("row") * rows, rows)
        col_mask = lax.dynamic_slice_in_dim(present, lax.axis_index("col") * cols, cols)
        grid = row_mask[:, None] * col_mask[None, :]
        left, right, gating = project(pair, grid, in_gain[0], in_shift[0], w_in[0], bias_in[0], hidden)
        mirrored = across(right, 0)
        lefts = jnp.stack([along(left, "col", step) for step in range(n)])
        rights = matched([along(mirrored, "row", step) for step in range(n)])
        mixed = jnp.einsum("sikh,sjkh->ijh", lefts, rights, preferred_element_type=jnp.float32)
        pair = finish(pair, mixed, gating, out_gain[0], out_shift[0], w_out[0], bias_out[0])
        left, right, gating = project(pair, grid, in_gain[1], in_shift[1], w_in[1], bias_in[1], hidden)
        lefts = jnp.stack([across(left, step) for step in range(n)])
        rights = matched([along(right, "row", step) for step in range(n)])
        mixed = jnp.einsum("skih,skjh->ijh", lefts, rights, preferred_element_type=jnp.float32)
        return finish(pair, mixed, gating, out_gain[1], out_shift[1], w_out[1], bias_out[1])

    placed = (P(("groups", "row"), "col", None), P("groups")) + (P(),) * 8
    return jax.shard_map(
        per_device, mesh=mesh, in_specs=placed, out_specs=P(("groups", "row"), "col", None), check_vma=False
    )
```

time: 112 us -> 107 us (0.955)
  blocking collectives: 44.3 us -> 0 us
  waiting for transfers between devices: 7.33 us -> 31.2 us
  starting transfers between devices: 3.7 us -> 19.7 us
  matrix products: 5.61 us -> 14.3 us
  local copies, waits for them, and re-layouts: 37.7 us -> 32.6 us
  other arithmetic: 12.5 us -> 7.97 us
    all_to_all x3 -> x0, blocking collectives: 44.3 us -> none  [the longest x2 33.6 us: update(): sides = lax.all_to_all(sides, ('row', 'col'), 0, 0, tiled=True)]
    ppermute x0 -> x14, waiting for transfers between devices: none -> 31.2 us  [the longest x9 31.2 us: along(): lax.ppermute(block, axis, [(k, (k + step) % n) for k in range(n)])]
    ppermute x0 -> x14, starting transfers between devices: none -> 19.7 us  [the longest x9 11.9 us: along(): lax.ppermute(block, axis, [(k, (k + step) % n) for k in range(n)])]
    dynamic_slice x1 -> x5, local copies, waits for them, and re-layouts: 0.08 us -> 14.1 us  [the longest x4 14 us: matched(): lax.dynamic_slice_in_dim(jnp.concatenate([jnp.stack(blocks)] * 2), start, n)]
    unnamed x20 -> x29, local copies, waits for them, and re-layouts: 15.2 us -> 1.5 us
    another operation x0 -> x2, local copies, waits for them, and re-layouts: none -> 11.5 us  [the longest x1 6.03 us: per_device(): lefts = jnp.stack([across(left, step) for step in range(n)])]
    mul x2 -> x0, other arithmetic: 8.75 us -> none  [update(): jax.nn.sigmoid(values[..., 1, :]) * values[..., 0, :]]
    dot_general x6, matrix products: 5.61 us -> 14.3 us  [the longest x1 4.72 us: per_device(): jnp.einsum('skih,skjh->ijh', lefts, rights, preferred_element_type=jnp.fl...]
  transfers between devices with their start and end apart: 1 -> 14, of which waited for: 1 -> 5; matrix products, arithmetic and copies ran while one was open for 0% -> 14% of each run, Pallas kernels for 0% -> 0%
where the time goes in v2:
time: 107 us; the launch traced here: 106 us
  local copies, waits for them, and re-layouts  32.6 us (30%)
  waiting for transfers between devices  31.2 us (29%)
  starting transfers between devices  19.7 us (18%)
  matrix products  14.3 us (13%)
  other arithmetic  7.97 us (7%)
    ppermute x9, waiting for transfers between devices, along(): lax.ppermute(block, axis, [(k, (k + step) % n) for k in range(n)])  31.2 us
    dynamic_slice x4, local copies, waits for them, and re-layouts, matched(): lax.dynamic_slice_in_dim(jnp.concatenate([jnp.stack(blocks)] * 2), start, n)  14 us
    ppermute x9, starting transfers between devices, along(): lax.ppermute(block, axis, [(k, (k + step) % n) for k in range(n)])  11.9 us
    ppermute x5, starting transfers between devices, across(): return lax.ppermute(block, ('row', 'col'), pairs)  7.79 us
    another operation x1, local copies, waits for them, and re-layouts, per_device(): lefts = jnp.stack([across(left, step) for step in range(n)])  6.03 us
    another operation x1, local copies, waits for them, and re-layouts, per_device(): lefts = jnp.stack([along(left, 'col', step) for step in range(n)])  5.49 us
    dot_general x1, matrix products, per_device(): jnp.einsum('skih,skjh->ijh', lefts, rights, preferred_element_type=jnp.fl...  4.72 us
    dot_general x1, matrix products, per_device(): jnp.einsum('sikh,sjkh->ijh', lefts, rights, preferred_element_type=jnp.fl...  4.1 us
  transfers between devices with their start and end apart: 14, of which 5 were waited for; matrix products, arithmetic and copies ran while one was open for 14% of the time, Pallas kernels for 0%

profile of v2, /device:TPU:0, one launch (start us, length us, event | category | flops | bytes accessed | tf_op | source)
XLA Modules:
  0.0 106.2 jit_solution(13830693165017533132)
XLA Ops:
  0.0 0.7 convert_element_type.43
  0.7 0.8 slice_reduce_fusion
  1.4 1.1 convert_reduce_fusion
  2.5 1.2 %fusion.9 = f32[24,24]{1,0:T(8,128)S(1)} fusion(bf16[24,24,128]{2,1,0:T(8,128)(2,1)} %param.10, f32[24,24]{1,0:T(8,128)S(1)} %broadcast_multiply_fusion.4), kind=kLoop, calls=%fused_computation.19 | loop fusion | flops 294336 | bytes 152064 | tf_op jit(solution)/shard_map/reduce_sum | solution.py:9
  3.7 0.8 slice_bitcast_fusion.3
  4.5 0.1 fusion.65
  4.6 0.1 broadcast_multiply_fusion
  4.6 1.5 %convolution_add_fusion.1 = f32[24,24,640]{2,1,0:T(8,128)S(1)} fusion(f32[640]{0:T(1024)S(1)} %get-tuple-element.6, bf16[2,128,640]{2,1,0:T(8,128)(2,1)} %param.14, bf16[24,24,128]{2,1,0:T(8,128)(2,1)} %param.10, f32[128]{0:T(128)S(1)} %get-tuple-element.20, f32[128]{0:T(128)S(1)} %get-tuple-element.29, f32[24,24]{1,0:T(8,128)S(1)} %add_rsqrt_fusion.3, ...), kind=kOutput, calls=%fused_computation.3 | convolution fusion | flops 95182848 | bytes 1794048 | tf_op jit(solution)/shard_map/dot_general | solution.py:15
  6.2 1.1 %copy-done = f32[24,24,640]{2,1,0:T(8,128)} copy-done((f32[24,24,640]{2,1,0:T(8,128)}, f32[24,24,640]{2,1,0:T(8,128)S(1)}, u32[]{:S(2)}) %copy-start) | copy-done | bytes 1474584
  7.3 0.2 fusion.27
  7.5 5.1 %collective-permute-start.6 = (bf16[24,24,128]{2,1,0:T(8,128)(2,1)S(1)}, bf16[24,24,128]{2,1,0:T(8,128)(2,1)S(1)}, u32[]{:S(2)}, u32[]{:S(2)}) collective-permute-start(bf16[24,24,128]{2,1,0:T(8,128)(2,1)S(1)} %get-tuple-element.9), channel_id=1, source_target_pairs={{0,3},{1,0},{2,1},{3,2},{4,7},{5,4},{6,5},{7,6},{8,11},{9,8},{10,9... | collective-permute-start | bytes 442376 | tf_op jit(solution)/shard_map/ppermute | solution.py:32
  12.6 1.0 collective-permute-start.4
  13.6 0.7 collective-permute-start
  14.3 2.6 %collective-permute-done.6 = bf16[24,24,128]{2,1,0:T(8,128)(2,1)S(1)} collective-permute-done((bf16[24,24,128]{2,1,0:T(8,128)(2,1)S(1)}, bf16[24,24,128]{2,1,0:T(8,128)(2,1)S(1)}, u32[]{:S(2)}, u32[]{:S(2)}) %collective-permute-start.6) | collective-permute-done | bytes 147488 | tf_op jit(solution)/shard_map/ppermute | solution.py:32
  16.9 12.1 %collective-permute-done.5 = bf16[24,24,128]{2,1,0:T(8,128)(2,1)S(1)} collective-permute-done((bf16[24,24,128]{2,1,0:T(8,128)(2,1)S(1)}, bf16[24,24,128]{2,1,0:T(8,128)(2,1)S(1)}, u32[]{:S(2)}, u32[]{:S(2)}) %collective-permute-start.5) | collective-permute-done | bytes 147488 | tf_op jit(solution)/shard_map/ppermute | solution.py:32
  29.0 0.9 pad_maximum_fusion
  29.8 5.5 %copy.46 = bf16[4,24,24,128]{2,1,0,3:T(8,128)(2,1)S(1)} copy(bf16[4,24,24,128]{3,2,1,0:T(8,128)(2,1)} %pad_maximum_fusion) | data formatting | bytes 1179648 | tf_op jit(solution)/shard_map/stack | solution.py:51
  35.4 0.3 collective-permute-start.2
  35.7 0.2 collective-permute-start.1
  35.9 7.6 %collective-permute-done.1 = bf16[24,24,128]{2,1,0:T(8,128)(2,1)S(1)} collective-permute-done((bf16[24,24,128]{2,1,0:T(8,128)(2,1)S(1)}, bf16[24,24,128]{2,1,0:T(8,128)(2,1)S(1)}, u32[]{:S(2)}, u32[]{:S(2)}) %collective-permute-start.1) | collective-permute-done | bytes 147488 | tf_op jit(solution)/shard_map/ppermute | solution.py:32
  43.8 0.9 constant_dynamic-slice_fusion.1
  44.7 6.0 %copy.45 = bf16[4,24,24,128]{2,1,0,3:T(8,128)(2,1)} copy(bf16[4,24,24,128]{3,2,1,0:T(8,128)(2,1)} %constant_dynamic-slice_fusion.1) | data formatting | bytes 1179648 | tf_op jit(solution)/shard_map/dynamic_slice | solution.py:40
  50.7 4.1 %bitcast_reduce_fusion.1 = (f32[24,24]{0,1:T(8,128)S(1)}, f32[128,24,24,1]{2,1,3,0:T(8,128)}) fusion(bf16[4,24,24,128]{2,1,0,3:T(8,128)(2,1)} %copy.45, bf16[4,24,24,128]{2,1,0,3:T(8,128)(2,1)S(1)} %copy.46), kind=kOutput, calls=%fused_computation.1 | convolution fusion | flops 14228928 | bytes 1476864 | tf_op jit(solution)/shard_map/sikh,sjkh->ijh/dot_general | solution.py:53
  54.9 0.1 copy.49
  54.9 1.9 %copy.47 = f32[128,24,24]{0,1,2:T(8,128)S(1)} copy(f32[128,24,24]{2,1,0:T(8,128)} %bitcast.100) | data formatting | bytes 589824 | tf_op jit(solution)/shard_map/sikh,sjkh->ijh/dot_general | solution.py:53
  56.8 0.3 multiply_reduce_fusion.2
  57.1 1.5 %fusion.66 = (f32[24,24]{1,0:T(8,128)S(1)}, f32[24,24,128]{2,1,0:T(8,128)S(1)}) fusion(f32[128]{0:T(128)S(1)} %get-tuple-element.16, bf16[2,128,128]{2,1,0:T(8,128)(2,1)S(1)} %copy-done.7, f32[128,24,24]{0,1,2:T(8,128)S(1)} %copy.47, f32[128]{0:T(128)S(1)} %get-tuple-element.31, f32[128]{0:T(128)S(1)} %get-tuple-element.12, ...), kind=kOutput, calls=%fused_computation.131 | convolution fusion | flops 19979712 | bytes 1093376 | tf_op jit(solution)/shard_map/dot_general | solution.py:24
  58.6 0.3 multiply_reduce_fusion.1
  58.9 0.5 convolution_add_fusion
  59.5 0.1 bitcast_dynamic-update-slice_fusion.6
  59.7 0.9 fusion.14
  60.6 1.7 %collective-permute-start.13 = (bf16[24,24,128]{2,1,0:T(8,128)(2,1)}, bf16[24,24,128]{2,1,0:T(8,128)(2,1)}, u32[]{:S(2)}, u32[]{:S(2)}) collective-permute-start(bf16[24,24,128]{2,1,0:T(8,128)(2,1)} %fusion.14), channel_id=1, source_target_pairs={{0,3},{1,7},{2,11},{3,15},{4,0},{5,4},{6,8},{7,12},{8,1},{9,5},{10... | collective-permute-start | bytes 442376 | tf_op jit(solution)/shard_map/ppermute | solution.py:36
  62.3 2.3 %collective-permute-start.12 = (bf16[24,24,128]{2,1,0:T(8,128)(2,1)}, bf16[24,24,128]{2,1,0:T(8,128)(2,1)}, u32[]{:S(2)}, u32[]{:S(2)}) collective-permute-start(bf16[24,24,128]{2,1,0:T(8,128)(2,1)} %fusion.14), channel_id=1, source_target_pairs={{0,2},{1,6},{2,10},{3,14},{4,3},{5,7},{6,11},{7,15},{8,0},{9,4},{1... | collective-permute-start | bytes 442376 | tf_op jit(solution)/shard_map/ppermute | solution.py:36
  64.5 0.4 collective-permute-start.11
  64.9 2.8 %collective-permute-start.10 = (bf16[24,24,128]{2,1,0:T(8,128)(2,1)}, bf16[24,24,128]{2,1,0:T(8,128)(2,1)}, u32[]{:S(2)}, u32[]{:S(2)}) collective-permute-start(bf16[24,24,128]{2,1,0:T(8,128)(2,1)} %fusion.14), channel_id=1, source_target_pairs={{0,0},{1,4},{2,8},{3,12},{4,1},{5,5},{6,9},{7,13},{8,2},{9,6},{10,... | collective-permute-start | bytes 442376 | tf_op jit(solution)/shard_map/ppermute | solution.py:36
  67.7 2.8 %collective-permute-start.8 = (bf16[24,24,128]{2,1,0:T(8,128)(2,1)S(1)}, bf16[24,24,128]{2,1,0:T(8,128)(2,1)S(1)}, u32[]{:S(2)}, u32[]{:S(2)}) collective-permute-start(bf16[24,24,128]{2,1,0:T(8,128)(2,1)S(1)} %get-tuple-element.8), channel_id=1, source_target_pairs={{0,8},{4,12},{8,0},{12,4},{1,9},{5,13},{9,1},{13,5},{2,10},{6,14},... | collective-permute-start | bytes 442376 | tf_op jit(solution)/shard_map/ppermute | solution.py:32
  70.5 6.3 %collective-permute-done.8 = bf16[24,24,128]{2,1,0:T(8,128)(2,1)S(1)} collective-permute-done((bf16[24,24,128]{2,1,0:T(8,128)(2,1)S(1)}, bf16[24,24,128]{2,1,0:T(8,128)(2,1)S(1)}, u32[]{:S(2)}, u32[]{:S(2)}) %collective-permute-start.8) | collective-permute-done | bytes 147488 | tf_op jit(solution)/shard_map/ppermute | solution.py:32
  76.8 2.4 %collective-permute-start.9 = (bf16[24,24,128]{2,1,0:T(8,128)(2,1)S(1)}, bf16[24,24,128]{2,1,0:T(8,128)(2,1)S(1)}, u32[]{:S(2)}, u32[]{:S(2)}) collective-permute-start(bf16[24,24,128]{2,1,0:T(8,128)(2,1)S(1)} %get-tuple-element.8), channel_id=1, source_target_pairs={{0,12},{4,0},{8,4},{12,8},{1,13},{5,1},{9,5},{13,9},{2,14},{6,2},{... | collective-permute-start | bytes 442376 | tf_op jit(solution)/shard_map/ppermute | solution.py:32
  79.3 2.6 %collective-permute-done.9 = bf16[24,24,128]{2,1,0:T(8,128)(2,1)S(1)} collective-permute-done((bf16[24,24,128]{2,1,0:T(8,128)(2,1)S(1)}, bf16[24,24,128]{2,1,0:T(8,128)(2,1)S(1)}, u32[]{:S(2)}, u32[]{:S(2)}) %collective-permute-start.9) | collective-permute-done | bytes 147488 | tf_op jit(solution)/shard_map/ppermute | solution.py:32
  82.1 0.9 constant_dynamic-slice_fusion
  83.0 6.2 %copy.52 = bf16[4,24,24,128]{1,2,0,3:T(8,128)(2,1)S(1)} copy(bf16[4,24,24,128]{3,2,1,0:T(8,128)(2,1)} %constant_dynamic-slice_fusion) | data formatting | bytes 1179648 | tf_op jit(solution)/shard_map/dynamic_slice | solution.py:40
  89.2 2.0 %pad_maximum_fusion.1 = bf16[4,24,24,128]{3,2,1,0:T(8,128)(2,1)} fusion(bf16[1,24,24,128]{3,2,1,0:T(8,128)(2,1)} %bitcast.32, bf16[1,24,24,128]{3,2,1,0:T(8,128)(2,1)} %bitcast.31, bf16[1,24,24,128]{3,2,1,0:T(8,128)(2,1)} %bitcast.30, bf16[1,24,24,128]{3,2,1,0:T(8,128)(2,1)} %bitcast.29), kind=kLoop, calls=%fused_computation.14 | loop fusion | flops 884736 | bytes 1179648 | tf_op jit(solution)/shard_map/stack | solution.py:56
  91.3 6.0 %copy.53 = bf16[4,24,24,128]{2,1,0,3:T(8,128)(2,1)} copy(bf16[4,24,24,128]{3,2,1,0:T(8,128)(2,1)} %pad_maximum_fusion.1) | data formatting | bytes 1179648 | tf_op jit(solution)/shard_map/stack | solution.py:56
  97.3 4.7 %bitcast_reduce_fusion = (f32[24,24]{0,1:T(8,128)S(1)}, f32[128,24,24,1]{2,1,3,0:T(8,128)}) fusion(bf16[4,24,24,128]{1,2,0,3:T(8,128)(2,1)S(1)} %copy.52, bf16[4,24,24,128]{2,1,0,3:T(8,128)(2,1)} %copy.53), kind=kOutput, calls=%fused_computation | convolution fusion | flops 14228928 | bytes 1476864 | tf_op jit(solution)/shard_map/skih,skjh->ijh/dot_general | solution.py:58
  102.0 0.1 copy.56
  102.1 1.9 %copy.54 = f32[128,24,24]{0,1,2:T(8,128)S(1)} copy(f32[128,24,24]{2,1,0:T(8,128)} %bitcast.101) | data formatting | bytes 589824 | tf_op jit(solution)/shard_map/skih,skjh->ijh/dot_general | solution.py:58
  104.0 0.3 multiply_reduce_fusion
  104.2 2.0 %fusion.6 = bf16[24,24,128]{2,1,0:T(8,128)(2,1)} fusion(f32[24,24,128]{2,1,0:T(8,128)S(1)} %get-tuple-element.26, f32[24,24,640]{2,1,0:T(8,128)} %copy-done.1, f32[128,24,24]{0,1,2:T(8,128)S(1)} %copy.54, f32[128]{0:T(128)S(1)} %get-tuple-element.15, f32[128]{0:T(128)S(1)} %get-tuple-element.32, f32[128]{0:T(128)S(1)} %get-tuple-element.11, ...), kind=kOutput, calls=%fused_computation.12 | convolution fusion | flops 19759104 | bytes 1091072 | tf_op jit(solution)/shard_map/dot_general | solution.py:24
  (52 shorter events, 0.6 us)
Async XLA Ops:
  6.2 1.1 %copy-start = (f32[24,24,640]{2,1,0:T(8,128)}, f32[24,24,640]{2,1,0:T(8,128)S(1)}, u32[]{:S(2)}) copy-start(f32[24,24,640]{2,1,0:T(8,128)S(1)} %convolution_add_fusion.1) | copy-start | bytes 4423684
  7.3 7.0 %copy-start.5 = (f32[2,128]{1,0:T(2,128)S(1)}, f32[2,128]{1,0:T(2,128)}, u32[]{:S(2)}) copy-start(f32[2,128]{1,0:T(2,128)} %param.19) | copy-start | bytes 3076
  7.3 7.0 %copy-start.6 = (f32[2,128]{1,0:T(2,128)S(1)}, f32[2,128]{1,0:T(2,128)}, u32[]{:S(2)}) copy-start(f32[2,128]{1,0:T(2,128)} %param.17) | copy-start | bytes 3076
  7.3 7.0 %copy-start.4 = (f32[2,128]{1,0:T(2,128)S(1)}, f32[2,128]{1,0:T(2,128)}, u32[]{:S(2)}) copy-start(f32[2,128]{1,0:T(2,128)} %param.16) | copy-start | bytes 3076
  7.5 9.4 %collective-permute-start.6 = (bf16[24,24,128]{2,1,0:T(8,128)(2,1)S(1)}, bf16[24,24,128]{2,1,0:T(8,128)(2,1)S(1)}, u32[]{:S(2)}, u32[]{:S(2)}) collective-permute-start(bf16[24,24,128]{2,1,0:T(8,128)(2,1)S(1)} %get-tuple-element.9), channel_id=1, source_target_pairs={{0,3},{1,0},{2,1},{3,2},{4,7},{5,4},{6,5},{7,6},{8,11},{9,8},{10,9... | collective-permute-start | bytes 442376 | tf_op jit(solution)/shard_map/ppermute | solution.py:32
  12.6 16.4 %collective-permute-start.5 = (bf16[24,24,128]{2,1,0:T(8,128)(2,1)S(1)}, bf16[24,24,128]{2,1,0:T(8,128)(2,1)S(1)}, u32[]{:S(2)}, u32[]{:S(2)}) collective-permute-start(bf16[24,24,128]{2,1,0:T(8,128)(2,1)S(1)} %get-tuple-element.9), channel_id=1, source_target_pairs={{0,2},{1,3},{2,0},{3,1},{4,6},{5,7},{6,4},{7,5},{8,10},{9,11},{10,... | collective-permute-start | bytes 442376 | tf_op jit(solution)/shard_map/ppermute | solution.py:32
  12.6 16.4 %collective-permute-start.4 = (bf16[24,24,128]{2,1,0:T(8,128)(2,1)S(1)}, bf16[24,24,128]{2,1,0:T(8,128)(2,1)S(1)}, u32[]{:S(2)}, u32[]{:S(2)}) collective-permute-start(bf16[24,24,128]{2,1,0:T(8,128)(2,1)S(1)} %get-tuple-element.9), channel_id=1, source_target_pairs={{0,1},{1,2},{2,3},{3,0},{4,5},{5,6},{6,7},{7,4},{8,9},{9,10},{10,1... | collective-permute-start | bytes 442376 | tf_op jit(solution)/shard_map/ppermute | solution.py:32
  13.6 21.7 %collective-permute-start = (bf16[24,24,128]{2,1,0:T(8,128)(2,1)S(1)}, bf16[24,24,128]{2,1,0:T(8,128)(2,1)S(1)}, u32[]{:S(2)}, u32[]{:S(2)}) collective-permute-start(bf16[24,24,128]{2,1,0:T(8,128)(2,1)S(1)} %get-tuple-element.10), channel_id=1, source_target_pairs={{0,0},{1,4},{2,8},{3,12},{4,1},{5,5},{6,9},{7,13},{8,2},{9,6},{10,... | collective-permute-start | bytes 442376 | tf_op jit(solution)/shard_map/ppermute | solution.py:36
  35.4 8.3 %collective-permute-start.3 = (bf16[24,24,128]{2,1,0:T(8,128)(2,1)S(1)}, bf16[24,24,128]{2,1,0:T(8,128)(2,1)S(1)}, u32[]{:S(2)}, u32[]{:S(2)}) collective-permute-start(bf16[24,24,128]{2,1,0:T(8,128)(2,1)S(1)} %collective-permute-done), channel_id=1, source_target_pairs={{0,12},{4,0},{8,4},{12,8},{1,13},{5,1},{9,5},{13,9},{2,14},{6,2},{... | collective-permute-start | bytes 442376 | tf_op jit(solution)/shard_map/ppermute | solution.py:32
  35.4 8.2 %collective-permute-start.2 = (bf16[24,24,128]{2,1,0:T(8,128)(2,1)S(1)}, bf16[24,24,128]{2,1,0:T(8,128)(2,1)S(1)}, u32[]{:S(2)}, u32[]{:S(2)}) collective-permute-start(bf16[24,24,128]{2,1,0:T(8,128)(2,1)S(1)} %collective-permute-done), channel_id=1, source_target_pairs={{0,8},{4,12},{8,0},{12,4},{1,9},{5,13},{9,1},{13,5},{2,10},{6,14},... | collective-permute-start | bytes 442376 | tf_op jit(solution)/shard_map/ppermute | solution.py:32
  35.7 7.9 %collective-permute-start.1 = (bf16[24,24,128]{2,1,0:T(8,128)(2,1)S(1)}, bf16[24,24,128]{2,1,0:T(8,128)(2,1)S(1)}, u32[]{:S(2)}, u32[]{:S(2)}) collective-permute-start(bf16[24,24,128]{2,1,0:T(8,128)(2,1)S(1)} %collective-permute-done), channel_id=1, source_target_pairs={{0,4},{4,8},{8,12},{12,0},{1,5},{5,9},{9,13},{13,1},{2,6},{6,10},{... | collective-permute-start | bytes 442376 | tf_op jit(solution)/shard_map/ppermute | solution.py:32
  54.8 2.3 %copy-start.2 = (bf16[24,24,128]{2,1,0:T(8,128)(2,1)S(1)}, bf16[24,24,128]{2,1,0:T(8,128)(2,1)}, u32[]{:S(2)}) copy-start(bf16[24,24,128]{2,1,0:T(8,128)(2,1)} %param.10) | copy-start | bytes 442372
  54.8 2.3 %copy-start.7 = (bf16[2,128,128]{2,1,0:T(8,128)(2,1)S(1)}, bf16[2,128,128]{2,1,0:T(8,128)(2,1)}, u32[]{:S(2)}) copy-start(bf16[2,128,128]{2,1,0:T(8,128)(2,1)} %param.18) | copy-start | bytes 196612
  57.1 1.8 %copy-start.3 = (bf16[2,128,640]{2,1,0:T(8,128)(2,1)S(1)}, bf16[2,128,640]{2,1,0:T(8,128)(2,1)}, u32[]{:S(2)}) copy-start(bf16[2,128,640]{2,1,0:T(8,128)(2,1)} %param.14) | copy-start | bytes 983044
  59.4 22.5 %copy-start.1 = (f32[24,24,640]{2,1,0:T(8,128)}, f32[24,24,640]{2,1,0:T(8,128)S(1)}, u32[]{:S(2)}) copy-start(f32[24,24,640]{2,1,0:T(8,128)S(1)} %convolution_add_fusion) | copy-start | bytes 4423684
  59.6 8.1 %collective-permute-start.7 = (bf16[24,24,128]{2,1,0:T(8,128)(2,1)S(1)}, bf16[24,24,128]{2,1,0:T(8,128)(2,1)S(1)}, u32[]{:S(2)}, u32[]{:S(2)}) collective-permute-start(bf16[24,24,128]{2,1,0:T(8,128)(2,1)S(1)} %get-tuple-element.8), channel_id=1, source_target_pairs={{0,4},{4,8},{8,12},{12,0},{1,5},{5,9},{9,13},{13,1},{2,6},{6,10},{... | collective-permute-start | bytes 442376 | tf_op jit(solution)/shard_map/ppermute | solution.py:32
  60.6 28.6 %collective-permute-start.13 = (bf16[24,24,128]{2,1,0:T(8,128)(2,1)}, bf16[24,24,128]{2,1,0:T(8,128)(2,1)}, u32[]{:S(2)}, u32[]{:S(2)}) collective-permute-start(bf16[24,24,128]{2,1,0:T(8,128)(2,1)} %fusion.14), channel_id=1, source_target_pairs={{0,3},{1,7},{2,11},{3,15},{4,0},{5,4},{6,8},{7,12},{8,1},{9,5},{10... | collective-permute-start | bytes 442376 | tf_op jit(solution)/shard_map/ppermute | solution.py:36
  62.3 26.9 %collective-permute-start.12 = (bf16[24,24,128]{2,1,0:T(8,128)(2,1)}, bf16[24,24,128]{2,1,0:T(8,128)(2,1)}, u32[]{:S(2)}, u32[]{:S(2)}) collective-permute-start(bf16[24,24,128]{2,1,0:T(8,128)(2,1)} %fusion.14), channel_id=1, source_target_pairs={{0,2},{1,6},{2,10},{3,14},{4,3},{5,7},{6,11},{7,15},{8,0},{9,4},{1... | collective-permute-start | bytes 442376 | tf_op jit(solution)/shard_map/ppermute | solution.py:36
  64.5 24.7 %collective-permute-start.11 = (bf16[24,24,128]{2,1,0:T(8,128)(2,1)}, bf16[24,24,128]{2,1,0:T(8,128)(2,1)}, u32[]{:S(2)}, u32[]{:S(2)}) collective-permute-start(bf16[24,24,128]{2,1,0:T(8,128)(2,1)} %fusion.14), channel_id=1, source_target_pairs={{0,1},{1,5},{2,9},{3,13},{4,2},{5,6},{6,10},{7,14},{8,3},{9,7},{10... | collective-permute-start | bytes 442376 | tf_op jit(solution)/shard_map/ppermute | solution.py:36
  64.9 24.3 %collective-permute-start.10 = (bf16[24,24,128]{2,1,0:T(8,128)(2,1)}, bf16[24,24,128]{2,1,0:T(8,128)(2,1)}, u32[]{:S(2)}, u32[]{:S(2)}) collective-permute-start(bf16[24,24,128]{2,1,0:T(8,128)(2,1)} %fusion.14), channel_id=1, source_target_pairs={{0,0},{1,4},{2,8},{3,12},{4,1},{5,5},{6,9},{7,13},{8,2},{9,6},{10,... | collective-permute-start | bytes 442376 | tf_op jit(solution)/shard_map/ppermute | solution.py:36
  67.7 9.1 %collective-permute-start.8 = (bf16[24,24,128]{2,1,0:T(8,128)(2,1)S(1)}, bf16[24,24,128]{2,1,0:T(8,128)(2,1)S(1)}, u32[]{:S(2)}, u32[]{:S(2)}) collective-permute-start(bf16[24,24,128]{2,1,0:T(8,128)(2,1)S(1)} %get-tuple-element.8), channel_id=1, source_target_pairs={{0,8},{4,12},{8,0},{12,4},{1,9},{5,13},{9,1},{13,5},{2,10},{6,14},... | collective-permute-start | bytes 442376 | tf_op jit(solution)/shard_map/ppermute | solution.py:32
  76.8 5.1 %collective-permute-start.9 = (bf16[24,24,128]{2,1,0:T(8,128)(2,1)S(1)}, bf16[24,24,128]{2,1,0:T(8,128)(2,1)S(1)}, u32[]{:S(2)}, u32[]{:S(2)}) collective-permute-start(bf16[24,24,128]{2,1,0:T(8,128)(2,1)S(1)} %get-tuple-element.8), channel_id=1, source_target_pairs={{0,12},{4,0},{8,4},{12,8},{1,13},{5,1},{9,5},{13,9},{2,14},{6,2},{... | collective-permute-start | bytes 442376 | tf_op jit(solution)/shard_map/ppermute | solution.py:32

commit v3 on v2

v3 whole, which is shorter than its diff:
```python
import functools

import jax
import jax.numpy as jnp
from jax import lax
from jax.experimental import pallas as pl
from jax.experimental.pallas import tpu as pltpu
from jax.sharding import PartitionSpec as P

F32, BF16 = jnp.float32, jnp.bfloat16


def dot(a, b):
    return jnp.dot(a, b, preferred_element_type=F32)


def split(values):
    high = values.astype(BF16)
    return jnp.concatenate([high, (values - high.astype(F32)).astype(BF16)], axis=1)


def constants(width):
    rows = lax.broadcasted_iota(jnp.int32, (2 * width, width), 0)
    cols = lax.broadcasted_iota(jnp.int32, (2 * width, width), 1)
    mean = jnp.full((2 * width, width), 1.0 / width, F32)
    center = jnp.where((rows == cols) | (rows == cols + width), 1.0, 0.0) - mean
    return center.astype(BF16), mean.astype(BF16)


def scaled(center, mean, gain, shift):
    spread = dot(split(center * center), mean)
    return (center * lax.rsqrt(spread + 1e-05) * gain + shift).astype(BF16)


def norm_pair(values, consts, gain, shift):
    return scaled(dot(values, consts[0][: values.shape[1]]), consts[1], gain, shift)


def norm_mixed(values, consts, gain, shift):
    return scaled(dot(split(values), consts[0]), consts[1], gain, shift)


def gated(normed, weights, bias, width):
    product = dot(normed, weights) + bias
    return (jnp.tanh(product[:, width:]) + 1.0) * product[:, :width]


def gate(normed, weights, bias):
    return 0.5 * jnp.tanh(dot(normed, weights) + bias) + 0.5


def masked(values, outer, inner):
    t = outer.shape[0]
    grid = jnp.concatenate([outer[k : k + 1] * inner for k in range(t)], axis=0)
    return (values * grid).astype(BF16)


def mix(out_ref, left_ref, right_ref, slots, left_at, right_at, t):
    width = out_ref.shape[1]
    for base in range(0, t, 8):

        def slot(s, total):
            ls, rs = left_at(s), right_at(s)

            def step(q, total):
                for u in range(4):
                    first = pl.multiple_of((q * 4 + u) * t, 8)
                    right = right_ref[rs, pl.ds(first, t), :]
                    total = tuple(
                        total[i] + left_ref[ls, pl.ds(first + base + i, 1), :] * right for i in range(8)
                    )
                return total

            return lax.fori_loop(0, t // 4, step, total)

        total = lax.fori_loop(0, slots, slot, (jnp.zeros((t, width), F32),) * 8)
        for i in range(8):
            out_ref[pl.ds((base + i) * t, t), :] = total[i]


def finish(pair, mixed, gating, consts, gain, shift, weights, bias):
    normout = norm_mixed(mixed, consts, gain, shift)
    return (pair.astype(F32) + gating * (dot(normout, weights) + bias)).astype(BF16)


def first_kernel(n, t, *refs):
    row_refs, col_refs = refs[:n], refs[n : 2 * n]
    mask, in_gain, in_shift, w_in, bias_in, out_gain, out_shift, w_out, bias_out = refs[2 * n : 2 * n + 9]
    pair_ref, left_ref, right_ref, held, wide, lefts, rights, mixed = refs[2 * n + 9 :]
    width = pair_ref.shape[1]
    r, c = lax.axis_index("row"), lax.axis_index("col")
    half = n // 2
    consts = constants(width)
    weights = [w_in[u] * 0.5 for u in range(2)]
    biases = [bias_in[u : u + 1] * 0.5 for u in range(2)]
    for m, ref in enumerate(row_refs + col_refs):
        held[m] = ref[...]

    def prepare(m, _):
        along_row = m < n
        s = jnp.where(along_row, m, m - n)
        turned = lax.rem(r - s + n, n)
        outer = jnp.where(along_row, lax.rem(c - s + n, n), lax.rem(turned, half) * 2 + turned // half)
        inner = jnp.where(along_row, r, c)
        outer = mask[pl.ds(pl.multiple_of(outer * t, 8), t), :]
        inner = mask[pl.ds(pl.multiple_of(inner * t, 8), t), :]
        wide[...] = held[m].astype(F32)
        values = jnp.concatenate([wide[pl.ds(k, t, stride=t), :] for k in range(t)], axis=0).astype(BF16)
        normed = norm_pair(values, consts, in_gain[0:1], in_shift[0:1])
        for k, target in enumerate((lefts, rights)):
            span = slice(2 * k * width, 2 * (k + 1) * width)
            side = gated(normed, weights[0][:, span], biases[0][:, span], width)
            target[m] = masked(side, outer, inner).astype(F32)
        return 0

    lax.fori_loop(0, 2 * n, prepare, 0)

    def place(b):
        return b // 2 + lax.rem(b, 2) * half

    def col_slot(s):
        return n + lax.rem(r - place(lax.rem(c - s + n, n)) + n, n)

    mix(mixed.at[0], lefts, rights, n, lambda s: s, col_slot, t)
    mix(mixed.at[1], lefts, rights, n, col_slot, lambda s: s, t)
    here = mask[pl.ds(pl.multiple_of(r * t, 8), t), :]
    there = mask[pl.ds(pl.multiple_of(c * t, 8), t), :]
    own = (0, n + lax.rem(r - place(r) + n, n))
    for k in range(2):
        pair = held[own[k]]
        normed = norm_pair(pair, consts, in_gain[0:1], in_shift[0:1])
        gating = gate(normed, weights[0][:, 4 * width :], biases[0][:, 4 * width :])
        updated = finish(
            pair, mixed[k], gating, consts, out_gain[0:1], out_shift[0:1], w_out[0], bias_out[0:1]
        )
        normed = norm_pair(updated, consts, in_gain[1:2], in_shift[1:2])
        if k == 0:
            pair_ref[...] = updated
            span = slice(2 * width, 4 * width)
            side = gated(normed, weights[1][:, span], biases[1][:, span], width)
            right_ref[...] = masked(side, here, there)
        else:
            side = gated(normed, weights[1][:, : 2 * width], biases[1][:, : 2 * width], width)
            left_ref[...] = masked(side, there, here)


def second_kernel(n, t, *refs):
    left_refs, right_refs = refs[:n], refs[n : 2 * n]
    pair, in_gain, in_shift, w_in, bias_in, out_gain, out_shift, w_out, bias_out = refs[2 * n : 2 * n + 9]
    out_ref, lefts, rights, mixed = refs[2 * n + 9 :]
    width = out_ref.shape[1]
    r, c = lax.axis_index("row"), lax.axis_index("col")
    consts = constants(width)
    for s in range(n):
        lefts[s] = left_refs[s][...].astype(F32)
        rights[s] = right_refs[s][...].astype(F32)
    mix(mixed, lefts, rights, n, lambda s: s, lambda s: lax.rem(r - c + s + n, n), t)
    normed = norm_pair(pair[...], consts, in_gain[1:2], in_shift[1:2])
    gating = gate(normed, w_in[1, :, 4 * width :] * 0.5, bias_in[1:2, 4 * width :] * 0.5)
    out_ref[...] = finish(
        pair[...], mixed[...], gating, consts, out_gain[1:2], out_shift[1:2], w_out[1], bias_out[1:2]
    )


def solution(mesh):
    n = mesh.shape["col"]
    half = n // 2

    def along(block, axis, step):
        return lax.ppermute(block, axis, [(k, (k + step) % n) for k in range(n)]) if step else block

    def mirrored(block):
        pairs = [(a * n + z, (z // 2 + z % 2 * half) * n + a) for a in range(n) for z in range(n)]
        return lax.ppermute(block, ("row", "col"), pairs)

    def per_device(pair, token_mask, in_gain, in_shift, w_in, bias_in, out_gain, out_shift, w_out, bias_out):
        t, _, width = pair.shape
        area = (t * t, width)
        block = jax.ShapeDtypeStruct(area, BF16)
        params = pltpu.CompilerParams(vmem_limit_bytes=48 * 1024 * 1024)
        mask = jnp.broadcast_to(token_mask.astype(F32)[:, None], (n * t, width))
        tensors = (in_gain, in_shift, w_in, bias_in, out_gain, out_shift, w_out, bias_out)
        pair = pair.reshape(area)
        col_block = mirrored(pair)
        rows = [along(pair, "col", step) for step in range(n)]
        cols = [along(col_block, "row", step) for step in range(n)]
        pair, left, right = pl.pallas_call(
            functools.partial(first_kernel, n, t),
            out_shape=(block,) * 3,
            scratch_shapes=[
                pltpu.VMEM((2 * n,) + area, BF16),
                pltpu.VMEM(area, F32),
                pltpu.VMEM((2 * n,) + area, F32),
                pltpu.VMEM((2 * n,) + area, F32),
                pltpu.VMEM((2,) + area, F32),
            ],
            compiler_params=params,
            name="first_update",
        )(*rows, *cols, mask, *tensors)
        lefts = [along(left, "col", step) for step in range(n)]
        rights = [along(right, "row", step) for step in range(n)]
        out = pl.pallas_call(
            functools.partial(second_kernel, n, t),
            out_shape=block,
            scratch_shapes=[
                pltpu.VMEM((n,) + area, F32),
                pltpu.VMEM((n,) + area, F32),
                pltpu.VMEM(area, F32),
            ],
            compiler_params=params,
            name="second_update",
        )(*lefts, *rights, pair, *tensors)
        return out.reshape(t, t, width)

    placed = (P(("groups", "row"), "col", None), P("groups")) + (P(),) * 8
    return jax.shard_map(
        per_device, mesh=mesh, in_specs=placed, out_specs=P(("groups", "row"), "col", None), check_vma=False
    )
```

time: 107 us -> 64.3 us (0.60)
  local copies, waits for them, and re-layouts: 32.6 us -> 2.83 us
  Pallas kernels: 0 us -> 17.1 us
  matrix products: 14.3 us -> 0 us
  waiting for transfers between devices: 31.2 us -> 20.4 us
  other arithmetic: 7.97 us -> 0.01 us
  starting transfers between devices: 19.7 us -> 23.5 us
    pallas_call x0 -> x2, Pallas kernels: none -> 17.1 us  [the longest x1 12.7 us: per_device(): pl.pallas_call(functools.partial(first_kernel, n, t), out_shape=(block,)...]
    dot_general x6 -> x0, matrix products: 14.3 us -> none  [the longest x1 4.72 us: per_device(): jnp.einsum('skih,skjh->ijh', lefts, rights, preferred_element_type=jnp.fl...]
    dynamic_slice x5 -> x0, local copies, waits for them, and re-layouts: 14.1 us -> none  [the longest x4 14 us: matched(): lax.dynamic_slice_in_dim(jnp.concatenate([jnp.stack(blocks)] * 2), start, n)]
    another operation x2 -> x0, local copies, waits for them, and re-layouts: 11.5 us -> none  [the longest x1 6.03 us: per_device(): lefts = jnp.stack([across(left, step) for step in range(n)])]
    ppermute x9 -> x12, waiting for transfers between devices: 31.2 us -> 20.4 us  [along(): lax.ppermute(block, axis, [(k, (k + step) % n) for k in range(n)])]
    ppermute x9 -> x12, starting transfers between devices: 11.9 us -> 21.8 us  [along(): lax.ppermute(block, axis, [(k, (k + step) % n) for k in range(n)])]
    ppermute x5 -> x1, starting transfers between devices: 7.79 us -> 1.69 us  [mirrored(): return lax.ppermute(block, ('row', 'col'), pairs)]
    dot_general x2 -> x0, local copies, waits for them, and re-layouts: 3.75 us -> none  [the longest x1 1.89 us: per_device(): jnp.einsum('sikh,sjkh->ijh', lefts, rights, preferred_element_type=jnp.fl...]
  transfers between devices with their start and end apart: 14 -> 13, of which waited for: 5 -> 4; matrix products, arithmetic and copies ran while one was open for 14% -> 0% of each run, Pallas kernels for 0% -> 0%
where the time goes in v3:
time: 64.3 us; the launch traced here: 64 us
  starting transfers between devices  23.5 us (37%)
  waiting for transfers between devices  20.4 us (32%)
  Pallas kernels  17.1 us (27%)
  local copies, waits for them, and re-layouts  2.83 us (4%)
    ppermute x12, starting transfers between devices, along(): lax.ppermute(block, axis, [(k, (k + step) % n) for k in range(n)])  21.8 us
    ppermute x12, waiting for transfers between devices, along(): lax.ppermute(block, axis, [(k, (k + step) % n) for k in range(n)])  20.4 us
    pallas_call x1, Pallas kernels, per_device(): pl.pallas_call(functools.partial(first_kernel, n, t), out_shape=(block,)...  12.7 us
    pallas_call x1, Pallas kernels, per_device(): pl.pallas_call(functools.partial(second_kernel, n, t), out_shape=block, s...  4.44 us
    unnamed x24, local copies, waits for them, and re-layouts  2.76 us
    ppermute x1, starting transfers between devices, mirrored(): return lax.ppermute(block, ('row', 'col'), pairs)  1.69 us
  transfers between devices with their start and end apart: 13, of which 4 were waited for; matrix products, arithmetic and copies ran while one was open for 0% of the time, Pallas kernels for 0%

profile of v3, /device:TPU:0, one launch (start us, length us, event | category | flops | bytes accessed | tf_op | source)
XLA Modules:
  0.0 64.0 jit_solution(2746984990689496694)
XLA Ops:
  0.0 0.0 copy-start.11
  0.0 1.7 %collective-permute-start.3 = (bf16[576,128]{1,0:T(8,128)(2,1)}, bf16[576,128]{1,0:T(8,128)(2,1)S(1)}, u32[]{:S(2)}, u32[]{:S(2)}) collective-permute-start(bf16[576,128]{1,0:T(8,128)(2,1)} %bitcast.2), channel_id=1, source_target_pairs={{0,0},{1,8},{2,4},{3,12},{4,1},{5,9},{6,5},{7,13},{8,2},{9,10},{10... | collective-permute-start | bytes 442376 | tf_op jit(solution)/shard_map/ppermute | solution.py:174
  1.7 6.0 %collective-permute-start.2 = (bf16[576,128]{1,0:T(8,128)(2,1)}, bf16[576,128]{1,0:T(8,128)(2,1)S(1)}, u32[]{:S(2)}, u32[]{:S(2)}) collective-permute-start(bf16[576,128]{1,0:T(8,128)(2,1)} %bitcast.3), channel_id=1, source_target_pairs={{0,3},{1,0},{2,1},{3,2},{4,7},{5,4},{6,5},{7,6},{8,11},{9,8},{10,9... | collective-permute-start | bytes 442376 | tf_op jit(solution)/shard_map/ppermute | solution.py:170
  7.7 0.2 collective-permute-start.1
  8.0 0.4 collective-permute-start
  8.4 0.0 collective-permute-done.3.refs_4_
  8.4 5.0 %collective-permute-start.6 = (bf16[576,128]{1,0:T(8,128)(2,1)S(1)}, bf16[576,128]{1,0:T(8,128)(2,1)S(1)}, u32[]{:S(2)}, u32[]{:S(2)}) collective-permute-start(bf16[576,128]{1,0:T(8,128)(2,1)S(1)} %collective-permute-done.3.refs_4_), channel_id=1, source_target_pairs={{0,12},{4,0},{8,4},{12,8},{1,13},{5,1},{9,5},{13,9},{2,14},{6,2},{... | collective-permute-start | bytes 442376 | tf_op jit(solution)/shard_map/ppermute | solution.py:170
  13.4 2.3 %collective-permute-start.5 = (bf16[576,128]{1,0:T(8,128)(2,1)S(1)}, bf16[576,128]{1,0:T(8,128)(2,1)S(1)}, u32[]{:S(2)}, u32[]{:S(2)}) collective-permute-start(bf16[576,128]{1,0:T(8,128)(2,1)S(1)} %collective-permute-done.3.refs_4_), channel_id=1, source_target_pairs={{0,8},{4,12},{8,0},{12,4},{1,9},{5,13},{9,1},{13,5},{2,10},{6,14},... | collective-permute-start | bytes 442376 | tf_op jit(solution)/shard_map/ppermute | solution.py:170
  15.7 0.1 collective-permute-done.2.refs_3_
  15.8 0.1 collective-permute-start.4
  15.9 0.0 copy-done.11
  15.9 0.0 copy-start.5
  15.9 0.0 copy-start.7
  15.9 0.0 copy-start.8
  16.0 0.0 copy-start.9
  16.0 0.0 copy-start.10
  16.0 10.1 %collective-permute-done.1.refs_2_ = bf16[576,128]{1,0:T(8,128)(2,1)S(1)} collective-permute-done((bf16[576,128]{1,0:T(8,128)(2,1)}, bf16[576,128]{1,0:T(8,128)(2,1)S(1)}, u32[]{:S(2)}, u32[]{:S(2)}) %collective-permute-start.1) | collective-permute-done | bytes 147488 | tf_op jit(solution)/shard_map/ppermute | solution.py:170
  26.1 0.0 collective-permute-done.refs_1_
  26.1 0.0 collective-permute-done.6.refs_7_
  26.1 0.0 collective-permute-done.5.refs_6_
  26.1 0.0 collective-permute-done.4.refs_5_
  26.1 0.1 broadcast_in_dim.2.refs_8_
  26.2 0.0 copy-done.5
  26.2 0.0 copy-done.6
  26.2 0.0 copy-done.7
  26.2 0.0 copy-done.8
  26.2 0.0 copy-done.9
  26.2 0.0 copy-done.10
  26.2 0.0 copy-start
  26.2 1.0 %copy-done = bf16[2,128,640]{2,1,0:T(8,128)(2,1)S(1)} copy-done((bf16[2,128,640]{2,1,0:T(8,128)(2,1)S(1)}, bf16[2,128,640]{2,1,0:T(8,128)(2,1)}, u32[]{:S(2)}) %copy-start) | copy-done | bytes 327704
  27.2 0.8 %copy-done.2 = bf16[2,128,128]{2,1,0:T(8,128)(2,1)S(1)} copy-done((bf16[2,128,128]{2,1,0:T(8,128)(2,1)S(1)}, bf16[2,128,128]{2,1,0:T(8,128)(2,1)}, u32[]{:S(2)}) %copy-start.2) | copy-done | bytes 65560
  28.0 0.9 %copy-done.4 = bf16[24,24,128]{2,1,0:T(8,128)(2,1)S(1)} copy-done((bf16[24,24,128]{2,1,0:T(8,128)(2,1)S(1)}, bf16[24,24,128]{2,1,0:T(8,128)(2,1)}, u32[]{:S(2)}) %copy-start.4) | copy-done | bytes 147480
  29.0 12.7 %first_update.1 = (bf16[576,128]{1,0:T(8,128)(2,1)S(1)}, bf16[576,128]{1,0:T(8,128)(2,1)S(1)}, bf16[576,128]{1,0:T(8,128)(2,1)S(1)}) custom-call(bf16[576,128]{1,0:T(8,128)(2,1)S(1)} %bitcast.6, bf16[576,128]{1,0:T(8,128)(2,1)S(1)} %collective-permute-done.refs_1_, bf16[576,128]{1,0:T(8,128)(2,1)S(1)} %collective-permute-done.1.refs_2_, ...), custom_call_target="tpu_custom_call" | custom-call | tf_op jit(solution)/shard_map/first_update/pallas_call | solution.py:187
  41.6 6.8 %collective-permute-start.9 = (bf16[576,128]{1,0:T(8,128)(2,1)S(1)}, bf16[576,128]{1,0:T(8,128)(2,1)S(1)}, u32[]{:S(2)}, u32[]{:S(2)}) collective-permute-start(bf16[576,128]{1,0:T(8,128)(2,1)S(1)} %get-tuple-element.8.refs_0_), channel_id=1, source_target_pairs={{0,3},{1,0},{2,1},{3,2},{4,7},{5,4},{6,5},{7,6},{8,11},{9,8},{10,9... | collective-permute-start | bytes 442376 | tf_op jit(solution)/shard_map/ppermute | solution.py:170
  48.5 0.0 collective-permute-start.8
  48.5 0.6 collective-permute-start.7
  49.1 0.0 collective-permute-start.12
  49.1 0.2 collective-permute-start.11
  49.3 3.5 %collective-permute-done.9.refs_3_ = bf16[576,128]{1,0:T(8,128)(2,1)S(1)} collective-permute-done((bf16[576,128]{1,0:T(8,128)(2,1)S(1)}, bf16[576,128]{1,0:T(8,128)(2,1)S(1)}, u32[]{:S(2)}, u32[]{:S(2)}) %collective-permute-start.9) | collective-permute-done | bytes 147488 | tf_op jit(solution)/shard_map/ppermute | solution.py:170
  52.8 0.0 collective-permute-start.10
  52.8 6.7 %collective-permute-done.8.refs_2_ = bf16[576,128]{1,0:T(8,128)(2,1)S(1)} collective-permute-done((bf16[576,128]{1,0:T(8,128)(2,1)S(1)}, bf16[576,128]{1,0:T(8,128)(2,1)S(1)}, u32[]{:S(2)}, u32[]{:S(2)}) %collective-permute-start.8) | collective-permute-done | bytes 147488 | tf_op jit(solution)/shard_map/ppermute | solution.py:170
  59.5 0.0 collective-permute-done.7.refs_1_
  59.5 0.0 collective-permute-done.12.refs_7_
  59.5 0.0 collective-permute-done.11.refs_6_
  59.5 0.0 collective-permute-done.10.refs_5_
  59.5 0.0 copy-done.1
  59.5 0.0 copy-done.3
  59.5 4.4 %second_update.1 = bf16[576,128]{1,0:T(8,128)(2,1)} custom-call(bf16[576,128]{1,0:T(8,128)(2,1)S(1)} %get-tuple-element.8.refs_0_, bf16[576,128]{1,0:T(8,128)(2,1)S(1)} %collective-permute-done.7.refs_1_, bf16[576,128]{1,0:T(8,128)(2,1)S(1)} %collective-permute-done.8.refs_2_, bf16[576,128]{1,0:T(8,128)(2,1)S(1)} %collective-permute-done.9.refs_3_, ...), custom_call_target="tpu_custom_call" | custom-call | tf_op jit(solution)/shard_map/second_update/pallas_call | solution.py:202
  (6 shorter events, 0.0 us)
Async XLA Ops:
  0.0 15.9 %copy-start.11 = (s32[96]{0:T(128)S(1)}, s32[96]{0:T(128)}, u32[]{:S(2)}) copy-start(s32[96]{0:T(128)} %param.11) | copy-start | bytes 1156
  0.0 8.4 %collective-permute-start.3 = (bf16[576,128]{1,0:T(8,128)(2,1)}, bf16[576,128]{1,0:T(8,128)(2,1)S(1)}, u32[]{:S(2)}, u32[]{:S(2)}) collective-permute-start(bf16[576,128]{1,0:T(8,128)(2,1)} %bitcast.2), channel_id=1, source_target_pairs={{0,0},{1,8},{2,4},{3,12},{4,1},{5,9},{6,5},{7,13},{8,2},{9,10},{10... | collective-permute-start | bytes 442376 | tf_op jit(solution)/shard_map/ppermute | solution.py:174
  1.7 14.1 %collective-permute-start.2 = (bf16[576,128]{1,0:T(8,128)(2,1)}, bf16[576,128]{1,0:T(8,128)(2,1)S(1)}, u32[]{:S(2)}, u32[]{:S(2)}) collective-permute-start(bf16[576,128]{1,0:T(8,128)(2,1)} %bitcast.3), channel_id=1, source_target_pairs={{0,3},{1,0},{2,1},{3,2},{4,7},{5,4},{6,5},{7,6},{8,11},{9,8},{10,9... | collective-permute-start | bytes 442376 | tf_op jit(solution)/shard_map/ppermute | solution.py:170
  7.7 18.3 %collective-permute-start.1 = (bf16[576,128]{1,0:T(8,128)(2,1)}, bf16[576,128]{1,0:T(8,128)(2,1)S(1)}, u32[]{:S(2)}, u32[]{:S(2)}) collective-permute-start(bf16[576,128]{1,0:T(8,128)(2,1)} %bitcast.4), channel_id=1, source_target_pairs={{0,2},{1,3},{2,0},{3,1},{4,6},{5,7},{6,4},{7,5},{8,10},{9,11},{10,... | collective-permute-start | bytes 442376 | tf_op jit(solution)/shard_map/ppermute | solution.py:170
  8.0 18.1 %collective-permute-start = (bf16[576,128]{1,0:T(8,128)(2,1)}, bf16[576,128]{1,0:T(8,128)(2,1)S(1)}, u32[]{:S(2)}, u32[]{:S(2)}) collective-permute-start(bf16[576,128]{1,0:T(8,128)(2,1)} %bitcast.5), channel_id=1, source_target_pairs={{0,1},{1,2},{2,3},{3,0},{4,5},{5,6},{6,7},{7,4},{8,9},{9,10},{10,1... | collective-permute-start | bytes 442376 | tf_op jit(solution)/shard_map/ppermute | solution.py:170
  8.4 17.7 %collective-permute-start.6 = (bf16[576,128]{1,0:T(8,128)(2,1)S(1)}, bf16[576,128]{1,0:T(8,128)(2,1)S(1)}, u32[]{:S(2)}, u32[]{:S(2)}) collective-permute-start(bf16[576,128]{1,0:T(8,128)(2,1)S(1)} %collective-permute-done.3.refs_4_), channel_id=1, source_target_pairs={{0,12},{4,0},{8,4},{12,8},{1,13},{5,1},{9,5},{13,9},{2,14},{6,2},{... | collective-permute-start | bytes 442376 | tf_op jit(solution)/shard_map/ppermute | solution.py:170
  13.4 12.7 %collective-permute-start.5 = (bf16[576,128]{1,0:T(8,128)(2,1)S(1)}, bf16[576,128]{1,0:T(8,128)(2,1)S(1)}, u32[]{:S(2)}, u32[]{:S(2)}) collective-permute-start(bf16[576,128]{1,0:T(8,128)(2,1)S(1)} %collective-permute-done.3.refs_4_), channel_id=1, source_target_pairs={{0,8},{4,12},{8,0},{12,4},{1,9},{5,13},{9,1},{13,5},{2,10},{6,14},... | collective-permute-start | bytes 442376 | tf_op jit(solution)/shard_map/ppermute | solution.py:170
  15.8 10.3 %collective-permute-start.4 = (bf16[576,128]{1,0:T(8,128)(2,1)S(1)}, bf16[576,128]{1,0:T(8,128)(2,1)S(1)}, u32[]{:S(2)}, u32[]{:S(2)}) collective-permute-start(bf16[576,128]{1,0:T(8,128)(2,1)S(1)} %collective-permute-done.3.refs_4_), channel_id=1, source_target_pairs={{0,4},{4,8},{8,12},{12,0},{1,5},{5,9},{9,13},{13,1},{2,6},{6,10},{... | collective-permute-start | bytes 442376 | tf_op jit(solution)/shard_map/ppermute | solution.py:170
  15.9 10.2 %copy-start.5 = (f32[2,640]{1,0:T(2,128)S(1)}, f32[2,640]{1,0:T(2,128)}, u32[]{:S(2)}) copy-start(f32[2,640]{1,0:T(2,128)} %refs_12_.3) | copy-start | bytes 15364
  15.9 10.2 %copy-start.6 = (f32[2,128]{1,0:T(2,128)S(1)}, f32[2,128]{1,0:T(2,128)}, u32[]{:S(2)}) copy-start(f32[2,128]{1,0:T(2,128)} %refs_9_.3) | copy-start | bytes 3076
  15.9 10.2 %copy-start.7 = (f32[2,128]{1,0:T(2,128)S(1)}, f32[2,128]{1,0:T(2,128)}, u32[]{:S(2)}) copy-start(f32[2,128]{1,0:T(2,128)} %refs_10_.3) | copy-start | bytes 3076
  15.9 10.2 %copy-start.8 = (f32[2,128]{1,0:T(2,128)S(1)}, f32[2,128]{1,0:T(2,128)}, u32[]{:S(2)}) copy-start(f32[2,128]{1,0:T(2,128)} %refs_13_.3) | copy-start | bytes 3076
  16.0 10.2 %copy-start.9 = (f32[2,128]{1,0:T(2,128)S(1)}, f32[2,128]{1,0:T(2,128)}, u32[]{:S(2)}) copy-start(f32[2,128]{1,0:T(2,128)} %refs_14_.3) | copy-start | bytes 3076
  16.0 10.2 %copy-start.10 = (f32[2,128]{1,0:T(2,128)S(1)}, f32[2,128]{1,0:T(2,128)}, u32[]{:S(2)}) copy-start(f32[2,128]{1,0:T(2,128)} %refs_16_.3) | copy-start | bytes 3076
  26.2 1.0 %copy-start = (bf16[2,128,640]{2,1,0:T(8,128)(2,1)S(1)}, bf16[2,128,640]{2,1,0:T(8,128)(2,1)}, u32[]{:S(2)}) copy-start(bf16[2,128,640]{2,1,0:T(8,128)(2,1)} %refs_11_.3) | copy-start | bytes 983044
  27.2 0.8 %copy-start.2 = (bf16[2,128,128]{2,1,0:T(8,128)(2,1)S(1)}, bf16[2,128,128]{2,1,0:T(8,128)(2,1)}, u32[]{:S(2)}) copy-start(bf16[2,128,128]{2,1,0:T(8,128)(2,1)} %refs_15_.3) | copy-start | bytes 196612
  28.0 0.9 %copy-start.4 = (bf16[24,24,128]{2,1,0:T(8,128)(2,1)S(1)}, bf16[24,24,128]{2,1,0:T(8,128)(2,1)}, u32[]{:S(2)}) copy-start(bf16[24,24,128]{2,1,0:T(8,128)(2,1)} %param.10) | copy-start | bytes 442372
  29.0 30.5 %copy-start.1 = (bf16[2,128,640]{2,1,0:T(8,128)(2,1)S(1)}, bf16[2,128,640]{2,1,0:T(8,128)(2,1)}, u32[]{:S(2)}) copy-start(bf16[2,128,640]{2,1,0:T(8,128)(2,1)} %refs_11_.3) | copy-start | bytes 983044
  29.0 30.5 %copy-start.3 = (bf16[2,128,128]{2,1,0:T(8,128)(2,1)S(1)}, bf16[2,128,128]{2,1,0:T(8,128)(2,1)}, u32[]{:S(2)}) copy-start(bf16[2,128,128]{2,1,0:T(8,128)(2,1)} %refs_15_.3) | copy-start | bytes 196612
  41.6 11.2 %collective-permute-start.9 = (bf16[576,128]{1,0:T(8,128)(2,1)S(1)}, bf16[576,128]{1,0:T(8,128)(2,1)S(1)}, u32[]{:S(2)}, u32[]{:S(2)}) collective-permute-start(bf16[576,128]{1,0:T(8,128)(2,1)S(1)} %get-tuple-element.8.refs_0_), channel_id=1, source_target_pairs={{0,3},{1,0},{2,1},{3,2},{4,7},{5,4},{6,5},{7,6},{8,11},{9,8},{10,9... | collective-permute-start | bytes 442376 | tf_op jit(solution)/shard_map/ppermute | solution.py:170
  48.5 11.0 %collective-permute-start.8 = (bf16[576,128]{1,0:T(8,128)(2,1)S(1)}, bf16[576,128]{1,0:T(8,128)(2,1)S(1)}, u32[]{:S(2)}, u32[]{:S(2)}) collective-permute-start(bf16[576,128]{1,0:T(8,128)(2,1)S(1)} %get-tuple-element.8.refs_0_), channel_id=1, source_target_pairs={{0,2},{1,3},{2,0},{3,1},{4,6},{5,7},{6,4},{7,5},{8,10},{9,11},{10,... | collective-permute-start | bytes 442376 | tf_op jit(solution)/shard_map/ppermute | solution.py:170
  48.5 11.0 %collective-permute-start.7 = (bf16[576,128]{1,0:T(8,128)(2,1)S(1)}, bf16[576,128]{1,0:T(8,128)(2,1)S(1)}, u32[]{:S(2)}, u32[]{:S(2)}) collective-permute-start(bf16[576,128]{1,0:T(8,128)(2,1)S(1)} %get-tuple-element.8.refs_0_), channel_id=1, source_target_pairs={{0,1},{1,2},{2,3},{3,0},{4,5},{5,6},{6,7},{7,4},{8,9},{9,10},{10,1... | collective-permute-start | bytes 442376 | tf_op jit(solution)/shard_map/ppermute | solution.py:170
  49.1 10.4 %collective-permute-start.12 = (bf16[576,128]{1,0:T(8,128)(2,1)S(1)}, bf16[576,128]{1,0:T(8,128)(2,1)S(1)}, u32[]{:S(2)}, u32[]{:S(2)}) collective-permute-start(bf16[576,128]{1,0:T(8,128)(2,1)S(1)} %get-tuple-element.9.refs_4_), channel_id=1, source_target_pairs={{0,12},{4,0},{8,4},{12,8},{1,13},{5,1},{9,5},{13,9},{2,14},{6,2},{... | collective-permute-start | bytes 442376 | tf_op jit(solution)/shard_map/ppermute | solution.py:170
  49.1 10.4 %collective-permute-start.11 = (bf16[576,128]{1,0:T(8,128)(2,1)S(1)}, bf16[576,128]{1,0:T(8,128)(2,1)S(1)}, u32[]{:S(2)}, u32[]{:S(2)}) collective-permute-start(bf16[576,128]{1,0:T(8,128)(2,1)S(1)} %get-tuple-element.9.refs_4_), channel_id=1, source_target_pairs={{0,8},{4,12},{8,0},{12,4},{1,9},{5,13},{9,1},{13,5},{2,10},{6,14},... | collective-permute-start | bytes 442376 | tf_op jit(solution)/shard_map/ppermute | solution.py:170
  52.8 6.7 %collective-permute-start.10 = (bf16[576,128]{1,0:T(8,128)(2,1)S(1)}, bf16[576,128]{1,0:T(8,128)(2,1)S(1)}, u32[]{:S(2)}, u32[]{:S(2)}) collective-permute-start(bf16[576,128]{1,0:T(8,128)(2,1)S(1)} %get-tuple-element.9.refs_4_), channel_id=1, source_target_pairs={{0,4},{4,8},{8,12},{12,0},{1,5},{5,9},{9,13},{13,1},{2,6},{6,10},{... | collective-permute-start | bytes 442376 | tf_op jit(solution)/shard_map/ppermute | solution.py:170

commit v4 on v2

v4 whole, which is shorter than its diff:
```python
import functools

import jax
import jax.numpy as jnp
from jax import lax
from jax.experimental import pallas as pl
from jax.experimental.pallas import tpu as pltpu
from jax.sharding import PartitionSpec as P

F32, BF16 = jnp.float32, jnp.bfloat16


def dot(a, b):
    return jnp.dot(a, b, preferred_element_type=F32)


def split(values):
    high = values.astype(BF16)
    return jnp.concatenate([high, (values - high.astype(F32)).astype(BF16)], axis=1)


def constants(width):
    rows = lax.broadcasted_iota(jnp.int32, (2 * width, width), 0)
    cols = lax.broadcasted_iota(jnp.int32, (2 * width, width), 1)
    mean = jnp.full((2 * width, width), 1.0 / width, F32)
    center = jnp.where((rows == cols) | (rows == cols + width), 1.0, 0.0) - mean
    return center.astype(BF16), mean.astype(BF16)


def scaled(center, mean, gain, shift):
    spread = dot(split(center * center), mean)
    return (center * lax.rsqrt(spread + 1e-05) * gain + shift).astype(BF16)


def norm_pair(values, consts, gain, shift):
    return scaled(dot(values, consts[0][: values.shape[1]]), consts[1], gain, shift)


def norm_mixed(values, consts, gain, shift):
    return scaled(dot(split(values), consts[0]), consts[1], gain, shift)


def gated(normed, weights, bias, width):
    product = dot(normed, weights) + bias
    return (jnp.tanh(product[:, width:]) + 1.0) * product[:, :width]


def gate(normed, weights, bias):
    return 0.5 * jnp.tanh(dot(normed, weights) + bias) + 0.5


def masked(values, outer, inner):
    t = outer.shape[0]
    grid = jnp.concatenate([outer[k : k + 1] * inner for k in range(t)], axis=0)
    return (values * grid).astype(BF16)


def mix(out_ref, old_ref, left, right, t):
    width = out_ref.shape[1]
    for base in range(0, t, 8):
        if old_ref is None:
            total = (jnp.zeros((t, width), F32),) * 8
        else:
            total = tuple(old_ref[pl.ds((base + i) * t, t), :] for i in range(8))

        def step(q, total):
            for u in range(4):
                first = pl.multiple_of((q * 4 + u) * t, 8)
                row = right(first)
                total = tuple(total[i] + left(first + base + i) * row for i in range(8))
            return total

        total = lax.fori_loop(0, t // 4, step, total)
        for i in range(8):
            out_ref[pl.ds((base + i) * t, t), :] = total[i]


def finish(pair, mixed, gating, consts, gain, shift, weights, bias):
    normout = norm_mixed(mixed, consts, gain, shift)
    return (pair.astype(F32) + gating * (dot(normout, weights) + bias)).astype(BF16)


def row_of(ref, *lead):
    return lambda at: ref[(*lead, pl.ds(at, 1), slice(None))]


def rows_of(ref, t, *lead):
    return lambda at: ref[(*lead, pl.ds(at, t), slice(None))]


def place(b, n):
    return b // 2 + lax.rem(b, 2) * (n // 2)


def mask_of(mask, b, t):
    return mask[pl.ds(pl.multiple_of(b * t, 8), t), :]


def sides(values_ref, wide, left_at, right_at, outer, inner, consts, in_gain, in_shift, weights, bias):
    t, width = outer.shape
    wide[...] = values_ref[...].astype(F32)
    values = jnp.concatenate([wide[pl.ds(k, t, stride=t), :] for k in range(t)], axis=0).astype(BF16)
    normed = norm_pair(values, consts, in_gain[0:1], in_shift[0:1])
    for k, target in enumerate((left_at, right_at)):
        span = slice(2 * k * width, 2 * (k + 1) * width)
        side = gated(normed, weights[:, span], bias[:, span], width)
        target[...] = masked(side, outer, inner).astype(F32)


def own_kernel(n, t, pair, mask, in_gain, in_shift, w_in, bias_in, left, right, gating, wide):
    width = pair.shape[1]
    r, c = lax.axis_index("row"), lax.axis_index("col")
    consts = constants(width)
    weights, bias = w_in[0] * 0.5, bias_in[0:1] * 0.5
    outer, inner = mask_of(mask, c, t), mask_of(mask, r, t)
    sides(pair, wide, left, right, outer, inner, consts, in_gain, in_shift, weights, bias)
    normed = norm_pair(pair[...], consts, in_gain[0:1], in_shift[0:1])
    gating[...] = gate(normed, weights[:, 4 * width :], bias[:, 4 * width :])


def column_kernel(n, t, *refs):
    blocks = refs[:n]
    mask, in_gain, in_shift, w_in, bias_in, own_left, own_right = refs[n : n + 7]
    lefts, rights, pair, gating, mixed, held, wide = refs[n + 7 :]
    width = wide.shape[1]
    r, c = lax.axis_index("row"), lax.axis_index("col")
    consts = constants(width)
    weights, bias = w_in[0] * 0.5, bias_in[0:1] * 0.5
    for s in range(n):
        held[s] = blocks[s][...]

    def prepare(b, _):
        s = r ^ place(b, n)
        outer, inner = mask_of(mask, b, t), mask_of(mask, c, t)
        sides(
            held.at[s], wide, lefts.at[b], rights.at[b], outer, inner, consts, in_gain, in_shift, weights, bias
        )
        return 0

    lax.fori_loop(0, n, prepare, 0)
    own = held[r ^ place(r, n)]
    pair[...] = own
    normed = norm_pair(own, consts, in_gain[0:1], in_shift[0:1])
    gating[...] = gate(normed, weights[:, 4 * width :], bias[:, 4 * width :])
    mix(mixed.at[0], None, row_of(own_left), rows_of(rights, t, c), t)
    mix(mixed.at[1], None, row_of(lefts, c), rows_of(own_right, t), t)


def slot_sum(n, t, slot, block, mask, in_gain, in_shift, w_in, bias_in, lefts, rights, old, mixed, wide, left, right):
    r, c = lax.axis_index("row"), lax.axis_index("col")
    consts = constants(wide.shape[1])
    weights, bias = w_in[0] * 0.5, bias_in[0:1] * 0.5
    b = c ^ slot
    outer, inner = mask_of(mask, b, t), mask_of(mask, r, t)
    sides(block, wide, left, right, outer, inner, consts, in_gain, in_shift, weights, bias)
    mix(mixed.at[0], old.at[0], row_of(left), rows_of(rights, t, b), t)
    mix(mixed.at[1], old.at[1], row_of(lefts, b), rows_of(right, t), t)


def slot_kernel(n, t, slot, *refs):
    slot_sum(n, t, slot, *refs)


def last_kernel(n, t, slot, *refs):
    block, mask, in_gain, in_shift, w_in, bias_in, lefts, rights, old = refs[:9]
    out_gain, out_shift, w_out, bias_out, pair, gating, col_pair, col_gating = refs[9:17]
    pair_ref, left_ref, right_ref, mixed, wide, left, right = refs[17:]
    slot_sum(
        n, t, slot, block, mask, in_gain, in_shift, w_in, bias_in, lefts, rights, old, mixed, wide, left, right
    )
    width = wide.shape[1]
    r, c = lax.axis_index("row"), lax.axis_index("col")
    consts = constants(width)
    weights, bias = w_in[1] * 0.5, bias_in[1:2] * 0.5
    here, there = mask_of(mask, r, t), mask_of(mask, c, t)
    for k, (base, factor) in enumerate(((pair, gating), (col_pair, col_gating))):
        updated = finish(
            base[...], mixed[k], factor[...], consts, out_gain[0:1], out_shift[0:1], w_out[0], bias_out[0:1]
        )
        normed = norm_pair(updated, consts, in_gain[1:2], in_shift[1:2])
        if k == 0:
            pair_ref[...] = updated
            span = slice(2 * width, 4 * width)
            right_ref[...] = masked(gated(normed, weights[:, span], bias[:, span], width), here, there)
        else:
            span = slice(0, 2 * width)
            left_ref[...] = masked(gated(normed, weights[:, span], bias[:, span], width), there, here)


def gate_kernel(pair, in_gain, in_shift, w_in, bias_in, gating):
    width = pair.shape[1]
    normed = norm_pair(pair[...], constants(width), in_gain[1:2], in_shift[1:2])
    gating[...] = gate(normed, w_in[1, :, 4 * width :] * 0.5, bias_in[1:2, 4 * width :] * 0.5)


def right_kernel(n, t, *refs):
    blocks, left = refs[:n], refs[n]
    rights, mixed, wide = refs[n + 1 :]
    r, c = lax.axis_index("row"), lax.axis_index("col")
    for s in range(n):
        rights[s] = blocks[s][...].astype(F32)
    wide[...] = left[...].astype(F32)
    mix(mixed, None, row_of(wide), rows_of(rights, t, r ^ c), t)


def left_sum(n, t, slot, left, rights, old, mixed, wide):
    r, c = lax.axis_index("row"), lax.axis_index("col")
    wide[...] = left[...].astype(F32)
    mix(mixed, old, row_of(wide), rows_of(rights, t, r ^ c ^ slot), t)


def left_kernel(n, t, slot, *refs):
    left_sum(n, t, slot, *refs)


def end_kernel(n, t, slot, left, rights, old, pair, gating, out_gain, out_shift, w_out, bias_out, out, mixed, wide):
    left_sum(n, t, slot, left, rights, old, mixed, wide)
    consts = constants(wide.shape[1])
    out[...] = finish(
        pair[...], mixed[...], gating[...], consts, out_gain[1:2], out_shift[1:2], w_out[1], bias_out[1:2]
    )


def solution(mesh):
    n = mesh.shape["col"]
    half = n // 2

    def along(block, axis, step):
        return lax.ppermute(block, axis, [(k, k ^ step) for k in range(n)])

    def mirrored(block):
        pairs = [(a * n + z, (z // 2 + z % 2 * half) * n + a) for a in range(n) for z in range(n)]
        return lax.ppermute(block, ("row", "col"), pairs)

    def plane(block):
        return [block] + [along(block, "row", step) for step in range(1, n)]

    def per_device(pair, token_mask, in_gain, in_shift, w_in, bias_in, out_gain, out_shift, w_out, bias_out):
        t, _, width = pair.shape
        area = (t * t, width)
        narrow, broad = jax.ShapeDtypeStruct(area, BF16), jax.ShapeDtypeStruct(area, F32)
        stacked = jax.ShapeDtypeStruct((n,) + area, F32)
        twice = jax.ShapeDtypeStruct((2,) + area, F32)
        scratch = pltpu.VMEM(area, F32)

        def call(kernel, name, outs, scratches, ops, *operands, alias=None):
            return pl.pallas_call(
                kernel,
                out_shape=outs,
                scratch_shapes=scratches,
                input_output_aliases=alias or {},

                compiler_params=pltpu.CompilerParams(vmem_limit_bytes=(16 + n) * 1024 * 1024),
                name=name,
            )(*operands)

        work = 2 * t**4 * width
        mask = jnp.broadcast_to(token_mask.astype(F32)[:, None], (n * t, width))
        ins = (mask, in_gain, in_shift, w_in, bias_in)
        outs = (out_gain, out_shift, w_out, bias_out)
        pair = pair.reshape(area)
        col_block = mirrored(pair)
        steps = [step for step in range(1, n) if step != half] + [half]
        rows = [along(pair, "col", step) for step in steps]
        own_left, own_right, gating = call(
            functools.partial(own_kernel, n, t), "own_sides", (broad,) * 3, [scratch], work, pair, *ins
        )
        lefts, rights, col_pair, col_gating, mixed = call(
            functools.partial(column_kernel, n, t),
            "column_sides",
            (stacked, stacked, narrow, broad, twice),
            [pltpu.VMEM((n,) + area, BF16), scratch],
            n * work,
            *plane(col_block),
            *ins,
            own_left,
            own_right,
        )
        for step, block in zip(steps[:-1], rows[:-1]):
            mixed = call(
                functools.partial(slot_kernel, n, t, step),
                "row_slot",
                twice,
                [scratch] * 3,
                work,
                block,
                *ins,
                lefts,
                rights,
                mixed,
                alias={8: 0},
            )
        pair, left, right = call(
            functools.partial(last_kernel, n, t, steps[-1]),
            "last_slot",
            (narrow,) * 3,
            [pltpu.VMEM((2,) + area, F32)] + [scratch] * 3,
            work,
            rows[-1],
            *ins,
            lefts,
            rights,
            mixed,
            *outs,
            pair,
            gating,
            col_pair,
            col_gating,
        )
        blocks = [along(left, "col", step) for step in steps]
        gating = call(gate_kernel, "gate", broad, [], work, pair, *ins[1:])
        rights, mixed = call(
            functools.partial(right_kernel, n, t), "right_slots", (stacked, broad), [scratch], work, *plane(right), left
        )
        for step, block in zip(steps[:-1], blocks[:-1]):
            mixed = call(
                functools.partial(left_kernel, n, t, step),
                "left_slot",
                broad,
                [scratch],
                work,
                block,
                rights,
                mixed,
                alias={2: 0},
            )
        out = call(
            functools.partial(end_kernel, n, t, steps[-1]),
            "end",
            narrow,
            [scratch] * 2,
            work,
            blocks[-1],
            rights,
            mixed,
            pair,
            gating,
            *outs,
        )
        return out.reshape(t, t, width)

    placed = (P(("groups", "row"), "col", None), P("groups")) + (P(),) * 8
    return jax.shard_map(
        per_device, mesh=mesh, in_specs=placed, out_specs=P(("groups", "row"), "col", None), check_vma=False
    )
```

time: 107 us -> 59.5 us (0.56)
  local copies, waits for them, and re-layouts: 32.6 us -> 6.37 us
  waiting for transfers between devices: 31.2 us -> 7.9 us
  Pallas kernels: 0 us -> 16.3 us
  matrix products: 14.3 us -> 0 us
  starting transfers between devices: 19.7 us -> 27.6 us
  other arithmetic: 7.97 us -> 0.66 us
    ppermute x14 -> x13, waiting for transfers between devices: 31.2 us -> 7.9 us  [the longest x12 7.9 us: along(): return lax.ppermute(block, axis, [(k, k ^ step) for k in range(n)])]
    pallas_call x0 -> x10, Pallas kernels: none -> 16.3 us  [call(): pl.pallas_call(kernel, out_shape=outs, scratch_shapes=scratches, input_ou...]
    dot_general x6 -> x0, matrix products: 14.3 us -> none  [the longest x1 4.72 us: per_device(): jnp.einsum('skih,skjh->ijh', lefts, rights, preferred_element_type=jnp.fl...]
    dynamic_slice x5 -> x0, local copies, waits for them, and re-layouts: 14.1 us -> none  [the longest x4 14 us: matched(): lax.dynamic_slice_in_dim(jnp.concatenate([jnp.stack(blocks)] * 2), start, n)]
    another operation x2 -> x0, local copies, waits for them, and re-layouts: 11.5 us -> none  [the longest x1 6.03 us: per_device(): lefts = jnp.stack([across(left, step) for step in range(n)])]
    ppermute x14 -> x13, starting transfers between devices: 19.7 us -> 27.6 us  [the longest x12 26.1 us: along(): return lax.ppermute(block, axis, [(k, k ^ step) for k in range(n)])]
    unnamed x29 -> x28, local copies, waits for them, and re-layouts: 1.5 us -> 6.3 us
    dot_general x2 -> x0, local copies, waits for them, and re-layouts: 3.75 us -> none  [the longest x1 1.89 us: per_device(): jnp.einsum('sikh,sjkh->ijh', lefts, rights, preferred_element_type=jnp.fl...]
  transfers between devices with their start and end apart: 14 -> 13, of which waited for: 5 -> 3; matrix products, arithmetic and copies ran while one was open for 14% -> 1% of each run, Pallas kernels for 0% -> 19%
where the time goes in v4:
time: 59.5 us; the launch traced here: 59.1 us
  starting transfers between devices  27.6 us (46%)
  Pallas kernels  16.3 us (27%)
  waiting for transfers between devices  7.9 us (13%)
  local copies, waits for them, and re-layouts  6.37 us (11%)
  other arithmetic  0.66 us (1%)
    ppermute x12, starting transfers between devices, along(): return lax.ppermute(block, axis, [(k, k ^ step) for k in range(n)])  26.1 us
    pallas_call x10, Pallas kernels, call(): pl.pallas_call(kernel, out_shape=outs, scratch_shapes=scratches, input_ou...  16.3 us
    ppermute x12, waiting for transfers between devices, along(): return lax.ppermute(block, axis, [(k, k ^ step) for k in range(n)])  7.9 us
    unnamed x28, local copies, waits for them, and re-layouts  6.3 us
    ppermute x1, starting transfers between devices, mirrored(): return lax.ppermute(block, ('row', 'col'), pairs)  1.56 us
  transfers between devices with their start and end apart: 13, of which 3 were waited for; matrix products, arithmetic and copies ran while one was open for 1% of the time, Pallas kernels for 19%

profile of v4, /device:TPU:0, one launch (start us, length us, event | category | flops | bytes accessed | tf_op | source)
XLA Modules:
  0.0 59.1 jit_solution(16993816127519114949)
XLA Ops:
  0.0 1.6 %collective-permute-start.1 = (bf16[576,128]{1,0:T(8,128)(2,1)}, bf16[576,128]{1,0:T(8,128)(2,1)S(1)}, u32[]{:S(2)}, u32[]{:S(2)}) collective-permute-start(bf16[576,128]{1,0:T(8,128)(2,1)} %bitcast.2), channel_id=1, source_target_pairs={{0,0},{1,8},{2,4},{3,12},{4,1},{5,9},{6,5},{7,13},{8,2},{9,10},{10... | collective-permute-start | bytes 442376 | tf_op jit(solution)/shard_map/ppermute | solution.py:233
  1.6 0.0 collective-permute-done.1.refs_0_
  1.6 11.6 %collective-permute-start.2 = (bf16[576,128]{1,0:T(8,128)(2,1)S(1)}, bf16[576,128]{1,0:T(8,128)(2,1)S(1)}, u32[]{:S(2)}, u32[]{:S(2)}) collective-permute-start(bf16[576,128]{1,0:T(8,128)(2,1)S(1)} %collective-permute-done.1.refs_0_), channel_id=1, source_target_pairs={{0,4},{4,0},{8,12},{12,8},{1,5},{5,1},{9,13},{13,9},{2,6},{6,2},{1... | collective-permute-start | bytes 442376 | tf_op jit(solution)/shard_map/ppermute | solution.py:229
  13.1 0.2 collective-permute-start.3
  13.4 1.1 %collective-permute-start.4 = (bf16[576,128]{1,0:T(8,128)(2,1)S(1)}, bf16[576,128]{1,0:T(8,128)(2,1)S(1)}, u32[]{:S(2)}, u32[]{:S(2)}) collective-permute-start(bf16[576,128]{1,0:T(8,128)(2,1)S(1)} %collective-permute-done.1.refs_0_), channel_id=1, source_target_pairs={{0,12},{4,8},{8,4},{12,0},{1,13},{5,9},{9,5},{13,1},{2,14},{6,10},... | collective-permute-start | bytes 442376 | tf_op jit(solution)/shard_map/ppermute | solution.py:229
  14.5 1.3 %collective-permute-start.6 = (bf16[576,128]{1,0:T(8,128)(2,1)}, bf16[576,128]{1,0:T(8,128)(2,1)S(1)}, u32[]{:S(2)}, u32[]{:S(2)}) collective-permute-start(bf16[576,128]{1,0:T(8,128)(2,1)} %bitcast.3), channel_id=1, source_target_pairs={{0,1},{1,0},{2,3},{3,2},{4,5},{5,4},{6,7},{7,6},{8,9},{9,8},{10,11... | collective-permute-start | bytes 442376 | tf_op jit(solution)/shard_map/ppermute | solution.py:229
  15.8 2.9 %collective-permute-start.5 = (bf16[576,128]{1,0:T(8,128)(2,1)}, bf16[576,128]{1,0:T(8,128)(2,1)S(1)}, u32[]{:S(2)}, u32[]{:S(2)}) collective-permute-start(bf16[576,128]{1,0:T(8,128)(2,1)} %bitcast.4), channel_id=1, source_target_pairs={{0,3},{1,2},{2,1},{3,0},{4,7},{5,6},{6,5},{7,4},{8,11},{9,10},{10,... | collective-permute-start | bytes 442376 | tf_op jit(solution)/shard_map/ppermute | solution.py:229
  18.8 0.0 collective-permute-done.2.refs_1_
  18.8 0.4 collective-permute-start
  19.1 0.7 %convert_element_type.3 = f32[96]{0:T(128)S(1)} convert(s32[96]{0:T(128)} %param.11) | non-fusion elementwise | flops 96 | bytes 768 | tf_op jit(solution)/shard_map/convert_element_type | solution.py:258
  19.8 0.1 broadcast_in_dim.2.mask.refs_4_.refs_1_
  19.9 1.0 %copy-done = bf16[2,128,640]{2,1,0:T(8,128)(2,1)S(1)} copy-done((bf16[2,128,640]{2,1,0:T(8,128)(2,1)S(1)}, bf16[2,128,640]{2,1,0:T(8,128)(2,1)}, u32[]{:S(2)}) %copy-start) | copy-done | bytes 327704
  20.8 0.9 %copy-done.3 = bf16[24,24,128]{2,1,0:T(8,128)(2,1)S(1)} copy-done((bf16[24,24,128]{2,1,0:T(8,128)(2,1)S(1)}, bf16[24,24,128]{2,1,0:T(8,128)(2,1)}, u32[]{:S(2)}) %copy-start.3) | copy-done | bytes 147480
  21.8 0.7 %copy-done.6 = f32[2,640]{1,0:T(2,128)S(1)} copy-done((f32[2,640]{1,0:T(2,128)S(1)}, f32[2,640]{1,0:T(2,128)}, u32[]{:S(2)}) %copy-start.6) | copy-done | bytes 5144
  22.4 0.7 %copy-done.7 = f32[2,128]{1,0:T(2,128)S(1)} copy-done((f32[2,128]{1,0:T(2,128)S(1)}, f32[2,128]{1,0:T(2,128)}, u32[]{:S(2)}) %copy-start.7) | copy-done | bytes 1048
  23.1 0.7 %copy-done.9 = f32[2,128]{1,0:T(2,128)S(1)} copy-done((f32[2,128]{1,0:T(2,128)S(1)}, f32[2,128]{1,0:T(2,128)}, u32[]{:S(2)}) %copy-start.9) | copy-done | bytes 1048
  23.8 1.0 %own_sides.1 = (f32[576,128]{1,0:T(8,128)S(1)}, f32[576,128]{1,0:T(8,128)S(1)}, f32[576,128]{1,0:T(8,128)S(1)}) custom-call(bf16[576,128]{1,0:T(8,128)(2,1)S(1)} %bitcast.6, f32[96,128]{1,0:T(8,128)S(1)} %broadcast_in_dim.2.mask.refs_4_.refs_1_, f32[2,128]{1,0:T(2,128)S(1)} %copy-done.7, f32[2,128]{1,0:T(2,128)S(1)} %copy-done.9, ...), custom_call_target="tpu_custom_call" | custom-call | tf_op jit(solution)/shard_map/own_sides/pallas_call | solution.py:247
  24.8 0.0 collective-permute-done.3.refs_2_
  24.8 0.0 collective-permute-done.4.refs_3_
  24.8 0.0 copy-start.1
  24.8 1.0 %copy-done.1 = bf16[2,128,640]{2,1,0:T(8,128)(2,1)S(1)} copy-done((bf16[2,128,640]{2,1,0:T(8,128)(2,1)S(1)}, bf16[2,128,640]{2,1,0:T(8,128)(2,1)}, u32[]{:S(2)}) %copy-start.1) | copy-done | bytes 327704
  25.8 0.7 %copy-done.8 = f32[2,128]{1,0:T(2,128)S(1)} copy-done((f32[2,128]{1,0:T(2,128)S(1)}, f32[2,128]{1,0:T(2,128)}, u32[]{:S(2)}) %copy-start.8) | copy-done | bytes 1048
  26.4 0.7 %copy-done.10 = f32[2,128]{1,0:T(2,128)S(1)} copy-done((f32[2,128]{1,0:T(2,128)S(1)}, f32[2,128]{1,0:T(2,128)}, u32[]{:S(2)}) %copy-start.10) | copy-done | bytes 1048
  27.1 4.1 %column_sides.1 = (f32[4,576,128]{2,1,0:T(8,128)S(1)}, f32[4,576,128]{2,1,0:T(8,128)S(1)}, bf16[576,128]{1,0:T(8,128)(2,1)S(1)}, f32[576,128]{1,0:T(8,128)S(1)}, f32[2,576,128]{2,1,0:T(8,128)S(1)}) custom-call(bf16[576,128]{1,0:T(8,128)(2,1)S(1)} %collective-permute-done.1.refs_0_, bf16[576,128]{1,0:T(8,128)(2,1)S(1)} %collective-permute-done.2.refs_1_, ...), custom_call_target="tpu_custom_call" | custom-call | tf_op jit(solution)/shard_map/column_sides/pallas_call | solution.py:247
  31.2 1.8 %row_slot.2.refs_8_ = f32[2,576,128]{2,1,0:T(8,128)S(1)} custom-call(bf16[576,128]{1,0:T(8,128)(2,1)S(1)} %collective-permute-done.6.refs_0_, f32[96,128]{1,0:T(8,128)S(1)} %broadcast_in_dim.2.mask.refs_4_.refs_1_, f32[2,128]{1,0:T(2,128)S(1)} %copy-done.8, f32[2,128]{1,0:T(2,128)S(1)} %copy-done.10, ...), custom_call_target="tpu_custom_call", output_to_operand_aliasing={{}: (8, {})} | custom-call | tf_op jit(solution)/shard_map/row_slot/pallas_call | solution.py:247
  33.0 0.0 copy-start.2
  33.0 0.0 copy-start.4
  33.0 0.0 copy-start.5
  33.0 0.0 copy-start.11
  33.0 0.0 copy-start.12
  33.0 0.0 copy-start.13
  33.1 1.8 %row_slot.3.refs_8_ = f32[2,576,128]{2,1,0:T(8,128)S(1)} custom-call(bf16[576,128]{1,0:T(8,128)(2,1)S(1)} %collective-permute-done.5.refs_0_, f32[96,128]{1,0:T(8,128)S(1)} %broadcast_in_dim.2.mask.refs_4_.refs_1_, f32[2,128]{1,0:T(2,128)S(1)} %copy-done.8, f32[2,128]{1,0:T(2,128)S(1)} %copy-done.10, ...), custom_call_target="tpu_custom_call", output_to_operand_aliasing={{}: (8, {})} | custom-call | tf_op jit(solution)/shard_map/row_slot/pallas_call | solution.py:247
  34.8 0.0 collective-permute-done.refs_0_
  34.9 3.5 %last_slot.1 = (bf16[576,128]{1,0:T(8,128)(2,1)S(1)}, bf16[576,128]{1,0:T(8,128)(2,1)S(1)}, bf16[576,128]{1,0:T(8,128)(2,1)S(1)}) custom-call(bf16[576,128]{1,0:T(8,128)(2,1)S(1)} %collective-permute-done.refs_0_, f32[96,128]{1,0:T(8,128)S(1)} %broadcast_in_dim.2.mask.refs_4_.refs_1_, f32[2,128]{1,0:T(2,128)S(1)} %copy-done.8, f32[2,128]{1,0:T(2,128)S(1)} %copy-done.10, ...), custom_call_target="tpu_custom_call" | custom-call | tf_op jit(solution)/shard_map/last_slot/pallas_call | solution.py:247
  38.4 1.1 %collective-permute-start.10 = (bf16[576,128]{1,0:T(8,128)(2,1)S(1)}, bf16[576,128]{1,0:T(8,128)(2,1)S(1)}, u32[]{:S(2)}, u32[]{:S(2)}) collective-permute-start(bf16[576,128]{1,0:T(8,128)(2,1)S(1)} %get-tuple-element.27.refs_0_), channel_id=1, source_target_pairs={{0,12},{4,8},{8,4},{12,0},{1,13},{5,9},{9,5},{13,1},{2,14},{6,10},... | collective-permute-start | bytes 442376 | tf_op jit(solution)/shard_map/ppermute | solution.py:229
  39.5 0.8 %collective-permute-start.8 = (bf16[576,128]{1,0:T(8,128)(2,1)S(1)}, bf16[576,128]{1,0:T(8,128)(2,1)S(1)}, u32[]{:S(2)}, u32[]{:S(2)}) collective-permute-start(bf16[576,128]{1,0:T(8,128)(2,1)S(1)} %get-tuple-element.27.refs_0_), channel_id=1, source_target_pairs={{0,4},{4,0},{8,12},{12,8},{1,5},{5,1},{9,13},{13,9},{2,6},{6,2},{1... | collective-permute-start | bytes 442376 | tf_op jit(solution)/shard_map/ppermute | solution.py:229
  40.3 0.3 collective-permute-start.9
  40.6 1.1 %collective-permute-start.12 = (bf16[576,128]{1,0:T(8,128)(2,1)S(1)}, bf16[576,128]{1,0:T(8,128)(2,1)S(1)}, u32[]{:S(2)}, u32[]{:S(2)}) collective-permute-start(bf16[576,128]{1,0:T(8,128)(2,1)S(1)} %get-tuple-element.26.refs_4_), channel_id=1, source_target_pairs={{0,1},{1,0},{2,3},{3,2},{4,5},{5,4},{6,7},{7,6},{8,9},{9,8},{10,11... | collective-permute-start | bytes 442376 | tf_op jit(solution)/shard_map/ppermute | solution.py:229
  41.7 2.9 %collective-permute-start.11 = (bf16[576,128]{1,0:T(8,128)(2,1)S(1)}, bf16[576,128]{1,0:T(8,128)(2,1)S(1)}, u32[]{:S(2)}, u32[]{:S(2)}) collective-permute-start(bf16[576,128]{1,0:T(8,128)(2,1)S(1)} %get-tuple-element.26.refs_4_), channel_id=1, source_target_pairs={{0,3},{1,2},{2,1},{3,0},{4,7},{5,6},{6,5},{7,4},{8,11},{9,10},{10,... | collective-permute-start | bytes 442376 | tf_op jit(solution)/shard_map/ppermute | solution.py:229
  44.6 2.3 %collective-permute-start.7 = (bf16[576,128]{1,0:T(8,128)(2,1)S(1)}, bf16[576,128]{1,0:T(8,128)(2,1)S(1)}, u32[]{:S(2)}, u32[]{:S(2)}) collective-permute-start(bf16[576,128]{1,0:T(8,128)(2,1)S(1)} %get-tuple-element.26.refs_4_), channel_id=1, source_target_pairs={{0,2},{1,3},{2,0},{3,1},{4,6},{5,7},{6,4},{7,5},{8,10},{9,11},{10,... | collective-permute-start | bytes 442376 | tf_op jit(solution)/shard_map/ppermute | solution.py:229
  46.9 0.5 gate.1.gating
  47.4 0.3 collective-permute-done.9.refs_2_
  47.7 0.7 %right_slots.1 = (f32[4,576,128]{2,1,0:T(8,128)S(1)}, f32[576,128]{1,0:T(8,128)S(1)}) custom-call(bf16[576,128]{1,0:T(8,128)(2,1)S(1)} %get-tuple-element.27.refs_0_, bf16[576,128]{1,0:T(8,128)(2,1)S(1)} %collective-permute-done.8.refs_1_, bf16[576,128]{1,0:T(8,128)(2,1)S(1)} %collective-permute-done.9.refs_2_, ...), custom_call_target="tpu_custom_call" | custom-call | tf_op jit(solution)/shard_map/right_slots/pallas_call | solution.py:247
  48.4 0.6 %left_slot.2.refs_2_ = f32[576,128]{1,0:T(8,128)S(1)} custom-call(bf16[576,128]{1,0:T(8,128)(2,1)S(1)} %collective-permute-done.12.refs_0_, f32[4,576,128]{2,1,0:T(8,128)S(1)} %get-tuple-element.28.refs_1_.rights, f32[576,128]{1,0:T(8,128)S(1)} %get-tuple-element.29.refs_2_), custom_call_target="tpu_custom_call", output_to_operand_aliasing={{}: (2, {})} | custom-call | tf_op jit(solution)/shard_map/left_slot/pallas_call | solution.py:247
  49.1 3.5 %collective-permute-done.11.refs_0_ = bf16[576,128]{1,0:T(8,128)(2,1)S(1)} collective-permute-done((bf16[576,128]{1,0:T(8,128)(2,1)S(1)}, bf16[576,128]{1,0:T(8,128)(2,1)S(1)}, u32[]{:S(2)}, u32[]{:S(2)}) %collective-permute-start.11) | collective-permute-done | bytes 147488 | tf_op jit(solution)/shard_map/ppermute | solution.py:229
  52.6 0.6 %left_slot.3.old = f32[576,128]{1,0:T(8,128)S(1)} custom-call(bf16[576,128]{1,0:T(8,128)(2,1)S(1)} %collective-permute-done.11.refs_0_, f32[4,576,128]{2,1,0:T(8,128)S(1)} %get-tuple-element.28.refs_1_.rights, f32[576,128]{1,0:T(8,128)S(1)} %left_slot.2.refs_2_), custom_call_target="tpu_custom_call", output_to_operand_aliasing={{}: (2, {})} | custom-call | tf_op jit(solution)/shard_map/left_slot/pallas_call | solution.py:247
  53.2 4.1 %collective-permute-done.7.left = bf16[576,128]{1,0:T(8,128)(2,1)S(1)} collective-permute-done((bf16[576,128]{1,0:T(8,128)(2,1)S(1)}, bf16[576,128]{1,0:T(8,128)(2,1)S(1)}, u32[]{:S(2)}, u32[]{:S(2)}) %collective-permute-start.7) | collective-permute-done | bytes 147488 | tf_op jit(solution)/shard_map/ppermute | solution.py:229
  57.3 1.9 %end.1 = bf16[576,128]{1,0:T(8,128)(2,1)} custom-call(bf16[576,128]{1,0:T(8,128)(2,1)S(1)} %collective-permute-done.7.left, f32[4,576,128]{2,1,0:T(8,128)S(1)} %get-tuple-element.28.refs_1_.rights, f32[576,128]{1,0:T(8,128)S(1)} %left_slot.3.old, bf16[576,128]{1,0:T(8,128)(2,1)S(1)} %get-tuple-element.30.pair, f32[576,128]{1,0:T(8,128)S(1)} %gate.1.gating, ...), custom_call_target="tpu_custom_call" | custom-call | tf_op jit(solution)/shard_map/end/pallas_call | solution.py:247
  (18 shorter events, 0.0 us)
Async XLA Ops:
  0.0 1.6 %collective-permute-start.1 = (bf16[576,128]{1,0:T(8,128)(2,1)}, bf16[576,128]{1,0:T(8,128)(2,1)S(1)}, u32[]{:S(2)}, u32[]{:S(2)}) collective-permute-start(bf16[576,128]{1,0:T(8,128)(2,1)} %bitcast.2), channel_id=1, source_target_pairs={{0,0},{1,8},{2,4},{3,12},{4,1},{5,9},{6,5},{7,13},{8,2},{9,10},{10... | collective-permute-start | bytes 442376 | tf_op jit(solution)/shard_map/ppermute | solution.py:233
  1.6 17.2 %collective-permute-start.2 = (bf16[576,128]{1,0:T(8,128)(2,1)S(1)}, bf16[576,128]{1,0:T(8,128)(2,1)S(1)}, u32[]{:S(2)}, u32[]{:S(2)}) collective-permute-start(bf16[576,128]{1,0:T(8,128)(2,1)S(1)} %collective-permute-done.1.refs_0_), channel_id=1, source_target_pairs={{0,4},{4,0},{8,12},{12,8},{1,5},{5,1},{9,13},{13,9},{2,6},{6,2},{1... | collective-permute-start | bytes 442376 | tf_op jit(solution)/shard_map/ppermute | solution.py:229
  13.1 11.6 %collective-permute-start.3 = (bf16[576,128]{1,0:T(8,128)(2,1)S(1)}, bf16[576,128]{1,0:T(8,128)(2,1)S(1)}, u32[]{:S(2)}, u32[]{:S(2)}) collective-permute-start(bf16[576,128]{1,0:T(8,128)(2,1)S(1)} %collective-permute-done.1.refs_0_), channel_id=1, source_target_pairs={{0,8},{4,12},{8,0},{12,4},{1,9},{5,13},{9,1},{13,5},{2,10},{6,14},... | collective-permute-start | bytes 442376 | tf_op jit(solution)/shard_map/ppermute | solution.py:229
  13.4 11.4 %collective-permute-start.4 = (bf16[576,128]{1,0:T(8,128)(2,1)S(1)}, bf16[576,128]{1,0:T(8,128)(2,1)S(1)}, u32[]{:S(2)}, u32[]{:S(2)}) collective-permute-start(bf16[576,128]{1,0:T(8,128)(2,1)S(1)} %collective-permute-done.1.refs_0_), channel_id=1, source_target_pairs={{0,12},{4,8},{8,4},{12,0},{1,13},{5,9},{9,5},{13,1},{2,14},{6,10},... | collective-permute-start | bytes 442376 | tf_op jit(solution)/shard_map/ppermute | solution.py:229
  14.5 16.7 %collective-permute-start.6 = (bf16[576,128]{1,0:T(8,128)(2,1)}, bf16[576,128]{1,0:T(8,128)(2,1)S(1)}, u32[]{:S(2)}, u32[]{:S(2)}) collective-permute-start(bf16[576,128]{1,0:T(8,128)(2,1)} %bitcast.3), channel_id=1, source_target_pairs={{0,1},{1,0},{2,3},{3,2},{4,5},{5,4},{6,7},{7,6},{8,9},{9,8},{10,11... | collective-permute-start | bytes 442376 | tf_op jit(solution)/shard_map/ppermute | solution.py:229
  15.8 17.2 %collective-permute-start.5 = (bf16[576,128]{1,0:T(8,128)(2,1)}, bf16[576,128]{1,0:T(8,128)(2,1)S(1)}, u32[]{:S(2)}, u32[]{:S(2)}) collective-permute-start(bf16[576,128]{1,0:T(8,128)(2,1)} %bitcast.4), channel_id=1, source_target_pairs={{0,3},{1,2},{2,1},{3,0},{4,7},{5,6},{6,5},{7,4},{8,11},{9,10},{10,... | collective-permute-start | bytes 442376 | tf_op jit(solution)/shard_map/ppermute | solution.py:229
  18.8 16.1 %collective-permute-start = (bf16[576,128]{1,0:T(8,128)(2,1)}, bf16[576,128]{1,0:T(8,128)(2,1)S(1)}, u32[]{:S(2)}, u32[]{:S(2)}) collective-permute-start(bf16[576,128]{1,0:T(8,128)(2,1)} %bitcast.5), channel_id=1, source_target_pairs={{0,2},{1,3},{2,0},{3,1},{4,6},{5,7},{6,4},{7,5},{8,10},{9,11},{10,... | collective-permute-start | bytes 442376 | tf_op jit(solution)/shard_map/ppermute | solution.py:229
  19.9 1.0 %copy-start = (bf16[2,128,640]{2,1,0:T(8,128)(2,1)S(1)}, bf16[2,128,640]{2,1,0:T(8,128)(2,1)}, u32[]{:S(2)}) copy-start(bf16[2,128,640]{2,1,0:T(8,128)(2,1)} %w_in.3) | copy-start | bytes 983044
  20.8 0.9 %copy-start.3 = (bf16[24,24,128]{2,1,0:T(8,128)(2,1)S(1)}, bf16[24,24,128]{2,1,0:T(8,128)(2,1)}, u32[]{:S(2)}) copy-start(bf16[24,24,128]{2,1,0:T(8,128)(2,1)} %param.10) | copy-start | bytes 442372
  21.8 0.7 %copy-start.6 = (f32[2,640]{1,0:T(2,128)S(1)}, f32[2,640]{1,0:T(2,128)}, u32[]{:S(2)}) copy-start(f32[2,640]{1,0:T(2,128)} %bias_in.3) | copy-start | bytes 15364
  22.4 0.7 %copy-start.7 = (f32[2,128]{1,0:T(2,128)S(1)}, f32[2,128]{1,0:T(2,128)}, u32[]{:S(2)}) copy-start(f32[2,128]{1,0:T(2,128)} %in_gain.3) | copy-start | bytes 3076
  23.1 0.7 %copy-start.9 = (f32[2,128]{1,0:T(2,128)S(1)}, f32[2,128]{1,0:T(2,128)}, u32[]{:S(2)}) copy-start(f32[2,128]{1,0:T(2,128)} %in_shift.3) | copy-start | bytes 3076
  24.8 1.0 %copy-start.1 = (bf16[2,128,640]{2,1,0:T(8,128)(2,1)S(1)}, bf16[2,128,640]{2,1,0:T(8,128)(2,1)}, u32[]{:S(2)}) copy-start(bf16[2,128,640]{2,1,0:T(8,128)(2,1)} %w_in.3) | copy-start | bytes 983044
  25.8 0.7 %copy-start.8 = (f32[2,128]{1,0:T(2,128)S(1)}, f32[2,128]{1,0:T(2,128)}, u32[]{:S(2)}) copy-start(f32[2,128]{1,0:T(2,128)} %in_gain.3) | copy-start | bytes 3076
  26.4 0.7 %copy-start.10 = (f32[2,128]{1,0:T(2,128)S(1)}, f32[2,128]{1,0:T(2,128)}, u32[]{:S(2)}) copy-start(f32[2,128]{1,0:T(2,128)} %in_shift.3) | copy-start | bytes 3076
  33.0 1.9 %copy-start.2 = (bf16[2,128,640]{2,1,0:T(8,128)(2,1)S(1)}, bf16[2,128,640]{2,1,0:T(8,128)(2,1)}, u32[]{:S(2)}) copy-start(bf16[2,128,640]{2,1,0:T(8,128)(2,1)} %w_in.3) | copy-start | bytes 983044
  33.0 1.9 %copy-start.4 = (bf16[24,24,128]{2,1,0:T(8,128)(2,1)S(1)}, bf16[24,24,128]{2,1,0:T(8,128)(2,1)}, u32[]{:S(2)}) copy-start(bf16[24,24,128]{2,1,0:T(8,128)(2,1)} %param.10) | copy-start | bytes 442372
  33.0 1.9 %copy-start.5 = (bf16[2,128,128]{2,1,0:T(8,128)(2,1)S(1)}, bf16[2,128,128]{2,1,0:T(8,128)(2,1)}, u32[]{:S(2)}) copy-start(bf16[2,128,128]{2,1,0:T(8,128)(2,1)} %w_out.1) | copy-start | bytes 196612
  33.0 1.9 %copy-start.11 = (f32[2,128]{1,0:T(2,128)S(1)}, f32[2,128]{1,0:T(2,128)}, u32[]{:S(2)}) copy-start(f32[2,128]{1,0:T(2,128)} %out_gain.1) | copy-start | bytes 3076
  33.0 1.9 %copy-start.12 = (f32[2,128]{1,0:T(2,128)S(1)}, f32[2,128]{1,0:T(2,128)}, u32[]{:S(2)}) copy-start(f32[2,128]{1,0:T(2,128)} %out_shift.1) | copy-start | bytes 3076
  33.0 1.9 %copy-start.13 = (f32[2,128]{1,0:T(2,128)S(1)}, f32[2,128]{1,0:T(2,128)}, u32[]{:S(2)}) copy-start(f32[2,128]{1,0:T(2,128)} %bias_out.1) | copy-start | bytes 3076
  38.4 6.2 %collective-permute-start.10 = (bf16[576,128]{1,0:T(8,128)(2,1)S(1)}, bf16[576,128]{1,0:T(8,128)(2,1)S(1)}, u32[]{:S(2)}, u32[]{:S(2)}) collective-permute-start(bf16[576,128]{1,0:T(8,128)(2,1)S(1)} %get-tuple-element.27.refs_0_), channel_id=1, source_target_pairs={{0,12},{4,8},{8,4},{12,0},{1,13},{5,9},{9,5},{13,1},{2,14},{6,10},... | collective-permute-start | bytes 442376 | tf_op jit(solution)/shard_map/ppermute | solution.py:229
  39.5 8.0 %collective-permute-start.8 = (bf16[576,128]{1,0:T(8,128)(2,1)S(1)}, bf16[576,128]{1,0:T(8,128)(2,1)S(1)}, u32[]{:S(2)}, u32[]{:S(2)}) collective-permute-start(bf16[576,128]{1,0:T(8,128)(2,1)S(1)} %get-tuple-element.27.refs_0_), channel_id=1, source_target_pairs={{0,4},{4,0},{8,12},{12,8},{1,5},{5,1},{9,13},{13,9},{2,6},{6,2},{1... | collective-permute-start | bytes 442376 | tf_op jit(solution)/shard_map/ppermute | solution.py:229
  40.3 7.5 %collective-permute-start.9 = (bf16[576,128]{1,0:T(8,128)(2,1)S(1)}, bf16[576,128]{1,0:T(8,128)(2,1)S(1)}, u32[]{:S(2)}, u32[]{:S(2)}) collective-permute-start(bf16[576,128]{1,0:T(8,128)(2,1)S(1)} %get-tuple-element.27.refs_0_), channel_id=1, source_target_pairs={{0,8},{4,12},{8,0},{12,4},{1,9},{5,13},{9,1},{13,5},{2,10},{6,14},... | collective-permute-start | bytes 442376 | tf_op jit(solution)/shard_map/ppermute | solution.py:229
  40.6 7.9 %collective-permute-start.12 = (bf16[576,128]{1,0:T(8,128)(2,1)S(1)}, bf16[576,128]{1,0:T(8,128)(2,1)S(1)}, u32[]{:S(2)}, u32[]{:S(2)}) collective-permute-start(bf16[576,128]{1,0:T(8,128)(2,1)S(1)} %get-tuple-element.26.refs_4_), channel_id=1, source_target_pairs={{0,1},{1,0},{2,3},{3,2},{4,5},{5,4},{6,7},{7,6},{8,9},{9,8},{10,11... | collective-permute-start | bytes 442376 | tf_op jit(solution)/shard_map/ppermute | solution.py:229
  41.7 10.9 %collective-permute-start.11 = (bf16[576,128]{1,0:T(8,128)(2,1)S(1)}, bf16[576,128]{1,0:T(8,128)(2,1)S(1)}, u32[]{:S(2)}, u32[]{:S(2)}) collective-permute-start(bf16[576,128]{1,0:T(8,128)(2,1)S(1)} %get-tuple-element.26.refs_4_), channel_id=1, source_target_pairs={{0,3},{1,2},{2,1},{3,0},{4,7},{5,6},{6,5},{7,4},{8,11},{9,10},{10,... | collective-permute-start | bytes 442376 | tf_op jit(solution)/shard_map/ppermute | solution.py:229
  44.6 12.7 %collective-permute-start.7 = (bf16[576,128]{1,0:T(8,128)(2,1)S(1)}, bf16[576,128]{1,0:T(8,128)(2,1)S(1)}, u32[]{:S(2)}, u32[]{:S(2)}) collective-permute-start(bf16[576,128]{1,0:T(8,128)(2,1)S(1)} %get-tuple-element.26.refs_4_), channel_id=1, source_target_pairs={{0,2},{1,3},{2,0},{3,1},{4,6},{5,7},{6,4},{7,5},{8,10},{9,11},{10,... | collective-permute-start | bytes 442376 | tf_op jit(solution)/shard_map/ppermute | solution.py:229

commit v5 on v4

--- a/solution.py
+++ b/solution.py
@@ -107,25 +107,40 @@
         target[...] = masked(side, outer, inner).astype(F32)
 
 
-def own_kernel(n, t, pair, mask, in_gain, in_shift, w_in, bias_in, left, right, gating, wide):
+def own_kernel(n, t, count, *refs):
+    sources, copies = refs[:count], refs[count : 2 * count - 3]
+    weights, bias, mask, left, right, gating = refs[2 * count - 3 : 2 * count + 3]
+    tokens, raw_weights, raw_bias, wide, arrived = refs[2 * count + 3 :]
+    pair, in_gain, in_shift = copies[:3]
     width = pair.shape[1]
-    r, c = lax.axis_index("row"), lax.axis_index("col")
+    targets = (tokens, raw_weights, raw_bias, *copies)
+    moves = [pltpu.make_async_copy(s, d, arrived.at[k]) for k, (s, d) in enumerate(zip(sources, targets))]
+    for move in moves:
+        move.start()
+    for move in moves:
+        move.wait()
+    r, c = lax.axis_index("row"), lax.axis_index("col")
+    rows = lax.broadcasted_iota(jnp.int32, (n * t, n * t), 0)
+    cols = lax.broadcasted_iota(jnp.int32, (n * t, n * t), 1)
+    spread = jnp.where(rows == cols, tokens[...].astype(F32), 0.0).astype(BF16)
+    mask[...] = dot(spread, jnp.ones((n * t, width), BF16))
+    weights[...] = raw_weights[...] * 0.5
+    bias[...] = raw_bias[...] * 0.5
     consts = constants(width)
-    weights, bias = w_in[0] * 0.5, bias_in[0:1] * 0.5
     outer, inner = mask_of(mask, c, t), mask_of(mask, r, t)
-    sides(pair, wide, left, right, outer, inner, consts, in_gain, in_shift, weights, bias)
+    sides(pair, wide, left, right, outer, inner, consts, in_gain, in_shift, weights[0], bias[0:1])
     normed = norm_pair(pair[...], consts, in_gain[0:1], in_shift[0:1])
-    gating[...] = gate(normed, weights[:, 4 * width :], bias[:, 4 * width :])
-
-
-def column_kernel(n, t, *refs):
-    blocks = refs[:n]
-    mask, in_gain, in_shift, w_in, bias_in, own_left, own_right = refs[n : n + 7]
-    lefts, rights, pair, gating, mixed, held, wide = refs[n + 7 :]
+    gating[...] = gate(normed, weights[0, :, 4 * width :], bias[0:1, 4 * width :])
+
+
+def column_kernel(n, t, steps, *refs):
+    blocks, rows = refs[:n], refs[n : 2 * n - 2]
+    mask, in_gain, in_shift, w_in, bias_in, own_left, own_right = refs[2 * n - 2 : 2 * n + 5]
+    lefts, rights, pair, gating, mixed, held, wide, left, right = refs[2 * n + 5 :]
     width = wide.shape[1]
     r, c = lax.axis_index("row"), lax.axis_index("col")
     consts = constants(width)
-    weights, bias = w_in[0] * 0.5, bias_in[0:1] * 0.5
+    weights, bias = w_in[0], bias_in[0:1]
     for s in range(n):
         held[s] = blocks[s][...]
 
@@ -144,21 +159,21 @@
     gating[...] = gate(normed, weights[:, 4 * width :], bias[:, 4 * width :])
     mix(mixed.at[0], None, row_of(own_left), rows_of(rights, t, c), t)
     mix(mixed.at[1], None, row_of(lefts, c), rows_of(own_right, t), t)
+    for step, block in zip(steps, rows):
+        slot_sum(
+            n, t, step, block, mask, in_gain, in_shift, w_in, bias_in, lefts, rights, mixed, mixed, wide, left, right
+        )
 
 
 def slot_sum(n, t, slot, block, mask, in_gain, in_shift, w_in, bias_in, lefts, rights, old, mixed, wide, left, right):
     r, c = lax.axis_index("row"), lax.axis_index("col")
     consts = constants(wide.shape[1])
-    weights, bias = w_in[0] * 0.5, bias_in[0:1] * 0.5
+    weights, bias = w_in[0], bias_in[0:1]
     b = c ^ slot
     outer, inner = mask_of(mask, b, t), mask_of(mask, r, t)
     sides(block, wide, left, right, outer, inner, consts, in_gain, in_shift, weights, bias)
     mix(mixed.at[0], old.at[0], row_of(left), rows_of(rights, t, b), t)
     mix(mixed.at[1], old.at[1], row_of(lefts, b), rows_of(right, t), t)
-
-
-def slot_kernel(n, t, slot, *refs):
-    slot_sum(n, t, slot, *refs)
 
 
 def last_kernel(n, t, slot, *refs):
@@ -171,7 +186,7 @@
     width = wide.shape[1]
     r, c = lax.axis_index("row"), lax.axis_index("col")
     consts = constants(width)
-    weights, bias = w_in[1] * 0.5, bias_in[1:2] * 0.5
+    weights, bias = w_in[1], bias_in[1:2]
     here, there = mask_of(mask, r, t), mask_of(mask, c, t)
     for k, (base, factor) in enumerate(((pair, gating), (col_pair, col_gating))):
         updated = finish(
@@ -190,7 +205,7 @@
 def gate_kernel(pair, in_gain, in_shift, w_in, bias_in, gating):
     width = pair.shape[1]
     normed = norm_pair(pair[...], constants(width), in_gain[1:2], in_shift[1:2])
-    gating[...] = gate(normed, w_in[1, :, 4 * width :] * 0.5, bias_in[1:2, 4 * width :] * 0.5)
+    gating[...] = gate(normed, w_in[1, :, 4 * width :], bias_in[1:2, 4 * width :])
 
 
 def right_kernel(n, t, *refs):
@@ -243,10 +258,11 @@
         twice = jax.ShapeDtypeStruct((2,) + area, F32)
         scratch = pltpu.VMEM(area, F32)
 
-        def call(kernel, name, outs, scratches, ops, *operands, alias=None):
+        def call(kernel, name, outs, scratches, *operands, alias=None, **specs):
             return pl.pallas_call(
                 kernel,
                 out_shape=outs,
+                **specs,
                 scratch_shapes=scratches,
                 input_output_aliases=alias or {},
 
@@ -254,48 +270,43 @@
                 name=name,
             )(*operands)
 
-        work = 2 * t**4 * width
-        mask = jnp.broadcast_to(token_mask.astype(F32)[:, None], (n * t, width))
-        ins = (mask, in_gain, in_shift, w_in, bias_in)
-        outs = (out_gain, out_shift, w_out, bias_out)
         pair = pair.reshape(area)
         col_block = mirrored(pair)
         steps = [step for step in range(1, n) if step != half] + [half]
         rows = [along(pair, "col", step) for step in steps]
-        own_left, own_right, gating = call(
-            functools.partial(own_kernel, n, t), "own_sides", (broad,) * 3, [scratch], work, pair, *ins
-        )
+        tokens = token_mask.reshape(1, n * t)
+        raw = (tokens, w_in, bias_in, pair, in_gain, in_shift, out_gain, out_shift, w_out, bias_out)
+        like = [jax.ShapeDtypeStruct(array.shape, array.dtype) for array in raw]
+        mask = jax.ShapeDtypeStruct((n * t, width), F32)
+        pair, in_gain, in_shift, *outs, w_in, bias_in, mask, own_left, own_right, gating = call(
+            functools.partial(own_kernel, n, t, len(raw)),
+            "own_sides",
+            (*like[3:], like[1], like[2], mask, broad, broad, broad),
+            [
+                *(pltpu.VMEM(array.shape, array.dtype) for array in raw[:3]),
+                scratch,
+                pltpu.SemaphoreType.DMA((len(raw),)),
+            ],
+            *raw,
+            in_specs=[pl.BlockSpec(memory_space=pltpu.MemorySpace.HBM)] * len(raw),
+        )
+        ins = (mask, in_gain, in_shift, w_in, bias_in)
         lefts, rights, col_pair, col_gating, mixed = call(
-            functools.partial(column_kernel, n, t),
+            functools.partial(column_kernel, n, t, steps[:-1]),
             "column_sides",
             (stacked, stacked, narrow, broad, twice),
-            [pltpu.VMEM((n,) + area, BF16), scratch],
-            n * work,
+            [pltpu.VMEM((n,) + area, BF16)] + [scratch] * 3,
             *plane(col_block),
+            *rows[:-1],
             *ins,
             own_left,
             own_right,
         )
-        for step, block in zip(steps[:-1], rows[:-1]):
-            mixed = call(
-                functools.partial(slot_kernel, n, t, step),
-                "row_slot",
-                twice,
-                [scratch] * 3,
-                work,
-                block,
-                *ins,
-                lefts,
-                rights,
-                mixed,
-                alias={8: 0},
-            )
         pair, left, right = call(
             functools.partial(last_kernel, n, t, steps[-1]),
             "last_slot",
             (narrow,) * 3,
             [pltpu.VMEM((2,) + area, F32)] + [scratch] * 3,
-            work,
             rows[-1],
             *ins,
             lefts,
@@ -308,9 +319,9 @@
             col_gating,
         )
         blocks = [along(left, "col", step) for step in steps]
-        gating = call(gate_kernel, "gate", broad, [], work, pair, *ins[1:])
+        gating = call(gate_kernel, "gate", broad, [], pair, *ins[1:])
         rights, mixed = call(
-            functools.partial(right_kernel, n, t), "right_slots", (stacked, broad), [scratch], work, *plane(right), left
+            functools.partial(right_kernel, n, t), "right_slots", (stacked, broad), [scratch], *plane(right), left
         )
         for step, block in zip(steps[:-1], blocks[:-1]):
             mixed = call(
@@ -318,7 +329,6 @@
                 "left_slot",
                 broad,
                 [scratch],
-                work,
                 block,
                 rights,
                 mixed,
@@ -329,7 +339,6 @@
             "end",
             narrow,
             [scratch] * 2,
-            work,
             blocks[-1],
             rights,
             mixed,

time: 59.5 us -> 59.6 us (level)
  starting transfers between devices: 27.6 us -> 24.1 us
  waiting for transfers between devices: 7.9 us -> 10.7 us
  local copies, waits for them, and re-layouts: 6.37 us -> 7.46 us
  other arithmetic: 0.66 us -> 0 us
  Pallas kernels: 16.3 us -> 16.9 us
    ppermute x12, starting transfers between devices: 26.1 us -> 22.6 us  [along(): return lax.ppermute(block, axis, [(k, k ^ step) for k in range(n)])]
    ppermute x12, waiting for transfers between devices: 7.9 us -> 10.7 us  [along(): return lax.ppermute(block, axis, [(k, k ^ step) for k in range(n)])]
    unnamed x28 -> x20, local copies, waits for them, and re-layouts: 6.3 us -> 7.46 us
    convert_element_type x1 -> x0, other arithmetic: 0.66 us -> none  [per_device(): mask = jnp.broadcast_to(token_mask.astype(F32)[:, None], (n * t, width))]
    pallas_call x10 -> x8, Pallas kernels: 16.3 us -> 16.9 us  [call(): pl.pallas_call(kernel, out_shape=outs, **specs, scratch_shapes=scratches,...]
  transfers between devices with their start and end apart: 13 -> 13, of which waited for: 3 -> 3; matrix products, arithmetic and copies ran while one was open for 1% -> 0% of each run, Pallas kernels for 19% -> 20%
where the time goes in v5:
time: 59.6 us; the launch traced here: 59.3 us
  starting transfers between devices  24.1 us (40%)
  Pallas kernels  16.9 us (28%)
  waiting for transfers between devices  10.7 us (18%)
  local copies, waits for them, and re-layouts  7.46 us (13%)
    ppermute x12, starting transfers between devices, along(): return lax.ppermute(block, axis, [(k, k ^ step) for k in range(n)])  22.6 us
    pallas_call x8, Pallas kernels, call(): pl.pallas_call(kernel, out_shape=outs, **specs, scratch_shapes=scratches,...  16.9 us
    ppermute x12, waiting for transfers between devices, along(): return lax.ppermute(block, axis, [(k, k ^ step) for k in range(n)])  10.7 us
    unnamed x20, local copies, waits for them, and re-layouts  7.46 us
    ppermute x1, starting transfers between devices, mirrored(): return lax.ppermute(block, ('row', 'col'), pairs)  1.56 us
  transfers between devices with their start and end apart: 13, of which 3 were waited for; matrix products, arithmetic and copies ran while one was open for 0% of the time, Pallas kernels for 20%

profile of v5, /device:TPU:0, one launch (start us, length us, event | category | flops | bytes accessed | tf_op | source)
XLA Modules:
  0.0 59.3 jit_solution(18041425754548704867)
XLA Ops:
  0.0 1.6 %collective-permute-start.1 = (bf16[576,128]{1,0:T(8,128)(2,1)}, bf16[576,128]{1,0:T(8,128)(2,1)S(1)}, u32[]{:S(2)}, u32[]{:S(2)}) collective-permute-start(bf16[576,128]{1,0:T(8,128)(2,1)} %bitcast.3), channel_id=1, source_target_pairs={{0,0},{1,8},{2,4},{3,12},{4,1},{5,9},{6,5},{7,13},{8,2},{9,10},{10... | collective-permute-start | bytes 442376 | tf_op jit(solution)/shard_map/ppermute | solution.py:248
  1.6 4.8 %collective-permute-start.5 = (bf16[576,128]{1,0:T(8,128)(2,1)}, bf16[576,128]{1,0:T(8,128)(2,1)S(1)}, u32[]{:S(2)}, u32[]{:S(2)}) collective-permute-start(bf16[576,128]{1,0:T(8,128)(2,1)} %bitcast.4), channel_id=1, source_target_pairs={{0,1},{1,0},{2,3},{3,2},{4,5},{5,4},{6,7},{7,6},{8,9},{9,8},{10,11... | collective-permute-start | bytes 442376 | tf_op jit(solution)/shard_map/ppermute | solution.py:244
  6.4 1.3 %collective-permute-start.6 = (bf16[576,128]{1,0:T(8,128)(2,1)}, bf16[576,128]{1,0:T(8,128)(2,1)S(1)}, u32[]{:S(2)}, u32[]{:S(2)}) collective-permute-start(bf16[576,128]{1,0:T(8,128)(2,1)} %bitcast.5), channel_id=1, source_target_pairs={{0,3},{1,2},{2,1},{3,0},{4,7},{5,6},{6,5},{7,4},{8,11},{9,10},{10,... | collective-permute-start | bytes 442376 | tf_op jit(solution)/shard_map/ppermute | solution.py:244
  7.7 0.0 collective-permute-done.1.refs_0_
  7.7 6.1 %collective-permute-start.2 = (bf16[576,128]{1,0:T(8,128)(2,1)S(1)}, bf16[576,128]{1,0:T(8,128)(2,1)S(1)}, u32[]{:S(2)}, u32[]{:S(2)}) collective-permute-start(bf16[576,128]{1,0:T(8,128)(2,1)S(1)} %collective-permute-done.1.refs_0_), channel_id=1, source_target_pairs={{0,4},{4,0},{8,12},{12,8},{1,5},{5,1},{9,13},{13,9},{2,6},{6,2},{1... | collective-permute-start | bytes 442376 | tf_op jit(solution)/shard_map/ppermute | solution.py:244
  13.8 1.8 %collective-permute-start.3 = (bf16[576,128]{1,0:T(8,128)(2,1)S(1)}, bf16[576,128]{1,0:T(8,128)(2,1)S(1)}, u32[]{:S(2)}, u32[]{:S(2)}) collective-permute-start(bf16[576,128]{1,0:T(8,128)(2,1)S(1)} %collective-permute-done.1.refs_0_), channel_id=1, source_target_pairs={{0,8},{4,12},{8,0},{12,4},{1,9},{5,13},{9,1},{13,5},{2,10},{6,14},... | collective-permute-start | bytes 442376 | tf_op jit(solution)/shard_map/ppermute | solution.py:244
  15.6 0.1 collective-permute-start.4
  15.7 3.1 %collective-permute-done.5.refs_4_ = bf16[576,128]{1,0:T(8,128)(2,1)S(1)} collective-permute-done((bf16[576,128]{1,0:T(8,128)(2,1)}, bf16[576,128]{1,0:T(8,128)(2,1)S(1)}, u32[]{:S(2)}, u32[]{:S(2)}) %collective-permute-start.5) | collective-permute-done | bytes 147488 | tf_op jit(solution)/shard_map/ppermute | solution.py:244
  18.8 0.0 collective-permute-start
  18.8 0.0 copy-start
  18.8 1.0 %copy-done = bf16[2,128,640]{2,1,0:T(8,128)(2,1)S(1)} copy-done((bf16[2,128,640]{2,1,0:T(8,128)(2,1)S(1)}, bf16[2,128,640]{2,1,0:T(8,128)(2,1)}, u32[]{:S(2)}) %copy-start) | copy-done | bytes 327704
  19.8 0.0 copy-start.1
  19.8 0.9 %copy-done.1 = bf16[24,24,128]{2,1,0:T(8,128)(2,1)S(1)} copy-done((bf16[24,24,128]{2,1,0:T(8,128)(2,1)S(1)}, bf16[24,24,128]{2,1,0:T(8,128)(2,1)}, u32[]{:S(2)}) %copy-start.1) | copy-done | bytes 147480
  20.7 0.0 copy-start.2
  20.7 0.8 %copy-done.2 = bf16[2,128,128]{2,1,0:T(8,128)(2,1)S(1)} copy-done((bf16[2,128,128]{2,1,0:T(8,128)(2,1)S(1)}, bf16[2,128,128]{2,1,0:T(8,128)(2,1)}, u32[]{:S(2)}) %copy-start.2) | copy-done | bytes 65560
  21.6 0.0 copy-start.3
  21.6 0.7 %copy-done.3 = f32[2,640]{1,0:T(2,128)S(1)} copy-done((f32[2,640]{1,0:T(2,128)S(1)}, f32[2,640]{1,0:T(2,128)}, u32[]{:S(2)}) %copy-start.3) | copy-done | bytes 5144
  22.3 0.7 %copy-done.4 = f32[2,128]{1,0:T(2,128)S(1)} copy-done((f32[2,128]{1,0:T(2,128)S(1)}, f32[2,128]{1,0:T(2,128)}, u32[]{:S(2)}) %copy-start.4) | copy-done | bytes 1048
  22.9 0.7 %copy-done.5 = f32[2,128]{1,0:T(2,128)S(1)} copy-done((f32[2,128]{1,0:T(2,128)S(1)}, f32[2,128]{1,0:T(2,128)}, u32[]{:S(2)}) %copy-start.5) | copy-done | bytes 1048
  23.6 0.7 %copy-done.6 = f32[2,128]{1,0:T(2,128)S(1)} copy-done((f32[2,128]{1,0:T(2,128)S(1)}, f32[2,128]{1,0:T(2,128)}, u32[]{:S(2)}) %copy-start.6) | copy-done | bytes 1048
  24.3 0.7 %copy-done.7 = f32[2,128]{1,0:T(2,128)S(1)} copy-done((f32[2,128]{1,0:T(2,128)S(1)}, f32[2,128]{1,0:T(2,128)}, u32[]{:S(2)}) %copy-start.7) | copy-done | bytes 1048
  25.0 0.7 %copy-done.8 = f32[2,128]{1,0:T(2,128)S(1)} copy-done((f32[2,128]{1,0:T(2,128)S(1)}, f32[2,128]{1,0:T(2,128)}, u32[]{:S(2)}) %copy-start.8) | copy-done | bytes 1048
  25.7 0.7 %copy-done.9 = s32[96]{0:T(128)S(1)} copy-done((s32[96]{0:T(128)S(1)}, s32[96]{0:T(128)}, u32[]{:S(2)}) %copy-start.9) | copy-done | bytes 408
  26.3 1.6 %own_sides.1 = (bf16[576,128]{1,0:T(8,128)(2,1)S(1)}, f32[2,128]{1,0:T(2,128)S(1)}, f32[2,128]{1,0:T(2,128)S(1)}, f32[2,128]{1,0:T(2,128)S(1)}, f32[2,128]{1,0:T...) custom-call(s32[1,96]{1,0:T(1,128)S(1)} %bitcast.8, ...), custom_call_target="tpu_custom_call" | custom-call | tf_op jit(solution)/shard_map/own_sides/pallas_call | solution.py:262
  27.9 0.0 collective-permute-done.6.refs_5_
  27.9 0.0 collective-permute-done.2.refs_1_
  27.9 0.0 collective-permute-done.3.refs_2_
  27.9 0.0 collective-permute-done.4.refs_3_
  27.9 7.6 %column_sides.1 = (f32[4,576,128]{2,1,0:T(8,128)S(1)}, f32[4,576,128]{2,1,0:T(8,128)S(1)}, bf16[576,128]{1,0:T(8,128)(2,1)S(1)}, f32[576,128]{1,0:T(8,128)S(1)}, f32[2,576,128]{2,1,0:T(8,128)S(1)}) custom-call(bf16[576,128]{1,0:T(8,128)(2,1)S(1)} %collective-permute-done.1.refs_0_, bf16[576,128]{1,0:T(8,128)(2,1)S(1)} %collective-permute-done.2.refs_1_, ...), custom_call_target="tpu_custom_call" | custom-call | tf_op jit(solution)/shard_map/column_sides/pallas_call | solution.py:262
  35.5 0.0 collective-permute-done.refs_0_
  35.5 3.4 %last_slot.1 = (bf16[576,128]{1,0:T(8,128)(2,1)S(1)}, bf16[576,128]{1,0:T(8,128)(2,1)S(1)}, bf16[576,128]{1,0:T(8,128)(2,1)S(1)}) custom-call(bf16[576,128]{1,0:T(8,128)(2,1)S(1)} %collective-permute-done.refs_0_, f32[96,128]{1,0:T(8,128)S(1)} %get-tuple-element.28.refs_6_.refs_1_, f32[2,128]{1,0:T(2,128)S(1)} %get-tuple-element.29.refs_7_.refs_2_.in_gain, ...), custom_call_target="tpu_custom_call" | custom-call | tf_op jit(solution)/shard_map/last_slot/pallas_call | solution.py:262
  38.9 0.1 collective-permute-start.10
  39.0 0.3 collective-permute-start.8
  39.3 1.9 %collective-permute-start.9 = (bf16[576,128]{1,0:T(8,128)(2,1)S(1)}, bf16[576,128]{1,0:T(8,128)(2,1)S(1)}, u32[]{:S(2)}, u32[]{:S(2)}) collective-permute-start(bf16[576,128]{1,0:T(8,128)(2,1)S(1)} %get-tuple-element.47.refs_0_), channel_id=1, source_target_pairs={{0,8},{4,12},{8,0},{12,4},{1,9},{5,13},{9,1},{13,5},{2,10},{6,14},... | collective-permute-start | bytes 442376 | tf_op jit(solution)/shard_map/ppermute | solution.py:244
  41.1 0.6 %collective-permute-start.12 = (bf16[576,128]{1,0:T(8,128)(2,1)S(1)}, bf16[576,128]{1,0:T(8,128)(2,1)S(1)}, u32[]{:S(2)}, u32[]{:S(2)}) collective-permute-start(bf16[576,128]{1,0:T(8,128)(2,1)S(1)} %get-tuple-element.46.refs_4_), channel_id=1, source_target_pairs={{0,1},{1,0},{2,3},{3,2},{4,5},{5,4},{6,7},{7,6},{8,9},{9,8},{10,11... | collective-permute-start | bytes 442376 | tf_op jit(solution)/shard_map/ppermute | solution.py:244
  41.8 3.8 %collective-permute-start.11 = (bf16[576,128]{1,0:T(8,128)(2,1)S(1)}, bf16[576,128]{1,0:T(8,128)(2,1)S(1)}, u32[]{:S(2)}, u32[]{:S(2)}) collective-permute-start(bf16[576,128]{1,0:T(8,128)(2,1)S(1)} %get-tuple-element.46.refs_4_), channel_id=1, source_target_pairs={{0,3},{1,2},{2,1},{3,0},{4,7},{5,6},{6,5},{7,4},{8,11},{9,10},{10,... | collective-permute-start | bytes 442376 | tf_op jit(solution)/shard_map/ppermute | solution.py:244
  45.5 0.0 collective-permute-done.10.refs_3_
  45.5 1.8 %collective-permute-start.7 = (bf16[576,128]{1,0:T(8,128)(2,1)S(1)}, bf16[576,128]{1,0:T(8,128)(2,1)S(1)}, u32[]{:S(2)}, u32[]{:S(2)}) collective-permute-start(bf16[576,128]{1,0:T(8,128)(2,1)S(1)} %get-tuple-element.46.refs_4_), channel_id=1, source_target_pairs={{0,2},{1,3},{2,0},{3,1},{4,6},{5,7},{6,4},{7,5},{8,10},{9,11},{10,... | collective-permute-start | bytes 442376 | tf_op jit(solution)/shard_map/ppermute | solution.py:244
  47.4 0.5 gate.1.gating
  47.9 0.0 collective-permute-done.8.refs_1_
  47.9 0.0 collective-permute-done.9.refs_2_
  47.9 0.7 %right_slots.1 = (f32[4,576,128]{2,1,0:T(8,128)S(1)}, f32[576,128]{1,0:T(8,128)S(1)}) custom-call(bf16[576,128]{1,0:T(8,128)(2,1)S(1)} %get-tuple-element.47.refs_0_, bf16[576,128]{1,0:T(8,128)(2,1)S(1)} %collective-permute-done.8.refs_1_, bf16[576,128]{1,0:T(8,128)(2,1)S(1)} %collective-permute-done.9.refs_2_, ...), custom_call_target="tpu_custom_call" | custom-call | tf_op jit(solution)/shard_map/right_slots/pallas_call | solution.py:262
  48.6 0.0 collective-permute-done.12.refs_0_
  48.7 0.6 %left_slot.2.refs_2_ = f32[576,128]{1,0:T(8,128)S(1)} custom-call(bf16[576,128]{1,0:T(8,128)(2,1)S(1)} %collective-permute-done.12.refs_0_, f32[4,576,128]{2,1,0:T(8,128)S(1)} %get-tuple-element.48.refs_1_.rights, f32[576,128]{1,0:T(8,128)S(1)} %get-tuple-element.49.refs_2_), custom_call_target="tpu_custom_call", output_to_operand_aliasing={{}: (2, {})} | custom-call | tf_op jit(solution)/shard_map/left_slot/pallas_call | solution.py:262
  49.3 4.2 %collective-permute-done.11.refs_0_ = bf16[576,128]{1,0:T(8,128)(2,1)S(1)} collective-permute-done((bf16[576,128]{1,0:T(8,128)(2,1)S(1)}, bf16[576,128]{1,0:T(8,128)(2,1)S(1)}, u32[]{:S(2)}, u32[]{:S(2)}) %collective-permute-start.11) | collective-permute-done | bytes 147488 | tf_op jit(solution)/shard_map/ppermute | solution.py:244
  53.5 0.6 %left_slot.3.old = f32[576,128]{1,0:T(8,128)S(1)} custom-call(bf16[576,128]{1,0:T(8,128)(2,1)S(1)} %collective-permute-done.11.refs_0_, f32[4,576,128]{2,1,0:T(8,128)S(1)} %get-tuple-element.48.refs_1_.rights, f32[576,128]{1,0:T(8,128)S(1)} %left_slot.2.refs_2_), custom_call_target="tpu_custom_call", output_to_operand_aliasing={{}: (2, {})} | custom-call | tf_op jit(solution)/shard_map/left_slot/pallas_call | solution.py:262
  54.1 3.3 %collective-permute-done.7.left = bf16[576,128]{1,0:T(8,128)(2,1)S(1)} collective-permute-done((bf16[576,128]{1,0:T(8,128)(2,1)S(1)}, bf16[576,128]{1,0:T(8,128)(2,1)S(1)}, u32[]{:S(2)}, u32[]{:S(2)}) %collective-permute-start.7) | collective-permute-done | bytes 147488 | tf_op jit(solution)/shard_map/ppermute | solution.py:244
  57.4 1.9 %end.1 = bf16[576,128]{1,0:T(8,128)(2,1)} custom-call(bf16[576,128]{1,0:T(8,128)(2,1)S(1)} %collective-permute-done.7.left, f32[4,576,128]{2,1,0:T(8,128)S(1)} %get-tuple-element.48.refs_1_.rights, f32[576,128]{1,0:T(8,128)S(1)} %left_slot.3.old, bf16[576,128]{1,0:T(8,128)(2,1)S(1)} %get-tuple-element.50.pair, f32[576,128]{1,0:T(8,128)S(1)} %gate.1.gating, ...), custom_call_target="tpu_custom_call" | custom-call | tf_op jit(solution)/shard_map/end/pallas_call | solution.py:262
  (6 shorter events, 0.0 us)
Async XLA Ops:
  0.0 7.7 %collective-permute-start.1 = (bf16[576,128]{1,0:T(8,128)(2,1)}, bf16[576,128]{1,0:T(8,128)(2,1)S(1)}, u32[]{:S(2)}, u32[]{:S(2)}) collective-permute-start(bf16[576,128]{1,0:T(8,128)(2,1)} %bitcast.3), channel_id=1, source_target_pairs={{0,0},{1,8},{2,4},{3,12},{4,1},{5,9},{6,5},{7,13},{8,2},{9,10},{10... | collective-permute-start | bytes 442376 | tf_op jit(solution)/shard_map/ppermute | solution.py:248
  1.6 17.3 %collective-permute-start.5 = (bf16[576,128]{1,0:T(8,128)(2,1)}, bf16[576,128]{1,0:T(8,128)(2,1)S(1)}, u32[]{:S(2)}, u32[]{:S(2)}) collective-permute-start(bf16[576,128]{1,0:T(8,128)(2,1)} %bitcast.4), channel_id=1, source_target_pairs={{0,1},{1,0},{2,3},{3,2},{4,5},{5,4},{6,7},{7,6},{8,9},{9,8},{10,11... | collective-permute-start | bytes 442376 | tf_op jit(solution)/shard_map/ppermute | solution.py:244
  6.4 21.5 %collective-permute-start.6 = (bf16[576,128]{1,0:T(8,128)(2,1)}, bf16[576,128]{1,0:T(8,128)(2,1)S(1)}, u32[]{:S(2)}, u32[]{:S(2)}) collective-permute-start(bf16[576,128]{1,0:T(8,128)(2,1)} %bitcast.5), channel_id=1, source_target_pairs={{0,3},{1,2},{2,1},{3,0},{4,7},{5,6},{6,5},{7,4},{8,11},{9,10},{10,... | collective-permute-start | bytes 442376 | tf_op jit(solution)/shard_map/ppermute | solution.py:244
  7.7 20.2 %collective-permute-start.2 = (bf16[576,128]{1,0:T(8,128)(2,1)S(1)}, bf16[576,128]{1,0:T(8,128)(2,1)S(1)}, u32[]{:S(2)}, u32[]{:S(2)}) collective-permute-start(bf16[576,128]{1,0:T(8,128)(2,1)S(1)} %collective-permute-done.1.refs_0_), channel_id=1, source_target_pairs={{0,4},{4,0},{8,12},{12,8},{1,5},{5,1},{9,13},{13,9},{2,6},{6,2},{1... | collective-permute-start | bytes 442376 | tf_op jit(solution)/shard_map/ppermute | solution.py:244
  13.8 14.1 %collective-permute-start.3 = (bf16[576,128]{1,0:T(8,128)(2,1)S(1)}, bf16[576,128]{1,0:T(8,128)(2,1)S(1)}, u32[]{:S(2)}, u32[]{:S(2)}) collective-permute-start(bf16[576,128]{1,0:T(8,128)(2,1)S(1)} %collective-permute-done.1.refs_0_), channel_id=1, source_target_pairs={{0,8},{4,12},{8,0},{12,4},{1,9},{5,13},{9,1},{13,5},{2,10},{6,14},... | collective-permute-start | bytes 442376 | tf_op jit(solution)/shard_map/ppermute | solution.py:244
  15.6 12.3 %collective-permute-start.4 = (bf16[576,128]{1,0:T(8,128)(2,1)S(1)}, bf16[576,128]{1,0:T(8,128)(2,1)S(1)}, u32[]{:S(2)}, u32[]{:S(2)}) collective-permute-start(bf16[576,128]{1,0:T(8,128)(2,1)S(1)} %collective-permute-done.1.refs_0_), channel_id=1, source_target_pairs={{0,12},{4,8},{8,4},{12,0},{1,13},{5,9},{9,5},{13,1},{2,14},{6,10},... | collective-permute-start | bytes 442376 | tf_op jit(solution)/shard_map/ppermute | solution.py:244
  18.8 16.6 %collective-permute-start = (bf16[576,128]{1,0:T(8,128)(2,1)}, bf16[576,128]{1,0:T(8,128)(2,1)S(1)}, u32[]{:S(2)}, u32[]{:S(2)}) collective-permute-start(bf16[576,128]{1,0:T(8,128)(2,1)} %bitcast.6), channel_id=1, source_target_pairs={{0,2},{1,3},{2,0},{3,1},{4,6},{5,7},{6,4},{7,5},{8,10},{9,11},{10,... | collective-permute-start | bytes 442376 | tf_op jit(solution)/shard_map/ppermute | solution.py:244
  18.8 1.0 %copy-start = (bf16[2,128,640]{2,1,0:T(8,128)(2,1)S(1)}, bf16[2,128,640]{2,1,0:T(8,128)(2,1)}, u32[]{:S(2)}) copy-start(bf16[2,128,640]{2,1,0:T(8,128)(2,1)} %refs_1_.1) | copy-start | bytes 983044
  19.8 0.9 %copy-start.1 = (bf16[24,24,128]{2,1,0:T(8,128)(2,1)S(1)}, bf16[24,24,128]{2,1,0:T(8,128)(2,1)}, u32[]{:S(2)}) copy-start(bf16[24,24,128]{2,1,0:T(8,128)(2,1)} %param.10) | copy-start | bytes 442372
  20.7 0.8 %copy-start.2 = (bf16[2,128,128]{2,1,0:T(8,128)(2,1)S(1)}, bf16[2,128,128]{2,1,0:T(8,128)(2,1)}, u32[]{:S(2)}) copy-start(bf16[2,128,128]{2,1,0:T(8,128)(2,1)} %refs_8_.1) | copy-start | bytes 196612
  21.6 0.7 %copy-start.3 = (f32[2,640]{1,0:T(2,128)S(1)}, f32[2,640]{1,0:T(2,128)}, u32[]{:S(2)}) copy-start(f32[2,640]{1,0:T(2,128)} %refs_2_.1) | copy-start | bytes 15364
  22.3 0.7 %copy-start.4 = (f32[2,128]{1,0:T(2,128)S(1)}, f32[2,128]{1,0:T(2,128)}, u32[]{:S(2)}) copy-start(f32[2,128]{1,0:T(2,128)} %refs_4_.1) | copy-start | bytes 3076
  22.9 0.7 %copy-start.5 = (f32[2,128]{1,0:T(2,128)S(1)}, f32[2,128]{1,0:T(2,128)}, u32[]{:S(2)}) copy-start(f32[2,128]{1,0:T(2,128)} %refs_5_.1) | copy-start | bytes 3076
  23.6 0.7 %copy-start.6 = (f32[2,128]{1,0:T(2,128)S(1)}, f32[2,128]{1,0:T(2,128)}, u32[]{:S(2)}) copy-start(f32[2,128]{1,0:T(2,128)} %refs_6_.1) | copy-start | bytes 3076
  24.3 0.7 %copy-start.7 = (f32[2,128]{1,0:T(2,128)S(1)}, f32[2,128]{1,0:T(2,128)}, u32[]{:S(2)}) copy-start(f32[2,128]{1,0:T(2,128)} %refs_7_.1) | copy-start | bytes 3076
  25.0 0.7 %copy-start.8 = (f32[2,128]{1,0:T(2,128)S(1)}, f32[2,128]{1,0:T(2,128)}, u32[]{:S(2)}) copy-start(f32[2,128]{1,0:T(2,128)} %refs_9_.1) | copy-start | bytes 3076
  25.7 0.7 %copy-start.9 = (s32[96]{0:T(128)S(1)}, s32[96]{0:T(128)}, u32[]{:S(2)}) copy-start(s32[96]{0:T(128)} %param.11) | copy-start | bytes 1156
  38.9 6.6 %collective-permute-start.10 = (bf16[576,128]{1,0:T(8,128)(2,1)S(1)}, bf16[576,128]{1,0:T(8,128)(2,1)S(1)}, u32[]{:S(2)}, u32[]{:S(2)}) collective-permute-start(bf16[576,128]{1,0:T(8,128)(2,1)S(1)} %get-tuple-element.47.refs_0_), channel_id=1, source_target_pairs={{0,12},{4,8},{8,4},{12,0},{1,13},{5,9},{9,5},{13,1},{2,14},{6,10},... | collective-permute-start | bytes 442376 | tf_op jit(solution)/shard_map/ppermute | solution.py:244
  39.0 8.9 %collective-permute-start.8 = (bf16[576,128]{1,0:T(8,128)(2,1)S(1)}, bf16[576,128]{1,0:T(8,128)(2,1)S(1)}, u32[]{:S(2)}, u32[]{:S(2)}) collective-permute-start(bf16[576,128]{1,0:T(8,128)(2,1)S(1)} %get-tuple-element.47.refs_0_), channel_id=1, source_target_pairs={{0,4},{4,0},{8,12},{12,8},{1,5},{5,1},{9,13},{13,9},{2,6},{6,2},{1... | collective-permute-start | bytes 442376 | tf_op jit(solution)/shard_map/ppermute | solution.py:244
  39.3 8.7 %collective-permute-start.9 = (bf16[576,128]{1,0:T(8,128)(2,1)S(1)}, bf16[576,128]{1,0:T(8,128)(2,1)S(1)}, u32[]{:S(2)}, u32[]{:S(2)}) collective-permute-start(bf16[576,128]{1,0:T(8,128)(2,1)S(1)} %get-tuple-element.47.refs_0_), channel_id=1, source_target_pairs={{0,8},{4,12},{8,0},{12,4},{1,9},{5,13},{9,1},{13,5},{2,10},{6,14},... | collective-permute-start | bytes 442376 | tf_op jit(solution)/shard_map/ppermute | solution.py:244
  41.1 7.5 %collective-permute-start.12 = (bf16[576,128]{1,0:T(8,128)(2,1)S(1)}, bf16[576,128]{1,0:T(8,128)(2,1)S(1)}, u32[]{:S(2)}, u32[]{:S(2)}) collective-permute-start(bf16[576,128]{1,0:T(8,128)(2,1)S(1)} %get-tuple-element.46.refs_4_), channel_id=1, source_target_pairs={{0,1},{1,0},{2,3},{3,2},{4,5},{5,4},{6,7},{7,6},{8,9},{9,8},{10,11... | collective-permute-start | bytes 442376 | tf_op jit(solution)/shard_map/ppermute | solution.py:244
  41.8 11.7 %collective-permute-start.11 = (bf16[576,128]{1,0:T(8,128)(2,1)S(1)}, bf16[576,128]{1,0:T(8,128)(2,1)S(1)}, u32[]{:S(2)}, u32[]{:S(2)}) collective-permute-start(bf16[576,128]{1,0:T(8,128)(2,1)S(1)} %get-tuple-element.46.refs_4_), channel_id=1, source_target_pairs={{0,3},{1,2},{2,1},{3,0},{4,7},{5,6},{6,5},{7,4},{8,11},{9,10},{10,... | collective-permute-start | bytes 442376 | tf_op jit(solution)/shard_map/ppermute | solution.py:244
  45.5 11.9 %collective-permute-start.7 = (bf16[576,128]{1,0:T(8,128)(2,1)S(1)}, bf16[576,128]{1,0:T(8,128)(2,1)S(1)}, u32[]{:S(2)}, u32[]{:S(2)}) collective-permute-start(bf16[576,128]{1,0:T(8,128)(2,1)S(1)} %get-tuple-element.46.refs_4_), channel_id=1, source_target_pairs={{0,2},{1,3},{2,0},{3,1},{4,6},{5,7},{6,4},{7,5},{8,10},{9,11},{10,... | collective-permute-start | bytes 442376 | tf_op jit(solution)/shard_map/ppermute | solution.py:244

commit v6 on v5

v6 whole, which is shorter than its diff:
```python
import functools

import jax
import jax.numpy as jnp
from jax import lax
from jax.experimental import pallas as pl
from jax.experimental.pallas import tpu as pltpu
from jax.sharding import PartitionSpec as P

F32, BF16 = jnp.float32, jnp.bfloat16


def dot(a, b):
    return jnp.dot(a, b, preferred_element_type=F32)


def split(values):
    high = values.astype(BF16)
    return jnp.concatenate([high, (values - high.astype(F32)).astype(BF16)], axis=1)


def constants(width):
    rows = lax.broadcasted_iota(jnp.int32, (2 * width, width), 0)
    cols = lax.broadcasted_iota(jnp.int32, (2 * width, width), 1)
    mean = jnp.full((2 * width, width), 1.0 / width, F32)
    center = jnp.where((rows == cols) | (rows == cols + width), 1.0, 0.0) - mean
    return center.astype(BF16), mean.astype(BF16)


def scaled(center, mean, gain, shift):
    spread = dot(split(center * center), mean)
    return (center * lax.rsqrt(spread + 1e-05) * gain + shift).astype(BF16)


def norm_pair(values, consts, gain, shift):
    return scaled(dot(values, consts[0][: values.shape[1]]), consts[1], gain, shift)


def norm_mixed(values, consts, gain, shift):
    return scaled(dot(split(values), consts[0]), consts[1], gain, shift)


def gated(normed, weights, bias, width):
    product = dot(normed, weights) + bias
    return (jnp.tanh(product[:, width:]) + 1.0) * product[:, :width]


def gate(normed, weights, bias):
    return 0.5 * jnp.tanh(dot(normed, weights) + bias) + 0.5


def masked(values, outer, inner):
    t = outer.shape[0]
    grid = jnp.concatenate([outer[k : k + 1] * inner for k in range(t)], axis=0)
    return (values * grid).astype(BF16)


def mix(out_ref, old_ref, left, right, t):
    width = out_ref.shape[1]
    for base in range(0, t, 8):
        if old_ref is None:
            total = (jnp.zeros((t, width), F32),) * 8
        else:
            total = tuple(old_ref[pl.ds((base + i) * t, t), :] for i in range(8))

        def step(q, total):
            for u in range(4):
                first = pl.multiple_of((q * 4 + u) * t, 8)
                row = right(first)
                total = tuple(total[i] + left(first + base + i) * row for i in range(8))
            return total

        total = lax.fori_loop(0, t // 4, step, total)
        for i in range(8):
            out_ref[pl.ds((base + i) * t, t), :] = total[i]


def finish(pair, mixed, gating, consts, gain, shift, weights, bias):
    normout = norm_mixed(mixed, consts, gain, shift)
    return (pair.astype(F32) + gating * (dot(normout, weights) + bias)).astype(BF16)


def row_of(ref, *lead):
    return lambda at: ref[(*lead, pl.ds(at, 1), slice(None))]


def rows_of(ref, t, *lead):
    return lambda at: ref[(*lead, pl.ds(at, t), slice(None))]


def place(b, n):
    return b // 2 + lax.rem(b, 2) * (n // 2)


TABLE_MASK = 24


def in_norm(table, u):
    return table[u : u + 1], table[2 + u : 3 + u]


def out_norm(table, u):
    return table[4 + u : 5 + u], table[6 + u : 7 + u]


def half_bias(table, u, first, last):
    return jnp.concatenate([table[k : k + 1] for k in range(10 + 5 * u + first, 10 + 5 * u + last)], axis=1) * 0.5


def mask_of(table, b, t):
    return table[pl.ds(pl.multiple_of(TABLE_MASK + b * t, 8), t), :]


def sides(values_ref, wide, left_at, right_at, outer, inner, consts, table, weights):
    t, width = outer.shape
    wide[...] = values_ref[...].astype(F32)
    values = jnp.concatenate([wide[pl.ds(k, t, stride=t), :] for k in range(t)], axis=0).astype(BF16)
    normed = norm_pair(values, consts, *in_norm(table, 0))
    for k, target in enumerate((left_at, right_at)):
        span = slice(2 * k * width, 2 * (k + 1) * width)
        side = gated(normed, weights[0, :, span], half_bias(table, 0, 2 * k, 2 * k + 2), width)
        target[...] = masked(side, outer, inner).astype(F32)


def gate_of(values, consts, table, weights, u):
    normed = norm_pair(values, consts, *in_norm(table, u))
    return gate(normed, weights[u, :, 4 * values.shape[1] :], half_bias(table, u, 4, 5))


def own_kernel(n, t, pair, table, w_in, weights, left, right, gating, wide):
    r, c = lax.axis_index("row"), lax.axis_index("col")
    consts = constants(wide.shape[1])
    weights[...] = w_in[...] * 0.5
    outer, inner = mask_of(table, c, t), mask_of(table, r, t)
    sides(pair, wide, left, right, outer, inner, consts, table, weights)
    gating[...] = gate_of(pair[...], consts, table, weights, 0)


def slot_sum(t, step, block, table, weights, lefts, rights, old, mixed, wide, left, right):
    r, c = lax.axis_index("row"), lax.axis_index("col")
    b = c ^ step
    outer, inner = mask_of(table, b, t), mask_of(table, r, t)
    sides(block, wide, left, right, outer, inner, constants(wide.shape[1]), table, weights)
    mix(mixed.at[0], old.at[0], row_of(left), rows_of(rights, t, b), t)
    mix(mixed.at[1], old.at[1], row_of(lefts, b), rows_of(right, t), t)


def column_kernel(n, t, steps, *refs):
    blocks, rows = refs[:n], refs[n : 2 * n - 2]
    table, weights, own_left, own_right = refs[2 * n - 2 : 2 * n + 2]
    lefts, rights, pair, gating, mixed, held, wide, left, right = refs[2 * n + 2 :]
    r, c = lax.axis_index("row"), lax.axis_index("col")
    consts = constants(wide.shape[1])
    for s in range(n):
        held[s] = blocks[s][...]

    def prepare(b, _):
        outer, inner = mask_of(table, b, t), mask_of(table, c, t)
        sides(held.at[r ^ place(b, n)], wide, lefts.at[b], rights.at[b], outer, inner, consts, table, weights)
        return 0

    lax.fori_loop(0, n, prepare, 0)
    own = held[r ^ place(r, n)]
    pair[...] = own
    gating[...] = gate_of(own, consts, table, weights, 0)
    mix(mixed.at[0], None, row_of(own_left), rows_of(rights, t, c), t)
    mix(mixed.at[1], None, row_of(lefts, c), rows_of(own_right, t), t)
    for step, block in zip(steps, rows):
        slot_sum(t, step, block, table, weights, lefts, rights, mixed, mixed, wide, left, right)


def last_kernel(n, t, step, *refs):
    block, table, weights, lefts, rights, old, w_out, pair, gating, col_pair, col_gating = refs[:11]
    pair_ref, left_ref, right_ref, mixed, wide, left, right = refs[11:]
    slot_sum(t, step, block, table, weights, lefts, rights, old, mixed, wide, left, right)
    width = wide.shape[1]
    r, c = lax.axis_index("row"), lax.axis_index("col")
    consts = constants(width)
    here, there = mask_of(table, r, t), mask_of(table, c, t)
    for k, (base, factor) in enumerate(((pair, gating), (col_pair, col_gating))):
        updated = finish(base[...], mixed[k], factor[...], consts, *out_norm(table, 0), w_out[0], table[8:9])
        normed = norm_pair(updated, consts, *in_norm(table, 1))
        if k == 0:
            pair_ref[...] = updated
            side = gated(normed, weights[1, :, 2 * width : 4 * width], half_bias(table, 1, 2, 4), width)
            right_ref[...] = masked(side, here, there)
        else:
            side = gated(normed, weights[1, :, : 2 * width], half_bias(table, 1, 0, 2), width)
            left_ref[...] = masked(side, there, here)


def gate_kernel(pair, table, weights, gating):
    gating[...] = gate_of(pair[...], constants(pair.shape[1]), table, weights, 1)


def right_kernel(n, t, *refs):
    blocks, left = refs[:n], refs[n]
    rights, mixed, wide = refs[n + 1 :]
    r, c = lax.axis_index("row"), lax.axis_index("col")
    for s in range(n):
        rights[s] = blocks[s][...].astype(F32)
    wide[...] = left[...].astype(F32)
    mix(mixed, None, row_of(wide), rows_of(rights, t, r ^ c), t)


def left_sum(n, t, slot, left, rights, old, mixed, wide):
    r, c = lax.axis_index("row"), lax.axis_index("col")
    wide[...] = left[...].astype(F32)
    mix(mixed, old, row_of(wide), rows_of(rights, t, r ^ c ^ slot), t)


def left_kernel(n, t, slot, *refs):
    left_sum(n, t, slot, *refs)


def end_kernel(n, t, slot, left, rights, old, pair, gating, table, w_out, out, mixed, wide):
    left_sum(n, t, slot, left, rights, old, mixed, wide)
    consts = constants(wide.shape[1])
    out[...] = finish(pair[...], mixed[...], gating[...], consts, *out_norm(table, 1), w_out[1], table[9:10])


def solution(mesh):
    n = mesh.shape["col"]
    half = n // 2

    def along(block, axis, step):
        return lax.ppermute(block, axis, [(k, k ^ step) for k in range(n)])

    def mirrored(block):
        pairs = [(a * n + z, (z // 2 + z % 2 * half) * n + a) for a in range(n) for z in range(n)]
        return lax.ppermute(block, ("row", "col"), pairs)

    def plane(block):
        return [block] + [along(block, "row", step) for step in range(1, n)]

    def per_device(pair, token_mask, in_gain, in_shift, w_in, bias_in, out_gain, out_shift, w_out, bias_out):
        t, _, width = pair.shape
        area = (t * t, width)
        narrow, broad = jax.ShapeDtypeStruct(area, BF16), jax.ShapeDtypeStruct(area, F32)
        stacked = jax.ShapeDtypeStruct((n,) + area, F32)
        twice = jax.ShapeDtypeStruct((2,) + area, F32)
        scratch = pltpu.VMEM(area, F32)

        def call(kernel, name, outs, scratches, *operands, alias=None, **specs):
            return pl.pallas_call(
                kernel,
                out_shape=outs,
                **specs,
                scratch_shapes=scratches,
                input_output_aliases=alias or {},

                compiler_params=pltpu.CompilerParams(vmem_limit_bytes=(16 + n) * 1024 * 1024),
                name=name,
            )(*operands)

        pair = pair.reshape(area)
        col_block = mirrored(pair)
        steps = [step for step in range(1, n) if step != half] + [half]
        rows = [along(pair, "col", step) for step in steps]
        mask = jnp.broadcast_to(token_mask.astype(F32)[:, None], (n * t, width))
        vectors = [in_gain, in_shift, out_gain, out_shift, bias_out, bias_in.reshape(-1, width)]
        table = jnp.concatenate(vectors + [jnp.zeros((TABLE_MASK - 20, width), F32), mask])
        weights, own_left, own_right, gating = call(
            functools.partial(own_kernel, n, t),
            "own_sides",
            (jax.ShapeDtypeStruct(w_in.shape, BF16), broad, broad, broad),
            [scratch],
            pair,
            table,
            w_in,
        )
        col_block, own_left = lax.optimization_barrier((col_block, own_left))
        lefts, rights, col_pair, col_gating, mixed = call(
            functools.partial(column_kernel, n, t, steps[:-1]),
            "column_sides",
            (stacked, stacked, narrow, broad, twice),
            [pltpu.VMEM((n,) + area, BF16)] + [scratch] * 3,
            *plane(col_block),
            *rows[:-1],
            table,
            weights,
            own_left,
            own_right,
        )
        pair, left, right = call(
            functools.partial(last_kernel, n, t, steps[-1]),
            "last_slot",
            (narrow,) * 3,
            [pltpu.VMEM((2,) + area, F32)] + [scratch] * 3,
            rows[-1],
            table,
            weights,
            lefts,
            rights,
            mixed,
            w_out,
            pair,
            gating,
            col_pair,
            col_gating,
        )
        blocks = [along(left, "col", step) for step in steps]
        gating = call(gate_kernel, "gate", broad, [], pair, table, weights)
        rights, mixed = call(
            functools.partial(right_kernel, n, t), "right_slots", (stacked, broad), [scratch], *plane(right), left
        )
        for step, block in zip(steps[:-1], blocks[:-1]):
            mixed = call(
                functools.partial(left_kernel, n, t, step),
                "left_slot",
                broad,
                [scratch],
                block,
                rights,
                mixed,
                alias={2: 0},
            )
        out = call(
            functools.partial(end_kernel, n, t, steps[-1]),
            "end",
            narrow,
            [scratch] * 2,
            blocks[-1],
            rights,
            mixed,
            pair,
            gating,
            table,
            w_out,
        )
        return out.reshape(t, t, width)

    placed = (P(("groups", "row"), "col", None), P("groups")) + (P(),) * 8
    return jax.shard_map(
        per_device, mesh=mesh, in_specs=placed, out_specs=P(("groups", "row"), "col", None), check_vma=False
    )
```

time: 59.6 us -> 55.4 us (0.930)
  starting transfers between devices: 24.1 us -> 18 us
  waiting for transfers between devices: 10.7 us -> 15.9 us
  local copies, waits for them, and re-layouts: 7.46 us -> 4.16 us
  Pallas kernels: 16.9 us -> 16.2 us
  other arithmetic: 0 us -> 0.66 us
    ppermute x12, starting transfers between devices: 22.6 us -> 16.5 us  [along(): return lax.ppermute(block, axis, [(k, k ^ step) for k in range(n)])]
    unnamed x20 -> x6, local copies, waits for them, and re-layouts: 7.46 us -> 1.88 us
    ppermute x12, waiting for transfers between devices: 10.7 us -> 15.9 us  [along(): return lax.ppermute(block, axis, [(k, k ^ step) for k in range(n)])]
    concatenate x0 -> x1, local copies, waits for them, and re-layouts: none -> 1.51 us  [per_device(): jnp.concatenate(vectors + [jnp.zeros((TABLE_MASK - 20, width), F32), mask])]
    reshape x0 -> x1, local copies, waits for them, and re-layouts: none -> 0.7 us  [per_device(): bias_in.reshape(-1, width)]
    convert_element_type x0 -> x1, other arithmetic: none -> 0.66 us  [per_device(): mask = jnp.broadcast_to(token_mask.astype(F32)[:, None], (n * t, width))]
    pallas_call x8, Pallas kernels: 16.9 us -> 16.2 us  [call(): pl.pallas_call(kernel, out_shape=outs, **specs, scratch_shapes=scratches,...]
  transfers between devices with their start and end apart: 13 -> 13, of which waited for: 3 -> 7; matrix products, arithmetic and copies ran while one was open for 0% -> 5% of each run, Pallas kernels for 20% -> 20%
where the time goes in v6:
time: 55.4 us; the launch traced here: 55.1 us
  starting transfers between devices  18 us (32%)
  Pallas kernels  16.2 us (29%)
  waiting for transfers between devices  15.9 us (29%)
  local copies, waits for them, and re-layouts  4.16 us (8%)
  other arithmetic  0.66 us (1%)
    ppermute x12, starting transfers between devices, along(): return lax.ppermute(block, axis, [(k, k ^ step) for k in range(n)])  16.5 us
    pallas_call x8, Pallas kernels, call(): pl.pallas_call(kernel, out_shape=outs, **specs, scratch_shapes=scratches,...  16.2 us
    ppermute x12, waiting for transfers between devices, along(): return lax.ppermute(block, axis, [(k, k ^ step) for k in range(n)])  15.9 us
    unnamed x6, local copies, waits for them, and re-layouts  1.88 us
    ppermute x1, starting transfers between devices, mirrored(): return lax.ppermute(block, ('row', 'col'), pairs)  1.56 us
    concatenate x1, local copies, waits for them, and re-layouts, per_device(): jnp.concatenate(vectors + [jnp.zeros((TABLE_MASK - 20, width), F32), mask])  1.51 us
  transfers between devices with their start and end apart: 13, of which 7 were waited for; matrix products, arithmetic and copies ran while one was open for 5% of the time, Pallas kernels for 20%

profile of v6, /device:TPU:0, one launch (start us, length us, event | category | flops | bytes accessed | tf_op | source)
XLA Modules:
  0.0 55.1 jit_solution(2831319676342196068)
XLA Ops:
  0.0 1.6 %collective-permute-start.1 = (bf16[576,128]{1,0:T(8,128)(2,1)}, bf16[576,128]{1,0:T(8,128)(2,1)S(1)}, u32[]{:S(2)}, u32[]{:S(2)}) collective-permute-start(bf16[576,128]{1,0:T(8,128)(2,1)} %bitcast.2), channel_id=1, source_target_pairs={{0,0},{1,8},{2,4},{3,12},{4,1},{5,9},{6,5},{7,13},{8,2},{9,10},{10... | collective-permute-start | bytes 442376 | tf_op jit(solution)/shard_map/ppermute | solution.py:231
  1.6 4.8 %collective-permute-start.5 = (bf16[576,128]{1,0:T(8,128)(2,1)}, bf16[576,128]{1,0:T(8,128)(2,1)S(1)}, u32[]{:S(2)}, u32[]{:S(2)}) collective-permute-start(bf16[576,128]{1,0:T(8,128)(2,1)} %bitcast.3), channel_id=1, source_target_pairs={{0,1},{1,0},{2,3},{3,2},{4,5},{5,4},{6,7},{7,6},{8,9},{9,8},{10,11... | collective-permute-start | bytes 442376 | tf_op jit(solution)/shard_map/ppermute | solution.py:227
  6.4 1.3 %collective-permute-start.6 = (bf16[576,128]{1,0:T(8,128)(2,1)}, bf16[576,128]{1,0:T(8,128)(2,1)S(1)}, u32[]{:S(2)}, u32[]{:S(2)}) collective-permute-start(bf16[576,128]{1,0:T(8,128)(2,1)} %bitcast.4), channel_id=1, source_target_pairs={{0,3},{1,2},{2,1},{3,0},{4,7},{5,6},{6,5},{7,4},{8,11},{9,10},{10,... | collective-permute-start | bytes 442376 | tf_op jit(solution)/shard_map/ppermute | solution.py:227
  7.7 0.7 %convert_element_type.3 = f32[96]{0:T(128)S(1)} convert(s32[96]{0:T(128)} %param.11) | non-fusion elementwise | flops 96 | bytes 768 | tf_op jit(solution)/shard_map/convert_element_type | solution.py:260
  8.3 0.7 %reshape.11 = f32[10,128]{1,0:T(8,128)S(1)} reshape(f32[2,640]{1,0:T(2,128)} %param.15) | data formatting | bytes 10240 | tf_op jit(solution)/shard_map/reshape | solution.py:261
  9.0 0.1 broadcast_in_dim.10
  9.1 1.5 %concatenate.3.table.refs_6_.refs_1_ = f32[120,128]{1,0:T(8,128)S(1)} concatenate(f32[2,128]{1,0:T(2,128)} %param.12, f32[2,128]{1,0:T(2,128)} %param.13, f32[2,128]{1,0:T(2,128)} %param.16, f32[2,128]{1,0:T(2,128)} %param.17, f32[2,128]{1,0:T(2,128)} %param.19, f32[10,128]{1,0:T(8,128)S(1)} %reshape.11, f32[4,128]{1,0:T(4,128)S(1)} %broadcast_in_dim.4, ...), dimensions={0} | concatenate | bytes 122880 | tf_op jit(solution)/shard_map/concatenate | solution.py:262
  10.6 0.0 copy-start
  10.6 0.9 %copy-done = bf16[24,24,128]{2,1,0:T(8,128)(2,1)S(1)} copy-done((bf16[24,24,128]{2,1,0:T(8,128)(2,1)S(1)}, bf16[24,24,128]{2,1,0:T(8,128)(2,1)}, u32[]{:S(2)}) %copy-start) | copy-done | bytes 147480
  11.5 0.0 copy-start.1
  11.5 1.0 %copy-done.1 = bf16[2,128,640]{2,1,0:T(8,128)(2,1)S(1)} copy-done((bf16[2,128,640]{2,1,0:T(8,128)(2,1)S(1)}, bf16[2,128,640]{2,1,0:T(8,128)(2,1)}, u32[]{:S(2)}) %copy-start.1) | copy-done | bytes 327704
  12.5 0.0 copy-start.2
  12.5 1.0 %own_sides.1 = (bf16[2,128,640]{2,1,0:T(8,128)(2,1)S(1)}, f32[576,128]{1,0:T(8,128)S(1)}, f32[576,128]{1,0:T(8,128)S(1)}, f32[576,128]{1,0:T(8,128)S(1)}) custom-call(bf16[576,128]{1,0:T(8,128)(2,1)S(1)} %bitcast.5, f32[120,128]{1,0:T(8,128)S(1)} %concatenate.3.table.refs_6_.refs_1_, bf16[2,128,640]{2,1,0:T(8,128)(2,1)S(1)} %copy-done.1), custom_call_target="tpu_custom_call" | custom-call | tf_op jit(solution)/shard_map/own_sides/pallas_call | solution.py:245
  13.5 0.0 collective-permute-done.1.refs_0_
  13.5 0.3 collective-permute-start.2
  13.8 1.8 %collective-permute-start.3 = (bf16[576,128]{1,0:T(8,128)(2,1)S(1)}, bf16[576,128]{1,0:T(8,128)(2,1)S(1)}, u32[]{:S(2)}, u32[]{:S(2)}) collective-permute-start(bf16[576,128]{1,0:T(8,128)(2,1)S(1)} %collective-permute-done.1.refs_0_), channel_id=1, source_target_pairs={{0,8},{4,12},{8,0},{12,4},{1,9},{5,13},{9,1},{13,5},{2,10},{6,14},... | collective-permute-start | bytes 442376 | tf_op jit(solution)/shard_map/ppermute | solution.py:227
  15.6 0.1 collective-permute-start.4
  15.7 3.1 %collective-permute-done.5.refs_4_ = bf16[576,128]{1,0:T(8,128)(2,1)S(1)} collective-permute-done((bf16[576,128]{1,0:T(8,128)(2,1)}, bf16[576,128]{1,0:T(8,128)(2,1)S(1)}, u32[]{:S(2)}, u32[]{:S(2)}) %collective-permute-start.5) | collective-permute-done | bytes 147488 | tf_op jit(solution)/shard_map/ppermute | solution.py:227
  18.8 0.0 collective-permute-start
  18.8 0.0 collective-permute-done.6.refs_5_
  18.8 0.0 collective-permute-done.2.refs_1_
  18.9 1.6 %collective-permute-done.3.refs_2_ = bf16[576,128]{1,0:T(8,128)(2,1)S(1)} collective-permute-done((bf16[576,128]{1,0:T(8,128)(2,1)S(1)}, bf16[576,128]{1,0:T(8,128)(2,1)S(1)}, u32[]{:S(2)}, u32[]{:S(2)}) %collective-permute-start.3) | collective-permute-done | bytes 147488 | tf_op jit(solution)/shard_map/ppermute | solution.py:227
  20.4 2.5 %collective-permute-done.4.refs_3_ = bf16[576,128]{1,0:T(8,128)(2,1)S(1)} collective-permute-done((bf16[576,128]{1,0:T(8,128)(2,1)S(1)}, bf16[576,128]{1,0:T(8,128)(2,1)S(1)}, u32[]{:S(2)}, u32[]{:S(2)}) %collective-permute-start.4) | collective-permute-done | bytes 147488 | tf_op jit(solution)/shard_map/ppermute | solution.py:227
  22.9 7.6 %column_sides.1 = (f32[4,576,128]{2,1,0:T(8,128)S(1)}, f32[4,576,128]{2,1,0:T(8,128)S(1)}, bf16[576,128]{1,0:T(8,128)(2,1)S(1)}, f32[576,128]{1,0:T(8,128)S(1)}, f32[2,576,128]{2,1,0:T(8,128)S(1)}) custom-call(bf16[576,128]{1,0:T(8,128)(2,1)S(1)} %collective-permute-done.1.refs_0_, bf16[576,128]{1,0:T(8,128)(2,1)S(1)} %collective-permute-done.2.refs_1_, ...), custom_call_target="tpu_custom_call" | custom-call | tf_op jit(solution)/shard_map/column_sides/pallas_call | solution.py:245
  30.5 0.0 collective-permute-done.refs_0_
  30.5 0.0 copy-done.2
  30.5 3.4 %last_slot.1 = (bf16[576,128]{1,0:T(8,128)(2,1)S(1)}, bf16[576,128]{1,0:T(8,128)(2,1)S(1)}, bf16[576,128]{1,0:T(8,128)(2,1)S(1)}) custom-call(bf16[576,128]{1,0:T(8,128)(2,1)S(1)} %collective-permute-done.refs_0_, f32[120,128]{1,0:T(8,128)S(1)} %concatenate.3.table.refs_6_.refs_1_, bf16[2,128,640]{2,1,0:T(8,128)(2,1)S(1)} %get-tuple-element.21.refs_7_.refs_2_.weights, ...), custom_call_target="tpu_custom_call" | custom-call | tf_op jit(solution)/shard_map/last_slot/pallas_call | solution.py:245
  33.9 1.6 %collective-permute-start.10 = (bf16[576,128]{1,0:T(8,128)(2,1)S(1)}, bf16[576,128]{1,0:T(8,128)(2,1)S(1)}, u32[]{:S(2)}, u32[]{:S(2)}) collective-permute-start(bf16[576,128]{1,0:T(8,128)(2,1)S(1)} %get-tuple-element.33.refs_0_), channel_id=1, source_target_pairs={{0,12},{4,8},{8,4},{12,0},{1,13},{5,9},{9,5},{13,1},{2,14},{6,10},... | collective-permute-start | bytes 442376 | tf_op jit(solution)/shard_map/ppermute | solution.py:227
  35.5 0.3 collective-permute-start.8
  35.8 0.3 collective-permute-start.9
  36.1 0.8 %collective-permute-start.12 = (bf16[576,128]{1,0:T(8,128)(2,1)S(1)}, bf16[576,128]{1,0:T(8,128)(2,1)S(1)}, u32[]{:S(2)}, u32[]{:S(2)}) collective-permute-start(bf16[576,128]{1,0:T(8,128)(2,1)S(1)} %get-tuple-element.32.refs_4_), channel_id=1, source_target_pairs={{0,1},{1,0},{2,3},{3,2},{4,5},{5,4},{6,7},{7,6},{8,9},{9,8},{10,11... | collective-permute-start | bytes 442376 | tf_op jit(solution)/shard_map/ppermute | solution.py:227
  36.9 2.9 %collective-permute-start.11 = (bf16[576,128]{1,0:T(8,128)(2,1)S(1)}, bf16[576,128]{1,0:T(8,128)(2,1)S(1)}, u32[]{:S(2)}, u32[]{:S(2)}) collective-permute-start(bf16[576,128]{1,0:T(8,128)(2,1)S(1)} %get-tuple-element.32.refs_4_), channel_id=1, source_target_pairs={{0,3},{1,2},{2,1},{3,0},{4,7},{5,6},{6,5},{7,4},{8,11},{9,10},{10,... | collective-permute-start | bytes 442376 | tf_op jit(solution)/shard_map/ppermute | solution.py:227
  39.8 0.1 collective-permute-done.10.refs_3_
  39.8 2.2 %collective-permute-start.7 = (bf16[576,128]{1,0:T(8,128)(2,1)S(1)}, bf16[576,128]{1,0:T(8,128)(2,1)S(1)}, u32[]{:S(2)}, u32[]{:S(2)}) collective-permute-start(bf16[576,128]{1,0:T(8,128)(2,1)S(1)} %get-tuple-element.32.refs_4_), channel_id=1, source_target_pairs={{0,2},{1,3},{2,0},{3,1},{4,6},{5,7},{6,4},{7,5},{8,10},{9,11},{10,... | collective-permute-start | bytes 442376 | tf_op jit(solution)/shard_map/ppermute | solution.py:227
  42.1 0.5 gate.1.gating
  42.6 0.0 collective-permute-done.8.refs_1_
  42.6 0.6 %collective-permute-done.9.refs_2_ = bf16[576,128]{1,0:T(8,128)(2,1)S(1)} collective-permute-done((bf16[576,128]{1,0:T(8,128)(2,1)S(1)}, bf16[576,128]{1,0:T(8,128)(2,1)S(1)}, u32[]{:S(2)}, u32[]{:S(2)}) %collective-permute-start.9) | collective-permute-done | bytes 147488 | tf_op jit(solution)/shard_map/ppermute | solution.py:227
  43.3 0.7 %right_slots.1 = (f32[4,576,128]{2,1,0:T(8,128)S(1)}, f32[576,128]{1,0:T(8,128)S(1)}) custom-call(bf16[576,128]{1,0:T(8,128)(2,1)S(1)} %get-tuple-element.33.refs_0_, bf16[576,128]{1,0:T(8,128)(2,1)S(1)} %collective-permute-done.8.refs_1_, bf16[576,128]{1,0:T(8,128)(2,1)S(1)} %collective-permute-done.9.refs_2_, ...), custom_call_target="tpu_custom_call" | custom-call | tf_op jit(solution)/shard_map/right_slots/pallas_call | solution.py:245
  43.9 0.0 collective-permute-done.12.refs_0_
  44.0 0.6 %left_slot.2.refs_2_ = f32[576,128]{1,0:T(8,128)S(1)} custom-call(bf16[576,128]{1,0:T(8,128)(2,1)S(1)} %collective-permute-done.12.refs_0_, f32[4,576,128]{2,1,0:T(8,128)S(1)} %get-tuple-element.34.refs_1_.rights, f32[576,128]{1,0:T(8,128)S(1)} %get-tuple-element.35.refs_2_), custom_call_target="tpu_custom_call", output_to_operand_aliasing={{}: (2, {})} | custom-call | tf_op jit(solution)/shard_map/left_slot/pallas_call | solution.py:245
  44.6 3.1 %collective-permute-done.11.refs_0_ = bf16[576,128]{1,0:T(8,128)(2,1)S(1)} collective-permute-done((bf16[576,128]{1,0:T(8,128)(2,1)S(1)}, bf16[576,128]{1,0:T(8,128)(2,1)S(1)}, u32[]{:S(2)}, u32[]{:S(2)}) %collective-permute-start.11) | collective-permute-done | bytes 147488 | tf_op jit(solution)/shard_map/ppermute | solution.py:227
  47.7 0.6 %left_slot.3.old = f32[576,128]{1,0:T(8,128)S(1)} custom-call(bf16[576,128]{1,0:T(8,128)(2,1)S(1)} %collective-permute-done.11.refs_0_, f32[4,576,128]{2,1,0:T(8,128)S(1)} %get-tuple-element.34.refs_1_.rights, f32[576,128]{1,0:T(8,128)S(1)} %left_slot.2.refs_2_), custom_call_target="tpu_custom_call", output_to_operand_aliasing={{}: (2, {})} | custom-call | tf_op jit(solution)/shard_map/left_slot/pallas_call | solution.py:245
  48.3 4.9 %collective-permute-done.7.left = bf16[576,128]{1,0:T(8,128)(2,1)S(1)} collective-permute-done((bf16[576,128]{1,0:T(8,128)(2,1)S(1)}, bf16[576,128]{1,0:T(8,128)(2,1)S(1)}, u32[]{:S(2)}, u32[]{:S(2)}) %collective-permute-start.7) | collective-permute-done | bytes 147488 | tf_op jit(solution)/shard_map/ppermute | solution.py:227
  53.2 1.8 %end.1 = bf16[576,128]{1,0:T(8,128)(2,1)} custom-call(bf16[576,128]{1,0:T(8,128)(2,1)S(1)} %collective-permute-done.7.left, f32[4,576,128]{2,1,0:T(8,128)S(1)} %get-tuple-element.34.refs_1_.rights, f32[576,128]{1,0:T(8,128)S(1)} %left_slot.3.old, bf16[576,128]{1,0:T(8,128)(2,1)S(1)} %get-tuple-element.36.pair, f32[576,128]{1,0:T(8,128)S(1)} %gate.1.gating, ...), custom_call_target="tpu_custom_call" | custom-call | tf_op jit(solution)/shard_map/end/pallas_call | solution.py:245
  (1 shorter events, 0.0 us)
Async XLA Ops:
  0.0 13.5 %collective-permute-start.1 = (bf16[576,128]{1,0:T(8,128)(2,1)}, bf16[576,128]{1,0:T(8,128)(2,1)S(1)}, u32[]{:S(2)}, u32[]{:S(2)}) collective-permute-start(bf16[576,128]{1,0:T(8,128)(2,1)} %bitcast.2), channel_id=1, source_target_pairs={{0,0},{1,8},{2,4},{3,12},{4,1},{5,9},{6,5},{7,13},{8,2},{9,10},{10... | collective-permute-start | bytes 442376 | tf_op jit(solution)/shard_map/ppermute | solution.py:231
  1.6 17.3 %collective-permute-start.5 = (bf16[576,128]{1,0:T(8,128)(2,1)}, bf16[576,128]{1,0:T(8,128)(2,1)S(1)}, u32[]{:S(2)}, u32[]{:S(2)}) collective-permute-start(bf16[576,128]{1,0:T(8,128)(2,1)} %bitcast.3), channel_id=1, source_target_pairs={{0,1},{1,0},{2,3},{3,2},{4,5},{5,4},{6,7},{7,6},{8,9},{9,8},{10,11... | collective-permute-start | bytes 442376 | tf_op jit(solution)/shard_map/ppermute | solution.py:227
  6.4 12.5 %collective-permute-start.6 = (bf16[576,128]{1,0:T(8,128)(2,1)}, bf16[576,128]{1,0:T(8,128)(2,1)S(1)}, u32[]{:S(2)}, u32[]{:S(2)}) collective-permute-start(bf16[576,128]{1,0:T(8,128)(2,1)} %bitcast.4), channel_id=1, source_target_pairs={{0,3},{1,2},{2,1},{3,0},{4,7},{5,6},{6,5},{7,4},{8,11},{9,10},{10,... | collective-permute-start | bytes 442376 | tf_op jit(solution)/shard_map/ppermute | solution.py:227
  10.6 0.9 %copy-start = (bf16[24,24,128]{2,1,0:T(8,128)(2,1)S(1)}, bf16[24,24,128]{2,1,0:T(8,128)(2,1)}, u32[]{:S(2)}) copy-start(bf16[24,24,128]{2,1,0:T(8,128)(2,1)} %param.10) | copy-start | bytes 442372
  11.5 1.0 %copy-start.1 = (bf16[2,128,640]{2,1,0:T(8,128)(2,1)S(1)}, bf16[2,128,640]{2,1,0:T(8,128)(2,1)}, u32[]{:S(2)}) copy-start(bf16[2,128,640]{2,1,0:T(8,128)(2,1)} %w_in.1) | copy-start | bytes 983044
  12.5 18.0 %copy-start.2 = (bf16[2,128,128]{2,1,0:T(8,128)(2,1)S(1)}, bf16[2,128,128]{2,1,0:T(8,128)(2,1)}, u32[]{:S(2)}) copy-start(bf16[2,128,128]{2,1,0:T(8,128)(2,1)} %w_out.1) | copy-start | bytes 196612
  13.5 5.3 %collective-permute-start.2 = (bf16[576,128]{1,0:T(8,128)(2,1)S(1)}, bf16[576,128]{1,0:T(8,128)(2,1)S(1)}, u32[]{:S(2)}, u32[]{:S(2)}) collective-permute-start(bf16[576,128]{1,0:T(8,128)(2,1)S(1)} %collective-permute-done.1.refs_0_), channel_id=1, source_target_pairs={{0,4},{4,0},{8,12},{12,8},{1,5},{5,1},{9,13},{13,9},{2,6},{6,2},{1... | collective-permute-start | bytes 442376 | tf_op jit(solution)/shard_map/ppermute | solution.py:227
  13.8 6.6 %collective-permute-start.3 = (bf16[576,128]{1,0:T(8,128)(2,1)S(1)}, bf16[576,128]{1,0:T(8,128)(2,1)S(1)}, u32[]{:S(2)}, u32[]{:S(2)}) collective-permute-start(bf16[576,128]{1,0:T(8,128)(2,1)S(1)} %collective-permute-done.1.refs_0_), channel_id=1, source_target_pairs={{0,8},{4,12},{8,0},{12,4},{1,9},{5,13},{9,1},{13,5},{2,10},{6,14},... | collective-permute-start | bytes 442376 | tf_op jit(solution)/shard_map/ppermute | solution.py:227
  15.6 7.3 %collective-permute-start.4 = (bf16[576,128]{1,0:T(8,128)(2,1)S(1)}, bf16[576,128]{1,0:T(8,128)(2,1)S(1)}, u32[]{:S(2)}, u32[]{:S(2)}) collective-permute-start(bf16[576,128]{1,0:T(8,128)(2,1)S(1)} %collective-permute-done.1.refs_0_), channel_id=1, source_target_pairs={{0,12},{4,8},{8,4},{12,0},{1,13},{5,9},{9,5},{13,1},{2,14},{6,10},... | collective-permute-start | bytes 442376 | tf_op jit(solution)/shard_map/ppermute | solution.py:227
  18.8 11.6 %collective-permute-start = (bf16[576,128]{1,0:T(8,128)(2,1)S(1)}, bf16[576,128]{1,0:T(8,128)(2,1)S(1)}, u32[]{:S(2)}, u32[]{:S(2)}) collective-permute-start(bf16[576,128]{1,0:T(8,128)(2,1)S(1)} %bitcast.6), channel_id=1, source_target_pairs={{0,2},{1,3},{2,0},{3,1},{4,6},{5,7},{6,4},{7,5},{8,10},{9,11},{10,... | collective-permute-start | bytes 442376 | tf_op jit(solution)/shard_map/ppermute | solution.py:227
  33.9 6.0 %collective-permute-start.10 = (bf16[576,128]{1,0:T(8,128)(2,1)S(1)}, bf16[576,128]{1,0:T(8,128)(2,1)S(1)}, u32[]{:S(2)}, u32[]{:S(2)}) collective-permute-start(bf16[576,128]{1,0:T(8,128)(2,1)S(1)} %get-tuple-element.33.refs_0_), channel_id=1, source_target_pairs={{0,12},{4,8},{8,4},{12,0},{1,13},{5,9},{9,5},{13,1},{2,14},{6,10},... | collective-permute-start | bytes 442376 | tf_op jit(solution)/shard_map/ppermute | solution.py:227
  35.5 7.2 %collective-permute-start.8 = (bf16[576,128]{1,0:T(8,128)(2,1)S(1)}, bf16[576,128]{1,0:T(8,128)(2,1)S(1)}, u32[]{:S(2)}, u32[]{:S(2)}) collective-permute-start(bf16[576,128]{1,0:T(8,128)(2,1)S(1)} %get-tuple-element.33.refs_0_), channel_id=1, source_target_pairs={{0,4},{4,0},{8,12},{12,8},{1,5},{5,1},{9,13},{13,9},{2,6},{6,2},{1... | collective-permute-start | bytes 442376 | tf_op jit(solution)/shard_map/ppermute | solution.py:227
  35.8 7.5 %collective-permute-start.9 = (bf16[576,128]{1,0:T(8,128)(2,1)S(1)}, bf16[576,128]{1,0:T(8,128)(2,1)S(1)}, u32[]{:S(2)}, u32[]{:S(2)}) collective-permute-start(bf16[576,128]{1,0:T(8,128)(2,1)S(1)} %get-tuple-element.33.refs_0_), channel_id=1, source_target_pairs={{0,8},{4,12},{8,0},{12,4},{1,9},{5,13},{9,1},{13,5},{2,10},{6,14},... | collective-permute-start | bytes 442376 | tf_op jit(solution)/shard_map/ppermute | solution.py:227
  36.1 7.9 %collective-permute-start.12 = (bf16[576,128]{1,0:T(8,128)(2,1)S(1)}, bf16[576,128]{1,0:T(8,128)(2,1)S(1)}, u32[]{:S(2)}, u32[]{:S(2)}) collective-permute-start(bf16[576,128]{1,0:T(8,128)(2,1)S(1)} %get-tuple-element.32.refs_4_), channel_id=1, source_target_pairs={{0,1},{1,0},{2,3},{3,2},{4,5},{5,4},{6,7},{7,6},{8,9},{9,8},{10,11... | collective-permute-start | bytes 442376 | tf_op jit(solution)/shard_map/ppermute | solution.py:227
  36.9 10.9 %collective-permute-start.11 = (bf16[576,128]{1,0:T(8,128)(2,1)S(1)}, bf16[576,128]{1,0:T(8,128)(2,1)S(1)}, u32[]{:S(2)}, u32[]{:S(2)}) collective-permute-start(bf16[576,128]{1,0:T(8,128)(2,1)S(1)} %get-tuple-element.32.refs_4_), channel_id=1, source_target_pairs={{0,3},{1,2},{2,1},{3,0},{4,7},{5,6},{6,5},{7,4},{8,11},{9,10},{10,... | collective-permute-start | bytes 442376 | tf_op jit(solution)/shard_map/ppermute | solution.py:227
  39.8 13.4 %collective-permute-start.7 = (bf16[576,128]{1,0:T(8,128)(2,1)S(1)}, bf16[576,128]{1,0:T(8,128)(2,1)S(1)}, u32[]{:S(2)}, u32[]{:S(2)}) collective-permute-start(bf16[576,128]{1,0:T(8,128)(2,1)S(1)} %get-tuple-element.32.refs_4_), channel_id=1, source_target_pairs={{0,2},{1,3},{2,0},{3,1},{4,6},{5,7},{6,4},{7,5},{8,10},{9,11},{10,... | collective-permute-start | bytes 442376 | tf_op jit(solution)/shard_map/ppermute | solution.py:227

commit v7 on v6

v7 whole, which is shorter than its diff:
```python
import functools

import jax
import jax.numpy as jnp
from jax import lax
from jax.experimental import pallas as pl
from jax.experimental.pallas import tpu as pltpu
from jax.sharding import PartitionSpec as P

F32, BF16 = jnp.float32, jnp.bfloat16


def dot(a, b):
    return jnp.dot(a, b, preferred_element_type=F32)


def split(values):
    high = values.astype(BF16)
    return jnp.concatenate([high, (values - high.astype(F32)).astype(BF16)], axis=1)


def constants(width):
    rows = lax.broadcasted_iota(jnp.int32, (2 * width, width), 0)
    cols = lax.broadcasted_iota(jnp.int32, (2 * width, width), 1)
    mean = jnp.full((2 * width, width), 1.0 / width, F32)
    center = jnp.where((rows == cols) | (rows == cols + width), 1.0, 0.0) - mean
    return center.astype(BF16), mean.astype(BF16)


def scaled(center, mean, gain, shift):
    spread = dot(split(center * center), mean)
    return (center * lax.rsqrt(spread + 1e-05) * gain + shift).astype(BF16)


def norm_pair(values, consts, gain, shift):
    return scaled(dot(values, consts[0][: values.shape[1]]), consts[1], gain, shift)


def norm_mixed(values, consts, gain, shift):
    return scaled(dot(split(values), consts[0]), consts[1], gain, shift)


def gated(normed, weights, bias, width):
    product = dot(normed, weights) + bias
    return (jnp.tanh(product[:, width:]) + 1.0) * product[:, :width]


def gate(normed, weights, bias):
    return 0.5 * jnp.tanh(dot(normed, weights) + bias) + 0.5


def masked(values, outer, inner):
    t = outer.shape[0]
    grid = jnp.concatenate([outer[k : k + 1] * inner for k in range(t)], axis=0)
    return (values * grid).astype(BF16)


def mix(out_ref, old_ref, lefts, rights, first, last, left_at, right_at, t):
    width = out_ref.shape[1]
    for base in range(0, t, 8):
        if old_ref is None:
            total = (jnp.zeros((t, width), F32),) * 8
        else:
            total = tuple(old_ref[pl.ds((base + i) * t, t), :] for i in range(8))

        def slot(s, total):
            ls, rs = left_at(s), right_at(s)

            def step(q, total):
                for u in range(4):
                    at = pl.multiple_of((q * 4 + u) * t, 8)
                    row = rights[rs, pl.ds(at, t), :]
                    total = tuple(total[i] + lefts[ls, pl.ds(at + base + i, 1), :] * row for i in range(8))
                return total

            return lax.fori_loop(0, t // 4, step, total)

        total = lax.fori_loop(first, last, slot, total)
        for i in range(8):
            out_ref[pl.ds((base + i) * t, t), :] = total[i]


def finish(pair, mixed, gating, consts, gain, shift, weights, bias):
    normout = norm_mixed(mixed, consts, gain, shift)
    return (pair.astype(F32) + gating * (dot(normout, weights) + bias)).astype(BF16)


TABLE_MASK = 24


def in_norm(table, u):
    return table[u : u + 1], table[2 + u : 3 + u]


def out_norm(table, u):
    return table[4 + u : 5 + u], table[6 + u : 7 + u]


def half_bias(table, u, first, last):
    return jnp.concatenate([table[k : k + 1] for k in range(10 + 5 * u + first, 10 + 5 * u + last)], axis=1) * 0.5


def mask_of(table, b, t):
    return table[pl.ds(pl.multiple_of(TABLE_MASK + b * t, 8), t), :]


def sides(values_ref, wide, left_at, right_at, outer, inner, consts, table, weights):
    t, width = outer.shape
    wide[...] = values_ref[...].astype(F32)
    values = jnp.concatenate([wide[pl.ds(k, t, stride=t), :] for k in range(t)], axis=0).astype(BF16)
    normed = norm_pair(values, consts, *in_norm(table, 0))
    for k, target in enumerate((left_at, right_at)):
        span = slice(2 * k * width, 2 * (k + 1) * width)
        side = gated(normed, weights[0, :, span], half_bias(table, 0, 2 * k, 2 * k + 2), width)
        target[...] = masked(side, outer, inner).astype(F32)


def gate_of(values, consts, table, weights, u):
    normed = norm_pair(values, consts, *in_norm(table, u))
    return gate(normed, weights[u, :, 4 * values.shape[1] :], half_bias(table, u, 4, 5))


def own_kernel(t, pair, table, w_in, weights, row_l, row_r, gating, wide):
    r, c = lax.axis_index("row"), lax.axis_index("col")
    consts = constants(wide.shape[1])
    weights[...] = w_in[...] * 0.5
    outer, inner = mask_of(table, c, t), mask_of(table, r, t)
    sides(pair, wide, row_l.at[0], row_r.at[0], outer, inner, consts, table, weights)
    gating[...] = gate_of(pair[...], consts, table, weights, 0)


def rows_kernel(t, count, *refs):
    blocks, (col_pair, table, weights) = refs[:count], refs[count : count + 3]
    row_l, row_r, col_l, col_r, col_gating, wide = refs[count + 5 :]
    r, c = lax.axis_index("row"), lax.axis_index("col")
    consts = constants(wide.shape[1])
    here, there = mask_of(table, r, t), mask_of(table, c, t)
    sides(col_pair, wide, col_l.at[0], col_r.at[0], here, there, consts, table, weights)
    col_gating[...] = gate_of(col_pair[...], consts, table, weights, 0)
    for s, block in enumerate(blocks, 1):
        outer = mask_of(table, c ^ s, t)
        sides(block, wide, row_l.at[s], row_r.at[s], outer, here, consts, table, weights)


def columns_kernel(n, t, *refs):
    blocks, (table, weights, row_l, row_r) = refs[: n - 1], refs[n - 1 : n + 3]
    col_l, col_r, mixed, wide = refs[n + 5 :]
    r, c = lax.axis_index("row"), lax.axis_index("col")
    consts = constants(wide.shape[1])
    for s, block in enumerate(blocks, 1):
        outer, inner = mask_of(table, r ^ s, t), mask_of(table, c, t)
        sides(block, wide, col_l.at[s], col_r.at[s], outer, inner, consts, table, weights)
    mix(mixed.at[0], None, row_l, col_r, 0, n - 1, lambda s: s, lambda s: r ^ c ^ s, t)
    mix(mixed.at[1], None, col_l, row_r, 0, n - 1, lambda s: r ^ c ^ s, lambda s: s, t)


def last_kernel(n, t, *refs):
    block, table, weights, col_l, col_r, old, w_out, pair, gating, col_pair, col_gating = refs[:11]
    pair_ref, left_ref, right_ref, mixed, wide, left, right = refs[11:]
    width = wide.shape[1]
    r, c = lax.axis_index("row"), lax.axis_index("col")
    consts = constants(width)
    here, there = mask_of(table, r, t), mask_of(table, c, t)
    outer = mask_of(table, c ^ (n - 1), t)
    sides(block, wide, left.at[0], right.at[0], outer, here, consts, table, weights)
    source = r ^ c ^ (n - 1)
    mix(mixed.at[0], old.at[0], left, col_r, 0, 1, lambda s: s, lambda s: source, t)
    mix(mixed.at[1], old.at[1], col_l, right, 0, 1, lambda s: source, lambda s: s, t)
    for k, (base, factor) in enumerate(((pair, gating), (col_pair, col_gating))):
        updated = finish(base[...], mixed[k], factor[...], consts, *out_norm(table, 0), w_out[0], table[8:9])
        normed = norm_pair(updated, consts, *in_norm(table, 1))
        if k == 0:
            pair_ref[...] = updated
            side = gated(normed, weights[1, :, 2 * width : 4 * width], half_bias(table, 1, 2, 4), width)
            right_ref[...] = masked(side, here, there)
        else:
            side = gated(normed, weights[1, :, : 2 * width], half_bias(table, 1, 0, 2), width)
            left_ref[...] = masked(side, there, here)


def gate_kernel(pair, table, weights, gating):
    gating[...] = gate_of(pair[...], constants(pair.shape[1]), table, weights, 1)


def middle_kernel(n, t, *refs):
    blocks, sources = refs[: n - 1], refs[n - 1 : 2 * n - 1]
    rights, mixed, lefts = refs[2 * n - 1 :]
    r, c = lax.axis_index("row"), lax.axis_index("col")
    for s in range(n - 1):
        lefts[s] = blocks[s][...].astype(F32)
    for s in range(n):
        rights[s] = sources[s][...].astype(F32)
    mix(mixed, None, lefts, rights, 0, n - 1, lambda s: s, lambda s: r ^ c ^ s, t)


def end_kernel(n, t, block, rights, old, pair, gating, table, w_out, out, mixed, left):
    r, c = lax.axis_index("row"), lax.axis_index("col")
    left[0] = block[...].astype(F32)
    mix(mixed, old, left, rights, 0, 1, lambda s: s, lambda s: r ^ c ^ (n - 1), t)
    consts = constants(mixed.shape[1])
    out[...] = finish(pair[...], mixed[...], gating[...], consts, *out_norm(table, 1), w_out[1], table[9:10])


def solution(mesh):
    n = mesh.shape["col"]

    def gather(block, axis, after=lambda block: block):
        held, step = {0: block}, n // 2
        while step:
            for s, part in list(held.items()):
                part = after(part) if s else part
                held[s ^ step] = lax.ppermute(part, axis, [(k, k ^ step) for k in range(n)])
            step //= 2
        return [held[s] for s in range(n)]

    def mirrored(block):
        return lax.ppermute(block, ("row", "col"), [(a * n + z, z * n + a) for a in range(n) for z in range(n)])

    def per_device(pair, token_mask, in_gain, in_shift, w_in, bias_in, out_gain, out_shift, w_out, bias_out):
        t, _, width = pair.shape
        area = (t * t, width)
        narrow, broad = jax.ShapeDtypeStruct(area, BF16), jax.ShapeDtypeStruct(area, F32)
        row_like = jax.ShapeDtypeStruct((n - 1,) + area, F32)
        col_like = jax.ShapeDtypeStruct((n,) + area, F32)
        twice = jax.ShapeDtypeStruct((2,) + area, F32)
        scratch = pltpu.VMEM(area, F32)

        def call(kernel, name, outs, scratches, *operands, alias=None, **specs):
            return pl.pallas_call(
                kernel,
                out_shape=outs,
                scratch_shapes=scratches,
                input_output_aliases=alias or {},

                compiler_params=pltpu.CompilerParams(vmem_limit_bytes=(16 + n) * 1024 * 1024),
                name=name,
            )(*operands)

        pair = pair.reshape(area)
        col_pair = mirrored(pair)
        mask = jnp.broadcast_to(token_mask.astype(F32)[:, None], (n * t, width))
        vectors = [in_gain, in_shift, out_gain, out_shift, bias_out, bias_in.reshape(-1, width)]
        table = jnp.concatenate(vectors + [jnp.zeros((TABLE_MASK - 20, width), F32), mask])
        weights, row_l, row_r, gating = call(
            functools.partial(own_kernel, t),
            "own_sides",
            (jax.ShapeDtypeStruct(w_in.shape, BF16), row_like, row_like, broad),
            [scratch],
            pair,
            table,
            w_in,
        )
        after = lambda block: lax.optimization_barrier((block, row_l))[0]
        rows, cols = gather(pair, "col", after), gather(after(col_pair), "row")
        row_l, row_r, col_l, col_r, col_gating = call(
            functools.partial(rows_kernel, t, n - 2),
            "row_sides",
            (row_like, row_like, col_like, col_like, broad),
            [scratch],
            *rows[1:-1],
            col_pair,
            table,
            weights,
            row_l,
            row_r,
            alias={n + 1: 0, n + 2: 1},
        )
        col_l, col_r, mixed = call(
            functools.partial(columns_kernel, n, t),
            "column_sides",
            (col_like, col_like, twice),
            [scratch],
            *cols[1:],
            table,
            weights,
            row_l,
            row_r,
            col_l,
            col_r,
            alias={n + 3: 0, n + 4: 1},
        )
        pair, left, right = call(
            functools.partial(last_kernel, n, t),
            "last_slot",
            (narrow,) * 3,
            [pltpu.VMEM((2,) + area, F32), scratch] + [pltpu.VMEM((1,) + area, F32)] * 2,
            rows[-1],
            table,
            weights,
            col_l,
            col_r,
            mixed,
            w_out,
            pair,
            gating,
            col_pair,
            col_gating,
        )
        lefts, rights = gather(left, "col"), gather(right, "row")
        gating = call(gate_kernel, "gate", broad, [], pair, table, weights)
        rights, mixed = call(
            functools.partial(middle_kernel, n, t),
            "middle_slots",
            (col_like, broad),
            [pltpu.VMEM((n - 1,) + area, F32)],
            *lefts[:-1],
            *rights,
        )
        out = call(
            functools.partial(end_kernel, n, t),
            "end",
            narrow,
            [scratch, pltpu.VMEM((1,) + area, F32)],
            lefts[-1],
            rights,
            mixed,
            pair,
            gating,
            table,
            w_out,
        )
        return out.reshape(t, t, width)

    placed = (P(("groups", "row"), "col", None), P("groups")) + (P(),) * 8
    return jax.shard_map(
        per_device, mesh=mesh, in_specs=placed, out_specs=P(("groups", "row"), "col", None), check_vma=False
    )
```

time: 55.4 us -> 54 us (0.975)
  starting transfers between devices: 18 us -> 15.9 us
  waiting for transfers between devices: 15.9 us -> 16.8 us
    ppermute x13, starting transfers between devices: 18 us -> 15.9 us  [the longest x12 14.4 us: gather(): held[s ^ step] = lax.ppermute(part, axis, [(k, k ^ step) for k in range(n)])]
    ppermute x13, waiting for transfers between devices: 15.9 us -> 16.8 us  [the longest x12 16.8 us: gather(): held[s ^ step] = lax.ppermute(part, axis, [(k, k ^ step) for k in range(n)])]
    pallas_call x8 -> x7, Pallas kernels: 16.2 us -> 16.1 us  [call(): pl.pallas_call(kernel, out_shape=outs, scratch_shapes=scratches, input_ou...]
where the time goes in v7:
time: 54 us; the launch traced here: 53.7 us
  waiting for transfers between devices  16.8 us (31%)
  Pallas kernels  16.1 us (30%)
  starting transfers between devices  15.9 us (29%)
  local copies, waits for them, and re-layouts  4.16 us (8%)
  other arithmetic  0.66 us (1%)
    ppermute x12, waiting for transfers between devices, gather(): held[s ^ step] = lax.ppermute(part, axis, [(k, k ^ step) for k in range(n)])  16.8 us
    pallas_call x7, Pallas kernels, call(): pl.pallas_call(kernel, out_shape=outs, scratch_shapes=scratches, input_ou...  16.1 us
    ppermute x12, starting transfers between devices, gather(): held[s ^ step] = lax.ppermute(part, axis, [(k, k ^ step) for k in range(n)])  14.4 us
    unnamed x6, local copies, waits for them, and re-layouts  1.88 us
    ppermute x1, starting transfers between devices, mirrored(): lax.ppermute(block, ('row', 'col'), [(a * n + z, z * n + a) for a in rang...  1.56 us
    concatenate x1, local copies, waits for them, and re-layouts, per_device(): jnp.concatenate(vectors + [jnp.zeros((TABLE_MASK - 20, width), F32), mask])  1.51 us
  transfers between devices with their start and end apart: 13, of which 7 were waited for; matrix products, arithmetic and copies ran while one was open for 5% of the time, Pallas kernels for 20%

profile of v7, /device:TPU:0, one launch (start us, length us, event | category | flops | bytes accessed | tf_op | source)
XLA Modules:
  0.0 53.7 jit_solution(14175958124557709076)
XLA Ops:
  0.0 1.6 %collective-permute-start.2 = (bf16[576,128]{1,0:T(8,128)(2,1)}, bf16[576,128]{1,0:T(8,128)(2,1)S(1)}, u32[]{:S(2)}, u32[]{:S(2)}) collective-permute-start(bf16[576,128]{1,0:T(8,128)(2,1)} %bitcast.2), channel_id=1, source_target_pairs={{0,0},{1,4},{2,8},{3,12},{4,1},{5,5},{6,9},{7,13},{8,2},{9,6},{10,... | collective-permute-start | bytes 442376 | tf_op jit(solution)/shard_map/ppermute | solution.py:217
  1.6 0.7 %convert_element_type.3 = f32[96]{0:T(128)S(1)} convert(s32[96]{0:T(128)} %param.11) | non-fusion elementwise | flops 96 | bytes 768 | tf_op jit(solution)/shard_map/convert_element_type | solution.py:241
  2.2 0.7 %reshape.11 = f32[10,128]{1,0:T(8,128)S(1)} reshape(f32[2,640]{1,0:T(2,128)} %param.15) | data formatting | bytes 10240 | tf_op jit(solution)/shard_map/reshape | solution.py:242
  2.9 0.1 broadcast_in_dim.10
  3.0 1.5 %concatenate.3.table.refs_3_.refs_1_ = f32[120,128]{1,0:T(8,128)S(1)} concatenate(f32[2,128]{1,0:T(2,128)} %param.12, f32[2,128]{1,0:T(2,128)} %param.13, f32[2,128]{1,0:T(2,128)} %param.16, f32[2,128]{1,0:T(2,128)} %param.17, f32[2,128]{1,0:T(2,128)} %param.19, f32[10,128]{1,0:T(8,128)S(1)} %reshape.11, f32[4,128]{1,0:T(4,128)S(1)} %broadcast_in_dim.4, ...), dimensions={0} | concatenate | bytes 122880 | tf_op jit(solution)/shard_map/concatenate | solution.py:243
  4.5 0.0 copy-start
  4.5 0.9 %copy-done = bf16[24,24,128]{2,1,0:T(8,128)(2,1)S(1)} copy-done((bf16[24,24,128]{2,1,0:T(8,128)(2,1)S(1)}, bf16[24,24,128]{2,1,0:T(8,128)(2,1)}, u32[]{:S(2)}) %copy-start) | copy-done | bytes 147480
  5.4 0.0 copy-start.1
  5.4 1.0 %copy-done.1 = bf16[2,128,640]{2,1,0:T(8,128)(2,1)S(1)} copy-done((bf16[2,128,640]{2,1,0:T(8,128)(2,1)S(1)}, bf16[2,128,640]{2,1,0:T(8,128)(2,1)}, u32[]{:S(2)}) %copy-start.1) | copy-done | bytes 327704
  6.4 1.0 %own_sides.1 = (bf16[2,128,640]{2,1,0:T(8,128)(2,1)S(1)}, f32[3,576,128]{2,1,0:T(8,128)S(1)}, f32[3,576,128]{2,1,0:T(8,128)S(1)}, f32[576,128]{1,0:T(8,128)S(1)}) custom-call(bf16[576,128]{1,0:T(8,128)(2,1)S(1)} %bitcast.3, f32[120,128]{1,0:T(8,128)S(1)} %concatenate.3.table.refs_3_.refs_1_, bf16[2,128,640]{2,1,0:T(8,128)(2,1)S(1)} %copy-done.1), custom_call_target="tpu_custom_call" | custom-call | tf_op jit(solution)/shard_map/own_sides/pallas_call | solution.py:229
  7.4 0.0 collective-permute-done.2.refs_2_.refs_9_
  7.4 8.9 %collective-permute-start.4 = (bf16[576,128]{1,0:T(8,128)(2,1)S(1)}, bf16[576,128]{1,0:T(8,128)(2,1)S(1)}, u32[]{:S(2)}, u32[]{:S(2)}) collective-permute-start(bf16[576,128]{1,0:T(8,128)(2,1)S(1)} %collective-permute-done.2.refs_2_.refs_9_), channel_id=1, source_target_pairs={{0,8},{4,12},{8,0},{12,4},{1,9},{5,13},{9,1},{13,5},{2,10},{6,14},... | collective-permute-start | bytes 442376 | tf_op jit(solution)/shard_map/ppermute | solution.py:212
  16.3 0.0 collective-permute-start
  16.3 0.2 collective-permute-start.6
  16.5 0.6 %collective-permute-start.3 = (bf16[576,128]{1,0:T(8,128)(2,1)S(1)}, bf16[576,128]{1,0:T(8,128)(2,1)S(1)}, u32[]{:S(2)}, u32[]{:S(2)}) collective-permute-start(bf16[576,128]{1,0:T(8,128)(2,1)S(1)} %collective-permute-done.2.refs_2_.refs_9_), channel_id=1, source_target_pairs={{0,4},{4,0},{8,12},{12,8},{1,5},{5,1},{9,13},{13,9},{2,6},{6,2},{1... | collective-permute-start | bytes 442376 | tf_op jit(solution)/shard_map/ppermute | solution.py:212
  17.1 2.3 %collective-permute-done.4.refs_1_ = bf16[576,128]{1,0:T(8,128)(2,1)S(1)} collective-permute-done((bf16[576,128]{1,0:T(8,128)(2,1)S(1)}, bf16[576,128]{1,0:T(8,128)(2,1)S(1)}, u32[]{:S(2)}, u32[]{:S(2)}) %collective-permute-start.4) | collective-permute-done | bytes 147488 | tf_op jit(solution)/shard_map/ppermute | solution.py:212
  19.4 0.0 collective-permute-start.5
  19.4 4.7 %collective-permute-done.refs_1_ = bf16[576,128]{1,0:T(8,128)(2,1)S(1)} collective-permute-done((bf16[576,128]{1,0:T(8,128)(2,1)S(1)}, bf16[576,128]{1,0:T(8,128)(2,1)S(1)}, u32[]{:S(2)}, u32[]{:S(2)}) %collective-permute-start) | collective-permute-done | bytes 147488 | tf_op jit(solution)/shard_map/ppermute | solution.py:212
  24.1 0.0 collective-permute-start.1
  24.1 0.1 collective-permute-done.6.refs_0_
  24.1 1.8 %row_sides.1 = (f32[3,576,128]{2,1,0:T(8,128)S(1)}, f32[3,576,128]{2,1,0:T(8,128)S(1)}, f32[4,576,128]{2,1,0:T(8,128)S(1)}, f32[4,576,128]{2,1,0:T(8,128)S(1)}, f32[576,128]{1,0:T(8,128)S(1)}) custom-call(bf16[576,128]{1,0:T(8,128)(2,1)S(1)} %collective-permute-done.6.refs_0_, ...), custom_call_target="tpu_custom_call", output_to_operand_aliasing={{0}: (5, {}), {1}: (6, {})} | custom-call | tf_op jit(solution)/shard_map/row_sides/pallas_call | solution.py:229
  26.0 0.0 collective-permute-done.3.refs_0_
  26.0 0.0 collective-permute-done.5.refs_2_
  26.0 0.0 copy-start.2
  26.0 5.4 %column_sides.1 = (f32[4,576,128]{2,1,0:T(8,128)S(1)}, f32[4,576,128]{2,1,0:T(8,128)S(1)}, f32[2,576,128]{2,1,0:T(8,128)S(1)}) custom-call(bf16[576,128]{1,0:T(8,128)(2,1)S(1)} %collective-permute-done.3.refs_0_, bf16[576,128]{1,0:T(8,128)(2,1)S(1)} %collective-permute-done.4.refs_1_, ...), custom_call_target="tpu_custom_call", output_to_operand_aliasing={{0}: (7, {}), {1}: (8, {})} | custom-call | tf_op jit(solution)/shard_map/column_sides/pallas_call | solution.py:229
  31.4 0.0 collective-permute-done.1.refs_0_
  31.4 0.0 copy-done.2
  31.4 3.4 %last_slot.1 = (bf16[576,128]{1,0:T(8,128)(2,1)S(1)}, bf16[576,128]{1,0:T(8,128)(2,1)S(1)}, bf16[576,128]{1,0:T(8,128)(2,1)S(1)}) custom-call(bf16[576,128]{1,0:T(8,128)(2,1)S(1)} %collective-permute-done.1.refs_0_, f32[120,128]{1,0:T(8,128)S(1)} %concatenate.3.table.refs_3_.refs_1_, bf16[2,128,640]{2,1,0:T(8,128)(2,1)S(1)} %get-tuple-element.26.refs_4_.refs_2_.weights, ...), custom_call_target="tpu_custom_call" | custom-call | tf_op jit(solution)/shard_map/last_slot/pallas_call | solution.py:229
  34.8 1.3 %collective-permute-start.11 = (bf16[576,128]{1,0:T(8,128)(2,1)S(1)}, bf16[576,128]{1,0:T(8,128)(2,1)S(1)}, u32[]{:S(2)}, u32[]{:S(2)}) collective-permute-start(bf16[576,128]{1,0:T(8,128)(2,1)S(1)} %get-tuple-element.39.refs_3_), channel_id=1, source_target_pairs={{0,8},{4,12},{8,0},{12,4},{1,9},{5,13},{9,1},{13,5},{2,10},{6,14},... | collective-permute-start | bytes 442376 | tf_op jit(solution)/shard_map/ppermute | solution.py:212
  36.1 3.4 %collective-permute-start.7 = (bf16[576,128]{1,0:T(8,128)(2,1)S(1)}, bf16[576,128]{1,0:T(8,128)(2,1)S(1)}, u32[]{:S(2)}, u32[]{:S(2)}) collective-permute-start(bf16[576,128]{1,0:T(8,128)(2,1)S(1)} %get-tuple-element.38.refs_0_), channel_id=1, source_target_pairs={{0,2},{1,3},{2,0},{3,1},{4,6},{5,7},{6,4},{7,5},{8,10},{9,11},{10,... | collective-permute-start | bytes 442376 | tf_op jit(solution)/shard_map/ppermute | solution.py:212
  39.5 0.0 collective-permute-start.9
  39.5 0.0 collective-permute-start.10
  39.5 0.7 %collective-permute-done.11.refs_5_ = bf16[576,128]{1,0:T(8,128)(2,1)S(1)} collective-permute-done((bf16[576,128]{1,0:T(8,128)(2,1)S(1)}, bf16[576,128]{1,0:T(8,128)(2,1)S(1)}, u32[]{:S(2)}, u32[]{:S(2)}) %collective-permute-start.11) | collective-permute-done | bytes 147488 | tf_op jit(solution)/shard_map/ppermute | solution.py:212
  40.1 0.0 collective-permute-start.12
  40.1 6.0 %collective-permute-done.7.refs_2_ = bf16[576,128]{1,0:T(8,128)(2,1)S(1)} collective-permute-done((bf16[576,128]{1,0:T(8,128)(2,1)S(1)}, bf16[576,128]{1,0:T(8,128)(2,1)S(1)}, u32[]{:S(2)}, u32[]{:S(2)}) %collective-permute-start.7) | collective-permute-done | bytes 147488 | tf_op jit(solution)/shard_map/ppermute | solution.py:212
  46.2 0.0 collective-permute-start.8
  46.2 0.5 %gate.1.gating = f32[576,128]{1,0:T(8,128)S(1)} custom-call(bf16[576,128]{1,0:T(8,128)(2,1)S(1)} %get-tuple-element.42.pair, f32[120,128]{1,0:T(8,128)S(1)} %concatenate.3.table.refs_3_.refs_1_, bf16[2,128,640]{2,1,0:T(8,128)(2,1)S(1)} %get-tuple-element.26.refs_4_.refs_2_.weights), custom_call_target="tpu_custom_call" | custom-call | tf_op jit(solution)/shard_map/gate/pallas_call | solution.py:229
  46.7 0.8 %collective-permute-done.9.refs_1_ = bf16[576,128]{1,0:T(8,128)(2,1)S(1)} collective-permute-done((bf16[576,128]{1,0:T(8,128)(2,1)S(1)}, bf16[576,128]{1,0:T(8,128)(2,1)S(1)}, u32[]{:S(2)}, u32[]{:S(2)}) %collective-permute-start.9) | collective-permute-done | bytes 147488 | tf_op jit(solution)/shard_map/ppermute | solution.py:212
  47.6 0.0 collective-permute-done.10.refs_4_
  47.6 0.0 collective-permute-done.12.refs_6_
  47.6 2.1 %middle_slots.1 = (f32[4,576,128]{2,1,0:T(8,128)S(1)}, f32[576,128]{1,0:T(8,128)S(1)}) custom-call(bf16[576,128]{1,0:T(8,128)(2,1)S(1)} %get-tuple-element.38.refs_0_, bf16[576,128]{1,0:T(8,128)(2,1)S(1)} %collective-permute-done.9.refs_1_, bf16[576,128]{1,0:T(8,128)(2,1)S(1)} %collective-permute-done.7.refs_2_, ...), custom_call_target="tpu_custom_call" | custom-call | tf_op jit(solution)/shard_map/middle_slots/pallas_call | solution.py:229
  49.7 2.2 %collective-permute-done.8.block = bf16[576,128]{1,0:T(8,128)(2,1)S(1)} collective-permute-done((bf16[576,128]{1,0:T(8,128)(2,1)S(1)}, bf16[576,128]{1,0:T(8,128)(2,1)S(1)}, u32[]{:S(2)}, u32[]{:S(2)}) %collective-permute-start.8) | collective-permute-done | bytes 147488 | tf_op jit(solution)/shard_map/ppermute | solution.py:212
  51.9 1.9 %end.1 = bf16[576,128]{1,0:T(8,128)(2,1)} custom-call(bf16[576,128]{1,0:T(8,128)(2,1)S(1)} %collective-permute-done.8.block, f32[4,576,128]{2,1,0:T(8,128)S(1)} %get-tuple-element.40.rights, f32[576,128]{1,0:T(8,128)S(1)} %get-tuple-element.41.old, bf16[576,128]{1,0:T(8,128)(2,1)S(1)} %get-tuple-element.42.pair, f32[576,128]{1,0:T(8,128)S(1)} %gate.1.gating, ...), custom_call_target="tpu_custom_call" | custom-call | tf_op jit(solution)/shard_map/end/pallas_call | solution.py:229
  (1 shorter events, 0.0 us)
Async XLA Ops:
  0.0 7.4 %collective-permute-start.2 = (bf16[576,128]{1,0:T(8,128)(2,1)}, bf16[576,128]{1,0:T(8,128)(2,1)S(1)}, u32[]{:S(2)}, u32[]{:S(2)}) collective-permute-start(bf16[576,128]{1,0:T(8,128)(2,1)} %bitcast.2), channel_id=1, source_target_pairs={{0,0},{1,4},{2,8},{3,12},{4,1},{5,5},{6,9},{7,13},{8,2},{9,6},{10,... | collective-permute-start | bytes 442376 | tf_op jit(solution)/shard_map/ppermute | solution.py:217
  4.5 0.9 %copy-start = (bf16[24,24,128]{2,1,0:T(8,128)(2,1)S(1)}, bf16[24,24,128]{2,1,0:T(8,128)(2,1)}, u32[]{:S(2)}) copy-start(bf16[24,24,128]{2,1,0:T(8,128)(2,1)} %param.10) | copy-start | bytes 442372
  5.4 1.0 %copy-start.1 = (bf16[2,128,640]{2,1,0:T(8,128)(2,1)S(1)}, bf16[2,128,640]{2,1,0:T(8,128)(2,1)}, u32[]{:S(2)}) copy-start(bf16[2,128,640]{2,1,0:T(8,128)(2,1)} %w_in.1) | copy-start | bytes 983044
  7.4 12.0 %collective-permute-start.4 = (bf16[576,128]{1,0:T(8,128)(2,1)S(1)}, bf16[576,128]{1,0:T(8,128)(2,1)S(1)}, u32[]{:S(2)}, u32[]{:S(2)}) collective-permute-start(bf16[576,128]{1,0:T(8,128)(2,1)S(1)} %collective-permute-done.2.refs_2_.refs_9_), channel_id=1, source_target_pairs={{0,8},{4,12},{8,0},{12,4},{1,9},{5,13},{9,1},{13,5},{2,10},{6,14},... | collective-permute-start | bytes 442376 | tf_op jit(solution)/shard_map/ppermute | solution.py:212
  16.3 7.8 %collective-permute-start = (bf16[576,128]{1,0:T(8,128)(2,1)S(1)}, bf16[576,128]{1,0:T(8,128)(2,1)S(1)}, u32[]{:S(2)}, u32[]{:S(2)}) collective-permute-start(bf16[576,128]{1,0:T(8,128)(2,1)S(1)} %bitcast.4), channel_id=1, source_target_pairs={{0,2},{1,3},{2,0},{3,1},{4,6},{5,7},{6,4},{7,5},{8,10},{9,11},{10,... | collective-permute-start | bytes 442376 | tf_op jit(solution)/shard_map/ppermute | solution.py:212
  16.3 7.9 %collective-permute-start.6 = (bf16[576,128]{1,0:T(8,128)(2,1)S(1)}, bf16[576,128]{1,0:T(8,128)(2,1)S(1)}, u32[]{:S(2)}, u32[]{:S(2)}) collective-permute-start(bf16[576,128]{1,0:T(8,128)(2,1)S(1)} %bitcast.5), channel_id=1, source_target_pairs={{0,1},{1,0},{2,3},{3,2},{4,5},{5,4},{6,7},{7,6},{8,9},{9,8},{10,11... | collective-permute-start | bytes 442376 | tf_op jit(solution)/shard_map/ppermute | solution.py:212
  16.5 9.5 %collective-permute-start.3 = (bf16[576,128]{1,0:T(8,128)(2,1)S(1)}, bf16[576,128]{1,0:T(8,128)(2,1)S(1)}, u32[]{:S(2)}, u32[]{:S(2)}) collective-permute-start(bf16[576,128]{1,0:T(8,128)(2,1)S(1)} %collective-permute-done.2.refs_2_.refs_9_), channel_id=1, source_target_pairs={{0,4},{4,0},{8,12},{12,8},{1,5},{5,1},{9,13},{13,9},{2,6},{6,2},{1... | collective-permute-start | bytes 442376 | tf_op jit(solution)/shard_map/ppermute | solution.py:212
  19.4 6.6 %collective-permute-start.5 = (bf16[576,128]{1,0:T(8,128)(2,1)S(1)}, bf16[576,128]{1,0:T(8,128)(2,1)S(1)}, u32[]{:S(2)}, u32[]{:S(2)}) collective-permute-start(bf16[576,128]{1,0:T(8,128)(2,1)S(1)} %collective-permute-done.4.refs_1_), channel_id=1, source_target_pairs={{0,4},{4,0},{8,12},{12,8},{1,5},{5,1},{9,13},{13,9},{2,6},{6,2},{1... | collective-permute-start | bytes 442376 | tf_op jit(solution)/shard_map/ppermute | solution.py:212
  24.1 7.4 %collective-permute-start.1 = (bf16[576,128]{1,0:T(8,128)(2,1)S(1)}, bf16[576,128]{1,0:T(8,128)(2,1)S(1)}, u32[]{:S(2)}, u32[]{:S(2)}) collective-permute-start(bf16[576,128]{1,0:T(8,128)(2,1)S(1)} %collective-permute-done.refs_1_), channel_id=1, source_target_pairs={{0,1},{1,0},{2,3},{3,2},{4,5},{5,4},{6,7},{7,6},{8,9},{9,8},{10,11... | collective-permute-start | bytes 442376 | tf_op jit(solution)/shard_map/ppermute | solution.py:212
  26.0 5.4 %copy-start.2 = (bf16[2,128,128]{2,1,0:T(8,128)(2,1)S(1)}, bf16[2,128,128]{2,1,0:T(8,128)(2,1)}, u32[]{:S(2)}) copy-start(bf16[2,128,128]{2,1,0:T(8,128)(2,1)} %w_out.1) | copy-start | bytes 196612
  34.8 5.3 %collective-permute-start.11 = (bf16[576,128]{1,0:T(8,128)(2,1)S(1)}, bf16[576,128]{1,0:T(8,128)(2,1)S(1)}, u32[]{:S(2)}, u32[]{:S(2)}) collective-permute-start(bf16[576,128]{1,0:T(8,128)(2,1)S(1)} %get-tuple-element.39.refs_3_), channel_id=1, source_target_pairs={{0,8},{4,12},{8,0},{12,4},{1,9},{5,13},{9,1},{13,5},{2,10},{6,14},... | collective-permute-start | bytes 442376 | tf_op jit(solution)/shard_map/ppermute | solution.py:212
  36.1 10.1 %collective-permute-start.7 = (bf16[576,128]{1,0:T(8,128)(2,1)S(1)}, bf16[576,128]{1,0:T(8,128)(2,1)S(1)}, u32[]{:S(2)}, u32[]{:S(2)}) collective-permute-start(bf16[576,128]{1,0:T(8,128)(2,1)S(1)} %get-tuple-element.38.refs_0_), channel_id=1, source_target_pairs={{0,2},{1,3},{2,0},{3,1},{4,6},{5,7},{6,4},{7,5},{8,10},{9,11},{10,... | collective-permute-start | bytes 442376 | tf_op jit(solution)/shard_map/ppermute | solution.py:212
  39.5 8.1 %collective-permute-start.9 = (bf16[576,128]{1,0:T(8,128)(2,1)S(1)}, bf16[576,128]{1,0:T(8,128)(2,1)S(1)}, u32[]{:S(2)}, u32[]{:S(2)}) collective-permute-start(bf16[576,128]{1,0:T(8,128)(2,1)S(1)} %get-tuple-element.38.refs_0_), channel_id=1, source_target_pairs={{0,1},{1,0},{2,3},{3,2},{4,5},{5,4},{6,7},{7,6},{8,9},{9,8},{10,11... | collective-permute-start | bytes 442376 | tf_op jit(solution)/shard_map/ppermute | solution.py:212
  39.5 8.1 %collective-permute-start.10 = (bf16[576,128]{1,0:T(8,128)(2,1)S(1)}, bf16[576,128]{1,0:T(8,128)(2,1)S(1)}, u32[]{:S(2)}, u32[]{:S(2)}) collective-permute-start(bf16[576,128]{1,0:T(8,128)(2,1)S(1)} %get-tuple-element.39.refs_3_), channel_id=1, source_target_pairs={{0,4},{4,0},{8,12},{12,8},{1,5},{5,1},{9,13},{13,9},{2,6},{6,2},{1... | collective-permute-start | bytes 442376 | tf_op jit(solution)/shard_map/ppermute | solution.py:212
  40.1 7.4 %collective-permute-start.12 = (bf16[576,128]{1,0:T(8,128)(2,1)S(1)}, bf16[576,128]{1,0:T(8,128)(2,1)S(1)}, u32[]{:S(2)}, u32[]{:S(2)}) collective-permute-start(bf16[576,128]{1,0:T(8,128)(2,1)S(1)} %collective-permute-done.11.refs_5_), channel_id=1, source_target_pairs={{0,4},{4,0},{8,12},{12,8},{1,5},{5,1},{9,13},{13,9},{2,6},{6,2},{1... | collective-permute-start | bytes 442376 | tf_op jit(solution)/shard_map/ppermute | solution.py:212
  46.2 5.7 %collective-permute-start.8 = (bf16[576,128]{1,0:T(8,128)(2,1)S(1)}, bf16[576,128]{1,0:T(8,128)(2,1)S(1)}, u32[]{:S(2)}, u32[]{:S(2)}) collective-permute-start(bf16[576,128]{1,0:T(8,128)(2,1)S(1)} %collective-permute-done.7.refs_2_), channel_id=1, source_target_pairs={{0,1},{1,0},{2,3},{3,2},{4,5},{5,4},{6,7},{7,6},{8,9},{9,8},{10,11... | collective-permute-start | bytes 442376 | tf_op jit(solution)/shard_map/ppermute | solution.py:212

commit v8 on v7

--- a/solution.py
+++ b/solution.py
@@ -142,40 +142,46 @@
         sides(block, wide, row_l.at[s], row_r.at[s], outer, here, consts, table, weights)
 
 
-def columns_kernel(n, t, *refs):
-    blocks, (table, weights, row_l, row_r) = refs[: n - 1], refs[n - 1 : n + 3]
-    col_l, col_r, mixed, wide = refs[n + 5 :]
+def columns_kernel(t, count, *refs):
+    blocks, (table, weights) = refs[:count], refs[count : count + 2]
+    col_l, col_r, wide = refs[count + 4 :]
     r, c = lax.axis_index("row"), lax.axis_index("col")
     consts = constants(wide.shape[1])
     for s, block in enumerate(blocks, 1):
         outer, inner = mask_of(table, r ^ s, t), mask_of(table, c, t)
         sides(block, wide, col_l.at[s], col_r.at[s], outer, inner, consts, table, weights)
-    mix(mixed.at[0], None, row_l, col_r, 0, n - 1, lambda s: s, lambda s: r ^ c ^ s, t)
-    mix(mixed.at[1], None, col_l, row_r, 0, n - 1, lambda s: r ^ c ^ s, lambda s: s, t)
-
-
-def last_kernel(n, t, *refs):
-    block, table, weights, col_l, col_r, old, w_out, pair, gating, col_pair, col_gating = refs[:11]
-    pair_ref, left_ref, right_ref, mixed, wide, left, right = refs[11:]
+
+
+def mirror_kernel(n, t, *refs):
+    row, col, table, weights, pair, gating, w_out = refs[:7]
+    left_ref, row_l, row_r, col_l, col_r, mixed, wide = refs[11:]
     width = wide.shape[1]
     r, c = lax.axis_index("row"), lax.axis_index("col")
     consts = constants(width)
     here, there = mask_of(table, r, t), mask_of(table, c, t)
-    outer = mask_of(table, c ^ (n - 1), t)
-    sides(block, wide, left.at[0], right.at[0], outer, here, consts, table, weights)
-    source = r ^ c ^ (n - 1)
-    mix(mixed.at[0], old.at[0], left, col_r, 0, 1, lambda s: s, lambda s: source, t)
-    mix(mixed.at[1], old.at[1], col_l, right, 0, 1, lambda s: source, lambda s: s, t)
-    for k, (base, factor) in enumerate(((pair, gating), (col_pair, col_gating))):
-        updated = finish(base[...], mixed[k], factor[...], consts, *out_norm(table, 0), w_out[0], table[8:9])
-        normed = norm_pair(updated, consts, *in_norm(table, 1))
-        if k == 0:
-            pair_ref[...] = updated
-            side = gated(normed, weights[1, :, 2 * width : 4 * width], half_bias(table, 1, 2, 4), width)
-            right_ref[...] = masked(side, here, there)
-        else:
-            side = gated(normed, weights[1, :, : 2 * width], half_bias(table, 1, 0, 2), width)
-            left_ref[...] = masked(side, there, here)
+    for block, left, right, outer, inner in (
+        (row, row_l, row_r, c ^ (n - 1), here),
+        (col, col_l, col_r, r ^ (n - 1), there),
+    ):
+        outer = mask_of(table, outer, t)
+        sides(block, wide, left.at[n - 1], right.at[n - 1], outer, inner, consts, table, weights)
+    mix(mixed, None, col_l, row_r, 0, n, lambda s: r ^ c ^ s, lambda s: s, t)
+    updated = finish(pair[...], mixed[...], gating[...], consts, *out_norm(table, 0), w_out[0], table[8:9])
+    normed = norm_pair(updated, consts, *in_norm(table, 1))
+    side = gated(normed, weights[1, :, : 2 * width], half_bias(table, 1, 0, 2), width)
+    left_ref[...] = masked(side, there, here)
+
+
+def own_end_kernel(n, t, row_l, col_r, table, weights, pair, gating, w_out, pair_ref, right_ref, mixed):
+    width = mixed.shape[1]
+    r, c = lax.axis_index("row"), lax.axis_index("col")
+    consts = constants(width)
+    mix(mixed, None, row_l, col_r, 0, n, lambda s: s, lambda s: r ^ c ^ s, t)
+    updated = finish(pair[...], mixed[...], gating[...], consts, *out_norm(table, 0), w_out[0], table[8:9])
+    pair_ref[...] = updated
+    normed = norm_pair(updated, consts, *in_norm(table, 1))
+    side = gated(normed, weights[1, :, 2 * width : 4 * width], half_bias(table, 1, 2, 4), width)
+    right_ref[...] = masked(side, mask_of(table, r, t), mask_of(table, c, t))
 
 
 def gate_kernel(pair, table, weights, gating):
@@ -220,9 +226,7 @@
         t, _, width = pair.shape
         area = (t * t, width)
         narrow, broad = jax.ShapeDtypeStruct(area, BF16), jax.ShapeDtypeStruct(area, F32)
-        row_like = jax.ShapeDtypeStruct((n - 1,) + area, F32)
-        col_like = jax.ShapeDtypeStruct((n,) + area, F32)
-        twice = jax.ShapeDtypeStruct((2,) + area, F32)
+        slots = jax.ShapeDtypeStruct((n,) + area, F32)
         scratch = pltpu.VMEM(area, F32)
 
         def call(kernel, name, outs, scratches, *operands, alias=None, **specs):
@@ -244,18 +248,19 @@
         weights, row_l, row_r, gating = call(
             functools.partial(own_kernel, t),
             "own_sides",
-            (jax.ShapeDtypeStruct(w_in.shape, BF16), row_like, row_like, broad),
+            (jax.ShapeDtypeStruct(w_in.shape, BF16), slots, slots, broad),
             [scratch],
             pair,
             table,
             w_in,
         )
         after = lambda block: lax.optimization_barrier((block, row_l))[0]
-        rows, cols = gather(pair, "col", after), gather(after(col_pair), "row")
+        rows = gather(pair, "col", after)
+        cols = gather(lax.optimization_barrier((col_pair, rows[n // 2], row_l))[0], "row")
         row_l, row_r, col_l, col_r, col_gating = call(
             functools.partial(rows_kernel, t, n - 2),
             "row_sides",
-            (row_like, row_like, col_like, col_like, broad),
+            (slots, slots, slots, slots, broad),
             [scratch],
             *rows[1:-1],
             col_pair,
@@ -265,43 +270,56 @@
             row_r,
             alias={n + 1: 0, n + 2: 1},
         )
-        col_l, col_r, mixed = call(
-            functools.partial(columns_kernel, n, t),
+        col_l, col_r = call(
+            functools.partial(columns_kernel, t, n - 2),
             "column_sides",
-            (col_like, col_like, twice),
+            (slots, slots),
             [scratch],
-            *cols[1:],
+            *cols[1:-1],
             table,
             weights,
+            col_l,
+            col_r,
+            alias={n: 0, n + 1: 1},
+        )
+        left, row_l, _, _, col_r = call(
+            functools.partial(mirror_kernel, n, t),
+            "mirror_end",
+            (narrow, slots, slots, slots, slots),
+            [scratch] * 2,
+            rows[-1],
+            cols[-1],
+            table,
+            weights,
+            col_pair,
+            col_gating,
+            w_out,
             row_l,
             row_r,
             col_l,
             col_r,
-            alias={n + 3: 0, n + 4: 1},
-        )
-        pair, left, right = call(
-            functools.partial(last_kernel, n, t),
-            "last_slot",
-            (narrow,) * 3,
-            [pltpu.VMEM((2,) + area, F32), scratch] + [pltpu.VMEM((1,) + area, F32)] * 2,
-            rows[-1],
+            alias={7: 1, 8: 2, 9: 3, 10: 4},
+        )
+        pair, right = call(
+            functools.partial(own_end_kernel, n, t),
+            "own_end",
+            (narrow, narrow),
+            [scratch],
+            row_l,
+            col_r,
             table,
             weights,
-            col_l,
-            col_r,
-            mixed,
-            w_out,
             pair,
             gating,
-            col_pair,
-            col_gating,
-        )
-        lefts, rights = gather(left, "col"), gather(right, "row")
+            w_out,
+        )
+        lefts = gather(left, "col")
+        rights = [right] + [lax.ppermute(right, "row", [(k, k ^ s) for k in range(n)]) for s in range(1, n)]
         gating = call(gate_kernel, "gate", broad, [], pair, table, weights)
         rights, mixed = call(
             functools.partial(middle_kernel, n, t),
             "middle_slots",
-            (col_like, broad),
+            (slots, broad),
             [pltpu.VMEM((n - 1,) + area, F32)],
             *lefts[:-1],
             *rights,

time: 54 us -> 53.4 us (0.989)
  starting transfers between devices: 15.9 us -> 14.5 us
    ppermute x0 -> x3, waiting for transfers between devices: none -> 3.87 us  [per_device(): lax.ppermute(right, 'row', [(k, k ^ s) for k in range(n)])]
    ppermute x12 -> x9, waiting for transfers between devices: 16.8 us -> 13.4 us  [gather(): held[s ^ step] = lax.ppermute(part, axis, [(k, k ^ step) for k in range(n)])]
    ppermute x12 -> x9, starting transfers between devices: 14.4 us -> 11 us  [gather(): held[s ^ step] = lax.ppermute(part, axis, [(k, k ^ step) for k in range(n)])]
    ppermute x0 -> x3, starting transfers between devices: none -> 1.92 us  [per_device(): lax.ppermute(right, 'row', [(k, k ^ s) for k in range(n)])]
    pallas_call x7 -> x8, Pallas kernels: 16.1 us -> 16.5 us  [call(): pl.pallas_call(kernel, out_shape=outs, scratch_shapes=scratches, input_ou...]
    unnamed x6 -> x8, local copies, waits for them, and re-layouts: 1.88 us -> 1.89 us
  transfers between devices with their start and end apart: 13 -> 13, of which waited for: 7 -> 7; matrix products, arithmetic and copies ran while one was open for 5% -> 6% of each run, Pallas kernels for 20% -> 19%
where the time goes in v8:
time: 53.4 us; the launch traced here: 53.2 us
  waiting for transfers between devices  17.2 us (32%)
  Pallas kernels  16.5 us (31%)
  starting transfers between devices  14.5 us (27%)
  local copies, waits for them, and re-layouts  4.17 us (8%)
  other arithmetic  0.66 us (1%)
    pallas_call x8, Pallas kernels, call(): pl.pallas_call(kernel, out_shape=outs, scratch_shapes=scratches, input_ou...  16.5 us
    ppermute x9, waiting for transfers between devices, gather(): held[s ^ step] = lax.ppermute(part, axis, [(k, k ^ step) for k in range(n)])  13.4 us
    ppermute x9, starting transfers between devices, gather(): held[s ^ step] = lax.ppermute(part, axis, [(k, k ^ step) for k in range(n)])  11 us
    ppermute x3, waiting for transfers between devices, per_device(): lax.ppermute(right, 'row', [(k, k ^ s) for k in range(n)])  3.87 us
    ppermute x3, starting transfers between devices, per_device(): lax.ppermute(right, 'row', [(k, k ^ s) for k in range(n)])  1.92 us
    unnamed x8, local copies, waits for them, and re-layouts  1.89 us
    ppermute x1, starting transfers between devices, mirrored(): lax.ppermute(block, ('row', 'col'), [(a * n + z, z * n + a) for a in rang...  1.56 us
    concatenate x1, local copies, waits for them, and re-layouts, per_device(): jnp.concatenate(vectors + [jnp.zeros((TABLE_MASK - 20, width), F32), mask])  1.51 us
  transfers between devices with their start and end apart: 13, of which 7 were waited for; matrix products, arithmetic and copies ran while one was open for 6% of the time, Pallas kernels for 19%

profile of v8, /device:TPU:0, one launch (start us, length us, event | category | flops | bytes accessed | tf_op | source)
XLA Modules:
  0.0 53.2 jit_solution(14014718404082896530)
XLA Ops:
  0.0 1.6 %collective-permute-start.2 = (bf16[576,128]{1,0:T(8,128)(2,1)}, bf16[576,128]{1,0:T(8,128)(2,1)S(1)}, u32[]{:S(2)}, u32[]{:S(2)}) collective-permute-start(bf16[576,128]{1,0:T(8,128)(2,1)} %bitcast.2), channel_id=1, source_target_pairs={{0,0},{1,4},{2,8},{3,12},{4,1},{5,5},{6,9},{7,13},{8,2},{9,6},{10,... | collective-permute-start | bytes 442376 | tf_op jit(solution)/shard_map/ppermute | solution.py:223
  1.6 5.7 %collective-permute-start = (bf16[576,128]{1,0:T(8,128)(2,1)}, bf16[576,128]{1,0:T(8,128)(2,1)S(1)}, u32[]{:S(2)}, u32[]{:S(2)}) collective-permute-start(bf16[576,128]{1,0:T(8,128)(2,1)} %bitcast.3), channel_id=1, source_target_pairs={{0,2},{1,3},{2,0},{3,1},{4,6},{5,7},{6,4},{7,5},{8,10},{9,11},{10,... | collective-permute-start | bytes 442376 | tf_op jit(solution)/shard_map/ppermute | solution.py:218
  7.3 0.7 %convert_element_type.3 = f32[96]{0:T(128)S(1)} convert(s32[96]{0:T(128)} %param.11) | non-fusion elementwise | flops 96 | bytes 768 | tf_op jit(solution)/shard_map/convert_element_type | solution.py:245
  7.9 0.7 %reshape.11 = f32[10,128]{1,0:T(8,128)S(1)} reshape(f32[2,640]{1,0:T(2,128)} %param.15) | data formatting | bytes 10240 | tf_op jit(solution)/shard_map/reshape | solution.py:246
  8.6 0.1 broadcast_in_dim.10
  8.7 1.5 %concatenate.3.table.refs_3_.refs_2_ = f32[120,128]{1,0:T(8,128)S(1)} concatenate(f32[2,128]{1,0:T(2,128)} %param.12, f32[2,128]{1,0:T(2,128)} %param.13, f32[2,128]{1,0:T(2,128)} %param.16, f32[2,128]{1,0:T(2,128)} %param.17, f32[2,128]{1,0:T(2,128)} %param.19, f32[10,128]{1,0:T(8,128)S(1)} %reshape.11, f32[4,128]{1,0:T(4,128)S(1)} %broadcast_in_dim.4, ...), dimensions={0} | concatenate | bytes 122880 | tf_op jit(solution)/shard_map/concatenate | solution.py:247
  10.2 0.0 copy-start.1
  10.2 0.9 %copy-done.1 = bf16[24,24,128]{2,1,0:T(8,128)(2,1)S(1)} copy-done((bf16[24,24,128]{2,1,0:T(8,128)(2,1)S(1)}, bf16[24,24,128]{2,1,0:T(8,128)(2,1)}, u32[]{:S(2)}) %copy-start.1) | copy-done | bytes 147480
  11.1 0.0 copy-start.3
  11.1 1.0 %copy-done.3 = bf16[2,128,640]{2,1,0:T(8,128)(2,1)S(1)} copy-done((bf16[2,128,640]{2,1,0:T(8,128)(2,1)S(1)}, bf16[2,128,640]{2,1,0:T(8,128)(2,1)}, u32[]{:S(2)}) %copy-start.3) | copy-done | bytes 327704
  12.1 1.0 %own_sides.1 = (bf16[2,128,640]{2,1,0:T(8,128)(2,1)S(1)}, f32[4,576,128]{2,1,0:T(8,128)S(1)}, f32[4,576,128]{2,1,0:T(8,128)S(1)}, f32[576,128]{1,0:T(8,128)S(1)}) custom-call(bf16[576,128]{1,0:T(8,128)(2,1)S(1)} %bitcast.4, f32[120,128]{1,0:T(8,128)S(1)} %concatenate.3.table.refs_3_.refs_2_, bf16[2,128,640]{2,1,0:T(8,128)(2,1)S(1)} %copy-done.3), custom_call_target="tpu_custom_call" | custom-call | tf_op jit(solution)/shard_map/own_sides/pallas_call | solution.py:233
  13.1 0.0 collective-permute-done.2.refs_2_.refs_4_
  13.1 8.0 %collective-permute-done.refs_1_ = bf16[576,128]{1,0:T(8,128)(2,1)S(1)} collective-permute-done((bf16[576,128]{1,0:T(8,128)(2,1)}, bf16[576,128]{1,0:T(8,128)(2,1)S(1)}, u32[]{:S(2)}, u32[]{:S(2)}) %collective-permute-start) | collective-permute-done | bytes 147488 | tf_op jit(solution)/shard_map/ppermute | solution.py:218
  21.1 0.0 collective-permute-start.3
  21.1 0.0 collective-permute-start.5
  21.1 0.0 collective-permute-start.6
  21.1 2.0 %collective-permute-start.1 = (bf16[576,128]{1,0:T(8,128)(2,1)S(1)}, bf16[576,128]{1,0:T(8,128)(2,1)S(1)}, u32[]{:S(2)}, u32[]{:S(2)}) collective-permute-start(bf16[576,128]{1,0:T(8,128)(2,1)S(1)} %collective-permute-done.refs_1_), channel_id=1, source_target_pairs={{0,1},{1,0},{2,3},{3,2},{4,5},{5,4},{6,7},{7,6},{8,9},{9,8},{10,11... | collective-permute-start | bytes 442376 | tf_op jit(solution)/shard_map/ppermute | solution.py:218
  23.1 3.5 %collective-permute-done.3.refs_1_ = bf16[576,128]{1,0:T(8,128)(2,1)S(1)} collective-permute-done((bf16[576,128]{1,0:T(8,128)(2,1)S(1)}, bf16[576,128]{1,0:T(8,128)(2,1)S(1)}, u32[]{:S(2)}, u32[]{:S(2)}) %collective-permute-start.3) | collective-permute-done | bytes 147488 | tf_op jit(solution)/shard_map/ppermute | solution.py:218
  26.6 0.0 collective-permute-start.4
  26.6 1.2 %collective-permute-done.5.refs_0_ = bf16[576,128]{1,0:T(8,128)(2,1)S(1)} collective-permute-done((bf16[576,128]{1,0:T(8,128)(2,1)S(1)}, bf16[576,128]{1,0:T(8,128)(2,1)S(1)}, u32[]{:S(2)}, u32[]{:S(2)}) %collective-permute-start.5) | collective-permute-done | bytes 147488 | tf_op jit(solution)/shard_map/ppermute | solution.py:218
  27.9 1.8 %row_sides.1 = (f32[4,576,128]{2,1,0:T(8,128)S(1)}, f32[4,576,128]{2,1,0:T(8,128)S(1)}, f32[4,576,128]{2,1,0:T(8,128)S(1)}, f32[4,576,128]{2,1,0:T(8,128)S(1)}, f32[576,128]{1,0:T(8,128)S(1)}) custom-call(bf16[576,128]{1,0:T(8,128)(2,1)S(1)} %collective-permute-done.5.refs_0_, ...), custom_call_target="tpu_custom_call", output_to_operand_aliasing={{0}: (5, {}), {1}: (6, {})} | custom-call | tf_op jit(solution)/shard_map/row_sides/pallas_call | solution.py:233
  29.7 0.0 collective-permute-done.6.refs_0_
  29.7 0.0 copy-start
  29.7 1.0 %column_sides.1 = (f32[4,576,128]{2,1,0:T(8,128)S(1)}, f32[4,576,128]{2,1,0:T(8,128)S(1)}) custom-call(bf16[576,128]{1,0:T(8,128)(2,1)S(1)} %collective-permute-done.6.refs_0_, bf16[576,128]{1,0:T(8,128)(2,1)S(1)} %collective-permute-done.3.refs_1_, f32[120,128]{1,0:T(8,128)S(1)} %concatenate.3.table.refs_3_.refs_2_, ...), custom_call_target="tpu_custom_call", output_to_operand_aliasing={{0}: (4, {}), {1}: (5, {})} | custom-call | tf_op jit(solution)/shard_map/column_sides/pallas_call | solution.py:233
  30.7 0.0 collective-permute-done.1.refs_0_
  30.8 0.0 collective-permute-done.4.refs_1_
  30.8 0.0 copy-done
  30.8 0.0 copy-start.2
  30.8 4.6 %mirror_end.1 = (bf16[576,128]{1,0:T(8,128)(2,1)S(1)}, f32[4,576,128]{2,1,0:T(8,128)S(1)}, f32[4,576,128]{2,1,0:T(8,128)S(1)}, f32[4,576,128]{2,1,0:T(8,128)S(1)}, f32[4,576,128]{2,1,0:T(8,128)S(1)}) custom-call(bf16[576,128]{1,0:T(8,128)(2,1)S(1)} %collective-permute-done.1.refs_0_, ...), custom_call_target="tpu_custom_call", output_to_operand_aliasing={{1}: (7, {}), {2}: (8, {}), {3}: (9, {}), {4}: (10, {})} | custom-call | tf_op jit(solution)/shard_map/mirror_end/pallas_call | solution.py:233
  35.4 1.2 %collective-permute-start.7 = (bf16[576,128]{1,0:T(8,128)(2,1)S(1)}, bf16[576,128]{1,0:T(8,128)(2,1)S(1)}, u32[]{:S(2)}, u32[]{:S(2)}) collective-permute-start(bf16[576,128]{1,0:T(8,128)(2,1)S(1)} %get-tuple-element.37.refs_0_), channel_id=1, source_target_pairs={{0,2},{1,3},{2,0},{3,1},{4,6},{5,7},{6,4},{7,5},{8,10},{9,11},{10,... | collective-permute-start | bytes 442376 | tf_op jit(solution)/shard_map/ppermute | solution.py:218
  36.6 0.0 copy-done.2
  36.6 3.6 %own_end.1 = (bf16[576,128]{1,0:T(8,128)(2,1)S(1)}, bf16[576,128]{1,0:T(8,128)(2,1)S(1)}) custom-call(f32[4,576,128]{2,1,0:T(8,128)S(1)} %get-tuple-element.38.row_l, f32[4,576,128]{2,1,0:T(8,128)S(1)} %get-tuple-element.39.col_r, f32[120,128]{1,0:T(8,128)S(1)} %concatenate.3.table.refs_3_.refs_2_, ...), custom_call_target="tpu_custom_call" | custom-call | tf_op jit(solution)/shard_map/own_end/pallas_call | solution.py:233
  40.1 0.1 collective-permute-start.12
  40.2 1.0 %collective-permute-start.11 = (bf16[576,128]{1,0:T(8,128)(2,1)S(1)}, bf16[576,128]{1,0:T(8,128)(2,1)S(1)}, u32[]{:S(2)}, u32[]{:S(2)}) collective-permute-start(bf16[576,128]{1,0:T(8,128)(2,1)S(1)} %get-tuple-element.41.refs_3_), channel_id=1, source_target_pairs={{0,8},{4,12},{8,0},{12,4},{1,9},{5,13},{9,1},{13,5},{2,10},{6,14},... | collective-permute-start | bytes 442376 | tf_op jit(solution)/shard_map/ppermute | solution.py:317
  41.2 0.8 %collective-permute-start.10 = (bf16[576,128]{1,0:T(8,128)(2,1)S(1)}, bf16[576,128]{1,0:T(8,128)(2,1)S(1)}, u32[]{:S(2)}, u32[]{:S(2)}) collective-permute-start(bf16[576,128]{1,0:T(8,128)(2,1)S(1)} %get-tuple-element.41.refs_3_), channel_id=1, source_target_pairs={{0,4},{4,0},{8,12},{12,8},{1,5},{5,1},{9,13},{13,9},{2,6},{6,2},{1... | collective-permute-start | bytes 442376 | tf_op jit(solution)/shard_map/ppermute | solution.py:317
  42.1 2.1 %collective-permute-start.9 = (bf16[576,128]{1,0:T(8,128)(2,1)S(1)}, bf16[576,128]{1,0:T(8,128)(2,1)S(1)}, u32[]{:S(2)}, u32[]{:S(2)}) collective-permute-start(bf16[576,128]{1,0:T(8,128)(2,1)S(1)} %get-tuple-element.37.refs_0_), channel_id=1, source_target_pairs={{0,1},{1,0},{2,3},{3,2},{4,5},{5,4},{6,7},{7,6},{8,9},{9,8},{10,11... | collective-permute-start | bytes 442376 | tf_op jit(solution)/shard_map/ppermute | solution.py:218
  44.1 0.0 collective-permute-done.7.refs_2_
  44.1 0.0 collective-permute-start.8
  44.2 0.5 %gate.1.gating = f32[576,128]{1,0:T(8,128)S(1)} custom-call(bf16[576,128]{1,0:T(8,128)(2,1)S(1)} %get-tuple-element.44.pair, f32[120,128]{1,0:T(8,128)S(1)} %concatenate.3.table.refs_3_.refs_2_, bf16[2,128,640]{2,1,0:T(8,128)(2,1)S(1)} %get-tuple-element.28.refs_4_.refs_3_.weights), custom_call_target="tpu_custom_call" | custom-call | tf_op jit(solution)/shard_map/gate/pallas_call | solution.py:233
  44.7 1.6 %collective-permute-done.12.refs_6_ = bf16[576,128]{1,0:T(8,128)(2,1)S(1)} collective-permute-done((bf16[576,128]{1,0:T(8,128)(2,1)S(1)}, bf16[576,128]{1,0:T(8,128)(2,1)S(1)}, u32[]{:S(2)}, u32[]{:S(2)}) %collective-permute-start.12) | collective-permute-done | bytes 147488 | tf_op jit(solution)/shard_map/ppermute | solution.py:317
  46.3 2.3 %collective-permute-done.11.refs_5_ = bf16[576,128]{1,0:T(8,128)(2,1)S(1)} collective-permute-done((bf16[576,128]{1,0:T(8,128)(2,1)S(1)}, bf16[576,128]{1,0:T(8,128)(2,1)S(1)}, u32[]{:S(2)}, u32[]{:S(2)}) %collective-permute-start.11) | collective-permute-done | bytes 147488 | tf_op jit(solution)/shard_map/ppermute | solution.py:317
  48.6 0.0 collective-permute-done.10.refs_4_
  48.6 0.2 collective-permute-done.9.refs_1_
  48.8 2.1 %middle_slots.1 = (f32[4,576,128]{2,1,0:T(8,128)S(1)}, f32[576,128]{1,0:T(8,128)S(1)}) custom-call(bf16[576,128]{1,0:T(8,128)(2,1)S(1)} %get-tuple-element.37.refs_0_, bf16[576,128]{1,0:T(8,128)(2,1)S(1)} %collective-permute-done.9.refs_1_, bf16[576,128]{1,0:T(8,128)(2,1)S(1)} %collective-permute-done.7.refs_2_, ...), custom_call_target="tpu_custom_call" | custom-call | tf_op jit(solution)/shard_map/middle_slots/pallas_call | solution.py:233
  50.9 0.4 collective-permute-done.8.block
  51.3 1.9 %end.1 = bf16[576,128]{1,0:T(8,128)(2,1)} custom-call(bf16[576,128]{1,0:T(8,128)(2,1)S(1)} %collective-permute-done.8.block, f32[4,576,128]{2,1,0:T(8,128)S(1)} %get-tuple-element.42.rights, f32[576,128]{1,0:T(8,128)S(1)} %get-tuple-element.43.old, bf16[576,128]{1,0:T(8,128)(2,1)S(1)} %get-tuple-element.44.pair, f32[576,128]{1,0:T(8,128)S(1)} %gate.1.gating, ...), custom_call_target="tpu_custom_call" | custom-call | tf_op jit(solution)/shard_map/end/pallas_call | solution.py:233
  (1 shorter events, 0.0 us)
Async XLA Ops:
  0.0 13.1 %collective-permute-start.2 = (bf16[576,128]{1,0:T(8,128)(2,1)}, bf16[576,128]{1,0:T(8,128)(2,1)S(1)}, u32[]{:S(2)}, u32[]{:S(2)}) collective-permute-start(bf16[576,128]{1,0:T(8,128)(2,1)} %bitcast.2), channel_id=1, source_target_pairs={{0,0},{1,4},{2,8},{3,12},{4,1},{5,5},{6,9},{7,13},{8,2},{9,6},{10,... | collective-permute-start | bytes 442376 | tf_op jit(solution)/shard_map/ppermute | solution.py:223
  1.6 19.6 %collective-permute-start = (bf16[576,128]{1,0:T(8,128)(2,1)}, bf16[576,128]{1,0:T(8,128)(2,1)S(1)}, u32[]{:S(2)}, u32[]{:S(2)}) collective-permute-start(bf16[576,128]{1,0:T(8,128)(2,1)} %bitcast.3), channel_id=1, source_target_pairs={{0,2},{1,3},{2,0},{3,1},{4,6},{5,7},{6,4},{7,5},{8,10},{9,11},{10,... | collective-permute-start | bytes 442376 | tf_op jit(solution)/shard_map/ppermute | solution.py:218
  10.2 0.9 %copy-start.1 = (bf16[24,24,128]{2,1,0:T(8,128)(2,1)S(1)}, bf16[24,24,128]{2,1,0:T(8,128)(2,1)}, u32[]{:S(2)}) copy-start(bf16[24,24,128]{2,1,0:T(8,128)(2,1)} %param.10) | copy-start | bytes 442372
  11.1 1.0 %copy-start.3 = (bf16[2,128,640]{2,1,0:T(8,128)(2,1)S(1)}, bf16[2,128,640]{2,1,0:T(8,128)(2,1)}, u32[]{:S(2)}) copy-start(bf16[2,128,640]{2,1,0:T(8,128)(2,1)} %w_in.1) | copy-start | bytes 983044
  21.1 5.5 %collective-permute-start.3 = (bf16[576,128]{1,0:T(8,128)(2,1)S(1)}, bf16[576,128]{1,0:T(8,128)(2,1)S(1)}, u32[]{:S(2)}, u32[]{:S(2)}) collective-permute-start(bf16[576,128]{1,0:T(8,128)(2,1)S(1)} %collective-permute-done.2.refs_2_.refs_4_), channel_id=1, source_target_pairs={{0,8},{4,12},{8,0},{12,4},{1,9},{5,13},{9,1},{13,5},{2,10},{6,14},... | collective-permute-start | bytes 442376 | tf_op jit(solution)/shard_map/ppermute | solution.py:218
  21.1 6.7 %collective-permute-start.5 = (bf16[576,128]{1,0:T(8,128)(2,1)S(1)}, bf16[576,128]{1,0:T(8,128)(2,1)S(1)}, u32[]{:S(2)}, u32[]{:S(2)}) collective-permute-start(bf16[576,128]{1,0:T(8,128)(2,1)S(1)} %bitcast.5), channel_id=1, source_target_pairs={{0,1},{1,0},{2,3},{3,2},{4,5},{5,4},{6,7},{7,6},{8,9},{9,8},{10,11... | collective-permute-start | bytes 442376 | tf_op jit(solution)/shard_map/ppermute | solution.py:218
  21.1 8.6 %collective-permute-start.6 = (bf16[576,128]{1,0:T(8,128)(2,1)S(1)}, bf16[576,128]{1,0:T(8,128)(2,1)S(1)}, u32[]{:S(2)}, u32[]{:S(2)}) collective-permute-start(bf16[576,128]{1,0:T(8,128)(2,1)S(1)} %collective-permute-done.2.refs_2_.refs_4_), channel_id=1, source_target_pairs={{0,4},{4,0},{8,12},{12,8},{1,5},{5,1},{9,13},{13,9},{2,6},{6,2},{1... | collective-permute-start | bytes 442376 | tf_op jit(solution)/shard_map/ppermute | solution.py:218
  21.1 9.6 %collective-permute-start.1 = (bf16[576,128]{1,0:T(8,128)(2,1)S(1)}, bf16[576,128]{1,0:T(8,128)(2,1)S(1)}, u32[]{:S(2)}, u32[]{:S(2)}) collective-permute-start(bf16[576,128]{1,0:T(8,128)(2,1)S(1)} %collective-permute-done.refs_1_), channel_id=1, source_target_pairs={{0,1},{1,0},{2,3},{3,2},{4,5},{5,4},{6,7},{7,6},{8,9},{9,8},{10,11... | collective-permute-start | bytes 442376 | tf_op jit(solution)/shard_map/ppermute | solution.py:218
  26.6 4.1 %collective-permute-start.4 = (bf16[576,128]{1,0:T(8,128)(2,1)S(1)}, bf16[576,128]{1,0:T(8,128)(2,1)S(1)}, u32[]{:S(2)}, u32[]{:S(2)}) collective-permute-start(bf16[576,128]{1,0:T(8,128)(2,1)S(1)} %collective-permute-done.3.refs_1_), channel_id=1, source_target_pairs={{0,4},{4,0},{8,12},{12,8},{1,5},{5,1},{9,13},{13,9},{2,6},{6,2},{1... | collective-permute-start | bytes 442376 | tf_op jit(solution)/shard_map/ppermute | solution.py:218
  29.7 1.1 %copy-start = (bf16[2,128,128]{2,1,0:T(8,128)(2,1)S(1)}, bf16[2,128,128]{2,1,0:T(8,128)(2,1)}, u32[]{:S(2)}) copy-start(bf16[2,128,128]{2,1,0:T(8,128)(2,1)} %w_out.3) | copy-start | bytes 196612
  30.8 5.8 %copy-start.2 = (bf16[24,24,128]{2,1,0:T(8,128)(2,1)S(1)}, bf16[24,24,128]{2,1,0:T(8,128)(2,1)}, u32[]{:S(2)}) copy-start(bf16[24,24,128]{2,1,0:T(8,128)(2,1)} %param.10) | copy-start | bytes 442372
  35.4 8.8 %collective-permute-start.7 = (bf16[576,128]{1,0:T(8,128)(2,1)S(1)}, bf16[576,128]{1,0:T(8,128)(2,1)S(1)}, u32[]{:S(2)}, u32[]{:S(2)}) collective-permute-start(bf16[576,128]{1,0:T(8,128)(2,1)S(1)} %get-tuple-element.37.refs_0_), channel_id=1, source_target_pairs={{0,2},{1,3},{2,0},{3,1},{4,6},{5,7},{6,4},{7,5},{8,10},{9,11},{10,... | collective-permute-start | bytes 442376 | tf_op jit(solution)/shard_map/ppermute | solution.py:218
  40.1 6.1 %collective-permute-start.12 = (bf16[576,128]{1,0:T(8,128)(2,1)S(1)}, bf16[576,128]{1,0:T(8,128)(2,1)S(1)}, u32[]{:S(2)}, u32[]{:S(2)}) collective-permute-start(bf16[576,128]{1,0:T(8,128)(2,1)S(1)} %get-tuple-element.41.refs_3_), channel_id=1, source_target_pairs={{0,12},{4,8},{8,4},{12,0},{1,13},{5,9},{9,5},{13,1},{2,14},{6,10},... | collective-permute-start | bytes 442376 | tf_op jit(solution)/shard_map/ppermute | solution.py:317
  40.2 8.4 %collective-permute-start.11 = (bf16[576,128]{1,0:T(8,128)(2,1)S(1)}, bf16[576,128]{1,0:T(8,128)(2,1)S(1)}, u32[]{:S(2)}, u32[]{:S(2)}) collective-permute-start(bf16[576,128]{1,0:T(8,128)(2,1)S(1)} %get-tuple-element.41.refs_3_), channel_id=1, source_target_pairs={{0,8},{4,12},{8,0},{12,4},{1,9},{5,13},{9,1},{13,5},{2,10},{6,14},... | collective-permute-start | bytes 442376 | tf_op jit(solution)/shard_map/ppermute | solution.py:317
  41.2 7.4 %collective-permute-start.10 = (bf16[576,128]{1,0:T(8,128)(2,1)S(1)}, bf16[576,128]{1,0:T(8,128)(2,1)S(1)}, u32[]{:S(2)}, u32[]{:S(2)}) collective-permute-start(bf16[576,128]{1,0:T(8,128)(2,1)S(1)} %get-tuple-element.41.refs_3_), channel_id=1, source_target_pairs={{0,4},{4,0},{8,12},{12,8},{1,5},{5,1},{9,13},{13,9},{2,6},{6,2},{1... | collective-permute-start | bytes 442376 | tf_op jit(solution)/shard_map/ppermute | solution.py:317
  42.1 6.7 %collective-permute-start.9 = (bf16[576,128]{1,0:T(8,128)(2,1)S(1)}, bf16[576,128]{1,0:T(8,128)(2,1)S(1)}, u32[]{:S(2)}, u32[]{:S(2)}) collective-permute-start(bf16[576,128]{1,0:T(8,128)(2,1)S(1)} %get-tuple-element.37.refs_0_), channel_id=1, source_target_pairs={{0,1},{1,0},{2,3},{3,2},{4,5},{5,4},{6,7},{7,6},{8,9},{9,8},{10,11... | collective-permute-start | bytes 442376 | tf_op jit(solution)/shard_map/ppermute | solution.py:218
  44.1 7.2 %collective-permute-start.8 = (bf16[576,128]{1,0:T(8,128)(2,1)S(1)}, bf16[576,128]{1,0:T(8,128)(2,1)S(1)}, u32[]{:S(2)}, u32[]{:S(2)}) collective-permute-start(bf16[576,128]{1,0:T(8,128)(2,1)S(1)} %collective-permute-done.7.refs_2_), channel_id=1, source_target_pairs={{0,1},{1,0},{2,3},{3,2},{4,5},{5,4},{6,7},{7,6},{8,9},{9,8},{10,11... | collective-permute-start | bytes 442376 | tf_op jit(solution)/shard_map/ppermute | solution.py:218

commit v9 on v8

--- a/solution.py
+++ b/solution.py
@@ -120,6 +120,14 @@
     return gate(normed, weights[u, :, 4 * values.shape[1] :], half_bias(table, u, 4, 5))
 
 
+def place(b, n):
+    return b // 2 + lax.rem(b, 2) * (n // 2)
+
+
+def placed_at(r, n):
+    return lax.rem(r, n // 2) * 2 + r // (n // 2)
+
+
 def own_kernel(t, pair, table, w_in, weights, row_l, row_r, gating, wide):
     r, c = lax.axis_index("row"), lax.axis_index("col")
     consts = constants(wide.shape[1])
@@ -130,13 +138,13 @@
 
 
 def rows_kernel(t, count, *refs):
-    blocks, (col_pair, table, weights) = refs[:count], refs[count : count + 3]
-    row_l, row_r, col_l, col_r, col_gating, wide = refs[count + 5 :]
+    blocks, (col_block, table, weights) = refs[:count], refs[count : count + 3]
+    row_l, row_r, col_l, col_r, wide = refs[count + 5 :]
     r, c = lax.axis_index("row"), lax.axis_index("col")
     consts = constants(wide.shape[1])
     here, there = mask_of(table, r, t), mask_of(table, c, t)
-    sides(col_pair, wide, col_l.at[0], col_r.at[0], here, there, consts, table, weights)
-    col_gating[...] = gate_of(col_pair[...], consts, table, weights, 0)
+    outer = mask_of(table, placed_at(r, count + 2), t)
+    sides(col_block, wide, col_l.at[0], col_r.at[0], outer, there, consts, table, weights)
     for s, block in enumerate(blocks, 1):
         outer = mask_of(table, c ^ s, t)
         sides(block, wide, row_l.at[s], row_r.at[s], outer, here, consts, table, weights)
@@ -148,25 +156,28 @@
     r, c = lax.axis_index("row"), lax.axis_index("col")
     consts = constants(wide.shape[1])
     for s, block in enumerate(blocks, 1):
-        outer, inner = mask_of(table, r ^ s, t), mask_of(table, c, t)
+        outer, inner = mask_of(table, placed_at(r ^ s, count + 2), t), mask_of(table, c, t)
         sides(block, wide, col_l.at[s], col_r.at[s], outer, inner, consts, table, weights)
 
 
 def mirror_kernel(n, t, *refs):
-    row, col, table, weights, pair, gating, w_out = refs[:7]
-    left_ref, row_l, row_r, col_l, col_r, mixed, wide = refs[11:]
+    row, cols, (table, weights, w_out) = refs[0], refs[1 : n + 1], refs[n + 1 : n + 4]
+    left_ref, row_l, row_r, col_l, col_r, mixed, wide, held = refs[n + 8 :]
     width = wide.shape[1]
     r, c = lax.axis_index("row"), lax.axis_index("col")
     consts = constants(width)
     here, there = mask_of(table, r, t), mask_of(table, c, t)
     for block, left, right, outer, inner in (
         (row, row_l, row_r, c ^ (n - 1), here),
-        (col, col_l, col_r, r ^ (n - 1), there),
+        (cols[-1], col_l, col_r, placed_at(r ^ (n - 1), n), there),
     ):
         outer = mask_of(table, outer, t)
         sides(block, wide, left.at[n - 1], right.at[n - 1], outer, inner, consts, table, weights)
-    mix(mixed, None, col_l, row_r, 0, n, lambda s: r ^ c ^ s, lambda s: s, t)
-    updated = finish(pair[...], mixed[...], gating[...], consts, *out_norm(table, 0), w_out[0], table[8:9])
+    mix(mixed, None, col_l, row_r, 0, n, lambda s: r ^ place(c ^ s, n), lambda s: s, t)
+    for s in range(n):
+        held[s] = cols[s][...]
+    pair = held[r ^ place(r, n)]
+    updated = finish(pair, mixed[...], gate_of(pair, consts, table, weights, 0), consts, *out_norm(table, 0), w_out[0], table[8:9])
     normed = norm_pair(updated, consts, *in_norm(table, 1))
     side = gated(normed, weights[1, :, : 2 * width], half_bias(table, 1, 0, 2), width)
     left_ref[...] = masked(side, there, here)
@@ -176,7 +187,7 @@
     width = mixed.shape[1]
     r, c = lax.axis_index("row"), lax.axis_index("col")
     consts = constants(width)
-    mix(mixed, None, row_l, col_r, 0, n, lambda s: s, lambda s: r ^ c ^ s, t)
+    mix(mixed, None, row_l, col_r, 0, n, lambda s: s, lambda s: r ^ place(c ^ s, n), t)
     updated = finish(pair[...], mixed[...], gating[...], consts, *out_norm(table, 0), w_out[0], table[8:9])
     pair_ref[...] = updated
     normed = norm_pair(updated, consts, *in_norm(table, 1))
@@ -220,7 +231,8 @@
         return [held[s] for s in range(n)]
 
     def mirrored(block):
-        return lax.ppermute(block, ("row", "col"), [(a * n + z, z * n + a) for a in range(n) for z in range(n)])
+        pairs = [(a * n + z, (z // 2 + z % 2 * (n // 2)) * n + a) for a in range(n) for z in range(n)]
+        return lax.ppermute(block, ("row", "col"), pairs)
 
     def per_device(pair, token_mask, in_gain, in_shift, w_in, bias_in, out_gain, out_shift, w_out, bias_out):
         t, _, width = pair.shape
@@ -241,7 +253,7 @@
             )(*operands)
 
         pair = pair.reshape(area)
-        col_pair = mirrored(pair)
+        col_block = mirrored(pair)
         mask = jnp.broadcast_to(token_mask.astype(F32)[:, None], (n * t, width))
         vectors = [in_gain, in_shift, out_gain, out_shift, bias_out, bias_in.reshape(-1, width)]
         table = jnp.concatenate(vectors + [jnp.zeros((TABLE_MASK - 20, width), F32), mask])
@@ -256,14 +268,14 @@
         )
         after = lambda block: lax.optimization_barrier((block, row_l))[0]
         rows = gather(pair, "col", after)
-        cols = gather(lax.optimization_barrier((col_pair, rows[n // 2], row_l))[0], "row")
-        row_l, row_r, col_l, col_r, col_gating = call(
+        cols = gather(lax.optimization_barrier((col_block, rows[1], rows[n // 2], row_l))[0], "row")
+        row_l, row_r, col_l, col_r = call(
             functools.partial(rows_kernel, t, n - 2),
             "row_sides",
-            (slots, slots, slots, slots, broad),
+            (slots,) * 4,
             [scratch],
             *rows[1:-1],
-            col_pair,
+            col_block,
             table,
             weights,
             row_l,
@@ -286,19 +298,17 @@
             functools.partial(mirror_kernel, n, t),
             "mirror_end",
             (narrow, slots, slots, slots, slots),
-            [scratch] * 2,
+            [scratch] * 2 + [pltpu.VMEM((n,) + area, BF16)],
             rows[-1],
-            cols[-1],
+            *cols,
             table,
             weights,
-            col_pair,
-            col_gating,
             w_out,
             row_l,
             row_r,
             col_l,
             col_r,
-            alias={7: 1, 8: 2, 9: 3, 10: 4},
+            alias={n + 4: 1, n + 5: 2, n + 6: 3, n + 7: 4},
         )
         pair, right = call(
             functools.partial(own_end_kernel, n, t),
@@ -314,6 +324,7 @@
             w_out,
         )
         lefts = gather(left, "col")
+        right = lax.optimization_barrier((right, lefts[1]))[0]
         rights = [right] + [lax.ppermute(right, "row", [(k, k ^ s) for k in range(n)]) for s in range(1, n)]
         gating = call(gate_kernel, "gate", broad, [], pair, table, weights)
         rights, mixed = call(

time: 53.4 us -> 56.1 us (1.051)
  starting transfers between devices: 14.5 us -> 16 us
  waiting for transfers between devices: 17.2 us -> 18.3 us
    ppermute x3, waiting for transfers between devices: 3.87 us -> 6.23 us  [per_device(): lax.ppermute(right, 'row', [(k, k ^ s) for k in range(n)])]
    ppermute x9, starting transfers between devices: 11 us -> 12.6 us  [gather(): held[s ^ step] = lax.ppermute(part, axis, [(k, k ^ step) for k in range(n)])]
    ppermute x9, waiting for transfers between devices: 13.4 us -> 12 us  [gather(): held[s ^ step] = lax.ppermute(part, axis, [(k, k ^ step) for k in range(n)])]
  transfers between devices with their start and end apart: 13 -> 13, of which waited for: 7 -> 6; matrix products, arithmetic and copies ran while one was open for 6% -> 5% of each run, Pallas kernels for 19% -> 17%
where the time goes in v9:
time: 56.1 us; the launch traced here: 55.9 us
  waiting for transfers between devices  18.3 us (33%)
  Pallas kernels  16.6 us (30%)
  starting transfers between devices  16 us (29%)
  local copies, waits for them, and re-layouts  4.17 us (7%)
  other arithmetic  0.66 us (1%)
    pallas_call x8, Pallas kernels, call(): pl.pallas_call(kernel, out_shape=outs, scratch_shapes=scratches, input_ou...  16.6 us
    ppermute x9, starting transfers between devices, gather(): held[s ^ step] = lax.ppermute(part, axis, [(k, k ^ step) for k in range(n)])  12.6 us
    ppermute x9, waiting for transfers between devices, gather(): held[s ^ step] = lax.ppermute(part, axis, [(k, k ^ step) for k in range(n)])  12 us
    ppermute x3, waiting for transfers between devices, per_device(): lax.ppermute(right, 'row', [(k, k ^ s) for k in range(n)])  6.23 us
    unnamed x8, local copies, waits for them, and re-layouts  1.89 us
    ppermute x3, starting transfers between devices, per_device(): lax.ppermute(right, 'row', [(k, k ^ s) for k in range(n)])  1.86 us
    ppermute x1, starting transfers between devices, mirrored(): return lax.ppermute(block, ('row', 'col'), pairs)  1.56 us
    concatenate x1, local copies, waits for them, and re-layouts, per_device(): jnp.concatenate(vectors + [jnp.zeros((TABLE_MASK - 20, width), F32), mask])  1.51 us
  transfers between devices with their start and end apart: 13, of which 6 were waited for; matrix products, arithmetic and copies ran while one was open for 5% of the time, Pallas kernels for 17%

profile of v9, /device:TPU:0, one launch (start us, length us, event | category | flops | bytes accessed | tf_op | source)
XLA Modules:
  0.0 55.9 jit_solution(9843346993420373912)
XLA Ops:
  0.0 3.0 %collective-permute-start.3 = (bf16[576,128]{1,0:T(8,128)(2,1)}, bf16[576,128]{1,0:T(8,128)(2,1)S(1)}, u32[]{:S(2)}, u32[]{:S(2)}) collective-permute-start(bf16[576,128]{1,0:T(8,128)(2,1)} %bitcast.2), channel_id=1, source_target_pairs={{0,1},{1,0},{2,3},{3,2},{4,5},{5,4},{6,7},{7,6},{8,9},{9,8},{10,11... | collective-permute-start | bytes 442376 | tf_op jit(solution)/shard_map/ppermute | solution.py:229
  3.0 1.6 %collective-permute-start.2 = (bf16[576,128]{1,0:T(8,128)(2,1)}, bf16[576,128]{1,0:T(8,128)(2,1)S(1)}, u32[]{:S(2)}, u32[]{:S(2)}) collective-permute-start(bf16[576,128]{1,0:T(8,128)(2,1)} %bitcast.3), channel_id=1, source_target_pairs={{0,0},{1,8},{2,4},{3,12},{4,1},{5,9},{6,5},{7,13},{8,2},{9,10},{10... | collective-permute-start | bytes 442376 | tf_op jit(solution)/shard_map/ppermute | solution.py:235
  4.6 3.0 %collective-permute-start = (bf16[576,128]{1,0:T(8,128)(2,1)}, bf16[576,128]{1,0:T(8,128)(2,1)S(1)}, u32[]{:S(2)}, u32[]{:S(2)}) collective-permute-start(bf16[576,128]{1,0:T(8,128)(2,1)} %bitcast.4), channel_id=1, source_target_pairs={{0,2},{1,3},{2,0},{3,1},{4,6},{5,7},{6,4},{7,5},{8,10},{9,11},{10,... | collective-permute-start | bytes 442376 | tf_op jit(solution)/shard_map/ppermute | solution.py:229
  7.6 0.7 %convert_element_type.3 = f32[96]{0:T(128)S(1)} convert(s32[96]{0:T(128)} %param.11) | non-fusion elementwise | flops 96 | bytes 768 | tf_op jit(solution)/shard_map/convert_element_type | solution.py:257
  8.3 0.7 %reshape.11 = f32[10,128]{1,0:T(8,128)S(1)} reshape(f32[2,640]{1,0:T(2,128)} %param.15) | data formatting | bytes 10240 | tf_op jit(solution)/shard_map/reshape | solution.py:258
  9.0 0.1 broadcast_in_dim.10
  9.0 1.5 %concatenate.3.table.refs_3_.refs_2_.refs_5_ = f32[120,128]{1,0:T(8,128)S(1)} concatenate(f32[2,128]{1,0:T(2,128)} %param.12, f32[2,128]{1,0:T(2,128)} %param.13, f32[2,128]{1,0:T(2,128)} %param.16, f32[2,128]{1,0:T(2,128)} %param.17, f32[2,128]{1,0:T(2,128)} %param.19, f32[10,128]{1,0:T(8,128)S(1)} %reshape.11, f32[4,128]{1,0:T(4,128)S(1)} %broadcast_in_dim.4, ...), dimensions={0} | concatenate | bytes 122880 | tf_op jit(solution)/shard_map/concatenate | solution.py:259
  10.5 0.0 copy-start.1
  10.5 0.9 %copy-done.1 = bf16[24,24,128]{2,1,0:T(8,128)(2,1)S(1)} copy-done((bf16[24,24,128]{2,1,0:T(8,128)(2,1)S(1)}, bf16[24,24,128]{2,1,0:T(8,128)(2,1)}, u32[]{:S(2)}) %copy-start.1) | copy-done | bytes 147480
  11.4 0.0 copy-start.3
  11.4 1.0 %copy-done.3 = bf16[2,128,640]{2,1,0:T(8,128)(2,1)S(1)} copy-done((bf16[2,128,640]{2,1,0:T(8,128)(2,1)S(1)}, bf16[2,128,640]{2,1,0:T(8,128)(2,1)}, u32[]{:S(2)}) %copy-start.3) | copy-done | bytes 327704
  12.4 1.0 %own_sides.1 = (bf16[2,128,640]{2,1,0:T(8,128)(2,1)S(1)}, f32[4,576,128]{2,1,0:T(8,128)S(1)}, f32[4,576,128]{2,1,0:T(8,128)S(1)}, f32[576,128]{1,0:T(8,128)S(1)}) custom-call(bf16[576,128]{1,0:T(8,128)(2,1)S(1)} %bitcast.5, f32[120,128]{1,0:T(8,128)S(1)} %concatenate.3.table.refs_3_.refs_2_.refs_5_, bf16[2,128,640]{2,1,0:T(8,128)(2,1)S(1)} %copy-done.3), custom_call_target="tpu_custom_call" | custom-call | tf_op jit(solution)/shard_map/own_sides/pallas_call | solution.py:245
  13.4 0.0 collective-permute-done.3.refs_0_
  13.4 0.0 collective-permute-done.2.refs_2_.refs_1_
  13.4 7.3 %collective-permute-done.refs_1_ = bf16[576,128]{1,0:T(8,128)(2,1)S(1)} collective-permute-done((bf16[576,128]{1,0:T(8,128)(2,1)}, bf16[576,128]{1,0:T(8,128)(2,1)S(1)}, u32[]{:S(2)}, u32[]{:S(2)}) %collective-permute-start) | collective-permute-done | bytes 147488 | tf_op jit(solution)/shard_map/ppermute | solution.py:229
  20.8 0.0 collective-permute-start.5
  20.8 0.0 collective-permute-start.4
  20.8 2.1 %collective-permute-start.1 = (bf16[576,128]{1,0:T(8,128)(2,1)S(1)}, bf16[576,128]{1,0:T(8,128)(2,1)S(1)}, u32[]{:S(2)}, u32[]{:S(2)}) collective-permute-start(bf16[576,128]{1,0:T(8,128)(2,1)S(1)} %collective-permute-done.refs_1_), channel_id=1, source_target_pairs={{0,1},{1,0},{2,3},{3,2},{4,5},{5,4},{6,7},{7,6},{8,9},{9,8},{10,11... | collective-permute-start | bytes 442376 | tf_op jit(solution)/shard_map/ppermute | solution.py:229
  22.9 3.0 %collective-permute-done.5.refs_1_.refs_3_ = bf16[576,128]{1,0:T(8,128)(2,1)S(1)} collective-permute-done((bf16[576,128]{1,0:T(8,128)(2,1)S(1)}, bf16[576,128]{1,0:T(8,128)(2,1)S(1)}, u32[]{:S(2)}, u32[]{:S(2)}) %collective-permute-start.5) | collective-permute-done | bytes 147488 | tf_op jit(solution)/shard_map/ppermute | solution.py:229
  25.9 0.0 collective-permute-start.6
  25.9 1.5 %row_sides.1 = (f32[4,576,128]{2,1,0:T(8,128)S(1)}, f32[4,576,128]{2,1,0:T(8,128)S(1)}, f32[4,576,128]{2,1,0:T(8,128)S(1)}, f32[4,576,128]{2,1,0:T(8,128)S(1)}) custom-call(bf16[576,128]{1,0:T(8,128)(2,1)S(1)} %collective-permute-done.3.refs_0_, bf16[576,128]{1,0:T(8,128)(2,1)S(1)} %collective-permute-done.refs_1_, ...), custom_call_target="tpu_custom_call", output_to_operand_aliasing={{0}: (5, {}), {1}: (6, {})} | custom-call | tf_op jit(solution)/shard_map/row_sides/pallas_call | solution.py:245
  27.4 0.0 collective-permute-done.4.refs_0_.refs_2_
  27.4 0.0 copy-start
  27.4 1.0 %column_sides.1 = (f32[4,576,128]{2,1,0:T(8,128)S(1)}, f32[4,576,128]{2,1,0:T(8,128)S(1)}) custom-call(bf16[576,128]{1,0:T(8,128)(2,1)S(1)} %collective-permute-done.4.refs_0_.refs_2_, bf16[576,128]{1,0:T(8,128)(2,1)S(1)} %collective-permute-done.5.refs_1_.refs_3_, ...), custom_call_target="tpu_custom_call", output_to_operand_aliasing={{0}: (4, {}), {1}: (5, {})} | custom-call | tf_op jit(solution)/shard_map/column_sides/pallas_call | solution.py:245
  28.4 0.0 collective-permute-done.1.refs_0_
  28.4 0.0 collective-permute-done.6.refs_4_
  28.4 0.0 copy-done
  28.4 0.0 copy-start.2
  28.4 5.0 %mirror_end.1 = (bf16[576,128]{1,0:T(8,128)(2,1)S(1)}, f32[4,576,128]{2,1,0:T(8,128)S(1)}, f32[4,576,128]{2,1,0:T(8,128)S(1)}, f32[4,576,128]{2,1,0:T(8,128)S(1)}, f32[4,576,128]{2,1,0:T(8,128)S(1)}) custom-call(bf16[576,128]{1,0:T(8,128)(2,1)S(1)} %collective-permute-done.1.refs_0_, ...), custom_call_target="tpu_custom_call", output_to_operand_aliasing={{1}: (8, {}), {2}: (9, {}), {3}: (10, {}), {4}: (11, {})} | custom-call | tf_op jit(solution)/shard_map/mirror_end/pallas_call | solution.py:245
  33.5 0.8 %collective-permute-start.9 = (bf16[576,128]{1,0:T(8,128)(2,1)S(1)}, bf16[576,128]{1,0:T(8,128)(2,1)S(1)}, u32[]{:S(2)}, u32[]{:S(2)}) collective-permute-start(bf16[576,128]{1,0:T(8,128)(2,1)S(1)} %get-tuple-element.36.refs_0_), channel_id=1, source_target_pairs={{0,1},{1,0},{2,3},{3,2},{4,5},{5,4},{6,7},{7,6},{8,9},{9,8},{10,11... | collective-permute-start | bytes 442376 | tf_op jit(solution)/shard_map/ppermute | solution.py:229
  34.3 3.3 %collective-permute-start.7 = (bf16[576,128]{1,0:T(8,128)(2,1)S(1)}, bf16[576,128]{1,0:T(8,128)(2,1)S(1)}, u32[]{:S(2)}, u32[]{:S(2)}) collective-permute-start(bf16[576,128]{1,0:T(8,128)(2,1)S(1)} %get-tuple-element.36.refs_0_), channel_id=1, source_target_pairs={{0,2},{1,3},{2,0},{3,1},{4,6},{5,7},{6,4},{7,5},{8,10},{9,11},{10,... | collective-permute-start | bytes 442376 | tf_op jit(solution)/shard_map/ppermute | solution.py:229
  37.6 0.0 copy-done.2
  37.6 3.6 %own_end.1 = (bf16[576,128]{1,0:T(8,128)(2,1)S(1)}, bf16[576,128]{1,0:T(8,128)(2,1)S(1)}) custom-call(f32[4,576,128]{2,1,0:T(8,128)S(1)} %get-tuple-element.37.row_l, f32[4,576,128]{2,1,0:T(8,128)S(1)} %get-tuple-element.38.col_r, f32[120,128]{1,0:T(8,128)S(1)} %concatenate.3.table.refs_3_.refs_2_.refs_5_, ...), custom_call_target="tpu_custom_call" | custom-call | tf_op jit(solution)/shard_map/own_end/pallas_call | solution.py:245
  41.2 1.5 %collective-permute-done.9.refs_1_ = bf16[576,128]{1,0:T(8,128)(2,1)S(1)} collective-permute-done((bf16[576,128]{1,0:T(8,128)(2,1)S(1)}, bf16[576,128]{1,0:T(8,128)(2,1)S(1)}, u32[]{:S(2)}, u32[]{:S(2)}) %collective-permute-start.9) | collective-permute-done | bytes 147488 | tf_op jit(solution)/shard_map/ppermute | solution.py:229
  42.8 0.0 collective-permute-start.12
  42.8 1.4 %collective-permute-start.11 = (bf16[576,128]{1,0:T(8,128)(2,1)S(1)}, bf16[576,128]{1,0:T(8,128)(2,1)S(1)}, u32[]{:S(2)}, u32[]{:S(2)}) collective-permute-start(bf16[576,128]{1,0:T(8,128)(2,1)S(1)} %get-tuple-element.41.refs_3_), channel_id=1, source_target_pairs={{0,8},{4,12},{8,0},{12,4},{1,9},{5,13},{9,1},{13,5},{2,10},{6,14},... | collective-permute-start | bytes 442376 | tf_op jit(solution)/shard_map/ppermute | solution.py:328
  44.1 0.5 collective-permute-start.10
  44.6 0.1 collective-permute-done.7.refs_2_
  44.8 0.3 collective-permute-start.8
  45.1 0.5 gate.1.gating
  45.6 3.3 %collective-permute-done.12.refs_6_ = bf16[576,128]{1,0:T(8,128)(2,1)S(1)} collective-permute-done((bf16[576,128]{1,0:T(8,128)(2,1)S(1)}, bf16[576,128]{1,0:T(8,128)(2,1)S(1)}, u32[]{:S(2)}, u32[]{:S(2)}) %collective-permute-start.12) | collective-permute-done | bytes 147488 | tf_op jit(solution)/shard_map/ppermute | solution.py:328
  48.9 3.0 %collective-permute-done.11.refs_5_ = bf16[576,128]{1,0:T(8,128)(2,1)S(1)} collective-permute-done((bf16[576,128]{1,0:T(8,128)(2,1)S(1)}, bf16[576,128]{1,0:T(8,128)(2,1)S(1)}, u32[]{:S(2)}, u32[]{:S(2)}) %collective-permute-start.11) | collective-permute-done | bytes 147488 | tf_op jit(solution)/shard_map/ppermute | solution.py:328
  51.9 0.0 collective-permute-done.10.refs_4_
  51.9 2.1 %middle_slots.1 = (f32[4,576,128]{2,1,0:T(8,128)S(1)}, f32[576,128]{1,0:T(8,128)S(1)}) custom-call(bf16[576,128]{1,0:T(8,128)(2,1)S(1)} %get-tuple-element.36.refs_0_, bf16[576,128]{1,0:T(8,128)(2,1)S(1)} %collective-permute-done.9.refs_1_, bf16[576,128]{1,0:T(8,128)(2,1)S(1)} %collective-permute-done.7.refs_2_, ...), custom_call_target="tpu_custom_call" | custom-call | tf_op jit(solution)/shard_map/middle_slots/pallas_call | solution.py:245
  54.0 0.0 collective-permute-done.8.block
  54.0 1.9 %end.1 = bf16[576,128]{1,0:T(8,128)(2,1)} custom-call(bf16[576,128]{1,0:T(8,128)(2,1)S(1)} %collective-permute-done.8.block, f32[4,576,128]{2,1,0:T(8,128)S(1)} %get-tuple-element.42.rights, f32[576,128]{1,0:T(8,128)S(1)} %get-tuple-element.43.old, bf16[576,128]{1,0:T(8,128)(2,1)S(1)} %get-tuple-element.44.pair, f32[576,128]{1,0:T(8,128)S(1)} %gate.1.gating, ...), custom_call_target="tpu_custom_call" | custom-call | tf_op jit(solution)/shard_map/end/pallas_call | solution.py:245
  (1 shorter events, 0.0 us)
Async XLA Ops:
  0.0 13.4 %collective-permute-start.3 = (bf16[576,128]{1,0:T(8,128)(2,1)}, bf16[576,128]{1,0:T(8,128)(2,1)S(1)}, u32[]{:S(2)}, u32[]{:S(2)}) collective-permute-start(bf16[576,128]{1,0:T(8,128)(2,1)} %bitcast.2), channel_id=1, source_target_pairs={{0,1},{1,0},{2,3},{3,2},{4,5},{5,4},{6,7},{7,6},{8,9},{9,8},{10,11... | collective-permute-start | bytes 442376 | tf_op jit(solution)/shard_map/ppermute | solution.py:229
  3.0 10.4 %collective-permute-start.2 = (bf16[576,128]{1,0:T(8,128)(2,1)}, bf16[576,128]{1,0:T(8,128)(2,1)S(1)}, u32[]{:S(2)}, u32[]{:S(2)}) collective-permute-start(bf16[576,128]{1,0:T(8,128)(2,1)} %bitcast.3), channel_id=1, source_target_pairs={{0,0},{1,8},{2,4},{3,12},{4,1},{5,9},{6,5},{7,13},{8,2},{9,10},{10... | collective-permute-start | bytes 442376 | tf_op jit(solution)/shard_map/ppermute | solution.py:235
  4.6 16.2 %collective-permute-start = (bf16[576,128]{1,0:T(8,128)(2,1)}, bf16[576,128]{1,0:T(8,128)(2,1)S(1)}, u32[]{:S(2)}, u32[]{:S(2)}) collective-permute-start(bf16[576,128]{1,0:T(8,128)(2,1)} %bitcast.4), channel_id=1, source_target_pairs={{0,2},{1,3},{2,0},{3,1},{4,6},{5,7},{6,4},{7,5},{8,10},{9,11},{10,... | collective-permute-start | bytes 442376 | tf_op jit(solution)/shard_map/ppermute | solution.py:229
  10.5 0.9 %copy-start.1 = (bf16[24,24,128]{2,1,0:T(8,128)(2,1)S(1)}, bf16[24,24,128]{2,1,0:T(8,128)(2,1)}, u32[]{:S(2)}) copy-start(bf16[24,24,128]{2,1,0:T(8,128)(2,1)} %param.10) | copy-start | bytes 442372
  11.4 1.0 %copy-start.3 = (bf16[2,128,640]{2,1,0:T(8,128)(2,1)S(1)}, bf16[2,128,640]{2,1,0:T(8,128)(2,1)}, u32[]{:S(2)}) copy-start(bf16[2,128,640]{2,1,0:T(8,128)(2,1)} %w_in.1) | copy-start | bytes 983044
  20.8 5.1 %collective-permute-start.5 = (bf16[576,128]{1,0:T(8,128)(2,1)S(1)}, bf16[576,128]{1,0:T(8,128)(2,1)S(1)}, u32[]{:S(2)}, u32[]{:S(2)}) collective-permute-start(bf16[576,128]{1,0:T(8,128)(2,1)S(1)} %collective-permute-done.2.refs_2_.refs_1_), channel_id=1, source_target_pairs={{0,8},{4,12},{8,0},{12,4},{1,9},{5,13},{9,1},{13,5},{2,10},{6,14},... | collective-permute-start | bytes 442376 | tf_op jit(solution)/shard_map/ppermute | solution.py:229
  20.8 6.6 %collective-permute-start.4 = (bf16[576,128]{1,0:T(8,128)(2,1)S(1)}, bf16[576,128]{1,0:T(8,128)(2,1)S(1)}, u32[]{:S(2)}, u32[]{:S(2)}) collective-permute-start(bf16[576,128]{1,0:T(8,128)(2,1)S(1)} %collective-permute-done.2.refs_2_.refs_1_), channel_id=1, source_target_pairs={{0,4},{4,0},{8,12},{12,8},{1,5},{5,1},{9,13},{13,9},{2,6},{6,2},{1... | collective-permute-start | bytes 442376 | tf_op jit(solution)/shard_map/ppermute | solution.py:229
  20.8 7.6 %collective-permute-start.1 = (bf16[576,128]{1,0:T(8,128)(2,1)S(1)}, bf16[576,128]{1,0:T(8,128)(2,1)S(1)}, u32[]{:S(2)}, u32[]{:S(2)}) collective-permute-start(bf16[576,128]{1,0:T(8,128)(2,1)S(1)} %collective-permute-done.refs_1_), channel_id=1, source_target_pairs={{0,1},{1,0},{2,3},{3,2},{4,5},{5,4},{6,7},{7,6},{8,9},{9,8},{10,11... | collective-permute-start | bytes 442376 | tf_op jit(solution)/shard_map/ppermute | solution.py:229
  25.9 2.5 %collective-permute-start.6 = (bf16[576,128]{1,0:T(8,128)(2,1)S(1)}, bf16[576,128]{1,0:T(8,128)(2,1)S(1)}, u32[]{:S(2)}, u32[]{:S(2)}) collective-permute-start(bf16[576,128]{1,0:T(8,128)(2,1)S(1)} %collective-permute-done.5.refs_1_.refs_3_), channel_id=1, source_target_pairs={{0,4},{4,0},{8,12},{12,8},{1,5},{5,1},{9,13},{13,9},{2,6},{6,2},{1... | collective-permute-start | bytes 442376 | tf_op jit(solution)/shard_map/ppermute | solution.py:229
  27.4 1.1 %copy-start = (bf16[2,128,128]{2,1,0:T(8,128)(2,1)S(1)}, bf16[2,128,128]{2,1,0:T(8,128)(2,1)}, u32[]{:S(2)}) copy-start(bf16[2,128,128]{2,1,0:T(8,128)(2,1)} %w_out.3) | copy-start | bytes 196612
  28.4 9.1 %copy-start.2 = (bf16[24,24,128]{2,1,0:T(8,128)(2,1)S(1)}, bf16[24,24,128]{2,1,0:T(8,128)(2,1)}, u32[]{:S(2)}) copy-start(bf16[24,24,128]{2,1,0:T(8,128)(2,1)} %param.10) | copy-start | bytes 442372
  33.5 9.3 %collective-permute-start.9 = (bf16[576,128]{1,0:T(8,128)(2,1)S(1)}, bf16[576,128]{1,0:T(8,128)(2,1)S(1)}, u32[]{:S(2)}, u32[]{:S(2)}) collective-permute-start(bf16[576,128]{1,0:T(8,128)(2,1)S(1)} %get-tuple-element.36.refs_0_), channel_id=1, source_target_pairs={{0,1},{1,0},{2,3},{3,2},{4,5},{5,4},{6,7},{7,6},{8,9},{9,8},{10,11... | collective-permute-start | bytes 442376 | tf_op jit(solution)/shard_map/ppermute | solution.py:229
  34.3 10.5 %collective-permute-start.7 = (bf16[576,128]{1,0:T(8,128)(2,1)S(1)}, bf16[576,128]{1,0:T(8,128)(2,1)S(1)}, u32[]{:S(2)}, u32[]{:S(2)}) collective-permute-start(bf16[576,128]{1,0:T(8,128)(2,1)S(1)} %get-tuple-element.36.refs_0_), channel_id=1, source_target_pairs={{0,2},{1,3},{2,0},{3,1},{4,6},{5,7},{6,4},{7,5},{8,10},{9,11},{10,... | collective-permute-start | bytes 442376 | tf_op jit(solution)/shard_map/ppermute | solution.py:229
  42.8 6.1 %collective-permute-start.12 = (bf16[576,128]{1,0:T(8,128)(2,1)S(1)}, bf16[576,128]{1,0:T(8,128)(2,1)S(1)}, u32[]{:S(2)}, u32[]{:S(2)}) collective-permute-start(bf16[576,128]{1,0:T(8,128)(2,1)S(1)} %get-tuple-element.41.refs_3_), channel_id=1, source_target_pairs={{0,12},{4,8},{8,4},{12,0},{1,13},{5,9},{9,5},{13,1},{2,14},{6,10},... | collective-permute-start | bytes 442376 | tf_op jit(solution)/shard_map/ppermute | solution.py:328
  42.8 9.1 %collective-permute-start.11 = (bf16[576,128]{1,0:T(8,128)(2,1)S(1)}, bf16[576,128]{1,0:T(8,128)(2,1)S(1)}, u32[]{:S(2)}, u32[]{:S(2)}) collective-permute-start(bf16[576,128]{1,0:T(8,128)(2,1)S(1)} %get-tuple-element.41.refs_3_), channel_id=1, source_target_pairs={{0,8},{4,12},{8,0},{12,4},{1,9},{5,13},{9,1},{13,5},{2,10},{6,14},... | collective-permute-start | bytes 442376 | tf_op jit(solution)/shard_map/ppermute | solution.py:328
  44.1 7.8 %collective-permute-start.10 = (bf16[576,128]{1,0:T(8,128)(2,1)S(1)}, bf16[576,128]{1,0:T(8,128)(2,1)S(1)}, u32[]{:S(2)}, u32[]{:S(2)}) collective-permute-start(bf16[576,128]{1,0:T(8,128)(2,1)S(1)} %get-tuple-element.41.refs_3_), channel_id=1, source_target_pairs={{0,4},{4,0},{8,12},{12,8},{1,5},{5,1},{9,13},{13,9},{2,6},{6,2},{1... | collective-permute-start | bytes 442376 | tf_op jit(solution)/shard_map/ppermute | solution.py:328
  44.8 9.2 %collective-permute-start.8 = (bf16[576,128]{1,0:T(8,128)(2,1)S(1)}, bf16[576,128]{1,0:T(8,128)(2,1)S(1)}, u32[]{:S(2)}, u32[]{:S(2)}) collective-permute-start(bf16[576,128]{1,0:T(8,128)(2,1)S(1)} %collective-permute-done.7.refs_2_), channel_id=1, source_target_pairs={{0,1},{1,0},{2,3},{3,2},{4,5},{5,4},{6,7},{7,6},{8,9},{9,8},{10,11... | collective-permute-start | bytes 442376 | tf_op jit(solution)/shard_map/ppermute | solution.py:229

commit v10 on v9

--- a/solution.py
+++ b/solution.py
@@ -266,9 +266,8 @@
             table,
             w_in,
         )
-        after = lambda block: lax.optimization_barrier((block, row_l))[0]
-        rows = gather(pair, "col", after)
-        cols = gather(lax.optimization_barrier((col_block, rows[1], rows[n // 2], row_l))[0], "row")
+        own_l = row_l
+        rows = gather(pair, "col", lambda block: lax.optimization_barrier((block, own_l))[0])
         row_l, row_r, col_l, col_r = call(
             functools.partial(rows_kernel, t, n - 2),
             "row_sides",
@@ -282,6 +281,8 @@
             row_r,
             alias={n + 1: 0, n + 2: 1},
         )
+        ready = lax.optimization_barrier((col_block, rows[1], rows[n // 2], own_l))[0]
+        cols = gather(ready, "row", lambda block: lax.optimization_barrier((block, row_l))[0])
         col_l, col_r = call(
             functools.partial(columns_kernel, t, n - 2),
             "column_sides",
@@ -324,7 +325,6 @@
             w_out,
         )
         lefts = gather(left, "col")
-        right = lax.optimization_barrier((right, lefts[1]))[0]
         rights = [right] + [lax.ppermute(right, "row", [(k, k ^ s) for k in range(n)]) for s in range(1, n)]
         gating = call(gate_kernel, "gate", broad, [], pair, table, weights)
         rights, mixed = call(

time: 56.1 us -> 52.8 us (0.941)
  waiting for transfers between devices: 18.3 us -> 13.7 us
  starting transfers between devices: 16 us -> 17.2 us
    ppermute x9, waiting for transfers between devices: 12 us -> 9.39 us  [gather(): held[s ^ step] = lax.ppermute(part, axis, [(k, k ^ step) for k in range(n)])]
    ppermute x3, waiting for transfers between devices: 6.23 us -> 4.31 us  [per_device(): lax.ppermute(right, 'row', [(k, k ^ s) for k in range(n)])]
    ppermute x9, starting transfers between devices: 12.6 us -> 13.8 us  [gather(): held[s ^ step] = lax.ppermute(part, axis, [(k, k ^ step) for k in range(n)])]
  transfers between devices with their start and end apart: 13 -> 13, of which waited for: 6 -> 5; matrix products, arithmetic and copies ran while one was open for 5% -> 6% of each run, Pallas kernels for 17% -> 19%
where the time goes in v10:
time: 52.8 us; the launch traced here: 52.5 us
  starting transfers between devices  17.2 us (33%)
  Pallas kernels  16.6 us (31%)
  waiting for transfers between devices  13.7 us (26%)
  local copies, waits for them, and re-layouts  4.16 us (8%)
  other arithmetic  0.66 us (1%)
    pallas_call x8, Pallas kernels, call(): pl.pallas_call(kernel, out_shape=outs, scratch_shapes=scratches, input_ou...  16.6 us
    ppermute x9, starting transfers between devices, gather(): held[s ^ step] = lax.ppermute(part, axis, [(k, k ^ step) for k in range(n)])  13.8 us
    ppermute x9, waiting for transfers between devices, gather(): held[s ^ step] = lax.ppermute(part, axis, [(k, k ^ step) for k in range(n)])  9.39 us
    ppermute x3, waiting for transfers between devices, per_device(): lax.ppermute(right, 'row', [(k, k ^ s) for k in range(n)])  4.31 us
    ppermute x3, starting transfers between devices, per_device(): lax.ppermute(right, 'row', [(k, k ^ s) for k in range(n)])  1.92 us
    unnamed x8, local copies, waits for them, and re-layouts  1.88 us
    ppermute x1, starting transfers between devices, mirrored(): return lax.ppermute(block, ('row', 'col'), pairs)  1.56 us
    concatenate x1, local copies, waits for them, and re-layouts, per_device(): jnp.concatenate(vectors + [jnp.zeros((TABLE_MASK - 20, width), F32), mask])  1.51 us
  transfers between devices with their start and end apart: 13, of which 5 were waited for; matrix products, arithmetic and copies ran while one was open for 6% of the time, Pallas kernels for 19%

profile of v10, /device:TPU:0, one launch (start us, length us, event | category | flops | bytes accessed | tf_op | source)
XLA Modules:
  0.0 52.5 jit_solution(17594834164670301254)
XLA Ops:
  0.0 3.0 %collective-permute-start.3 = (bf16[576,128]{1,0:T(8,128)(2,1)}, bf16[576,128]{1,0:T(8,128)(2,1)S(1)}, u32[]{:S(2)}, u32[]{:S(2)}) collective-permute-start(bf16[576,128]{1,0:T(8,128)(2,1)} %bitcast.2), channel_id=1, source_target_pairs={{0,1},{1,0},{2,3},{3,2},{4,5},{5,4},{6,7},{7,6},{8,9},{9,8},{10,11... | collective-permute-start | bytes 442376 | tf_op jit(solution)/shard_map/ppermute | solution.py:229
  3.0 1.6 %collective-permute-start.2 = (bf16[576,128]{1,0:T(8,128)(2,1)}, bf16[576,128]{1,0:T(8,128)(2,1)S(1)}, u32[]{:S(2)}, u32[]{:S(2)}) collective-permute-start(bf16[576,128]{1,0:T(8,128)(2,1)} %bitcast.3), channel_id=1, source_target_pairs={{0,0},{1,8},{2,4},{3,12},{4,1},{5,9},{6,5},{7,13},{8,2},{9,10},{10... | collective-permute-start | bytes 442376 | tf_op jit(solution)/shard_map/ppermute | solution.py:235
  4.6 3.0 %collective-permute-start = (bf16[576,128]{1,0:T(8,128)(2,1)}, bf16[576,128]{1,0:T(8,128)(2,1)S(1)}, u32[]{:S(2)}, u32[]{:S(2)}) collective-permute-start(bf16[576,128]{1,0:T(8,128)(2,1)} %bitcast.4), channel_id=1, source_target_pairs={{0,2},{1,3},{2,0},{3,1},{4,6},{5,7},{6,4},{7,5},{8,10},{9,11},{10,... | collective-permute-start | bytes 442376 | tf_op jit(solution)/shard_map/ppermute | solution.py:229
  7.6 0.7 %convert_element_type.3 = f32[96]{0:T(128)S(1)} convert(s32[96]{0:T(128)} %param.11) | non-fusion elementwise | flops 96 | bytes 768 | tf_op jit(solution)/shard_map/convert_element_type | solution.py:257
  8.3 0.7 %reshape.11 = f32[10,128]{1,0:T(8,128)S(1)} reshape(f32[2,640]{1,0:T(2,128)} %param.15) | data formatting | bytes 10240 | tf_op jit(solution)/shard_map/reshape | solution.py:258
  9.0 0.1 broadcast_in_dim.10
  9.0 1.5 %concatenate.3.table.refs_3_.refs_2_.refs_5_ = f32[120,128]{1,0:T(8,128)S(1)} concatenate(f32[2,128]{1,0:T(2,128)} %param.12, f32[2,128]{1,0:T(2,128)} %param.13, f32[2,128]{1,0:T(2,128)} %param.16, f32[2,128]{1,0:T(2,128)} %param.17, f32[2,128]{1,0:T(2,128)} %param.19, f32[10,128]{1,0:T(8,128)S(1)} %reshape.11, f32[4,128]{1,0:T(4,128)S(1)} %broadcast_in_dim.4, ...), dimensions={0} | concatenate | bytes 122880 | tf_op jit(solution)/shard_map/concatenate | solution.py:259
  10.5 0.0 copy-start.1
  10.5 0.9 %copy-done.1 = bf16[24,24,128]{2,1,0:T(8,128)(2,1)S(1)} copy-done((bf16[24,24,128]{2,1,0:T(8,128)(2,1)S(1)}, bf16[24,24,128]{2,1,0:T(8,128)(2,1)}, u32[]{:S(2)}) %copy-start.1) | copy-done | bytes 147480
  11.4 0.0 copy-start.3
  11.4 1.0 %copy-done.3 = bf16[2,128,640]{2,1,0:T(8,128)(2,1)S(1)} copy-done((bf16[2,128,640]{2,1,0:T(8,128)(2,1)S(1)}, bf16[2,128,640]{2,1,0:T(8,128)(2,1)}, u32[]{:S(2)}) %copy-start.3) | copy-done | bytes 327704
  12.4 1.0 %own_sides.1 = (bf16[2,128,640]{2,1,0:T(8,128)(2,1)S(1)}, f32[4,576,128]{2,1,0:T(8,128)S(1)}, f32[4,576,128]{2,1,0:T(8,128)S(1)}, f32[576,128]{1,0:T(8,128)S(1)}) custom-call(bf16[576,128]{1,0:T(8,128)(2,1)S(1)} %bitcast.5, f32[120,128]{1,0:T(8,128)S(1)} %concatenate.3.table.refs_3_.refs_2_.refs_5_, bf16[2,128,640]{2,1,0:T(8,128)(2,1)S(1)} %copy-done.3), custom_call_target="tpu_custom_call" | custom-call | tf_op jit(solution)/shard_map/own_sides/pallas_call | solution.py:245
  13.4 0.0 collective-permute-done.3.refs_0_
  13.4 0.0 collective-permute-done.2.refs_2_.refs_1_
  13.4 7.3 %collective-permute-done.refs_1_ = bf16[576,128]{1,0:T(8,128)(2,1)S(1)} collective-permute-done((bf16[576,128]{1,0:T(8,128)(2,1)}, bf16[576,128]{1,0:T(8,128)(2,1)S(1)}, u32[]{:S(2)}, u32[]{:S(2)}) %collective-permute-start) | collective-permute-done | bytes 147488 | tf_op jit(solution)/shard_map/ppermute | solution.py:229
  20.8 0.0 collective-permute-start.5
  20.8 0.0 collective-permute-start.4
  20.8 2.1 %collective-permute-start.1 = (bf16[576,128]{1,0:T(8,128)(2,1)S(1)}, bf16[576,128]{1,0:T(8,128)(2,1)S(1)}, u32[]{:S(2)}, u32[]{:S(2)}) collective-permute-start(bf16[576,128]{1,0:T(8,128)(2,1)S(1)} %collective-permute-done.refs_1_), channel_id=1, source_target_pairs={{0,1},{1,0},{2,3},{3,2},{4,5},{5,4},{6,7},{7,6},{8,9},{9,8},{10,11... | collective-permute-start | bytes 442376 | tf_op jit(solution)/shard_map/ppermute | solution.py:229
  22.9 1.5 %row_sides.1 = (f32[4,576,128]{2,1,0:T(8,128)S(1)}, f32[4,576,128]{2,1,0:T(8,128)S(1)}, f32[4,576,128]{2,1,0:T(8,128)S(1)}, f32[4,576,128]{2,1,0:T(8,128)S(1)}) custom-call(bf16[576,128]{1,0:T(8,128)(2,1)S(1)} %collective-permute-done.3.refs_0_, bf16[576,128]{1,0:T(8,128)(2,1)S(1)} %collective-permute-done.refs_1_, ...), custom_call_target="tpu_custom_call", output_to_operand_aliasing={{0}: (5, {}), {1}: (6, {})} | custom-call | tf_op jit(solution)/shard_map/row_sides/pallas_call | solution.py:245
  24.4 1.5 %collective-permute-done.5.refs_1_.refs_3_ = bf16[576,128]{1,0:T(8,128)(2,1)S(1)} collective-permute-done((bf16[576,128]{1,0:T(8,128)(2,1)S(1)}, bf16[576,128]{1,0:T(8,128)(2,1)S(1)}, u32[]{:S(2)}, u32[]{:S(2)}) %collective-permute-start.5) | collective-permute-done | bytes 147488 | tf_op jit(solution)/shard_map/ppermute | solution.py:229
  25.9 0.0 collective-permute-start.6
  25.9 0.0 collective-permute-done.4.refs_0_.refs_2_
  25.9 0.0 copy-start
  25.9 1.0 %column_sides.1 = (f32[4,576,128]{2,1,0:T(8,128)S(1)}, f32[4,576,128]{2,1,0:T(8,128)S(1)}) custom-call(bf16[576,128]{1,0:T(8,128)(2,1)S(1)} %collective-permute-done.4.refs_0_.refs_2_, bf16[576,128]{1,0:T(8,128)(2,1)S(1)} %collective-permute-done.5.refs_1_.refs_3_, ...), custom_call_target="tpu_custom_call", output_to_operand_aliasing={{0}: (4, {}), {1}: (5, {})} | custom-call | tf_op jit(solution)/shard_map/column_sides/pallas_call | solution.py:245
  26.9 0.5 collective-permute-done.1.refs_0_
  27.4 0.0 collective-permute-done.6.refs_4_
  27.4 0.0 copy-done
  27.4 0.0 copy-start.2
  27.4 5.0 %mirror_end.1 = (bf16[576,128]{1,0:T(8,128)(2,1)S(1)}, f32[4,576,128]{2,1,0:T(8,128)S(1)}, f32[4,576,128]{2,1,0:T(8,128)S(1)}, f32[4,576,128]{2,1,0:T(8,128)S(1)}, f32[4,576,128]{2,1,0:T(8,128)S(1)}) custom-call(bf16[576,128]{1,0:T(8,128)(2,1)S(1)} %collective-permute-done.1.refs_0_, ...), custom_call_target="tpu_custom_call", output_to_operand_aliasing={{1}: (8, {}), {2}: (9, {}), {3}: (10, {}), {4}: (11, {})} | custom-call | tf_op jit(solution)/shard_map/mirror_end/pallas_call | solution.py:245
  32.5 3.3 %collective-permute-start.7 = (bf16[576,128]{1,0:T(8,128)(2,1)S(1)}, bf16[576,128]{1,0:T(8,128)(2,1)S(1)}, u32[]{:S(2)}, u32[]{:S(2)}) collective-permute-start(bf16[576,128]{1,0:T(8,128)(2,1)S(1)} %get-tuple-element.37.refs_0_), channel_id=1, source_target_pairs={{0,2},{1,3},{2,0},{3,1},{4,6},{5,7},{6,4},{7,5},{8,10},{9,11},{10,... | collective-permute-start | bytes 442376 | tf_op jit(solution)/shard_map/ppermute | solution.py:229
  35.8 0.0 copy-done.2
  35.8 3.6 %own_end.1 = (bf16[576,128]{1,0:T(8,128)(2,1)S(1)}, bf16[576,128]{1,0:T(8,128)(2,1)S(1)}) custom-call(f32[4,576,128]{2,1,0:T(8,128)S(1)} %get-tuple-element.38.row_l, f32[4,576,128]{2,1,0:T(8,128)S(1)} %get-tuple-element.39.col_r, f32[120,128]{1,0:T(8,128)S(1)} %concatenate.3.table.refs_3_.refs_2_.refs_5_, ...), custom_call_target="tpu_custom_call" | custom-call | tf_op jit(solution)/shard_map/own_end/pallas_call | solution.py:245
  39.5 0.1 collective-permute-start.12
  39.5 1.3 %collective-permute-start.11 = (bf16[576,128]{1,0:T(8,128)(2,1)S(1)}, bf16[576,128]{1,0:T(8,128)(2,1)S(1)}, u32[]{:S(2)}, u32[]{:S(2)}) collective-permute-start(bf16[576,128]{1,0:T(8,128)(2,1)S(1)} %get-tuple-element.41.refs_3_), channel_id=1, source_target_pairs={{0,8},{4,12},{8,0},{12,4},{1,9},{5,13},{9,1},{13,5},{2,10},{6,14},... | collective-permute-start | bytes 442376 | tf_op jit(solution)/shard_map/ppermute | solution.py:328
  40.8 0.6 %collective-permute-start.10 = (bf16[576,128]{1,0:T(8,128)(2,1)S(1)}, bf16[576,128]{1,0:T(8,128)(2,1)S(1)}, u32[]{:S(2)}, u32[]{:S(2)}) collective-permute-start(bf16[576,128]{1,0:T(8,128)(2,1)S(1)} %get-tuple-element.41.refs_3_), channel_id=1, source_target_pairs={{0,4},{4,0},{8,12},{12,8},{1,5},{5,1},{9,13},{13,9},{2,6},{6,2},{1... | collective-permute-start | bytes 442376 | tf_op jit(solution)/shard_map/ppermute | solution.py:328
  41.4 1.7 %collective-permute-start.9 = (bf16[576,128]{1,0:T(8,128)(2,1)S(1)}, bf16[576,128]{1,0:T(8,128)(2,1)S(1)}, u32[]{:S(2)}, u32[]{:S(2)}) collective-permute-start(bf16[576,128]{1,0:T(8,128)(2,1)S(1)} %get-tuple-element.37.refs_0_), channel_id=1, source_target_pairs={{0,1},{1,0},{2,3},{3,2},{4,5},{5,4},{6,7},{7,6},{8,9},{9,8},{10,11... | collective-permute-start | bytes 442376 | tf_op jit(solution)/shard_map/ppermute | solution.py:229
  43.1 0.0 collective-permute-done.7.refs_2_
  43.1 0.5 collective-permute-start.8
  43.6 0.5 %gate.1.gating = f32[576,128]{1,0:T(8,128)S(1)} custom-call(bf16[576,128]{1,0:T(8,128)(2,1)S(1)} %get-tuple-element.44.pair, f32[120,128]{1,0:T(8,128)S(1)} %concatenate.3.table.refs_3_.refs_2_.refs_5_, bf16[2,128,640]{2,1,0:T(8,128)(2,1)S(1)} %get-tuple-element.28.refs_4_.refs_3_.refs_6_.weights), custom_call_target="tpu_custom_call" | custom-call | tf_op jit(solution)/shard_map/gate/pallas_call | solution.py:245
  44.2 1.5 %collective-permute-done.12.refs_6_ = bf16[576,128]{1,0:T(8,128)(2,1)S(1)} collective-permute-done((bf16[576,128]{1,0:T(8,128)(2,1)S(1)}, bf16[576,128]{1,0:T(8,128)(2,1)S(1)}, u32[]{:S(2)}, u32[]{:S(2)}) %collective-permute-start.12) | collective-permute-done | bytes 147488 | tf_op jit(solution)/shard_map/ppermute | solution.py:328
  45.7 2.8 %collective-permute-done.11.refs_5_ = bf16[576,128]{1,0:T(8,128)(2,1)S(1)} collective-permute-done((bf16[576,128]{1,0:T(8,128)(2,1)S(1)}, bf16[576,128]{1,0:T(8,128)(2,1)S(1)}, u32[]{:S(2)}, u32[]{:S(2)}) %collective-permute-start.11) | collective-permute-done | bytes 147488 | tf_op jit(solution)/shard_map/ppermute | solution.py:328
  48.5 0.0 collective-permute-done.10.refs_4_
  48.5 0.0 collective-permute-done.9.refs_1_
  48.5 2.1 %middle_slots.1 = (f32[4,576,128]{2,1,0:T(8,128)S(1)}, f32[576,128]{1,0:T(8,128)S(1)}) custom-call(bf16[576,128]{1,0:T(8,128)(2,1)S(1)} %get-tuple-element.37.refs_0_, bf16[576,128]{1,0:T(8,128)(2,1)S(1)} %collective-permute-done.9.refs_1_, bf16[576,128]{1,0:T(8,128)(2,1)S(1)} %collective-permute-done.7.refs_2_, ...), custom_call_target="tpu_custom_call" | custom-call | tf_op jit(solution)/shard_map/middle_slots/pallas_call | solution.py:245
  50.6 0.0 collective-permute-done.8.block
  50.6 1.9 %end.1 = bf16[576,128]{1,0:T(8,128)(2,1)} custom-call(bf16[576,128]{1,0:T(8,128)(2,1)S(1)} %collective-permute-done.8.block, f32[4,576,128]{2,1,0:T(8,128)S(1)} %get-tuple-element.42.rights, f32[576,128]{1,0:T(8,128)S(1)} %get-tuple-element.43.old, bf16[576,128]{1,0:T(8,128)(2,1)S(1)} %get-tuple-element.44.pair, f32[576,128]{1,0:T(8,128)S(1)} %gate.1.gating, ...), custom_call_target="tpu_custom_call" | custom-call | tf_op jit(solution)/shard_map/end/pallas_call | solution.py:245
  (1 shorter events, 0.0 us)
Async XLA Ops:
  0.0 13.4 %collective-permute-start.3 = (bf16[576,128]{1,0:T(8,128)(2,1)}, bf16[576,128]{1,0:T(8,128)(2,1)S(1)}, u32[]{:S(2)}, u32[]{:S(2)}) collective-permute-start(bf16[576,128]{1,0:T(8,128)(2,1)} %bitcast.2), channel_id=1, source_target_pairs={{0,1},{1,0},{2,3},{3,2},{4,5},{5,4},{6,7},{7,6},{8,9},{9,8},{10,11... | collective-permute-start | bytes 442376 | tf_op jit(solution)/shard_map/ppermute | solution.py:229
  3.0 10.4 %collective-permute-start.2 = (bf16[576,128]{1,0:T(8,128)(2,1)}, bf16[576,128]{1,0:T(8,128)(2,1)S(1)}, u32[]{:S(2)}, u32[]{:S(2)}) collective-permute-start(bf16[576,128]{1,0:T(8,128)(2,1)} %bitcast.3), channel_id=1, source_target_pairs={{0,0},{1,8},{2,4},{3,12},{4,1},{5,9},{6,5},{7,13},{8,2},{9,10},{10... | collective-permute-start | bytes 442376 | tf_op jit(solution)/shard_map/ppermute | solution.py:235
  4.6 16.2 %collective-permute-start = (bf16[576,128]{1,0:T(8,128)(2,1)}, bf16[576,128]{1,0:T(8,128)(2,1)S(1)}, u32[]{:S(2)}, u32[]{:S(2)}) collective-permute-start(bf16[576,128]{1,0:T(8,128)(2,1)} %bitcast.4), channel_id=1, source_target_pairs={{0,2},{1,3},{2,0},{3,1},{4,6},{5,7},{6,4},{7,5},{8,10},{9,11},{10,... | collective-permute-start | bytes 442376 | tf_op jit(solution)/shard_map/ppermute | solution.py:229
  10.5 0.9 %copy-start.1 = (bf16[24,24,128]{2,1,0:T(8,128)(2,1)S(1)}, bf16[24,24,128]{2,1,0:T(8,128)(2,1)}, u32[]{:S(2)}) copy-start(bf16[24,24,128]{2,1,0:T(8,128)(2,1)} %param.10) | copy-start | bytes 442372
  11.4 1.0 %copy-start.3 = (bf16[2,128,640]{2,1,0:T(8,128)(2,1)S(1)}, bf16[2,128,640]{2,1,0:T(8,128)(2,1)}, u32[]{:S(2)}) copy-start(bf16[2,128,640]{2,1,0:T(8,128)(2,1)} %w_in.1) | copy-start | bytes 983044
  20.8 5.1 %collective-permute-start.5 = (bf16[576,128]{1,0:T(8,128)(2,1)S(1)}, bf16[576,128]{1,0:T(8,128)(2,1)S(1)}, u32[]{:S(2)}, u32[]{:S(2)}) collective-permute-start(bf16[576,128]{1,0:T(8,128)(2,1)S(1)} %collective-permute-done.2.refs_2_.refs_1_), channel_id=1, source_target_pairs={{0,8},{4,12},{8,0},{12,4},{1,9},{5,13},{9,1},{13,5},{2,10},{6,14},... | collective-permute-start | bytes 442376 | tf_op jit(solution)/shard_map/ppermute | solution.py:229
  20.8 5.1 %collective-permute-start.4 = (bf16[576,128]{1,0:T(8,128)(2,1)S(1)}, bf16[576,128]{1,0:T(8,128)(2,1)S(1)}, u32[]{:S(2)}, u32[]{:S(2)}) collective-permute-start(bf16[576,128]{1,0:T(8,128)(2,1)S(1)} %collective-permute-done.2.refs_2_.refs_1_), channel_id=1, source_target_pairs={{0,4},{4,0},{8,12},{12,8},{1,5},{5,1},{9,13},{13,9},{2,6},{6,2},{1... | collective-permute-start | bytes 442376 | tf_op jit(solution)/shard_map/ppermute | solution.py:229
  20.8 6.7 %collective-permute-start.1 = (bf16[576,128]{1,0:T(8,128)(2,1)S(1)}, bf16[576,128]{1,0:T(8,128)(2,1)S(1)}, u32[]{:S(2)}, u32[]{:S(2)}) collective-permute-start(bf16[576,128]{1,0:T(8,128)(2,1)S(1)} %collective-permute-done.refs_1_), channel_id=1, source_target_pairs={{0,1},{1,0},{2,3},{3,2},{4,5},{5,4},{6,7},{7,6},{8,9},{9,8},{10,11... | collective-permute-start | bytes 442376 | tf_op jit(solution)/shard_map/ppermute | solution.py:229
  25.9 1.5 %collective-permute-start.6 = (bf16[576,128]{1,0:T(8,128)(2,1)S(1)}, bf16[576,128]{1,0:T(8,128)(2,1)S(1)}, u32[]{:S(2)}, u32[]{:S(2)}) collective-permute-start(bf16[576,128]{1,0:T(8,128)(2,1)S(1)} %collective-permute-done.5.refs_1_.refs_3_), channel_id=1, source_target_pairs={{0,4},{4,0},{8,12},{12,8},{1,5},{5,1},{9,13},{13,9},{2,6},{6,2},{1... | collective-permute-start | bytes 442376 | tf_op jit(solution)/shard_map/ppermute | solution.py:229
  25.9 1.5 %copy-start = (bf16[2,128,128]{2,1,0:T(8,128)(2,1)S(1)}, bf16[2,128,128]{2,1,0:T(8,128)(2,1)}, u32[]{:S(2)}) copy-start(bf16[2,128,128]{2,1,0:T(8,128)(2,1)} %w_out.3) | copy-start | bytes 196612
  27.4 8.4 %copy-start.2 = (bf16[24,24,128]{2,1,0:T(8,128)(2,1)S(1)}, bf16[24,24,128]{2,1,0:T(8,128)(2,1)}, u32[]{:S(2)}) copy-start(bf16[24,24,128]{2,1,0:T(8,128)(2,1)} %param.10) | copy-start | bytes 442372
  32.5 10.7 %collective-permute-start.7 = (bf16[576,128]{1,0:T(8,128)(2,1)S(1)}, bf16[576,128]{1,0:T(8,128)(2,1)S(1)}, u32[]{:S(2)}, u32[]{:S(2)}) collective-permute-start(bf16[576,128]{1,0:T(8,128)(2,1)S(1)} %get-tuple-element.37.refs_0_), channel_id=1, source_target_pairs={{0,2},{1,3},{2,0},{3,1},{4,6},{5,7},{6,4},{7,5},{8,10},{9,11},{10,... | collective-permute-start | bytes 442376 | tf_op jit(solution)/shard_map/ppermute | solution.py:229
  39.5 6.2 %collective-permute-start.12 = (bf16[576,128]{1,0:T(8,128)(2,1)S(1)}, bf16[576,128]{1,0:T(8,128)(2,1)S(1)}, u32[]{:S(2)}, u32[]{:S(2)}) collective-permute-start(bf16[576,128]{1,0:T(8,128)(2,1)S(1)} %get-tuple-element.41.refs_3_), channel_id=1, source_target_pairs={{0,12},{4,8},{8,4},{12,0},{1,13},{5,9},{9,5},{13,1},{2,14},{6,10},... | collective-permute-start | bytes 442376 | tf_op jit(solution)/shard_map/ppermute | solution.py:328
  39.5 8.9 %collective-permute-start.11 = (bf16[576,128]{1,0:T(8,128)(2,1)S(1)}, bf16[576,128]{1,0:T(8,128)(2,1)S(1)}, u32[]{:S(2)}, u32[]{:S(2)}) collective-permute-start(bf16[576,128]{1,0:T(8,128)(2,1)S(1)} %get-tuple-element.41.refs_3_), channel_id=1, source_target_pairs={{0,8},{4,12},{8,0},{12,4},{1,9},{5,13},{9,1},{13,5},{2,10},{6,14},... | collective-permute-start | bytes 442376 | tf_op jit(solution)/shard_map/ppermute | solution.py:328
  40.8 7.7 %collective-permute-start.10 = (bf16[576,128]{1,0:T(8,128)(2,1)S(1)}, bf16[576,128]{1,0:T(8,128)(2,1)S(1)}, u32[]{:S(2)}, u32[]{:S(2)}) collective-permute-start(bf16[576,128]{1,0:T(8,128)(2,1)S(1)} %get-tuple-element.41.refs_3_), channel_id=1, source_target_pairs={{0,4},{4,0},{8,12},{12,8},{1,5},{5,1},{9,13},{13,9},{2,6},{6,2},{1... | collective-permute-start | bytes 442376 | tf_op jit(solution)/shard_map/ppermute | solution.py:328
  41.4 7.1 %collective-permute-start.9 = (bf16[576,128]{1,0:T(8,128)(2,1)S(1)}, bf16[576,128]{1,0:T(8,128)(2,1)S(1)}, u32[]{:S(2)}, u32[]{:S(2)}) collective-permute-start(bf16[576,128]{1,0:T(8,128)(2,1)S(1)} %get-tuple-element.37.refs_0_), channel_id=1, source_target_pairs={{0,1},{1,0},{2,3},{3,2},{4,5},{5,4},{6,7},{7,6},{8,9},{9,8},{10,11... | collective-permute-start | bytes 442376 | tf_op jit(solution)/shard_map/ppermute | solution.py:229
  43.1 7.5 %collective-permute-start.8 = (bf16[576,128]{1,0:T(8,128)(2,1)S(1)}, bf16[576,128]{1,0:T(8,128)(2,1)S(1)}, u32[]{:S(2)}, u32[]{:S(2)}) collective-permute-start(bf16[576,128]{1,0:T(8,128)(2,1)S(1)} %collective-permute-done.7.refs_2_), channel_id=1, source_target_pairs={{0,1},{1,0},{2,3},{3,2},{4,5},{5,4},{6,7},{7,6},{8,9},{9,8},{10,11... | collective-permute-start | bytes 442376 | tf_op jit(solution)/shard_map/ppermute | solution.py:229

commit v11 on v10

--- a/solution.py
+++ b/solution.py
@@ -230,6 +230,11 @@
             step //= 2
         return [held[s] for s in range(n)]
 
+    def direct(block, near):
+        return [block] + [
+            lax.ppermute(near if s == 1 else block, "row", [(k, k ^ s) for k in range(n)]) for s in range(1, n)
+        ]
+
     def mirrored(block):
         pairs = [(a * n + z, (z // 2 + z % 2 * (n // 2)) * n + a) for a in range(n) for z in range(n)]
         return lax.ppermute(block, ("row", "col"), pairs)
@@ -281,8 +286,8 @@
             row_r,
             alias={n + 1: 0, n + 2: 1},
         )
-        ready = lax.optimization_barrier((col_block, rows[1], rows[n // 2], own_l))[0]
-        cols = gather(ready, "row", lambda block: lax.optimization_barrier((block, row_l))[0])
+        ready = lax.optimization_barrier((col_block, own_l))[0]
+        cols = direct(ready, ready)
         col_l, col_r = call(
             functools.partial(columns_kernel, t, n - 2),
             "column_sides",
@@ -325,7 +330,8 @@
             w_out,
         )
         lefts = gather(left, "col")
-        rights = [right] + [lax.ppermute(right, "row", [(k, k ^ s) for k in range(n)]) for s in range(1, n)]
+        near = lax.optimization_barrier((right, lefts[1]))[0]
+        rights = direct(right, lax.optimization_barrier((right, lefts[1]))[0])
         gating = call(gate_kernel, "gate", broad, [], pair, table, weights)
         rights, mixed = call(
             functools.partial(middle_kernel, n, t),

time: 52.8 us -> 51.2 us (0.970)
  waiting for transfers between devices: 13.7 us -> 7.85 us
  starting transfers between devices: 17.2 us -> 21.5 us
    ppermute x9 -> x6, waiting for transfers between devices: 9.39 us -> 3.56 us  [gather(): held[s ^ step] = lax.ppermute(part, axis, [(k, k ^ step) for k in range(n)])]
    ppermute x3 -> x6, starting transfers between devices: 1.92 us -> 7.29 us  [direct(): lax.ppermute(near if s == 1 else block, 'row', [(k, k ^ s) for k in range...]
    ppermute x9 -> x6, starting transfers between devices: 13.8 us -> 12.7 us  [gather(): held[s ^ step] = lax.ppermute(part, axis, [(k, k ^ step) for k in range(n)])]
    ppermute x3 -> x6, waiting for transfers between devices: 4.31 us -> 4.29 us  [direct(): lax.ppermute(near if s == 1 else block, 'row', [(k, k ^ s) for k in range...]
where the time goes in v11:
time: 51.2 us; the launch traced here: 50.9 us
  starting transfers between devices  21.5 us (42%)
  Pallas kernels  16.6 us (32%)
  waiting for transfers between devices  7.85 us (15%)
  local copies, waits for them, and re-layouts  4.16 us (8%)
  other arithmetic  0.66 us (1%)
    pallas_call x8, Pallas kernels, call(): pl.pallas_call(kernel, out_shape=outs, scratch_shapes=scratches, input_ou...  16.6 us
    ppermute x6, starting transfers between devices, gather(): held[s ^ step] = lax.ppermute(part, axis, [(k, k ^ step) for k in range(n)])  12.7 us
    ppermute x6, starting transfers between devices, direct(): lax.ppermute(near if s == 1 else block, 'row', [(k, k ^ s) for k in range...  7.29 us
    ppermute x6, waiting for transfers between devices, direct(): lax.ppermute(near if s == 1 else block, 'row', [(k, k ^ s) for k in range...  4.29 us
    ppermute x6, waiting for transfers between devices, gather(): held[s ^ step] = lax.ppermute(part, axis, [(k, k ^ step) for k in range(n)])  3.56 us
    unnamed x8, local copies, waits for them, and re-layouts  1.89 us
    ppermute x1, starting transfers between devices, mirrored(): return lax.ppermute(block, ('row', 'col'), pairs)  1.56 us
    concatenate x1, local copies, waits for them, and re-layouts, per_device(): jnp.concatenate(vectors + [jnp.zeros((TABLE_MASK - 20, width), F32), mask])  1.51 us
  transfers between devices with their start and end apart: 13, of which 5 were waited for; matrix products, arithmetic and copies ran while one was open for 6% of the time, Pallas kernels for 19%

profile of v11, /device:TPU:0, one launch (start us, length us, event | category | flops | bytes accessed | tf_op | source)
XLA Modules:
  0.0 50.9 jit_solution(16306266184184049403)
XLA Ops:
  0.0 1.6 %collective-permute-start.2 = (bf16[576,128]{1,0:T(8,128)(2,1)}, bf16[576,128]{1,0:T(8,128)(2,1)S(1)}, u32[]{:S(2)}, u32[]{:S(2)}) collective-permute-start(bf16[576,128]{1,0:T(8,128)(2,1)} %bitcast.2), channel_id=1, source_target_pairs={{0,0},{1,8},{2,4},{3,12},{4,1},{5,9},{6,5},{7,13},{8,2},{9,10},{10... | collective-permute-start | bytes 442376 | tf_op jit(solution)/shard_map/ppermute | solution.py:240
  1.6 4.5 %collective-permute-start = (bf16[576,128]{1,0:T(8,128)(2,1)}, bf16[576,128]{1,0:T(8,128)(2,1)S(1)}, u32[]{:S(2)}, u32[]{:S(2)}) collective-permute-start(bf16[576,128]{1,0:T(8,128)(2,1)} %bitcast.3), channel_id=1, source_target_pairs={{0,2},{1,3},{2,0},{3,1},{4,6},{5,7},{6,4},{7,5},{8,10},{9,11},{10,... | collective-permute-start | bytes 442376 | tf_op jit(solution)/shard_map/ppermute | solution.py:229
  6.0 2.2 %collective-permute-start.6 = (bf16[576,128]{1,0:T(8,128)(2,1)}, bf16[576,128]{1,0:T(8,128)(2,1)S(1)}, u32[]{:S(2)}, u32[]{:S(2)}) collective-permute-start(bf16[576,128]{1,0:T(8,128)(2,1)} %bitcast.4), channel_id=1, source_target_pairs={{0,1},{1,0},{2,3},{3,2},{4,5},{5,4},{6,7},{7,6},{8,9},{9,8},{10,11... | collective-permute-start | bytes 442376 | tf_op jit(solution)/shard_map/ppermute | solution.py:229
  8.2 0.7 %convert_element_type.3 = f32[96]{0:T(128)S(1)} convert(s32[96]{0:T(128)} %param.11) | non-fusion elementwise | flops 96 | bytes 768 | tf_op jit(solution)/shard_map/convert_element_type | solution.py:262
  8.8 0.7 %reshape.11 = f32[10,128]{1,0:T(8,128)S(1)} reshape(f32[2,640]{1,0:T(2,128)} %param.15) | data formatting | bytes 10240 | tf_op jit(solution)/shard_map/reshape | solution.py:263
  9.5 0.1 broadcast_in_dim.10
  9.6 1.5 %concatenate.3.table.refs_3_.refs_2_.refs_5_ = f32[120,128]{1,0:T(8,128)S(1)} concatenate(f32[2,128]{1,0:T(2,128)} %param.12, f32[2,128]{1,0:T(2,128)} %param.13, f32[2,128]{1,0:T(2,128)} %param.16, f32[2,128]{1,0:T(2,128)} %param.17, f32[2,128]{1,0:T(2,128)} %param.19, f32[10,128]{1,0:T(8,128)S(1)} %reshape.11, f32[4,128]{1,0:T(4,128)S(1)} %broadcast_in_dim.4, ...), dimensions={0} | concatenate | bytes 122880 | tf_op jit(solution)/shard_map/concatenate | solution.py:264
  11.1 0.0 copy-start.1
  11.1 0.9 %copy-done.1 = bf16[24,24,128]{2,1,0:T(8,128)(2,1)S(1)} copy-done((bf16[24,24,128]{2,1,0:T(8,128)(2,1)S(1)}, bf16[24,24,128]{2,1,0:T(8,128)(2,1)}, u32[]{:S(2)}) %copy-start.1) | copy-done | bytes 147480
  12.0 0.0 copy-start.3
  12.0 1.0 %copy-done.3 = bf16[2,128,640]{2,1,0:T(8,128)(2,1)S(1)} copy-done((bf16[2,128,640]{2,1,0:T(8,128)(2,1)S(1)}, bf16[2,128,640]{2,1,0:T(8,128)(2,1)}, u32[]{:S(2)}) %copy-start.3) | copy-done | bytes 327704
  13.0 1.0 %own_sides.1 = (bf16[2,128,640]{2,1,0:T(8,128)(2,1)S(1)}, f32[4,576,128]{2,1,0:T(8,128)S(1)}, f32[4,576,128]{2,1,0:T(8,128)S(1)}, f32[576,128]{1,0:T(8,128)S(1)}) custom-call(bf16[576,128]{1,0:T(8,128)(2,1)S(1)} %bitcast.5, f32[120,128]{1,0:T(8,128)S(1)} %concatenate.3.table.refs_3_.refs_2_.refs_5_, bf16[2,128,640]{2,1,0:T(8,128)(2,1)S(1)} %copy-done.3), custom_call_target="tpu_custom_call" | custom-call | tf_op jit(solution)/shard_map/own_sides/pallas_call | solution.py:250
  14.0 0.0 collective-permute-done.2.refs_2_.refs_1_
  14.0 1.0 %collective-permute-start.4 = (bf16[576,128]{1,0:T(8,128)(2,1)S(1)}, bf16[576,128]{1,0:T(8,128)(2,1)S(1)}, u32[]{:S(2)}, u32[]{:S(2)}) collective-permute-start(bf16[576,128]{1,0:T(8,128)(2,1)S(1)} %collective-permute-done.2.refs_2_.refs_1_), channel_id=1, source_target_pairs={{0,8},{4,12},{8,0},{12,4},{1,9},{5,13},{9,1},{13,5},{2,10},{6,14},... | collective-permute-start | bytes 442376 | tf_op jit(solution)/shard_map/ppermute | solution.py:235
  15.0 2.0 %collective-permute-start.3 = (bf16[576,128]{1,0:T(8,128)(2,1)S(1)}, bf16[576,128]{1,0:T(8,128)(2,1)S(1)}, u32[]{:S(2)}, u32[]{:S(2)}) collective-permute-start(bf16[576,128]{1,0:T(8,128)(2,1)S(1)} %collective-permute-done.2.refs_2_.refs_1_), channel_id=1, source_target_pairs={{0,4},{4,0},{8,12},{12,8},{1,5},{5,1},{9,13},{13,9},{2,6},{6,2},{1... | collective-permute-start | bytes 442376 | tf_op jit(solution)/shard_map/ppermute | solution.py:235
  16.9 2.7 %collective-permute-done.refs_1_ = bf16[576,128]{1,0:T(8,128)(2,1)S(1)} collective-permute-done((bf16[576,128]{1,0:T(8,128)(2,1)}, bf16[576,128]{1,0:T(8,128)(2,1)S(1)}, u32[]{:S(2)}, u32[]{:S(2)}) %collective-permute-start) | collective-permute-done | bytes 147488 | tf_op jit(solution)/shard_map/ppermute | solution.py:229
  19.6 0.0 collective-permute-start.1
  19.6 1.8 %collective-permute-start.5 = (bf16[576,128]{1,0:T(8,128)(2,1)S(1)}, bf16[576,128]{1,0:T(8,128)(2,1)S(1)}, u32[]{:S(2)}, u32[]{:S(2)}) collective-permute-start(bf16[576,128]{1,0:T(8,128)(2,1)S(1)} %collective-permute-done.2.refs_2_.refs_1_), channel_id=1, source_target_pairs={{0,12},{4,8},{8,4},{12,0},{1,13},{5,9},{9,5},{13,1},{2,14},{6,10},... | collective-permute-start | bytes 442376 | tf_op jit(solution)/shard_map/ppermute | solution.py:235
  21.5 0.0 collective-permute-done.6.refs_0_
  21.5 1.5 %row_sides.1 = (f32[4,576,128]{2,1,0:T(8,128)S(1)}, f32[4,576,128]{2,1,0:T(8,128)S(1)}, f32[4,576,128]{2,1,0:T(8,128)S(1)}, f32[4,576,128]{2,1,0:T(8,128)S(1)}) custom-call(bf16[576,128]{1,0:T(8,128)(2,1)S(1)} %collective-permute-done.6.refs_0_, bf16[576,128]{1,0:T(8,128)(2,1)S(1)} %collective-permute-done.refs_1_, ...), custom_call_target="tpu_custom_call", output_to_operand_aliasing={{0}: (5, {}), {1}: (6, {})} | custom-call | tf_op jit(solution)/shard_map/row_sides/pallas_call | solution.py:250
  22.9 0.0 collective-permute-done.4.refs_1_.refs_3_
  22.9 0.0 collective-permute-done.3.refs_0_.refs_2_
  22.9 0.0 copy-start
  22.9 1.0 %column_sides.1 = (f32[4,576,128]{2,1,0:T(8,128)S(1)}, f32[4,576,128]{2,1,0:T(8,128)S(1)}) custom-call(bf16[576,128]{1,0:T(8,128)(2,1)S(1)} %collective-permute-done.3.refs_0_.refs_2_, bf16[576,128]{1,0:T(8,128)(2,1)S(1)} %collective-permute-done.4.refs_1_.refs_3_, ...), custom_call_target="tpu_custom_call", output_to_operand_aliasing={{0}: (4, {}), {1}: (5, {})} | custom-call | tf_op jit(solution)/shard_map/column_sides/pallas_call | solution.py:250
  24.0 0.9 %collective-permute-done.1.refs_0_ = bf16[576,128]{1,0:T(8,128)(2,1)S(1)} collective-permute-done((bf16[576,128]{1,0:T(8,128)(2,1)S(1)}, bf16[576,128]{1,0:T(8,128)(2,1)S(1)}, u32[]{:S(2)}, u32[]{:S(2)}) %collective-permute-start.1) | collective-permute-done | bytes 147488 | tf_op jit(solution)/shard_map/ppermute | solution.py:229
  24.8 0.6 %collective-permute-done.5.refs_4_ = bf16[576,128]{1,0:T(8,128)(2,1)S(1)} collective-permute-done((bf16[576,128]{1,0:T(8,128)(2,1)S(1)}, bf16[576,128]{1,0:T(8,128)(2,1)S(1)}, u32[]{:S(2)}, u32[]{:S(2)}) %collective-permute-start.5) | collective-permute-done | bytes 147488 | tf_op jit(solution)/shard_map/ppermute | solution.py:235
  25.4 0.0 copy-done
  25.4 0.0 copy-start.2
  25.4 5.0 %mirror_end.1 = (bf16[576,128]{1,0:T(8,128)(2,1)S(1)}, f32[4,576,128]{2,1,0:T(8,128)S(1)}, f32[4,576,128]{2,1,0:T(8,128)S(1)}, f32[4,576,128]{2,1,0:T(8,128)S(1)}, f32[4,576,128]{2,1,0:T(8,128)S(1)}) custom-call(bf16[576,128]{1,0:T(8,128)(2,1)S(1)} %collective-permute-done.1.refs_0_, ...), custom_call_target="tpu_custom_call", output_to_operand_aliasing={{1}: (8, {}), {2}: (9, {}), {3}: (10, {}), {4}: (11, {})} | custom-call | tf_op jit(solution)/shard_map/mirror_end/pallas_call | solution.py:250
  30.5 1.8 %collective-permute-start.9 = (bf16[576,128]{1,0:T(8,128)(2,1)S(1)}, bf16[576,128]{1,0:T(8,128)(2,1)S(1)}, u32[]{:S(2)}, u32[]{:S(2)}) collective-permute-start(bf16[576,128]{1,0:T(8,128)(2,1)S(1)} %get-tuple-element.36.refs_0_), channel_id=1, source_target_pairs={{0,1},{1,0},{2,3},{3,2},{4,5},{5,4},{6,7},{7,6},{8,9},{9,8},{10,11... | collective-permute-start | bytes 442376 | tf_op jit(solution)/shard_map/ppermute | solution.py:229
  32.3 1.6 %collective-permute-start.7 = (bf16[576,128]{1,0:T(8,128)(2,1)S(1)}, bf16[576,128]{1,0:T(8,128)(2,1)S(1)}, u32[]{:S(2)}, u32[]{:S(2)}) collective-permute-start(bf16[576,128]{1,0:T(8,128)(2,1)S(1)} %get-tuple-element.36.refs_0_), channel_id=1, source_target_pairs={{0,2},{1,3},{2,0},{3,1},{4,6},{5,7},{6,4},{7,5},{8,10},{9,11},{10,... | collective-permute-start | bytes 442376 | tf_op jit(solution)/shard_map/ppermute | solution.py:229
  33.9 0.0 copy-done.2
  33.9 3.6 %own_end.1 = (bf16[576,128]{1,0:T(8,128)(2,1)S(1)}, bf16[576,128]{1,0:T(8,128)(2,1)S(1)}) custom-call(f32[4,576,128]{2,1,0:T(8,128)S(1)} %get-tuple-element.37.row_l, f32[4,576,128]{2,1,0:T(8,128)S(1)} %get-tuple-element.38.col_r, f32[120,128]{1,0:T(8,128)S(1)} %concatenate.3.table.refs_3_.refs_2_.refs_5_, ...), custom_call_target="tpu_custom_call" | custom-call | tf_op jit(solution)/shard_map/own_end/pallas_call | solution.py:250
  37.5 1.8 %collective-permute-start.12 = (bf16[576,128]{1,0:T(8,128)(2,1)S(1)}, bf16[576,128]{1,0:T(8,128)(2,1)S(1)}, u32[]{:S(2)}, u32[]{:S(2)}) collective-permute-start(bf16[576,128]{1,0:T(8,128)(2,1)S(1)} %get-tuple-element.41.refs_3_), channel_id=1, source_target_pairs={{0,12},{4,8},{8,4},{12,0},{1,13},{5,9},{9,5},{13,1},{2,14},{6,10},... | collective-permute-start | bytes 442376 | tf_op jit(solution)/shard_map/ppermute | solution.py:235
  39.4 0.6 %collective-permute-start.11 = (bf16[576,128]{1,0:T(8,128)(2,1)S(1)}, bf16[576,128]{1,0:T(8,128)(2,1)S(1)}, u32[]{:S(2)}, u32[]{:S(2)}) collective-permute-start(bf16[576,128]{1,0:T(8,128)(2,1)S(1)} %get-tuple-element.41.refs_3_), channel_id=1, source_target_pairs={{0,8},{4,12},{8,0},{12,4},{1,9},{5,13},{9,1},{13,5},{2,10},{6,14},... | collective-permute-start | bytes 442376 | tf_op jit(solution)/shard_map/ppermute | solution.py:235
  40.0 0.0 collective-permute-done.9.refs_1_
  40.0 0.0 collective-permute-start.10
  40.0 0.0 collective-permute-done.7.refs_2_
  40.0 2.6 %collective-permute-start.8 = (bf16[576,128]{1,0:T(8,128)(2,1)S(1)}, bf16[576,128]{1,0:T(8,128)(2,1)S(1)}, u32[]{:S(2)}, u32[]{:S(2)}) collective-permute-start(bf16[576,128]{1,0:T(8,128)(2,1)S(1)} %collective-permute-done.7.refs_2_), channel_id=1, source_target_pairs={{0,1},{1,0},{2,3},{3,2},{4,5},{5,4},{6,7},{7,6},{8,9},{9,8},{10,11... | collective-permute-start | bytes 442376 | tf_op jit(solution)/shard_map/ppermute | solution.py:229
  42.7 0.5 %gate.1.gating = f32[576,128]{1,0:T(8,128)S(1)} custom-call(bf16[576,128]{1,0:T(8,128)(2,1)S(1)} %get-tuple-element.44.pair, f32[120,128]{1,0:T(8,128)S(1)} %concatenate.3.table.refs_3_.refs_2_.refs_5_, bf16[2,128,640]{2,1,0:T(8,128)(2,1)S(1)} %get-tuple-element.28.refs_4_.refs_3_.refs_6_.weights), custom_call_target="tpu_custom_call" | custom-call | tf_op jit(solution)/shard_map/gate/pallas_call | solution.py:250
  43.2 0.4 collective-permute-done.12.refs_6_
  43.6 3.3 %collective-permute-done.11.refs_5_ = bf16[576,128]{1,0:T(8,128)(2,1)S(1)} collective-permute-done((bf16[576,128]{1,0:T(8,128)(2,1)S(1)}, bf16[576,128]{1,0:T(8,128)(2,1)S(1)}, u32[]{:S(2)}, u32[]{:S(2)}) %collective-permute-start.11) | collective-permute-done | bytes 147488 | tf_op jit(solution)/shard_map/ppermute | solution.py:235
  46.9 0.0 collective-permute-done.10.refs_4_
  46.9 2.1 %middle_slots.1 = (f32[4,576,128]{2,1,0:T(8,128)S(1)}, f32[576,128]{1,0:T(8,128)S(1)}) custom-call(bf16[576,128]{1,0:T(8,128)(2,1)S(1)} %get-tuple-element.36.refs_0_, bf16[576,128]{1,0:T(8,128)(2,1)S(1)} %collective-permute-done.9.refs_1_, bf16[576,128]{1,0:T(8,128)(2,1)S(1)} %collective-permute-done.7.refs_2_, ...), custom_call_target="tpu_custom_call" | custom-call | tf_op jit(solution)/shard_map/middle_slots/pallas_call | solution.py:250
  49.0 0.0 collective-permute-done.8.block
  49.1 1.9 %end.1 = bf16[576,128]{1,0:T(8,128)(2,1)} custom-call(bf16[576,128]{1,0:T(8,128)(2,1)S(1)} %collective-permute-done.8.block, f32[4,576,128]{2,1,0:T(8,128)S(1)} %get-tuple-element.42.rights, f32[576,128]{1,0:T(8,128)S(1)} %get-tuple-element.43.old, bf16[576,128]{1,0:T(8,128)(2,1)S(1)} %get-tuple-element.44.pair, f32[576,128]{1,0:T(8,128)S(1)} %gate.1.gating, ...), custom_call_target="tpu_custom_call" | custom-call | tf_op jit(solution)/shard_map/end/pallas_call | solution.py:250
  (1 shorter events, 0.0 us)
Async XLA Ops:
  0.0 14.0 %collective-permute-start.2 = (bf16[576,128]{1,0:T(8,128)(2,1)}, bf16[576,128]{1,0:T(8,128)(2,1)S(1)}, u32[]{:S(2)}, u32[]{:S(2)}) collective-permute-start(bf16[576,128]{1,0:T(8,128)(2,1)} %bitcast.2), channel_id=1, source_target_pairs={{0,0},{1,8},{2,4},{3,12},{4,1},{5,9},{6,5},{7,13},{8,2},{9,10},{10... | collective-permute-start | bytes 442376 | tf_op jit(solution)/shard_map/ppermute | solution.py:240
  1.6 18.1 %collective-permute-start = (bf16[576,128]{1,0:T(8,128)(2,1)}, bf16[576,128]{1,0:T(8,128)(2,1)S(1)}, u32[]{:S(2)}, u32[]{:S(2)}) collective-permute-start(bf16[576,128]{1,0:T(8,128)(2,1)} %bitcast.3), channel_id=1, source_target_pairs={{0,2},{1,3},{2,0},{3,1},{4,6},{5,7},{6,4},{7,5},{8,10},{9,11},{10,... | collective-permute-start | bytes 442376 | tf_op jit(solution)/shard_map/ppermute | solution.py:229
  6.0 15.4 %collective-permute-start.6 = (bf16[576,128]{1,0:T(8,128)(2,1)}, bf16[576,128]{1,0:T(8,128)(2,1)S(1)}, u32[]{:S(2)}, u32[]{:S(2)}) collective-permute-start(bf16[576,128]{1,0:T(8,128)(2,1)} %bitcast.4), channel_id=1, source_target_pairs={{0,1},{1,0},{2,3},{3,2},{4,5},{5,4},{6,7},{7,6},{8,9},{9,8},{10,11... | collective-permute-start | bytes 442376 | tf_op jit(solution)/shard_map/ppermute | solution.py:229
  11.1 0.9 %copy-start.1 = (bf16[24,24,128]{2,1,0:T(8,128)(2,1)S(1)}, bf16[24,24,128]{2,1,0:T(8,128)(2,1)}, u32[]{:S(2)}) copy-start(bf16[24,24,128]{2,1,0:T(8,128)(2,1)} %param.10) | copy-start | bytes 442372
  12.0 1.0 %copy-start.3 = (bf16[2,128,640]{2,1,0:T(8,128)(2,1)S(1)}, bf16[2,128,640]{2,1,0:T(8,128)(2,1)}, u32[]{:S(2)}) copy-start(bf16[2,128,640]{2,1,0:T(8,128)(2,1)} %w_in.1) | copy-start | bytes 983044
  14.0 8.9 %collective-permute-start.4 = (bf16[576,128]{1,0:T(8,128)(2,1)S(1)}, bf16[576,128]{1,0:T(8,128)(2,1)S(1)}, u32[]{:S(2)}, u32[]{:S(2)}) collective-permute-start(bf16[576,128]{1,0:T(8,128)(2,1)S(1)} %collective-permute-done.2.refs_2_.refs_1_), channel_id=1, source_target_pairs={{0,8},{4,12},{8,0},{12,4},{1,9},{5,13},{9,1},{13,5},{2,10},{6,14},... | collective-permute-start | bytes 442376 | tf_op jit(solution)/shard_map/ppermute | solution.py:235
  15.0 8.0 %collective-permute-start.3 = (bf16[576,128]{1,0:T(8,128)(2,1)S(1)}, bf16[576,128]{1,0:T(8,128)(2,1)S(1)}, u32[]{:S(2)}, u32[]{:S(2)}) collective-permute-start(bf16[576,128]{1,0:T(8,128)(2,1)S(1)} %collective-permute-done.2.refs_2_.refs_1_), channel_id=1, source_target_pairs={{0,4},{4,0},{8,12},{12,8},{1,5},{5,1},{9,13},{13,9},{2,6},{6,2},{1... | collective-permute-start | bytes 442376 | tf_op jit(solution)/shard_map/ppermute | solution.py:235
  19.6 5.2 %collective-permute-start.1 = (bf16[576,128]{1,0:T(8,128)(2,1)S(1)}, bf16[576,128]{1,0:T(8,128)(2,1)S(1)}, u32[]{:S(2)}, u32[]{:S(2)}) collective-permute-start(bf16[576,128]{1,0:T(8,128)(2,1)S(1)} %collective-permute-done.refs_1_), channel_id=1, source_target_pairs={{0,1},{1,0},{2,3},{3,2},{4,5},{5,4},{6,7},{7,6},{8,9},{9,8},{10,11... | collective-permute-start | bytes 442376 | tf_op jit(solution)/shard_map/ppermute | solution.py:229
  19.6 5.8 %collective-permute-start.5 = (bf16[576,128]{1,0:T(8,128)(2,1)S(1)}, bf16[576,128]{1,0:T(8,128)(2,1)S(1)}, u32[]{:S(2)}, u32[]{:S(2)}) collective-permute-start(bf16[576,128]{1,0:T(8,128)(2,1)S(1)} %collective-permute-done.2.refs_2_.refs_1_), channel_id=1, source_target_pairs={{0,12},{4,8},{8,4},{12,0},{1,13},{5,9},{9,5},{13,1},{2,14},{6,10},... | collective-permute-start | bytes 442376 | tf_op jit(solution)/shard_map/ppermute | solution.py:235
  22.9 2.5 %copy-start = (bf16[2,128,128]{2,1,0:T(8,128)(2,1)S(1)}, bf16[2,128,128]{2,1,0:T(8,128)(2,1)}, u32[]{:S(2)}) copy-start(bf16[2,128,128]{2,1,0:T(8,128)(2,1)} %w_out.3) | copy-start | bytes 196612
  25.4 8.4 %copy-start.2 = (bf16[24,24,128]{2,1,0:T(8,128)(2,1)S(1)}, bf16[24,24,128]{2,1,0:T(8,128)(2,1)}, u32[]{:S(2)}) copy-start(bf16[24,24,128]{2,1,0:T(8,128)(2,1)} %param.10) | copy-start | bytes 442372
  30.5 9.5 %collective-permute-start.9 = (bf16[576,128]{1,0:T(8,128)(2,1)S(1)}, bf16[576,128]{1,0:T(8,128)(2,1)S(1)}, u32[]{:S(2)}, u32[]{:S(2)}) collective-permute-start(bf16[576,128]{1,0:T(8,128)(2,1)S(1)} %get-tuple-element.36.refs_0_), channel_id=1, source_target_pairs={{0,1},{1,0},{2,3},{3,2},{4,5},{5,4},{6,7},{7,6},{8,9},{9,8},{10,11... | collective-permute-start | bytes 442376 | tf_op jit(solution)/shard_map/ppermute | solution.py:229
  32.3 7.8 %collective-permute-start.7 = (bf16[576,128]{1,0:T(8,128)(2,1)S(1)}, bf16[576,128]{1,0:T(8,128)(2,1)S(1)}, u32[]{:S(2)}, u32[]{:S(2)}) collective-permute-start(bf16[576,128]{1,0:T(8,128)(2,1)S(1)} %get-tuple-element.36.refs_0_), channel_id=1, source_target_pairs={{0,2},{1,3},{2,0},{3,1},{4,6},{5,7},{6,4},{7,5},{8,10},{9,11},{10,... | collective-permute-start | bytes 442376 | tf_op jit(solution)/shard_map/ppermute | solution.py:229
  37.5 6.1 %collective-permute-start.12 = (bf16[576,128]{1,0:T(8,128)(2,1)S(1)}, bf16[576,128]{1,0:T(8,128)(2,1)S(1)}, u32[]{:S(2)}, u32[]{:S(2)}) collective-permute-start(bf16[576,128]{1,0:T(8,128)(2,1)S(1)} %get-tuple-element.41.refs_3_), channel_id=1, source_target_pairs={{0,12},{4,8},{8,4},{12,0},{1,13},{5,9},{9,5},{13,1},{2,14},{6,10},... | collective-permute-start | bytes 442376 | tf_op jit(solution)/shard_map/ppermute | solution.py:235
  39.4 7.6 %collective-permute-start.11 = (bf16[576,128]{1,0:T(8,128)(2,1)S(1)}, bf16[576,128]{1,0:T(8,128)(2,1)S(1)}, u32[]{:S(2)}, u32[]{:S(2)}) collective-permute-start(bf16[576,128]{1,0:T(8,128)(2,1)S(1)} %get-tuple-element.41.refs_3_), channel_id=1, source_target_pairs={{0,8},{4,12},{8,0},{12,4},{1,9},{5,13},{9,1},{13,5},{2,10},{6,14},... | collective-permute-start | bytes 442376 | tf_op jit(solution)/shard_map/ppermute | solution.py:235
  40.0 6.9 %collective-permute-start.10 = (bf16[576,128]{1,0:T(8,128)(2,1)S(1)}, bf16[576,128]{1,0:T(8,128)(2,1)S(1)}, u32[]{:S(2)}, u32[]{:S(2)}) collective-permute-start(bf16[576,128]{1,0:T(8,128)(2,1)S(1)} %get-tuple-element.41.refs_3_), channel_id=1, source_target_pairs={{0,4},{4,0},{8,12},{12,8},{1,5},{5,1},{9,13},{13,9},{2,6},{6,2},{1... | collective-permute-start | bytes 442376 | tf_op jit(solution)/shard_map/ppermute | solution.py:235
  40.0 9.0 %collective-permute-start.8 = (bf16[576,128]{1,0:T(8,128)(2,1)S(1)}, bf16[576,128]{1,0:T(8,128)(2,1)S(1)}, u32[]{:S(2)}, u32[]{:S(2)}) collective-permute-start(bf16[576,128]{1,0:T(8,128)(2,1)S(1)} %collective-permute-done.7.refs_2_), channel_id=1, source_target_pairs={{0,1},{1,0},{2,3},{3,2},{4,5},{5,4},{6,7},{7,6},{8,9},{9,8},{10,11... | collective-permute-start | bytes 442376 | tf_op jit(solution)/shard_map/ppermute | solution.py:229

commit v12 on v10

--- a/solution.py
+++ b/solution.py
@@ -128,6 +128,14 @@
     return lax.rem(r, n // 2) * 2 + r // (n // 2)
 
 
+def early_pairs(late, n):
+    return jnp.where(late == n - 1, n - 1, n - 2), lambda i: i + jnp.where(i >= late, 1, 0)
+
+
+def late_pairs(late, n):
+    return jnp.where(late == n - 1, 1, 2), lambda i: jnp.where(i == 0, n - 1, late)
+
+
 def own_kernel(t, pair, table, w_in, weights, row_l, row_r, gating, wide):
     r, c = lax.axis_index("row"), lax.axis_index("col")
     consts = constants(wide.shape[1])
@@ -150,19 +158,22 @@
         sides(block, wide, row_l.at[s], row_r.at[s], outer, here, consts, table, weights)
 
 
-def columns_kernel(t, count, *refs):
-    blocks, (table, weights) = refs[:count], refs[count : count + 2]
-    col_l, col_r, wide = refs[count + 4 :]
+def columns_kernel(n, t, *refs):
+    blocks, (table, weights, row_r) = refs[: n - 2], refs[n - 2 : n + 1]
+    col_l, col_r, mixed, wide = refs[n + 3 :]
     r, c = lax.axis_index("row"), lax.axis_index("col")
     consts = constants(wide.shape[1])
     for s, block in enumerate(blocks, 1):
-        outer, inner = mask_of(table, placed_at(r ^ s, count + 2), t), mask_of(table, c, t)
+        outer, inner = mask_of(table, placed_at(r ^ s, n), t), mask_of(table, c, t)
         sides(block, wide, col_l.at[s], col_r.at[s], outer, inner, consts, table, weights)
+    count, slot = early_pairs(c ^ placed_at(r ^ (n - 1), n), n)
+    mix(mixed, None, col_l, row_r, 0, count, lambda i: r ^ place(c ^ slot(i), n), slot, t)
 
 
 def mirror_kernel(n, t, *refs):
     row, cols, (table, weights, w_out) = refs[0], refs[1 : n + 1], refs[n + 1 : n + 4]
-    left_ref, row_l, row_r, col_l, col_r, mixed, wide, held = refs[n + 8 :]
+    old = refs[n + 8]
+    left_ref, row_l, row_r, col_l, col_r, mixed, wide, held = refs[n + 9 :]
     width = wide.shape[1]
     r, c = lax.axis_index("row"), lax.axis_index("col")
     consts = constants(width)
@@ -173,7 +184,8 @@
     ):
         outer = mask_of(table, outer, t)
         sides(block, wide, left.at[n - 1], right.at[n - 1], outer, inner, consts, table, weights)
-    mix(mixed, None, col_l, row_r, 0, n, lambda s: r ^ place(c ^ s, n), lambda s: s, t)
+    count, slot = late_pairs(c ^ placed_at(r ^ (n - 1), n), n)
+    mix(mixed, old, col_l, row_r, 0, count, lambda i: r ^ place(c ^ slot(i), n), slot, t)
     for s in range(n):
         held[s] = cols[s][...]
     pair = held[r ^ place(r, n)]
@@ -199,21 +211,26 @@
     gating[...] = gate_of(pair[...], constants(pair.shape[1]), table, weights, 1)
 
 
+def left_kernel(n, *refs):
+    for s in range(n - 1):
+        refs[n - 1][s] = refs[s][...].astype(F32)
+
+
 def middle_kernel(n, t, *refs):
-    blocks, sources = refs[: n - 1], refs[n - 1 : 2 * n - 1]
-    rights, mixed, lefts = refs[2 * n - 1 :]
+    sources, (lefts, rights, mixed) = refs[: n - 1], refs[n - 1 :]
     r, c = lax.axis_index("row"), lax.axis_index("col")
     for s in range(n - 1):
-        lefts[s] = blocks[s][...].astype(F32)
-    for s in range(n):
         rights[s] = sources[s][...].astype(F32)
-    mix(mixed, None, lefts, rights, 0, n - 1, lambda s: s, lambda s: r ^ c ^ s, t)
-
-
-def end_kernel(n, t, block, rights, old, pair, gating, table, w_out, out, mixed, left):
-    r, c = lax.axis_index("row"), lax.axis_index("col")
-    left[0] = block[...].astype(F32)
-    mix(mixed, old, left, rights, 0, 1, lambda s: s, lambda s: r ^ c ^ (n - 1), t)
+    count, slot = early_pairs(r ^ c ^ (n - 1), n)
+    mix(mixed, None, lefts, rights, 0, count, slot, lambda i: r ^ c ^ slot(i), t)
+
+
+def end_kernel(n, t, left, right, old, pair, gating, table, w_out, left_in, right_in, out, lefts, rights, mixed):
+    r, c = lax.axis_index("row"), lax.axis_index("col")
+    lefts[n - 1] = left[...].astype(F32)
+    rights[n - 1] = right[...].astype(F32)
+    count, slot = late_pairs(r ^ c ^ (n - 1), n)
+    mix(mixed, old, lefts, rights, 0, count, slot, lambda i: r ^ c ^ slot(i), t)
     consts = constants(mixed.shape[1])
     out[...] = finish(pair[...], mixed[...], gating[...], consts, *out_norm(table, 1), w_out[1], table[9:10])
 
@@ -221,14 +238,17 @@
 def solution(mesh):
     n = mesh.shape["col"]
 
-    def gather(block, axis, after=lambda block: block):
+    def gather(block, axis, after):
         held, step = {0: block}, n // 2
         while step:
             for s, part in list(held.items()):
-                part = after(part) if s else part
+                part = lax.optimization_barrier((part, after(s, step)))[0]
                 held[s ^ step] = lax.ppermute(part, axis, [(k, k ^ step) for k in range(n)])
             step //= 2
         return [held[s] for s in range(n)]
+
+    def direct(block):
+        return [block] + [lax.ppermute(block, "row", [(k, k ^ s) for k in range(n)]) for s in range(1, n)]
 
     def mirrored(block):
         pairs = [(a * n + z, (z // 2 + z % 2 * (n // 2)) * n + a) for a in range(n) for z in range(n)]
@@ -241,12 +261,15 @@
         slots = jax.ShapeDtypeStruct((n,) + area, F32)
         scratch = pltpu.VMEM(area, F32)
 
-        def call(kernel, name, outs, scratches, *operands, alias=None, **specs):
+        def call(kernel, name, outs, scratches, *operands, alias=None, weight=0):
             return pl.pallas_call(
                 kernel,
                 out_shape=outs,
                 scratch_shapes=scratches,
                 input_output_aliases=alias or {},
+                cost_estimate=pl.CostEstimate(
+                    flops=weight * 10**9, bytes_accessed=weight * 10**6, transcendentals=0
+                ) if weight else None,
 
                 compiler_params=pltpu.CompilerParams(vmem_limit_bytes=(16 + n) * 1024 * 1024),
                 name=name,
@@ -267,7 +290,7 @@
             w_in,
         )
         own_l = row_l
-        rows = gather(pair, "col", lambda block: lax.optimization_barrier((block, own_l))[0])
+        rows = gather(pair, "col", lambda s, step: own_l if s else ())
         row_l, row_r, col_l, col_r = call(
             functools.partial(rows_kernel, t, n - 2),
             "row_sides",
@@ -281,19 +304,19 @@
             row_r,
             alias={n + 1: 0, n + 2: 1},
         )
-        ready = lax.optimization_barrier((col_block, rows[1], rows[n // 2], own_l))[0]
-        cols = gather(ready, "row", lambda block: lax.optimization_barrier((block, row_l))[0])
-        col_l, col_r = call(
-            functools.partial(columns_kernel, t, n - 2),
+        cols = direct(lax.optimization_barrier((col_block, own_l))[0])
+        col_l, col_r, mixed = call(
+            functools.partial(columns_kernel, n, t),
             "column_sides",
-            (slots, slots),
+            (slots, slots, broad),
             [scratch],
             *cols[1:-1],
             table,
             weights,
+            row_r,
             col_l,
             col_r,
-            alias={n: 0, n + 1: 1},
+            alias={n + 1: 0, n + 2: 1},
         )
         left, row_l, _, _, col_r = call(
             functools.partial(mirror_kernel, n, t),
@@ -309,6 +332,7 @@
             row_r,
             col_l,
             col_r,
+            mixed,
             alias={n + 4: 1, n + 5: 2, n + 6: 3, n + 7: 4},
         )
         pair, right = call(
@@ -324,29 +348,28 @@
             gating,
             w_out,
         )
-        lefts = gather(left, "col")
-        rights = [right] + [lax.ppermute(right, "row", [(k, k ^ s) for k in range(n)]) for s in range(1, n)]
+        lefts = gather(left, "col", lambda s, step: ())
+        left_slots = call(functools.partial(left_kernel, n), "left_slots", slots, [], *lefts[:-1], weight=20)
+        rights = gather(right, "row", lambda s, step: left_slots if s else lefts[1] if step == 1 else ())
         gating = call(gate_kernel, "gate", broad, [], pair, table, weights)
-        rights, mixed = call(
-            functools.partial(middle_kernel, n, t),
-            "middle_slots",
-            (slots, broad),
-            [pltpu.VMEM((n - 1,) + area, F32)],
-            *lefts[:-1],
-            *rights,
-        )
-        out = call(
+        right_slots, mixed = call(
+            functools.partial(middle_kernel, n, t), "middle_slots", (slots, broad), [], *rights[:-1], left_slots
+        )
+        out, _, _ = call(
             functools.partial(end_kernel, n, t),
             "end",
-            narrow,
-            [scratch, pltpu.VMEM((1,) + area, F32)],
+            (narrow, slots, slots),
+            [scratch],
             lefts[-1],
-            rights,
+            rights[-1],
             mixed,
             pair,
             gating,
             table,
             w_out,
+            left_slots,
+            right_slots,
+            alias={7: 1, 8: 2},
         )
         return out.reshape(t, t, width)
 

time: 52.8 us -> 47.9 us (0.907)
  waiting for transfers between devices: 13.7 us -> 3.57 us
  starting transfers between devices: 17.2 us -> 21.9 us
    ppermute x9, waiting for transfers between devices: 9.39 us -> 3.56 us  [gather(): held[s ^ step] = lax.ppermute(part, axis, [(k, k ^ step) for k in range(n)])]
    ppermute x3, waiting for transfers between devices: 4.31 us -> 0.01 us  [direct(): lax.ppermute(block, 'row', [(k, k ^ s) for k in range(n)])]
    ppermute x3, starting transfers between devices: 1.92 us -> 4.78 us  [direct(): lax.ppermute(block, 'row', [(k, k ^ s) for k in range(n)])]
    ppermute x9, starting transfers between devices: 13.8 us -> 15.5 us  [gather(): held[s ^ step] = lax.ppermute(part, axis, [(k, k ^ step) for k in range(n)])]
    pallas_call x8 -> x9, Pallas kernels: 16.6 us -> 16.8 us  [call(): pl.pallas_call(kernel, out_shape=outs, scratch_shapes=scratches, input_ou...]
  transfers between devices with their start and end apart: 13 -> 13, of which waited for: 5 -> 3; matrix products, arithmetic and copies ran while one was open for 6% -> 6% of each run, Pallas kernels for 19% -> 25%
where the time goes in v12:
time: 47.9 us; the launch traced here: 47.2 us
  starting transfers between devices  21.9 us (46%)
  Pallas kernels  16.8 us (35%)
  local copies, waits for them, and re-layouts  4.17 us (9%)
  waiting for transfers between devices  3.57 us (7%)
  other arithmetic  0.66 us (1%)
    pallas_call x9, Pallas kernels, call(): pl.pallas_call(kernel, out_shape=outs, scratch_shapes=scratches, input_ou...  16.8 us
    ppermute x9, starting transfers between devices, gather(): held[s ^ step] = lax.ppermute(part, axis, [(k, k ^ step) for k in range(n)])  15.5 us
    ppermute x3, starting transfers between devices, direct(): lax.ppermute(block, 'row', [(k, k ^ s) for k in range(n)])  4.78 us
    ppermute x9, waiting for transfers between devices, gather(): held[s ^ step] = lax.ppermute(part, axis, [(k, k ^ step) for k in range(n)])  3.56 us
    unnamed x8, local copies, waits for them, and re-layouts  1.89 us
    ppermute x1, starting transfers between devices, mirrored(): return lax.ppermute(block, ('row', 'col'), pairs)  1.56 us
    concatenate x1, local copies, waits for them, and re-layouts, per_device(): jnp.concatenate(vectors + [jnp.zeros((TABLE_MASK - 20, width), F32), mask])  1.51 us
  transfers between devices with their start and end apart: 13, of which 3 were waited for; matrix products, arithmetic and copies ran while one was open for 6% of the time, Pallas kernels for 25%

profile of v12, /device:TPU:0, one launch (start us, length us, event | category | flops | bytes accessed | tf_op | source)
XLA Modules:
  0.0 47.2 jit_solution(6973568291756783597)
XLA Ops:
  0.0 1.6 %collective-permute-start.2 = (bf16[576,128]{1,0:T(8,128)(2,1)}, bf16[576,128]{1,0:T(8,128)(2,1)S(1)}, u32[]{:S(2)}, u32[]{:S(2)}) collective-permute-start(bf16[576,128]{1,0:T(8,128)(2,1)} %bitcast.2), channel_id=1, source_target_pairs={{0,0},{1,8},{2,4},{3,12},{4,1},{5,9},{6,5},{7,13},{8,2},{9,10},{10... | collective-permute-start | bytes 442376 | tf_op jit(solution)/shard_map/ppermute | solution.py:255
  1.6 4.5 %collective-permute-start = (bf16[576,128]{1,0:T(8,128)(2,1)}, bf16[576,128]{1,0:T(8,128)(2,1)S(1)}, u32[]{:S(2)}, u32[]{:S(2)}) collective-permute-start(bf16[576,128]{1,0:T(8,128)(2,1)} %bitcast.3), channel_id=1, source_target_pairs={{0,2},{1,3},{2,0},{3,1},{4,6},{5,7},{6,4},{7,5},{8,10},{9,11},{10,... | collective-permute-start | bytes 442376 | tf_op jit(solution)/shard_map/ppermute | solution.py:246
  6.0 2.2 %collective-permute-start.6 = (bf16[576,128]{1,0:T(8,128)(2,1)}, bf16[576,128]{1,0:T(8,128)(2,1)S(1)}, u32[]{:S(2)}, u32[]{:S(2)}) collective-permute-start(bf16[576,128]{1,0:T(8,128)(2,1)} %bitcast.4), channel_id=1, source_target_pairs={{0,1},{1,0},{2,3},{3,2},{4,5},{5,4},{6,7},{7,6},{8,9},{9,8},{10,11... | collective-permute-start | bytes 442376 | tf_op jit(solution)/shard_map/ppermute | solution.py:246
  8.2 0.7 %convert_element_type.3 = f32[96]{0:T(128)S(1)} convert(s32[96]{0:T(128)} %param.11) | non-fusion elementwise | flops 96 | bytes 768 | tf_op jit(solution)/shard_map/convert_element_type | solution.py:280
  8.8 0.7 %reshape.11 = f32[10,128]{1,0:T(8,128)S(1)} reshape(f32[2,640]{1,0:T(2,128)} %param.15) | data formatting | bytes 10240 | tf_op jit(solution)/shard_map/reshape | solution.py:281
  9.5 0.1 broadcast_in_dim.10
  9.6 1.5 %concatenate.3.table.refs_3_.refs_2_.refs_5_ = f32[120,128]{1,0:T(8,128)S(1)} concatenate(f32[2,128]{1,0:T(2,128)} %param.12, f32[2,128]{1,0:T(2,128)} %param.13, f32[2,128]{1,0:T(2,128)} %param.16, f32[2,128]{1,0:T(2,128)} %param.17, f32[2,128]{1,0:T(2,128)} %param.19, f32[10,128]{1,0:T(8,128)S(1)} %reshape.11, f32[4,128]{1,0:T(4,128)S(1)} %broadcast_in_dim.4, ...), dimensions={0} | concatenate | bytes 122880 | tf_op jit(solution)/shard_map/concatenate | solution.py:282
  11.1 0.0 copy-start.1
  11.1 0.9 %copy-done.1 = bf16[24,24,128]{2,1,0:T(8,128)(2,1)S(1)} copy-done((bf16[24,24,128]{2,1,0:T(8,128)(2,1)S(1)}, bf16[24,24,128]{2,1,0:T(8,128)(2,1)}, u32[]{:S(2)}) %copy-start.1) | copy-done | bytes 147480
  12.0 0.0 copy-start.3
  12.0 1.0 %copy-done.3 = bf16[2,128,640]{2,1,0:T(8,128)(2,1)S(1)} copy-done((bf16[2,128,640]{2,1,0:T(8,128)(2,1)S(1)}, bf16[2,128,640]{2,1,0:T(8,128)(2,1)}, u32[]{:S(2)}) %copy-start.3) | copy-done | bytes 327704
  13.0 1.0 %own_sides.1 = (bf16[2,128,640]{2,1,0:T(8,128)(2,1)S(1)}, f32[4,576,128]{2,1,0:T(8,128)S(1)}, f32[4,576,128]{2,1,0:T(8,128)S(1)}, f32[576,128]{1,0:T(8,128)S(1)}) custom-call(bf16[576,128]{1,0:T(8,128)(2,1)S(1)} %bitcast.5, f32[120,128]{1,0:T(8,128)S(1)} %concatenate.3.table.refs_3_.refs_2_.refs_5_, bf16[2,128,640]{2,1,0:T(8,128)(2,1)S(1)} %copy-done.3), custom_call_target="tpu_custom_call" | custom-call | tf_op jit(solution)/shard_map/own_sides/pallas_call | solution.py:265
  14.0 0.0 collective-permute-done.2.refs_2_.refs_1_
  14.0 1.0 %collective-permute-start.4 = (bf16[576,128]{1,0:T(8,128)(2,1)S(1)}, bf16[576,128]{1,0:T(8,128)(2,1)S(1)}, u32[]{:S(2)}, u32[]{:S(2)}) collective-permute-start(bf16[576,128]{1,0:T(8,128)(2,1)S(1)} %collective-permute-done.2.refs_2_.refs_1_), channel_id=1, source_target_pairs={{0,8},{4,12},{8,0},{12,4},{1,9},{5,13},{9,1},{13,5},{2,10},{6,14},... | collective-permute-start | bytes 442376 | tf_op jit(solution)/shard_map/ppermute | solution.py:251
  15.0 2.0 %collective-permute-start.3 = (bf16[576,128]{1,0:T(8,128)(2,1)S(1)}, bf16[576,128]{1,0:T(8,128)(2,1)S(1)}, u32[]{:S(2)}, u32[]{:S(2)}) collective-permute-start(bf16[576,128]{1,0:T(8,128)(2,1)S(1)} %collective-permute-done.2.refs_2_.refs_1_), channel_id=1, source_target_pairs={{0,4},{4,0},{8,12},{12,8},{1,5},{5,1},{9,13},{13,9},{2,6},{6,2},{1... | collective-permute-start | bytes 442376 | tf_op jit(solution)/shard_map/ppermute | solution.py:251
  16.9 2.7 %collective-permute-done.refs_1_ = bf16[576,128]{1,0:T(8,128)(2,1)S(1)} collective-permute-done((bf16[576,128]{1,0:T(8,128)(2,1)}, bf16[576,128]{1,0:T(8,128)(2,1)S(1)}, u32[]{:S(2)}, u32[]{:S(2)}) %collective-permute-start) | collective-permute-done | bytes 147488 | tf_op jit(solution)/shard_map/ppermute | solution.py:246
  19.6 0.0 collective-permute-start.1
  19.6 1.8 %collective-permute-start.5 = (bf16[576,128]{1,0:T(8,128)(2,1)S(1)}, bf16[576,128]{1,0:T(8,128)(2,1)S(1)}, u32[]{:S(2)}, u32[]{:S(2)}) collective-permute-start(bf16[576,128]{1,0:T(8,128)(2,1)S(1)} %collective-permute-done.2.refs_2_.refs_1_), channel_id=1, source_target_pairs={{0,12},{4,8},{8,4},{12,0},{1,13},{5,9},{9,5},{13,1},{2,14},{6,10},... | collective-permute-start | bytes 442376 | tf_op jit(solution)/shard_map/ppermute | solution.py:251
  21.5 0.0 collective-permute-done.6.refs_0_
  21.5 1.5 %row_sides.1 = (f32[4,576,128]{2,1,0:T(8,128)S(1)}, f32[4,576,128]{2,1,0:T(8,128)S(1)}, f32[4,576,128]{2,1,0:T(8,128)S(1)}, f32[4,576,128]{2,1,0:T(8,128)S(1)}) custom-call(bf16[576,128]{1,0:T(8,128)(2,1)S(1)} %collective-permute-done.6.refs_0_, bf16[576,128]{1,0:T(8,128)(2,1)S(1)} %collective-permute-done.refs_1_, ...), custom_call_target="tpu_custom_call", output_to_operand_aliasing={{0}: (5, {}), {1}: (6, {})} | custom-call | tf_op jit(solution)/shard_map/row_sides/pallas_call | solution.py:265
  22.9 0.0 collective-permute-done.4.refs_1_.refs_3_
  22.9 0.0 collective-permute-done.3.refs_0_.refs_2_
  22.9 0.0 copy-start
  22.9 3.1 %column_sides.1 = (f32[4,576,128]{2,1,0:T(8,128)S(1)}, f32[4,576,128]{2,1,0:T(8,128)S(1)}, f32[576,128]{1,0:T(8,128)S(1)}) custom-call(bf16[576,128]{1,0:T(8,128)(2,1)S(1)} %collective-permute-done.3.refs_0_.refs_2_, bf16[576,128]{1,0:T(8,128)(2,1)S(1)} %collective-permute-done.4.refs_1_.refs_3_, ...), custom_call_target="tpu_custom_call", output_to_operand_aliasing={{0}: (5, {}), {1}: (6, {})} | custom-call | tf_op jit(solution)/shard_map/column_sides/pallas_call | solution.py:265
  26.0 0.0 collective-permute-done.1.refs_0_
  26.0 0.0 collective-permute-done.5.refs_4_
  26.0 0.0 copy-done
  26.1 0.0 copy-start.2
  26.1 3.1 %mirror_end.1 = (bf16[576,128]{1,0:T(8,128)(2,1)S(1)}, f32[4,576,128]{2,1,0:T(8,128)S(1)}, f32[4,576,128]{2,1,0:T(8,128)S(1)}, f32[4,576,128]{2,1,0:T(8,128)S(1)}, f32[4,576,128]{2,1,0:T(8,128)S(1)}) custom-call(bf16[576,128]{1,0:T(8,128)(2,1)S(1)} %collective-permute-done.1.refs_0_, ...), custom_call_target="tpu_custom_call", output_to_operand_aliasing={{1}: (8, {}), {2}: (9, {}), {3}: (10, {}), {4}: (11, {})} | custom-call | tf_op jit(solution)/shard_map/mirror_end/pallas_call | solution.py:265
  29.1 1.8 %collective-permute-start.10 = (bf16[576,128]{1,0:T(8,128)(2,1)S(1)}, bf16[576,128]{1,0:T(8,128)(2,1)S(1)}, u32[]{:S(2)}, u32[]{:S(2)}) collective-permute-start(bf16[576,128]{1,0:T(8,128)(2,1)S(1)} %get-tuple-element.40.refs_0_), channel_id=1, source_target_pairs={{0,1},{1,0},{2,3},{3,2},{4,5},{5,4},{6,7},{7,6},{8,9},{9,8},{10,11... | collective-permute-start | bytes 442376 | tf_op jit(solution)/shard_map/ppermute | solution.py:246
  31.0 1.6 %collective-permute-start.7 = (bf16[576,128]{1,0:T(8,128)(2,1)S(1)}, bf16[576,128]{1,0:T(8,128)(2,1)S(1)}, u32[]{:S(2)}, u32[]{:S(2)}) collective-permute-start(bf16[576,128]{1,0:T(8,128)(2,1)S(1)} %get-tuple-element.40.refs_0_), channel_id=1, source_target_pairs={{0,2},{1,3},{2,0},{3,1},{4,6},{5,7},{6,4},{7,5},{8,10},{9,11},{10,... | collective-permute-start | bytes 442376 | tf_op jit(solution)/shard_map/ppermute | solution.py:246
  32.6 0.0 copy-done.2
  32.6 3.6 %own_end.1 = (bf16[576,128]{1,0:T(8,128)(2,1)S(1)}, bf16[576,128]{1,0:T(8,128)(2,1)S(1)}) custom-call(f32[4,576,128]{2,1,0:T(8,128)S(1)} %get-tuple-element.41.row_l, f32[4,576,128]{2,1,0:T(8,128)S(1)} %get-tuple-element.42.col_r, f32[120,128]{1,0:T(8,128)S(1)} %concatenate.3.table.refs_3_.refs_2_.refs_5_, ...), custom_call_target="tpu_custom_call" | custom-call | tf_op jit(solution)/shard_map/own_end/pallas_call | solution.py:265
  36.2 2.4 %collective-permute-start.9 = (bf16[576,128]{1,0:T(8,128)(2,1)S(1)}, bf16[576,128]{1,0:T(8,128)(2,1)S(1)}, u32[]{:S(2)}, u32[]{:S(2)}) collective-permute-start(bf16[576,128]{1,0:T(8,128)(2,1)S(1)} %get-tuple-element.46.refs_0_), channel_id=1, source_target_pairs={{0,8},{4,12},{8,0},{12,4},{1,9},{5,13},{9,1},{13,5},{2,10},{6,14},... | collective-permute-start | bytes 442376 | tf_op jit(solution)/shard_map/ppermute | solution.py:246
  38.6 0.0 collective-permute-done.10.refs_1_
  38.6 0.0 collective-permute-start.12
  38.6 0.0 collective-permute-done.7.refs_2_
  38.6 3.1 %collective-permute-start.8 = (bf16[576,128]{1,0:T(8,128)(2,1)S(1)}, bf16[576,128]{1,0:T(8,128)(2,1)S(1)}, u32[]{:S(2)}, u32[]{:S(2)}) collective-permute-start(bf16[576,128]{1,0:T(8,128)(2,1)S(1)} %collective-permute-done.7.refs_2_), channel_id=1, source_target_pairs={{0,1},{1,0},{2,3},{3,2},{4,5},{5,4},{6,7},{7,6},{8,9},{9,8},{10,11... | collective-permute-start | bytes 442376 | tf_op jit(solution)/shard_map/ppermute | solution.py:246
  41.7 0.1 left_slots.1.refs_3_.left_in
  41.8 0.7 %collective-permute-done.9.refs_2_ = bf16[576,128]{1,0:T(8,128)(2,1)S(1)} collective-permute-done((bf16[576,128]{1,0:T(8,128)(2,1)S(1)}, bf16[576,128]{1,0:T(8,128)(2,1)S(1)}, u32[]{:S(2)}, u32[]{:S(2)}) %collective-permute-start.9) | collective-permute-done | bytes 147488 | tf_op jit(solution)/shard_map/ppermute | solution.py:246
  42.5 0.0 collective-permute-start.11
  42.5 0.5 %gate.1.gating = f32[576,128]{1,0:T(8,128)S(1)} custom-call(bf16[576,128]{1,0:T(8,128)(2,1)S(1)} %get-tuple-element.48.pair, f32[120,128]{1,0:T(8,128)S(1)} %concatenate.3.table.refs_3_.refs_2_.refs_5_, bf16[2,128,640]{2,1,0:T(8,128)(2,1)S(1)} %get-tuple-element.31.refs_4_.refs_3_.refs_6_.weights), custom_call_target="tpu_custom_call" | custom-call | tf_op jit(solution)/shard_map/gate/pallas_call | solution.py:265
  43.0 0.0 collective-permute-done.12.refs_1_
  43.0 2.1 %middle_slots.1 = (f32[4,576,128]{2,1,0:T(8,128)S(1)}, f32[576,128]{1,0:T(8,128)S(1)}) custom-call(bf16[576,128]{1,0:T(8,128)(2,1)S(1)} %get-tuple-element.46.refs_0_, bf16[576,128]{1,0:T(8,128)(2,1)S(1)} %collective-permute-done.12.refs_1_, bf16[576,128]{1,0:T(8,128)(2,1)S(1)} %collective-permute-done.9.refs_2_, f32[4,576,128]{2,1,0:T(8,128)S(1)} %left_slots.1.refs_3_.left_in), custom_call_target="tpu_custom_call" | custom-call | tf_op jit(solution)/shard_map/middle_slots/pallas_call | solution.py:265
  45.1 0.2 collective-permute-done.8.left
  45.2 0.0 collective-permute-done.11.right
  45.3 1.9 %end.1 = (bf16[576,128]{1,0:T(8,128)(2,1)}, f32[4,576,128]{2,1,0:T(8,128)S(1)}, f32[4,576,128]{2,1,0:T(8,128)S(1)}) custom-call(bf16[576,128]{1,0:T(8,128)(2,1)S(1)} %collective-permute-done.8.left, bf16[576,128]{1,0:T(8,128)(2,1)S(1)} %collective-permute-done.11.right, ...), custom_call_target="tpu_custom_call", output_to_operand_aliasing={{1}: (7, {}), {2}: (8, {})} | custom-call | tf_op jit(solution)/shard_map/end/pallas_call | solution.py:265
  (1 shorter events, 0.0 us)
Async XLA Ops:
  0.0 14.0 %collective-permute-start.2 = (bf16[576,128]{1,0:T(8,128)(2,1)}, bf16[576,128]{1,0:T(8,128)(2,1)S(1)}, u32[]{:S(2)}, u32[]{:S(2)}) collective-permute-start(bf16[576,128]{1,0:T(8,128)(2,1)} %bitcast.2), channel_id=1, source_target_pairs={{0,0},{1,8},{2,4},{3,12},{4,1},{5,9},{6,5},{7,13},{8,2},{9,10},{10... | collective-permute-start | bytes 442376 | tf_op jit(solution)/shard_map/ppermute | solution.py:255
  1.6 18.1 %collective-permute-start = (bf16[576,128]{1,0:T(8,128)(2,1)}, bf16[576,128]{1,0:T(8,128)(2,1)S(1)}, u32[]{:S(2)}, u32[]{:S(2)}) collective-permute-start(bf16[576,128]{1,0:T(8,128)(2,1)} %bitcast.3), channel_id=1, source_target_pairs={{0,2},{1,3},{2,0},{3,1},{4,6},{5,7},{6,4},{7,5},{8,10},{9,11},{10,... | collective-permute-start | bytes 442376 | tf_op jit(solution)/shard_map/ppermute | solution.py:246
  6.0 15.4 %collective-permute-start.6 = (bf16[576,128]{1,0:T(8,128)(2,1)}, bf16[576,128]{1,0:T(8,128)(2,1)S(1)}, u32[]{:S(2)}, u32[]{:S(2)}) collective-permute-start(bf16[576,128]{1,0:T(8,128)(2,1)} %bitcast.4), channel_id=1, source_target_pairs={{0,1},{1,0},{2,3},{3,2},{4,5},{5,4},{6,7},{7,6},{8,9},{9,8},{10,11... | collective-permute-start | bytes 442376 | tf_op jit(solution)/shard_map/ppermute | solution.py:246
  11.1 0.9 %copy-start.1 = (bf16[24,24,128]{2,1,0:T(8,128)(2,1)S(1)}, bf16[24,24,128]{2,1,0:T(8,128)(2,1)}, u32[]{:S(2)}) copy-start(bf16[24,24,128]{2,1,0:T(8,128)(2,1)} %param.10) | copy-start | bytes 442372
  12.0 1.0 %copy-start.3 = (bf16[2,128,640]{2,1,0:T(8,128)(2,1)S(1)}, bf16[2,128,640]{2,1,0:T(8,128)(2,1)}, u32[]{:S(2)}) copy-start(bf16[2,128,640]{2,1,0:T(8,128)(2,1)} %w_in.1) | copy-start | bytes 983044
  14.0 8.9 %collective-permute-start.4 = (bf16[576,128]{1,0:T(8,128)(2,1)S(1)}, bf16[576,128]{1,0:T(8,128)(2,1)S(1)}, u32[]{:S(2)}, u32[]{:S(2)}) collective-permute-start(bf16[576,128]{1,0:T(8,128)(2,1)S(1)} %collective-permute-done.2.refs_2_.refs_1_), channel_id=1, source_target_pairs={{0,8},{4,12},{8,0},{12,4},{1,9},{5,13},{9,1},{13,5},{2,10},{6,14},... | collective-permute-start | bytes 442376 | tf_op jit(solution)/shard_map/ppermute | solution.py:251
  15.0 8.0 %collective-permute-start.3 = (bf16[576,128]{1,0:T(8,128)(2,1)S(1)}, bf16[576,128]{1,0:T(8,128)(2,1)S(1)}, u32[]{:S(2)}, u32[]{:S(2)}) collective-permute-start(bf16[576,128]{1,0:T(8,128)(2,1)S(1)} %collective-permute-done.2.refs_2_.refs_1_), channel_id=1, source_target_pairs={{0,4},{4,0},{8,12},{12,8},{1,5},{5,1},{9,13},{13,9},{2,6},{6,2},{1... | collective-permute-start | bytes 442376 | tf_op jit(solution)/shard_map/ppermute | solution.py:251
  19.6 6.4 %collective-permute-start.1 = (bf16[576,128]{1,0:T(8,128)(2,1)S(1)}, bf16[576,128]{1,0:T(8,128)(2,1)S(1)}, u32[]{:S(2)}, u32[]{:S(2)}) collective-permute-start(bf16[576,128]{1,0:T(8,128)(2,1)S(1)} %collective-permute-done.refs_1_), channel_id=1, source_target_pairs={{0,1},{1,0},{2,3},{3,2},{4,5},{5,4},{6,7},{7,6},{8,9},{9,8},{10,11... | collective-permute-start | bytes 442376 | tf_op jit(solution)/shard_map/ppermute | solution.py:246
  19.6 6.4 %collective-permute-start.5 = (bf16[576,128]{1,0:T(8,128)(2,1)S(1)}, bf16[576,128]{1,0:T(8,128)(2,1)S(1)}, u32[]{:S(2)}, u32[]{:S(2)}) collective-permute-start(bf16[576,128]{1,0:T(8,128)(2,1)S(1)} %collective-permute-done.2.refs_2_.refs_1_), channel_id=1, source_target_pairs={{0,12},{4,8},{8,4},{12,0},{1,13},{5,9},{9,5},{13,1},{2,14},{6,10},... | collective-permute-start | bytes 442376 | tf_op jit(solution)/shard_map/ppermute | solution.py:251
  22.9 3.1 %copy-start = (bf16[2,128,128]{2,1,0:T(8,128)(2,1)S(1)}, bf16[2,128,128]{2,1,0:T(8,128)(2,1)}, u32[]{:S(2)}) copy-start(bf16[2,128,128]{2,1,0:T(8,128)(2,1)} %w_out.3) | copy-start | bytes 196612
  26.1 6.5 %copy-start.2 = (bf16[24,24,128]{2,1,0:T(8,128)(2,1)S(1)}, bf16[24,24,128]{2,1,0:T(8,128)(2,1)}, u32[]{:S(2)}) copy-start(bf16[24,24,128]{2,1,0:T(8,128)(2,1)} %param.10) | copy-start | bytes 442372
  29.1 9.5 %collective-permute-start.10 = (bf16[576,128]{1,0:T(8,128)(2,1)S(1)}, bf16[576,128]{1,0:T(8,128)(2,1)S(1)}, u32[]{:S(2)}, u32[]{:S(2)}) collective-permute-start(bf16[576,128]{1,0:T(8,128)(2,1)S(1)} %get-tuple-element.40.refs_0_), channel_id=1, source_target_pairs={{0,1},{1,0},{2,3},{3,2},{4,5},{5,4},{6,7},{7,6},{8,9},{9,8},{10,11... | collective-permute-start | bytes 442376 | tf_op jit(solution)/shard_map/ppermute | solution.py:246
  31.0 7.7 %collective-permute-start.7 = (bf16[576,128]{1,0:T(8,128)(2,1)S(1)}, bf16[576,128]{1,0:T(8,128)(2,1)S(1)}, u32[]{:S(2)}, u32[]{:S(2)}) collective-permute-start(bf16[576,128]{1,0:T(8,128)(2,1)S(1)} %get-tuple-element.40.refs_0_), channel_id=1, source_target_pairs={{0,2},{1,3},{2,0},{3,1},{4,6},{5,7},{6,4},{7,5},{8,10},{9,11},{10,... | collective-permute-start | bytes 442376 | tf_op jit(solution)/shard_map/ppermute | solution.py:246
  36.2 6.2 %collective-permute-start.9 = (bf16[576,128]{1,0:T(8,128)(2,1)S(1)}, bf16[576,128]{1,0:T(8,128)(2,1)S(1)}, u32[]{:S(2)}, u32[]{:S(2)}) collective-permute-start(bf16[576,128]{1,0:T(8,128)(2,1)S(1)} %get-tuple-element.46.refs_0_), channel_id=1, source_target_pairs={{0,8},{4,12},{8,0},{12,4},{1,9},{5,13},{9,1},{13,5},{2,10},{6,14},... | collective-permute-start | bytes 442376 | tf_op jit(solution)/shard_map/ppermute | solution.py:246
  38.6 4.4 %collective-permute-start.12 = (bf16[576,128]{1,0:T(8,128)(2,1)S(1)}, bf16[576,128]{1,0:T(8,128)(2,1)S(1)}, u32[]{:S(2)}, u32[]{:S(2)}) collective-permute-start(bf16[576,128]{1,0:T(8,128)(2,1)S(1)} %get-tuple-element.46.refs_0_), channel_id=1, source_target_pairs={{0,4},{4,0},{8,12},{12,8},{1,5},{5,1},{9,13},{13,9},{2,6},{6,2},{1... | collective-permute-start | bytes 442376 | tf_op jit(solution)/shard_map/ppermute | solution.py:246
  38.6 6.6 %collective-permute-start.8 = (bf16[576,128]{1,0:T(8,128)(2,1)S(1)}, bf16[576,128]{1,0:T(8,128)(2,1)S(1)}, u32[]{:S(2)}, u32[]{:S(2)}) collective-permute-start(bf16[576,128]{1,0:T(8,128)(2,1)S(1)} %collective-permute-done.7.refs_2_), channel_id=1, source_target_pairs={{0,1},{1,0},{2,3},{3,2},{4,5},{5,4},{6,7},{7,6},{8,9},{9,8},{10,11... | collective-permute-start | bytes 442376 | tf_op jit(solution)/shard_map/ppermute | solution.py:246
  42.5 2.8 %collective-permute-start.11 = (bf16[576,128]{1,0:T(8,128)(2,1)S(1)}, bf16[576,128]{1,0:T(8,128)(2,1)S(1)}, u32[]{:S(2)}, u32[]{:S(2)}) collective-permute-start(bf16[576,128]{1,0:T(8,128)(2,1)S(1)} %collective-permute-done.9.refs_2_), channel_id=1, source_target_pairs={{0,4},{4,0},{8,12},{12,8},{1,5},{5,1},{9,13},{13,9},{2,6},{6,2},{1... | collective-permute-start | bytes 442376 | tf_op jit(solution)/shard_map/ppermute | solution.py:246

commit v13 on v12

--- a/solution.py
+++ b/solution.py
@@ -145,27 +145,28 @@
     gating[...] = gate_of(pair[...], consts, table, weights, 0)
 
 
-def rows_kernel(t, count, *refs):
-    blocks, (col_block, table, weights) = refs[:count], refs[count : count + 3]
-    row_l, row_r, col_l, col_r, wide = refs[count + 5 :]
+def early_kernel(n, t, row, col, table, weights, left_in, right_in, row_l, row_r, col_l, col_r, wide):
     r, c = lax.axis_index("row"), lax.axis_index("col")
     consts = constants(wide.shape[1])
     here, there = mask_of(table, r, t), mask_of(table, c, t)
-    outer = mask_of(table, placed_at(r, count + 2), t)
-    sides(col_block, wide, col_l.at[0], col_r.at[0], outer, there, consts, table, weights)
-    for s, block in enumerate(blocks, 1):
+    outer = mask_of(table, placed_at(r, n), t)
+    sides(col, wide, col_l.at[0], col_r.at[0], outer, there, consts, table, weights)
+    outer = mask_of(table, c ^ 1, t)
+    sides(row, wide, row_l.at[1], row_r.at[1], outer, here, consts, table, weights)
+
+
+def middle_sides_kernel(n, t, *refs):
+    rows, cols, (table, weights) = refs[: n - 3], refs[n - 3 : 2 * n - 5], refs[2 * n - 5 : 2 * n - 3]
+    row_l, row_r, col_l, col_r, mixed, wide = refs[2 * n + 1 :]
+    r, c = lax.axis_index("row"), lax.axis_index("col")
+    consts = constants(wide.shape[1])
+    here, there = mask_of(table, r, t), mask_of(table, c, t)
+    for s, block in enumerate(rows, 2):
         outer = mask_of(table, c ^ s, t)
         sides(block, wide, row_l.at[s], row_r.at[s], outer, here, consts, table, weights)
-
-
-def columns_kernel(n, t, *refs):
-    blocks, (table, weights, row_r) = refs[: n - 2], refs[n - 2 : n + 1]
-    col_l, col_r, mixed, wide = refs[n + 3 :]
-    r, c = lax.axis_index("row"), lax.axis_index("col")
-    consts = constants(wide.shape[1])
-    for s, block in enumerate(blocks, 1):
-        outer, inner = mask_of(table, placed_at(r ^ s, n), t), mask_of(table, c, t)
-        sides(block, wide, col_l.at[s], col_r.at[s], outer, inner, consts, table, weights)
+    for s, block in enumerate(cols, 1):
+        outer = mask_of(table, placed_at(r ^ s, n), t)
+        sides(block, wide, col_l.at[s], col_r.at[s], outer, there, consts, table, weights)
     count, slot = early_pairs(c ^ placed_at(r ^ (n - 1), n), n)
     mix(mixed, None, col_l, row_r, 0, count, lambda i: r ^ place(c ^ slot(i), n), slot, t)
 
@@ -290,33 +291,37 @@
             w_in,
         )
         own_l = row_l
-        rows = gather(pair, "col", lambda s, step: own_l if s else ())
+        near = lax.ppermute(pair, "col", [(k, k ^ 1) for k in range(n)])
         row_l, row_r, col_l, col_r = call(
-            functools.partial(rows_kernel, t, n - 2),
-            "row_sides",
+            functools.partial(early_kernel, n, t),
+            "early_sides",
             (slots,) * 4,
             [scratch],
-            *rows[1:-1],
+            near,
             col_block,
             table,
             weights,
             row_l,
             row_r,
-            alias={n + 1: 0, n + 2: 1},
-        )
+            alias={4: 0, 5: 1},
+        )
+        rows = gather(pair, "col", lambda s, step: row_l if s else ())
+        rows[1] = near
         cols = direct(lax.optimization_barrier((col_block, own_l))[0])
-        col_l, col_r, mixed = call(
-            functools.partial(columns_kernel, n, t),
-            "column_sides",
-            (slots, slots, broad),
-            [scratch],
+        row_l, row_r, col_l, col_r, mixed = call(
+            functools.partial(middle_sides_kernel, n, t),
+            "middle_sides",
+            (slots,) * 4 + (broad,),
+            [scratch],
+            *rows[2:-1],
             *cols[1:-1],
             table,
             weights,
+            row_l,
             row_r,
             col_l,
             col_r,
-            alias={n + 1: 0, n + 2: 1},
+            alias={2 * n - 3: 0, 2 * n - 2: 1, 2 * n - 1: 2, 2 * n: 3},
         )
         left, row_l, _, _, col_r = call(
             functools.partial(mirror_kernel, n, t),
@@ -350,7 +355,7 @@
         )
         lefts = gather(left, "col", lambda s, step: ())
         left_slots = call(functools.partial(left_kernel, n), "left_slots", slots, [], *lefts[:-1], weight=20)
-        rights = gather(right, "row", lambda s, step: left_slots if s else lefts[1] if step == 1 else ())
+        rights = gather(right, "row", lambda s, step: left_slots if s else ())
         gating = call(gate_kernel, "gate", broad, [], pair, table, weights)
         right_slots, mixed = call(
             functools.partial(middle_kernel, n, t), "middle_slots", (slots, broad), [], *rights[:-1], left_slots

time: 47.9 us -> 47.9 us (level)
  waiting for transfers between devices: 3.57 us -> 9.53 us
  starting transfers between devices: 21.9 us -> 16.3 us
    ppermute x9 -> x8, starting transfers between devices: 15.5 us -> 6.23 us  [gather(): held[s ^ step] = lax.ppermute(part, axis, [(k, k ^ step) for k in range(n)])]
    ppermute x0 -> x1, starting transfers between devices: none -> 4.81 us  [per_device(): near = lax.ppermute(pair, 'col', [(k, k ^ 1) for k in range(n)])]
    ppermute x3, waiting for transfers between devices: 0.01 us -> 4.19 us  [direct(): lax.ppermute(block, 'row', [(k, k ^ s) for k in range(n)])]
    ppermute x9 -> x8, waiting for transfers between devices: 3.56 us -> 5.33 us  [gather(): held[s ^ step] = lax.ppermute(part, axis, [(k, k ^ step) for k in range(n)])]
    ppermute x3, starting transfers between devices: 4.78 us -> 3.66 us  [direct(): lax.ppermute(block, 'row', [(k, k ^ s) for k in range(n)])]
    unnamed x8 -> x6, local copies, waits for them, and re-layouts: 1.89 us -> 1.88 us
  transfers between devices with their start and end apart: 13 -> 13, of which waited for: 3 -> 4; matrix products, arithmetic and copies ran while one was open for 6% -> 6% of each run, Pallas kernels for 25% -> 25%
where the time goes in v13:
time: 47.9 us; the launch traced here: 47.5 us
  Pallas kernels  16.8 us (35%)
  starting transfers between devices  16.3 us (34%)
  waiting for transfers between devices  9.53 us (20%)
  local copies, waits for them, and re-layouts  4.16 us (9%)
  other arithmetic  0.66 us (1%)
    pallas_call x9, Pallas kernels, call(): pl.pallas_call(kernel, out_shape=outs, scratch_shapes=scratches, input_ou...  16.8 us
    ppermute x8, starting transfers between devices, gather(): held[s ^ step] = lax.ppermute(part, axis, [(k, k ^ step) for k in range(n)])  6.23 us
    ppermute x8, waiting for transfers between devices, gather(): held[s ^ step] = lax.ppermute(part, axis, [(k, k ^ step) for k in range(n)])  5.33 us
    ppermute x1, starting transfers between devices, per_device(): near = lax.ppermute(pair, 'col', [(k, k ^ 1) for k in range(n)])  4.81 us
    ppermute x3, waiting for transfers between devices, direct(): lax.ppermute(block, 'row', [(k, k ^ s) for k in range(n)])  4.19 us
    ppermute x3, starting transfers between devices, direct(): lax.ppermute(block, 'row', [(k, k ^ s) for k in range(n)])  3.66 us
    unnamed x6, local copies, waits for them, and re-layouts  1.88 us
    ppermute x1, starting transfers between devices, mirrored(): return lax.ppermute(block, ('row', 'col'), pairs)  1.56 us
  transfers between devices with their start and end apart: 13, of which 4 were waited for; matrix products, arithmetic and copies ran while one was open for 6% of the time, Pallas kernels for 25%

profile of v13, /device:TPU:0, one launch (start us, length us, event | category | flops | bytes accessed | tf_op | source)
XLA Modules:
  0.0 47.5 jit_solution(12679642077230895293)
XLA Ops:
  0.0 1.6 %collective-permute-start.2 = (bf16[576,128]{1,0:T(8,128)(2,1)}, bf16[576,128]{1,0:T(8,128)(2,1)S(1)}, u32[]{:S(2)}, u32[]{:S(2)}) collective-permute-start(bf16[576,128]{1,0:T(8,128)(2,1)} %bitcast.2), channel_id=1, source_target_pairs={{0,0},{1,8},{2,4},{3,12},{4,1},{5,9},{6,5},{7,13},{8,2},{9,10},{10... | collective-permute-start | bytes 442376 | tf_op jit(solution)/shard_map/ppermute | solution.py:256
  1.6 4.8 %collective-permute-start.1 = (bf16[576,128]{1,0:T(8,128)(2,1)}, bf16[576,128]{1,0:T(8,128)(2,1)S(1)}, u32[]{:S(2)}, u32[]{:S(2)}) collective-permute-start(bf16[576,128]{1,0:T(8,128)(2,1)} %bitcast.3), channel_id=1, source_target_pairs={{0,1},{1,0},{2,3},{3,2},{4,5},{5,4},{6,7},{7,6},{8,9},{9,8},{10,11... | collective-permute-start | bytes 442376 | tf_op jit(solution)/shard_map/ppermute | solution.py:294
  6.4 1.8 %collective-permute-start = (bf16[576,128]{1,0:T(8,128)(2,1)}, bf16[576,128]{1,0:T(8,128)(2,1)S(1)}, u32[]{:S(2)}, u32[]{:S(2)}) collective-permute-start(bf16[576,128]{1,0:T(8,128)(2,1)} %bitcast.4), channel_id=1, source_target_pairs={{0,2},{1,3},{2,0},{3,1},{4,6},{5,7},{6,4},{7,5},{8,10},{9,11},{10,... | collective-permute-start | bytes 442376 | tf_op jit(solution)/shard_map/ppermute | solution.py:247
  8.2 0.7 %convert_element_type.3 = f32[96]{0:T(128)S(1)} convert(s32[96]{0:T(128)} %param.11) | non-fusion elementwise | flops 96 | bytes 768 | tf_op jit(solution)/shard_map/convert_element_type | solution.py:281
  8.8 0.7 %reshape.11 = f32[10,128]{1,0:T(8,128)S(1)} reshape(f32[2,640]{1,0:T(2,128)} %param.15) | data formatting | bytes 10240 | tf_op jit(solution)/shard_map/reshape | solution.py:282
  9.5 0.1 broadcast_in_dim.10
  9.6 1.5 %concatenate.3.table.refs_3_.refs_5_ = f32[120,128]{1,0:T(8,128)S(1)} concatenate(f32[2,128]{1,0:T(2,128)} %param.12, f32[2,128]{1,0:T(2,128)} %param.13, f32[2,128]{1,0:T(2,128)} %param.16, f32[2,128]{1,0:T(2,128)} %param.17, f32[2,128]{1,0:T(2,128)} %param.19, f32[10,128]{1,0:T(8,128)S(1)} %reshape.11, f32[4,128]{1,0:T(4,128)S(1)} %broadcast_in_dim.4, ...), dimensions={0} | concatenate | bytes 122880 | tf_op jit(solution)/shard_map/concatenate | solution.py:283
  11.1 0.0 copy-start.1
  11.1 0.9 %copy-done.1 = bf16[24,24,128]{2,1,0:T(8,128)(2,1)S(1)} copy-done((bf16[24,24,128]{2,1,0:T(8,128)(2,1)S(1)}, bf16[24,24,128]{2,1,0:T(8,128)(2,1)}, u32[]{:S(2)}) %copy-start.1) | copy-done | bytes 147480
  12.0 0.0 copy-start.2
  12.0 1.0 %copy-done.2 = bf16[2,128,640]{2,1,0:T(8,128)(2,1)S(1)} copy-done((bf16[2,128,640]{2,1,0:T(8,128)(2,1)S(1)}, bf16[2,128,640]{2,1,0:T(8,128)(2,1)}, u32[]{:S(2)}) %copy-start.2) | copy-done | bytes 327704
  13.0 1.0 %own_sides.1 = (bf16[2,128,640]{2,1,0:T(8,128)(2,1)S(1)}, f32[4,576,128]{2,1,0:T(8,128)S(1)}, f32[4,576,128]{2,1,0:T(8,128)S(1)}, f32[576,128]{1,0:T(8,128)S(1)}) custom-call(bf16[576,128]{1,0:T(8,128)(2,1)S(1)} %bitcast.5, f32[120,128]{1,0:T(8,128)S(1)} %concatenate.3.table.refs_3_.refs_5_, bf16[2,128,640]{2,1,0:T(8,128)(2,1)S(1)} %copy-done.2), custom_call_target="tpu_custom_call" | custom-call | tf_op jit(solution)/shard_map/own_sides/pallas_call | solution.py:266
  14.0 0.0 collective-permute-done.2.col.refs_1_
  14.0 0.4 collective-permute-start.6
  14.4 3.2 %collective-permute-start.5 = (bf16[576,128]{1,0:T(8,128)(2,1)S(1)}, bf16[576,128]{1,0:T(8,128)(2,1)S(1)}, u32[]{:S(2)}, u32[]{:S(2)}) collective-permute-start(bf16[576,128]{1,0:T(8,128)(2,1)S(1)} %collective-permute-done.2.col.refs_1_), channel_id=1, source_target_pairs={{0,8},{4,12},{8,0},{12,4},{1,9},{5,13},{9,1},{13,5},{2,10},{6,14},... | collective-permute-start | bytes 442376 | tf_op jit(solution)/shard_map/ppermute | solution.py:252
  17.6 0.1 collective-permute-start.4
  17.6 0.0 collective-permute-done.1.row
  17.7 1.0 %early_sides.1 = (f32[4,576,128]{2,1,0:T(8,128)S(1)}, f32[4,576,128]{2,1,0:T(8,128)S(1)}, f32[4,576,128]{2,1,0:T(8,128)S(1)}, f32[4,576,128]{2,1,0:T(8,128)S(1)}) custom-call(bf16[576,128]{1,0:T(8,128)(2,1)S(1)} %collective-permute-done.1.row, bf16[576,128]{1,0:T(8,128)(2,1)S(1)} %collective-permute-done.2.col.refs_1_, ...), custom_call_target="tpu_custom_call", output_to_operand_aliasing={{0}: (4, {}), {1}: (5, {})} | custom-call | tf_op jit(solution)/shard_map/early_sides/pallas_call | solution.py:266
  18.7 1.0 %collective-permute-done.refs_0_ = bf16[576,128]{1,0:T(8,128)(2,1)S(1)} collective-permute-done((bf16[576,128]{1,0:T(8,128)(2,1)}, bf16[576,128]{1,0:T(8,128)(2,1)S(1)}, u32[]{:S(2)}, u32[]{:S(2)}) %collective-permute-start) | collective-permute-done | bytes 147488 | tf_op jit(solution)/shard_map/ppermute | solution.py:247
  19.6 0.0 collective-permute-start.3
  19.6 4.2 %collective-permute-done.5.refs_2_.refs_3_ = bf16[576,128]{1,0:T(8,128)(2,1)S(1)} collective-permute-done((bf16[576,128]{1,0:T(8,128)(2,1)S(1)}, bf16[576,128]{1,0:T(8,128)(2,1)S(1)}, u32[]{:S(2)}, u32[]{:S(2)}) %collective-permute-start.5) | collective-permute-done | bytes 147488 | tf_op jit(solution)/shard_map/ppermute | solution.py:252
  23.8 0.0 collective-permute-done.4.refs_1_.refs_2_
  23.8 0.0 copy-start
  23.8 3.5 %middle_sides.1 = (f32[4,576,128]{2,1,0:T(8,128)S(1)}, f32[4,576,128]{2,1,0:T(8,128)S(1)}, f32[4,576,128]{2,1,0:T(8,128)S(1)}, f32[4,576,128]{2,1,0:T(8,128)S(1)}, f32[576,128]{1,0:T(8,128)S(1)}) custom-call(bf16[576,128]{1,0:T(8,128)(2,1)S(1)} %collective-permute-done.refs_0_, ...), custom_call_target="tpu_custom_call", output_to_operand_aliasing={{0}: (5, {}), {1}: (6, {}), {2}: (7, {}), {3}: (8, {})} | custom-call | tf_op jit(solution)/shard_map/middle_sides/pallas_call | solution.py:266
  27.3 0.0 collective-permute-done.6.refs_4_
  27.3 0.0 collective-permute-done.3.refs_0_
  27.4 0.0 copy-done
  27.4 3.0 %mirror_end.1 = (bf16[576,128]{1,0:T(8,128)(2,1)S(1)}, f32[4,576,128]{2,1,0:T(8,128)S(1)}, f32[4,576,128]{2,1,0:T(8,128)S(1)}, f32[4,576,128]{2,1,0:T(8,128)S(1)}, f32[4,576,128]{2,1,0:T(8,128)S(1)}) custom-call(bf16[576,128]{1,0:T(8,128)(2,1)S(1)} %collective-permute-done.3.refs_0_, ...), custom_call_target="tpu_custom_call", output_to_operand_aliasing={{1}: (8, {}), {2}: (9, {}), {3}: (10, {}), {4}: (11, {})} | custom-call | tf_op jit(solution)/shard_map/mirror_end/pallas_call | solution.py:266
  30.4 0.9 %collective-permute-start.7 = (bf16[576,128]{1,0:T(8,128)(2,1)S(1)}, bf16[576,128]{1,0:T(8,128)(2,1)S(1)}, u32[]{:S(2)}, u32[]{:S(2)}) collective-permute-start(bf16[576,128]{1,0:T(8,128)(2,1)S(1)} %get-tuple-element.43.refs_0_), channel_id=1, source_target_pairs={{0,2},{1,3},{2,0},{3,1},{4,6},{5,7},{6,4},{7,5},{8,10},{9,11},{10,... | collective-permute-start | bytes 442376 | tf_op jit(solution)/shard_map/ppermute | solution.py:247
  31.3 1.4 %collective-permute-start.10 = (bf16[576,128]{1,0:T(8,128)(2,1)S(1)}, bf16[576,128]{1,0:T(8,128)(2,1)S(1)}, u32[]{:S(2)}, u32[]{:S(2)}) collective-permute-start(bf16[576,128]{1,0:T(8,128)(2,1)S(1)} %get-tuple-element.43.refs_0_), channel_id=1, source_target_pairs={{0,1},{1,0},{2,3},{3,2},{4,5},{5,4},{6,7},{7,6},{8,9},{9,8},{10,11... | collective-permute-start | bytes 442376 | tf_op jit(solution)/shard_map/ppermute | solution.py:247
  32.7 3.6 %own_end.1 = (bf16[576,128]{1,0:T(8,128)(2,1)S(1)}, bf16[576,128]{1,0:T(8,128)(2,1)S(1)}) custom-call(f32[4,576,128]{2,1,0:T(8,128)S(1)} %get-tuple-element.44.row_l, f32[4,576,128]{2,1,0:T(8,128)S(1)} %get-tuple-element.45.col_r, f32[120,128]{1,0:T(8,128)S(1)} %concatenate.3.table.refs_3_.refs_5_, ...), custom_call_target="tpu_custom_call" | custom-call | tf_op jit(solution)/shard_map/own_end/pallas_call | solution.py:266
  36.4 0.1 collective-permute-start.12
  36.4 2.1 %collective-permute-start.9 = (bf16[576,128]{1,0:T(8,128)(2,1)S(1)}, bf16[576,128]{1,0:T(8,128)(2,1)S(1)}, u32[]{:S(2)}, u32[]{:S(2)}) collective-permute-start(bf16[576,128]{1,0:T(8,128)(2,1)S(1)} %get-tuple-element.47.refs_0_), channel_id=1, source_target_pairs={{0,8},{4,12},{8,0},{12,4},{1,9},{5,13},{9,1},{13,5},{2,10},{6,14},... | collective-permute-start | bytes 442376 | tf_op jit(solution)/shard_map/ppermute | solution.py:247
  38.5 1.2 %collective-permute-done.7.refs_2_ = bf16[576,128]{1,0:T(8,128)(2,1)S(1)} collective-permute-done((bf16[576,128]{1,0:T(8,128)(2,1)S(1)}, bf16[576,128]{1,0:T(8,128)(2,1)S(1)}, u32[]{:S(2)}, u32[]{:S(2)}) %collective-permute-start.7) | collective-permute-done | bytes 147488 | tf_op jit(solution)/shard_map/ppermute | solution.py:247
  39.7 0.0 collective-permute-start.8
  39.7 0.0 collective-permute-done.10.refs_1_
  39.7 0.1 left_slots.1.refs_3_.left_in
  39.8 3.2 %collective-permute-done.9.refs_2_ = bf16[576,128]{1,0:T(8,128)(2,1)S(1)} collective-permute-done((bf16[576,128]{1,0:T(8,128)(2,1)S(1)}, bf16[576,128]{1,0:T(8,128)(2,1)S(1)}, u32[]{:S(2)}, u32[]{:S(2)}) %collective-permute-start.9) | collective-permute-done | bytes 147488 | tf_op jit(solution)/shard_map/ppermute | solution.py:247
  42.9 0.0 collective-permute-start.11
  42.9 0.5 %gate.1.gating = f32[576,128]{1,0:T(8,128)S(1)} custom-call(bf16[576,128]{1,0:T(8,128)(2,1)S(1)} %get-tuple-element.50.pair, f32[120,128]{1,0:T(8,128)S(1)} %concatenate.3.table.refs_3_.refs_5_, bf16[2,128,640]{2,1,0:T(8,128)(2,1)S(1)} %get-tuple-element.29.weights.refs_4_.refs_6_), custom_call_target="tpu_custom_call" | custom-call | tf_op jit(solution)/shard_map/gate/pallas_call | solution.py:266
  43.5 0.0 collective-permute-done.12.refs_1_
  43.5 2.1 %middle_slots.1 = (f32[4,576,128]{2,1,0:T(8,128)S(1)}, f32[576,128]{1,0:T(8,128)S(1)}) custom-call(bf16[576,128]{1,0:T(8,128)(2,1)S(1)} %get-tuple-element.47.refs_0_, bf16[576,128]{1,0:T(8,128)(2,1)S(1)} %collective-permute-done.12.refs_1_, bf16[576,128]{1,0:T(8,128)(2,1)S(1)} %collective-permute-done.9.refs_2_, f32[4,576,128]{2,1,0:T(8,128)S(1)} %left_slots.1.refs_3_.left_in), custom_call_target="tpu_custom_call" | custom-call | tf_op jit(solution)/shard_map/middle_slots/pallas_call | solution.py:266
  45.6 0.0 collective-permute-done.8.left
  45.6 0.0 collective-permute-done.11.right
  45.6 1.9 %end.1 = (bf16[576,128]{1,0:T(8,128)(2,1)}, f32[4,576,128]{2,1,0:T(8,128)S(1)}, f32[4,576,128]{2,1,0:T(8,128)S(1)}) custom-call(bf16[576,128]{1,0:T(8,128)(2,1)S(1)} %collective-permute-done.8.left, bf16[576,128]{1,0:T(8,128)(2,1)S(1)} %collective-permute-done.11.right, ...), custom_call_target="tpu_custom_call", output_to_operand_aliasing={{1}: (7, {}), {2}: (8, {})} | custom-call | tf_op jit(solution)/shard_map/end/pallas_call | solution.py:266
  (1 shorter events, 0.0 us)
Async XLA Ops:
  0.0 14.0 %collective-permute-start.2 = (bf16[576,128]{1,0:T(8,128)(2,1)}, bf16[576,128]{1,0:T(8,128)(2,1)S(1)}, u32[]{:S(2)}, u32[]{:S(2)}) collective-permute-start(bf16[576,128]{1,0:T(8,128)(2,1)} %bitcast.2), channel_id=1, source_target_pairs={{0,0},{1,8},{2,4},{3,12},{4,1},{5,9},{6,5},{7,13},{8,2},{9,10},{10... | collective-permute-start | bytes 442376 | tf_op jit(solution)/shard_map/ppermute | solution.py:256
  1.6 16.1 %collective-permute-start.1 = (bf16[576,128]{1,0:T(8,128)(2,1)}, bf16[576,128]{1,0:T(8,128)(2,1)S(1)}, u32[]{:S(2)}, u32[]{:S(2)}) collective-permute-start(bf16[576,128]{1,0:T(8,128)(2,1)} %bitcast.3), channel_id=1, source_target_pairs={{0,1},{1,0},{2,3},{3,2},{4,5},{5,4},{6,7},{7,6},{8,9},{9,8},{10,11... | collective-permute-start | bytes 442376 | tf_op jit(solution)/shard_map/ppermute | solution.py:294
  6.4 13.2 %collective-permute-start = (bf16[576,128]{1,0:T(8,128)(2,1)}, bf16[576,128]{1,0:T(8,128)(2,1)S(1)}, u32[]{:S(2)}, u32[]{:S(2)}) collective-permute-start(bf16[576,128]{1,0:T(8,128)(2,1)} %bitcast.4), channel_id=1, source_target_pairs={{0,2},{1,3},{2,0},{3,1},{4,6},{5,7},{6,4},{7,5},{8,10},{9,11},{10,... | collective-permute-start | bytes 442376 | tf_op jit(solution)/shard_map/ppermute | solution.py:247
  11.1 0.9 %copy-start.1 = (bf16[24,24,128]{2,1,0:T(8,128)(2,1)S(1)}, bf16[24,24,128]{2,1,0:T(8,128)(2,1)}, u32[]{:S(2)}) copy-start(bf16[24,24,128]{2,1,0:T(8,128)(2,1)} %param.10) | copy-start | bytes 442372
  12.0 1.0 %copy-start.2 = (bf16[2,128,640]{2,1,0:T(8,128)(2,1)S(1)}, bf16[2,128,640]{2,1,0:T(8,128)(2,1)}, u32[]{:S(2)}) copy-start(bf16[2,128,640]{2,1,0:T(8,128)(2,1)} %w_in.1) | copy-start | bytes 983044
  14.0 13.3 %collective-permute-start.6 = (bf16[576,128]{1,0:T(8,128)(2,1)S(1)}, bf16[576,128]{1,0:T(8,128)(2,1)S(1)}, u32[]{:S(2)}, u32[]{:S(2)}) collective-permute-start(bf16[576,128]{1,0:T(8,128)(2,1)S(1)} %collective-permute-done.2.col.refs_1_), channel_id=1, source_target_pairs={{0,12},{4,8},{8,4},{12,0},{1,13},{5,9},{9,5},{13,1},{2,14},{6,10},... | collective-permute-start | bytes 442376 | tf_op jit(solution)/shard_map/ppermute | solution.py:252
  14.4 9.4 %collective-permute-start.5 = (bf16[576,128]{1,0:T(8,128)(2,1)S(1)}, bf16[576,128]{1,0:T(8,128)(2,1)S(1)}, u32[]{:S(2)}, u32[]{:S(2)}) collective-permute-start(bf16[576,128]{1,0:T(8,128)(2,1)S(1)} %collective-permute-done.2.col.refs_1_), channel_id=1, source_target_pairs={{0,8},{4,12},{8,0},{12,4},{1,9},{5,13},{9,1},{13,5},{2,10},{6,14},... | collective-permute-start | bytes 442376 | tf_op jit(solution)/shard_map/ppermute | solution.py:252
  17.6 6.2 %collective-permute-start.4 = (bf16[576,128]{1,0:T(8,128)(2,1)S(1)}, bf16[576,128]{1,0:T(8,128)(2,1)S(1)}, u32[]{:S(2)}, u32[]{:S(2)}) collective-permute-start(bf16[576,128]{1,0:T(8,128)(2,1)S(1)} %collective-permute-done.2.col.refs_1_), channel_id=1, source_target_pairs={{0,4},{4,0},{8,12},{12,8},{1,5},{5,1},{9,13},{13,9},{2,6},{6,2},{1... | collective-permute-start | bytes 442376 | tf_op jit(solution)/shard_map/ppermute | solution.py:252
  19.6 7.7 %collective-permute-start.3 = (bf16[576,128]{1,0:T(8,128)(2,1)S(1)}, bf16[576,128]{1,0:T(8,128)(2,1)S(1)}, u32[]{:S(2)}, u32[]{:S(2)}) collective-permute-start(bf16[576,128]{1,0:T(8,128)(2,1)S(1)} %collective-permute-done.refs_0_), channel_id=1, source_target_pairs={{0,1},{1,0},{2,3},{3,2},{4,5},{5,4},{6,7},{7,6},{8,9},{9,8},{10,11... | collective-permute-start | bytes 442376 | tf_op jit(solution)/shard_map/ppermute | solution.py:247
  23.8 3.5 %copy-start = (bf16[2,128,128]{2,1,0:T(8,128)(2,1)S(1)}, bf16[2,128,128]{2,1,0:T(8,128)(2,1)}, u32[]{:S(2)}) copy-start(bf16[2,128,128]{2,1,0:T(8,128)(2,1)} %w_out.3) | copy-start | bytes 196612
  30.4 9.3 %collective-permute-start.7 = (bf16[576,128]{1,0:T(8,128)(2,1)S(1)}, bf16[576,128]{1,0:T(8,128)(2,1)S(1)}, u32[]{:S(2)}, u32[]{:S(2)}) collective-permute-start(bf16[576,128]{1,0:T(8,128)(2,1)S(1)} %get-tuple-element.43.refs_0_), channel_id=1, source_target_pairs={{0,2},{1,3},{2,0},{3,1},{4,6},{5,7},{6,4},{7,5},{8,10},{9,11},{10,... | collective-permute-start | bytes 442376 | tf_op jit(solution)/shard_map/ppermute | solution.py:247
  31.3 8.4 %collective-permute-start.10 = (bf16[576,128]{1,0:T(8,128)(2,1)S(1)}, bf16[576,128]{1,0:T(8,128)(2,1)S(1)}, u32[]{:S(2)}, u32[]{:S(2)}) collective-permute-start(bf16[576,128]{1,0:T(8,128)(2,1)S(1)} %get-tuple-element.43.refs_0_), channel_id=1, source_target_pairs={{0,1},{1,0},{2,3},{3,2},{4,5},{5,4},{6,7},{7,6},{8,9},{9,8},{10,11... | collective-permute-start | bytes 442376 | tf_op jit(solution)/shard_map/ppermute | solution.py:247
  36.4 7.1 %collective-permute-start.12 = (bf16[576,128]{1,0:T(8,128)(2,1)S(1)}, bf16[576,128]{1,0:T(8,128)(2,1)S(1)}, u32[]{:S(2)}, u32[]{:S(2)}) collective-permute-start(bf16[576,128]{1,0:T(8,128)(2,1)S(1)} %get-tuple-element.47.refs_0_), channel_id=1, source_target_pairs={{0,4},{4,0},{8,12},{12,8},{1,5},{5,1},{9,13},{13,9},{2,6},{6,2},{1... | collective-permute-start | bytes 442376 | tf_op jit(solution)/shard_map/ppermute | solution.py:247
  36.4 6.5 %collective-permute-start.9 = (bf16[576,128]{1,0:T(8,128)(2,1)S(1)}, bf16[576,128]{1,0:T(8,128)(2,1)S(1)}, u32[]{:S(2)}, u32[]{:S(2)}) collective-permute-start(bf16[576,128]{1,0:T(8,128)(2,1)S(1)} %get-tuple-element.47.refs_0_), channel_id=1, source_target_pairs={{0,8},{4,12},{8,0},{12,4},{1,9},{5,13},{9,1},{13,5},{2,10},{6,14},... | collective-permute-start | bytes 442376 | tf_op jit(solution)/shard_map/ppermute | solution.py:247
  39.7 5.9 %collective-permute-start.8 = (bf16[576,128]{1,0:T(8,128)(2,1)S(1)}, bf16[576,128]{1,0:T(8,128)(2,1)S(1)}, u32[]{:S(2)}, u32[]{:S(2)}) collective-permute-start(bf16[576,128]{1,0:T(8,128)(2,1)S(1)} %collective-permute-done.7.refs_2_), channel_id=1, source_target_pairs={{0,1},{1,0},{2,3},{3,2},{4,5},{5,4},{6,7},{7,6},{8,9},{9,8},{10,11... | collective-permute-start | bytes 442376 | tf_op jit(solution)/shard_map/ppermute | solution.py:247
  42.9 2.6 %collective-permute-start.11 = (bf16[576,128]{1,0:T(8,128)(2,1)S(1)}, bf16[576,128]{1,0:T(8,128)(2,1)S(1)}, u32[]{:S(2)}, u32[]{:S(2)}) collective-permute-start(bf16[576,128]{1,0:T(8,128)(2,1)S(1)} %collective-permute-done.9.refs_2_), channel_id=1, source_target_pairs={{0,4},{4,0},{8,12},{12,8},{1,5},{5,1},{9,13},{13,9},{2,6},{6,2},{1... | collective-permute-start | bytes 442376 | tf_op jit(solution)/shard_map/ppermute | solution.py:247

commit v14 on v13

--- a/solution.py
+++ b/solution.py
@@ -145,23 +145,19 @@
     gating[...] = gate_of(pair[...], consts, table, weights, 0)
 
 
-def early_kernel(n, t, row, col, table, weights, left_in, right_in, row_l, row_r, col_l, col_r, wide):
+def early_kernel(n, t, col, table, weights, col_l, col_r, wide):
+    r, c = lax.axis_index("row"), lax.axis_index("col")
+    outer, inner = mask_of(table, placed_at(r, n), t), mask_of(table, c, t)
+    sides(col, wide, col_l.at[0], col_r.at[0], outer, inner, constants(wide.shape[1]), table, weights)
+
+
+def middle_sides_kernel(n, t, *refs):
+    rows, cols, (table, weights) = refs[: n - 2], refs[n - 2 : 2 * n - 4], refs[2 * n - 4 : 2 * n - 2]
+    row_l, row_r, col_l, col_r, mixed, wide = refs[2 * n + 2 :]
     r, c = lax.axis_index("row"), lax.axis_index("col")
     consts = constants(wide.shape[1])
     here, there = mask_of(table, r, t), mask_of(table, c, t)
-    outer = mask_of(table, placed_at(r, n), t)
-    sides(col, wide, col_l.at[0], col_r.at[0], outer, there, consts, table, weights)
-    outer = mask_of(table, c ^ 1, t)
-    sides(row, wide, row_l.at[1], row_r.at[1], outer, here, consts, table, weights)
-
-
-def middle_sides_kernel(n, t, *refs):
-    rows, cols, (table, weights) = refs[: n - 3], refs[n - 3 : 2 * n - 5], refs[2 * n - 5 : 2 * n - 3]
-    row_l, row_r, col_l, col_r, mixed, wide = refs[2 * n + 1 :]
-    r, c = lax.axis_index("row"), lax.axis_index("col")
-    consts = constants(wide.shape[1])
-    here, there = mask_of(table, r, t), mask_of(table, c, t)
-    for s, block in enumerate(rows, 2):
+    for s, block in enumerate(rows, 1):
         outer = mask_of(table, c ^ s, t)
         sides(block, wide, row_l.at[s], row_r.at[s], outer, here, consts, table, weights)
     for s, block in enumerate(cols, 1):
@@ -217,6 +213,10 @@
         refs[n - 1][s] = refs[s][...].astype(F32)
 
 
+def widen_kernel(block, out):
+    out[...] = block[...].astype(F32)
+
+
 def middle_kernel(n, t, *refs):
     sources, (lefts, rights, mixed) = refs[: n - 1], refs[n - 1 :]
     r, c = lax.axis_index("row"), lax.axis_index("col")
@@ -228,7 +228,7 @@
 
 def end_kernel(n, t, left, right, old, pair, gating, table, w_out, left_in, right_in, out, lefts, rights, mixed):
     r, c = lax.axis_index("row"), lax.axis_index("col")
-    lefts[n - 1] = left[...].astype(F32)
+    lefts[n - 1] = left[...]
     rights[n - 1] = right[...].astype(F32)
     count, slot = late_pairs(r ^ c ^ (n - 1), n)
     mix(mixed, old, lefts, rights, 0, count, slot, lambda i: r ^ c ^ slot(i), t)
@@ -291,29 +291,17 @@
             w_in,
         )
         own_l = row_l
-        near = lax.ppermute(pair, "col", [(k, k ^ 1) for k in range(n)])
-        row_l, row_r, col_l, col_r = call(
-            functools.partial(early_kernel, n, t),
-            "early_sides",
-            (slots,) * 4,
-            [scratch],
-            near,
-            col_block,
-            table,
-            weights,
-            row_l,
-            row_r,
-            alias={4: 0, 5: 1},
-        )
-        rows = gather(pair, "col", lambda s, step: row_l if s else ())
-        rows[1] = near
+        col_l, col_r = call(
+            functools.partial(early_kernel, n, t), "early_sides", (slots,) * 2, [scratch], col_block, table, weights
+        )
+        rows = gather(pair, "col", lambda s, step: (own_l, col_l) if s else ())
         cols = direct(lax.optimization_barrier((col_block, own_l))[0])
         row_l, row_r, col_l, col_r, mixed = call(
             functools.partial(middle_sides_kernel, n, t),
             "middle_sides",
             (slots,) * 4 + (broad,),
             [scratch],
-            *rows[2:-1],
+            *rows[1:-1],
             *cols[1:-1],
             table,
             weights,
@@ -321,7 +309,7 @@
             row_r,
             col_l,
             col_r,
-            alias={2 * n - 3: 0, 2 * n - 2: 1, 2 * n - 1: 2, 2 * n: 3},
+            alias={2 * n - 2: 0, 2 * n - 1: 1, 2 * n: 2, 2 * n + 1: 3},
         )
         left, row_l, _, _, col_r = call(
             functools.partial(mirror_kernel, n, t),
@@ -360,12 +348,13 @@
         right_slots, mixed = call(
             functools.partial(middle_kernel, n, t), "middle_slots", (slots, broad), [], *rights[:-1], left_slots
         )
+        left_last = call(widen_kernel, "left_last", broad, [], lefts[-1], weight=30)
         out, _, _ = call(
             functools.partial(end_kernel, n, t),
             "end",
             (narrow, slots, slots),
             [scratch],
-            lefts[-1],
+            left_last,
             rights[-1],
             mixed,
             pair,

time: 47.9 us -> 48.9 us (1.021)
  starting transfers between devices: 16.3 us -> 20.2 us
  waiting for transfers between devices: 9.53 us -> 6.56 us
    ppermute x8 -> x9, starting transfers between devices: 6.23 us -> 14.3 us  [gather(): held[s ^ step] = lax.ppermute(part, axis, [(k, k ^ step) for k in range(n)])]
    ppermute x1 -> x0, starting transfers between devices: 4.81 us -> none  [per_device(): near = lax.ppermute(pair, 'col', [(k, k ^ 1) for k in range(n)])]
    ppermute x3, waiting for transfers between devices: 4.19 us -> 1.24 us  [direct(): lax.ppermute(block, 'row', [(k, k ^ s) for k in range(n)])]
    ppermute x3, starting transfers between devices: 3.66 us -> 4.43 us  [direct(): lax.ppermute(block, 'row', [(k, k ^ s) for k in range(n)])]
    ppermute x8 -> x9, waiting for transfers between devices: 5.33 us -> 5.32 us  [gather(): held[s ^ step] = lax.ppermute(part, axis, [(k, k ^ step) for k in range(n)])]
    pallas_call x9 -> x10, Pallas kernels: 16.8 us -> 16.8 us  [call(): pl.pallas_call(kernel, out_shape=outs, scratch_shapes=scratches, input_ou...]
    unnamed x6 -> x8, local copies, waits for them, and re-layouts: 1.88 us -> 1.89 us
  transfers between devices with their start and end apart: 13 -> 13, of which waited for: 4 -> 3; matrix products, arithmetic and copies ran while one was open for 6% -> 6% of each run, Pallas kernels for 25% -> 24%
where the time goes in v14:
time: 48.9 us; the launch traced here: 48.6 us
  starting transfers between devices  20.2 us (41%)
  Pallas kernels  16.8 us (34%)
  waiting for transfers between devices  6.56 us (13%)
  local copies, waits for them, and re-layouts  4.16 us (9%)
  other arithmetic  0.66 us (1%)
    pallas_call x10, Pallas kernels, call(): pl.pallas_call(kernel, out_shape=outs, scratch_shapes=scratches, input_ou...  16.8 us
    ppermute x9, starting transfers between devices, gather(): held[s ^ step] = lax.ppermute(part, axis, [(k, k ^ step) for k in range(n)])  14.3 us
    ppermute x9, waiting for transfers between devices, gather(): held[s ^ step] = lax.ppermute(part, axis, [(k, k ^ step) for k in range(n)])  5.32 us
    ppermute x3, starting transfers between devices, direct(): lax.ppermute(block, 'row', [(k, k ^ s) for k in range(n)])  4.43 us
    unnamed x8, local copies, waits for them, and re-layouts  1.89 us
    ppermute x1, starting transfers between devices, mirrored(): return lax.ppermute(block, ('row', 'col'), pairs)  1.56 us
    concatenate x1, local copies, waits for them, and re-layouts, per_device(): jnp.concatenate(vectors + [jnp.zeros((TABLE_MASK - 20, width), F32), mask])  1.51 us
    ppermute x3, waiting for transfers between devices, direct(): lax.ppermute(block, 'row', [(k, k ^ s) for k in range(n)])  1.24 us
  transfers between devices with their start and end apart: 13, of which 3 were waited for; matrix products, arithmetic and copies ran while one was open for 6% of the time, Pallas kernels for 24%

profile of v14, /device:TPU:0, one launch (start us, length us, event | category | flops | bytes accessed | tf_op | source)
XLA Modules:
  0.0 48.6 jit_solution(16321757450502789546)
XLA Ops:
  0.0 1.6 %collective-permute-start.1 = (bf16[576,128]{1,0:T(8,128)(2,1)}, bf16[576,128]{1,0:T(8,128)(2,1)S(1)}, u32[]{:S(2)}, u32[]{:S(2)}) collective-permute-start(bf16[576,128]{1,0:T(8,128)(2,1)} %bitcast.2), channel_id=1, source_target_pairs={{0,0},{1,8},{2,4},{3,12},{4,1},{5,9},{6,5},{7,13},{8,2},{9,10},{10... | collective-permute-start | bytes 442376 | tf_op jit(solution)/shard_map/ppermute | solution.py:256
  1.6 4.5 %collective-permute-start = (bf16[576,128]{1,0:T(8,128)(2,1)}, bf16[576,128]{1,0:T(8,128)(2,1)S(1)}, u32[]{:S(2)}, u32[]{:S(2)}) collective-permute-start(bf16[576,128]{1,0:T(8,128)(2,1)} %bitcast.3), channel_id=1, source_target_pairs={{0,2},{1,3},{2,0},{3,1},{4,6},{5,7},{6,4},{7,5},{8,10},{9,11},{10,... | collective-permute-start | bytes 442376 | tf_op jit(solution)/shard_map/ppermute | solution.py:247
  6.0 2.2 %collective-permute-start.6 = (bf16[576,128]{1,0:T(8,128)(2,1)}, bf16[576,128]{1,0:T(8,128)(2,1)S(1)}, u32[]{:S(2)}, u32[]{:S(2)}) collective-permute-start(bf16[576,128]{1,0:T(8,128)(2,1)} %bitcast.4), channel_id=1, source_target_pairs={{0,1},{1,0},{2,3},{3,2},{4,5},{5,4},{6,7},{7,6},{8,9},{9,8},{10,11... | collective-permute-start | bytes 442376 | tf_op jit(solution)/shard_map/ppermute | solution.py:247
  8.2 0.7 %convert_element_type.3 = f32[96]{0:T(128)S(1)} convert(s32[96]{0:T(128)} %param.11) | non-fusion elementwise | flops 96 | bytes 768 | tf_op jit(solution)/shard_map/convert_element_type | solution.py:281
  8.8 0.7 %reshape.11 = f32[10,128]{1,0:T(8,128)S(1)} reshape(f32[2,640]{1,0:T(2,128)} %param.15) | data formatting | bytes 10240 | tf_op jit(solution)/shard_map/reshape | solution.py:282
  9.5 0.1 broadcast_in_dim.10
  9.6 1.5 %concatenate.3.table.refs_4_.refs_5_ = f32[120,128]{1,0:T(8,128)S(1)} concatenate(f32[2,128]{1,0:T(2,128)} %param.12, f32[2,128]{1,0:T(2,128)} %param.13, f32[2,128]{1,0:T(2,128)} %param.16, f32[2,128]{1,0:T(2,128)} %param.17, f32[2,128]{1,0:T(2,128)} %param.19, f32[10,128]{1,0:T(8,128)S(1)} %reshape.11, f32[4,128]{1,0:T(4,128)S(1)} %broadcast_in_dim.4, ...), dimensions={0} | concatenate | bytes 122880 | tf_op jit(solution)/shard_map/concatenate | solution.py:283
  11.1 0.0 copy-start.1
  11.1 0.9 %copy-done.1 = bf16[24,24,128]{2,1,0:T(8,128)(2,1)S(1)} copy-done((bf16[24,24,128]{2,1,0:T(8,128)(2,1)S(1)}, bf16[24,24,128]{2,1,0:T(8,128)(2,1)}, u32[]{:S(2)}) %copy-start.1) | copy-done | bytes 147480
  12.0 0.0 copy-start.3
  12.0 1.0 %copy-done.3 = bf16[2,128,640]{2,1,0:T(8,128)(2,1)S(1)} copy-done((bf16[2,128,640]{2,1,0:T(8,128)(2,1)S(1)}, bf16[2,128,640]{2,1,0:T(8,128)(2,1)}, u32[]{:S(2)}) %copy-start.3) | copy-done | bytes 327704
  13.0 1.0 %own_sides.1 = (bf16[2,128,640]{2,1,0:T(8,128)(2,1)S(1)}, f32[4,576,128]{2,1,0:T(8,128)S(1)}, f32[4,576,128]{2,1,0:T(8,128)S(1)}, f32[576,128]{1,0:T(8,128)S(1)}) custom-call(bf16[576,128]{1,0:T(8,128)(2,1)S(1)} %bitcast.5, f32[120,128]{1,0:T(8,128)S(1)} %concatenate.3.table.refs_4_.refs_5_, bf16[2,128,640]{2,1,0:T(8,128)(2,1)S(1)} %copy-done.3), custom_call_target="tpu_custom_call" | custom-call | tf_op jit(solution)/shard_map/own_sides/pallas_call | solution.py:266
  14.0 0.0 collective-permute-done.1.col.refs_1_
  14.0 2.9 %collective-permute-start.3 = (bf16[576,128]{1,0:T(8,128)(2,1)S(1)}, bf16[576,128]{1,0:T(8,128)(2,1)S(1)}, u32[]{:S(2)}, u32[]{:S(2)}) collective-permute-start(bf16[576,128]{1,0:T(8,128)(2,1)S(1)} %collective-permute-done.1.col.refs_1_), channel_id=1, source_target_pairs={{0,4},{4,0},{8,12},{12,8},{1,5},{5,1},{9,13},{13,9},{2,6},{6,2},{1... | collective-permute-start | bytes 442376 | tf_op jit(solution)/shard_map/ppermute | solution.py:252
  16.9 0.0 collective-permute-start.4
  16.9 0.6 %early_sides.1 = (f32[4,576,128]{2,1,0:T(8,128)S(1)}, f32[4,576,128]{2,1,0:T(8,128)S(1)}) custom-call(bf16[576,128]{1,0:T(8,128)(2,1)S(1)} %collective-permute-done.1.col.refs_1_, f32[120,128]{1,0:T(8,128)S(1)} %concatenate.3.table.refs_4_.refs_5_, bf16[2,128,640]{2,1,0:T(8,128)(2,1)S(1)} %get-tuple-element.28.weights.refs_5_.refs_6_), custom_call_target="tpu_custom_call" | custom-call | tf_op jit(solution)/shard_map/early_sides/pallas_call | solution.py:266
  17.5 2.1 %collective-permute-done.refs_1_ = bf16[576,128]{1,0:T(8,128)(2,1)S(1)} collective-permute-done((bf16[576,128]{1,0:T(8,128)(2,1)}, bf16[576,128]{1,0:T(8,128)(2,1)S(1)}, u32[]{:S(2)}, u32[]{:S(2)}) %collective-permute-start) | collective-permute-done | bytes 147488 | tf_op jit(solution)/shard_map/ppermute | solution.py:247
  19.6 0.4 collective-permute-start.2
  20.0 1.5 %collective-permute-start.5 = (bf16[576,128]{1,0:T(8,128)(2,1)S(1)}, bf16[576,128]{1,0:T(8,128)(2,1)S(1)}, u32[]{:S(2)}, u32[]{:S(2)}) collective-permute-start(bf16[576,128]{1,0:T(8,128)(2,1)S(1)} %collective-permute-done.1.col.refs_1_), channel_id=1, source_target_pairs={{0,12},{4,8},{8,4},{12,0},{1,13},{5,9},{9,5},{13,1},{2,14},{6,10},... | collective-permute-start | bytes 442376 | tf_op jit(solution)/shard_map/ppermute | solution.py:252
  21.5 0.0 collective-permute-done.6.refs_0_
  21.5 0.0 collective-permute-done.3.refs_2_
  21.5 1.2 %collective-permute-done.4.refs_3_ = bf16[576,128]{1,0:T(8,128)(2,1)S(1)} collective-permute-done((bf16[576,128]{1,0:T(8,128)(2,1)S(1)}, bf16[576,128]{1,0:T(8,128)(2,1)S(1)}, u32[]{:S(2)}, u32[]{:S(2)}) %collective-permute-start.4) | collective-permute-done | bytes 147488 | tf_op jit(solution)/shard_map/ppermute | solution.py:252
  22.7 0.0 copy-start
  22.7 3.9 %middle_sides.1 = (f32[4,576,128]{2,1,0:T(8,128)S(1)}, f32[4,576,128]{2,1,0:T(8,128)S(1)}, f32[4,576,128]{2,1,0:T(8,128)S(1)}, f32[4,576,128]{2,1,0:T(8,128)S(1)}, f32[576,128]{1,0:T(8,128)S(1)}) custom-call(bf16[576,128]{1,0:T(8,128)(2,1)S(1)} %collective-permute-done.6.refs_0_, ...), custom_call_target="tpu_custom_call", output_to_operand_aliasing={{0}: (6, {}), {1}: (7, {}), {2}: (8, {}), {3}: (9, {})} | custom-call | tf_op jit(solution)/shard_map/middle_sides/pallas_call | solution.py:266
  26.7 0.0 collective-permute-done.2.refs_0_
  26.7 0.0 collective-permute-done.5.refs_4_
  26.7 0.0 copy-done
  26.7 0.0 copy-start.2
  26.7 3.1 %mirror_end.1 = (bf16[576,128]{1,0:T(8,128)(2,1)S(1)}, f32[4,576,128]{2,1,0:T(8,128)S(1)}, f32[4,576,128]{2,1,0:T(8,128)S(1)}, f32[4,576,128]{2,1,0:T(8,128)S(1)}, f32[4,576,128]{2,1,0:T(8,128)S(1)}) custom-call(bf16[576,128]{1,0:T(8,128)(2,1)S(1)} %collective-permute-done.2.refs_0_, ...), custom_call_target="tpu_custom_call", output_to_operand_aliasing={{1}: (8, {}), {2}: (9, {}), {3}: (10, {}), {4}: (11, {})} | custom-call | tf_op jit(solution)/shard_map/mirror_end/pallas_call | solution.py:266
  29.7 3.1 %collective-permute-start.7 = (bf16[576,128]{1,0:T(8,128)(2,1)S(1)}, bf16[576,128]{1,0:T(8,128)(2,1)S(1)}, u32[]{:S(2)}, u32[]{:S(2)}) collective-permute-start(bf16[576,128]{1,0:T(8,128)(2,1)S(1)} %get-tuple-element.39.refs_0_), channel_id=1, source_target_pairs={{0,2},{1,3},{2,0},{3,1},{4,6},{5,7},{6,4},{7,5},{8,10},{9,11},{10,... | collective-permute-start | bytes 442376 | tf_op jit(solution)/shard_map/ppermute | solution.py:247
  32.8 1.5 %collective-permute-start.10 = (bf16[576,128]{1,0:T(8,128)(2,1)S(1)}, bf16[576,128]{1,0:T(8,128)(2,1)S(1)}, u32[]{:S(2)}, u32[]{:S(2)}) collective-permute-start(bf16[576,128]{1,0:T(8,128)(2,1)S(1)} %get-tuple-element.39.refs_0_), channel_id=1, source_target_pairs={{0,1},{1,0},{2,3},{3,2},{4,5},{5,4},{6,7},{7,6},{8,9},{9,8},{10,11... | collective-permute-start | bytes 442376 | tf_op jit(solution)/shard_map/ppermute | solution.py:247
  34.3 0.0 copy-done.2
  34.3 3.6 %own_end.1 = (bf16[576,128]{1,0:T(8,128)(2,1)S(1)}, bf16[576,128]{1,0:T(8,128)(2,1)S(1)}) custom-call(f32[4,576,128]{2,1,0:T(8,128)S(1)} %get-tuple-element.40.row_l, f32[4,576,128]{2,1,0:T(8,128)S(1)} %get-tuple-element.41.col_r, f32[120,128]{1,0:T(8,128)S(1)} %concatenate.3.table.refs_4_.refs_5_, ...), custom_call_target="tpu_custom_call" | custom-call | tf_op jit(solution)/shard_map/own_end/pallas_call | solution.py:266
  38.0 0.1 collective-permute-start.12
  38.0 2.0 %collective-permute-start.9 = (bf16[576,128]{1,0:T(8,128)(2,1)S(1)}, bf16[576,128]{1,0:T(8,128)(2,1)S(1)}, u32[]{:S(2)}, u32[]{:S(2)}) collective-permute-start(bf16[576,128]{1,0:T(8,128)(2,1)S(1)} %get-tuple-element.43.refs_0_), channel_id=1, source_target_pairs={{0,8},{4,12},{8,0},{12,4},{1,9},{5,13},{9,1},{13,5},{2,10},{6,14},... | collective-permute-start | bytes 442376 | tf_op jit(solution)/shard_map/ppermute | solution.py:247
  40.0 0.5 %gate.1.gating = f32[576,128]{1,0:T(8,128)S(1)} custom-call(bf16[576,128]{1,0:T(8,128)(2,1)S(1)} %get-tuple-element.46.pair, f32[120,128]{1,0:T(8,128)S(1)} %concatenate.3.table.refs_4_.refs_5_, bf16[2,128,640]{2,1,0:T(8,128)(2,1)S(1)} %get-tuple-element.28.weights.refs_5_.refs_6_), custom_call_target="tpu_custom_call" | custom-call | tf_op jit(solution)/shard_map/gate/pallas_call | solution.py:266
  40.6 0.0 collective-permute-done.7.refs_2_
  40.6 0.7 %collective-permute-start.8 = (bf16[576,128]{1,0:T(8,128)(2,1)S(1)}, bf16[576,128]{1,0:T(8,128)(2,1)S(1)}, u32[]{:S(2)}, u32[]{:S(2)}) collective-permute-start(bf16[576,128]{1,0:T(8,128)(2,1)S(1)} %collective-permute-done.7.refs_2_), channel_id=1, source_target_pairs={{0,1},{1,0},{2,3},{3,2},{4,5},{5,4},{6,7},{7,6},{8,9},{9,8},{10,11... | collective-permute-start | bytes 442376 | tf_op jit(solution)/shard_map/ppermute | solution.py:247
  41.3 0.0 collective-permute-done.10.refs_1_
  41.3 0.1 left_slots.1.refs_3_.left_in
  41.3 3.2 %collective-permute-done.9.refs_2_ = bf16[576,128]{1,0:T(8,128)(2,1)S(1)} collective-permute-done((bf16[576,128]{1,0:T(8,128)(2,1)S(1)}, bf16[576,128]{1,0:T(8,128)(2,1)S(1)}, u32[]{:S(2)}, u32[]{:S(2)}) %collective-permute-start.9) | collective-permute-done | bytes 147488 | tf_op jit(solution)/shard_map/ppermute | solution.py:247
  44.5 0.0 collective-permute-start.11
  44.5 0.0 collective-permute-done.12.refs_1_
  44.5 2.1 %middle_slots.1 = (f32[4,576,128]{2,1,0:T(8,128)S(1)}, f32[576,128]{1,0:T(8,128)S(1)}) custom-call(bf16[576,128]{1,0:T(8,128)(2,1)S(1)} %get-tuple-element.43.refs_0_, bf16[576,128]{1,0:T(8,128)(2,1)S(1)} %collective-permute-done.12.refs_1_, bf16[576,128]{1,0:T(8,128)(2,1)S(1)} %collective-permute-done.9.refs_2_, f32[4,576,128]{2,1,0:T(8,128)S(1)} %left_slots.1.refs_3_.left_in), custom_call_target="tpu_custom_call" | custom-call | tf_op jit(solution)/shard_map/middle_slots/pallas_call | solution.py:266
  46.6 0.0 collective-permute-done.8.block
  46.6 0.0 collective-permute-done.11.right
  46.6 1.9 %end.1 = (bf16[576,128]{1,0:T(8,128)(2,1)}, f32[4,576,128]{2,1,0:T(8,128)S(1)}, f32[4,576,128]{2,1,0:T(8,128)S(1)}) custom-call(f32[576,128]{1,0:T(8,128)S(1)} %left_last.1.left, bf16[576,128]{1,0:T(8,128)(2,1)S(1)} %collective-permute-done.11.right, f32[576,128]{1,0:T(8,128)S(1)} %get-tuple-element.45.old, ...), custom_call_target="tpu_custom_call", output_to_operand_aliasing={{1}: (7, {}), {2}: (8, {})} | custom-call | tf_op jit(solution)/shard_map/end/pallas_call | solution.py:266
  (2 shorter events, 0.0 us)
Async XLA Ops:
  0.0 14.0 %collective-permute-start.1 = (bf16[576,128]{1,0:T(8,128)(2,1)}, bf16[576,128]{1,0:T(8,128)(2,1)S(1)}, u32[]{:S(2)}, u32[]{:S(2)}) collective-permute-start(bf16[576,128]{1,0:T(8,128)(2,1)} %bitcast.2), channel_id=1, source_target_pairs={{0,0},{1,8},{2,4},{3,12},{4,1},{5,9},{6,5},{7,13},{8,2},{9,10},{10... | collective-permute-start | bytes 442376 | tf_op jit(solution)/shard_map/ppermute | solution.py:256
  1.6 18.1 %collective-permute-start = (bf16[576,128]{1,0:T(8,128)(2,1)}, bf16[576,128]{1,0:T(8,128)(2,1)S(1)}, u32[]{:S(2)}, u32[]{:S(2)}) collective-permute-start(bf16[576,128]{1,0:T(8,128)(2,1)} %bitcast.3), channel_id=1, source_target_pairs={{0,2},{1,3},{2,0},{3,1},{4,6},{5,7},{6,4},{7,5},{8,10},{9,11},{10,... | collective-permute-start | bytes 442376 | tf_op jit(solution)/shard_map/ppermute | solution.py:247
  6.0 15.4 %collective-permute-start.6 = (bf16[576,128]{1,0:T(8,128)(2,1)}, bf16[576,128]{1,0:T(8,128)(2,1)S(1)}, u32[]{:S(2)}, u32[]{:S(2)}) collective-permute-start(bf16[576,128]{1,0:T(8,128)(2,1)} %bitcast.4), channel_id=1, source_target_pairs={{0,1},{1,0},{2,3},{3,2},{4,5},{5,4},{6,7},{7,6},{8,9},{9,8},{10,11... | collective-permute-start | bytes 442376 | tf_op jit(solution)/shard_map/ppermute | solution.py:247
  11.1 0.9 %copy-start.1 = (bf16[24,24,128]{2,1,0:T(8,128)(2,1)S(1)}, bf16[24,24,128]{2,1,0:T(8,128)(2,1)}, u32[]{:S(2)}) copy-start(bf16[24,24,128]{2,1,0:T(8,128)(2,1)} %param.10) | copy-start | bytes 442372
  12.0 1.0 %copy-start.3 = (bf16[2,128,640]{2,1,0:T(8,128)(2,1)S(1)}, bf16[2,128,640]{2,1,0:T(8,128)(2,1)}, u32[]{:S(2)}) copy-start(bf16[2,128,640]{2,1,0:T(8,128)(2,1)} %w_in.1) | copy-start | bytes 983044
  14.0 7.5 %collective-permute-start.3 = (bf16[576,128]{1,0:T(8,128)(2,1)S(1)}, bf16[576,128]{1,0:T(8,128)(2,1)S(1)}, u32[]{:S(2)}, u32[]{:S(2)}) collective-permute-start(bf16[576,128]{1,0:T(8,128)(2,1)S(1)} %collective-permute-done.1.col.refs_1_), channel_id=1, source_target_pairs={{0,4},{4,0},{8,12},{12,8},{1,5},{5,1},{9,13},{13,9},{2,6},{6,2},{1... | collective-permute-start | bytes 442376 | tf_op jit(solution)/shard_map/ppermute | solution.py:252
  16.9 5.8 %collective-permute-start.4 = (bf16[576,128]{1,0:T(8,128)(2,1)S(1)}, bf16[576,128]{1,0:T(8,128)(2,1)S(1)}, u32[]{:S(2)}, u32[]{:S(2)}) collective-permute-start(bf16[576,128]{1,0:T(8,128)(2,1)S(1)} %collective-permute-done.1.col.refs_1_), channel_id=1, source_target_pairs={{0,8},{4,12},{8,0},{12,4},{1,9},{5,13},{9,1},{13,5},{2,10},{6,14},... | collective-permute-start | bytes 442376 | tf_op jit(solution)/shard_map/ppermute | solution.py:252
  19.6 7.0 %collective-permute-start.2 = (bf16[576,128]{1,0:T(8,128)(2,1)S(1)}, bf16[576,128]{1,0:T(8,128)(2,1)S(1)}, u32[]{:S(2)}, u32[]{:S(2)}) collective-permute-start(bf16[576,128]{1,0:T(8,128)(2,1)S(1)} %collective-permute-done.refs_1_), channel_id=1, source_target_pairs={{0,1},{1,0},{2,3},{3,2},{4,5},{5,4},{6,7},{7,6},{8,9},{9,8},{10,11... | collective-permute-start | bytes 442376 | tf_op jit(solution)/shard_map/ppermute | solution.py:247
  20.0 6.7 %collective-permute-start.5 = (bf16[576,128]{1,0:T(8,128)(2,1)S(1)}, bf16[576,128]{1,0:T(8,128)(2,1)S(1)}, u32[]{:S(2)}, u32[]{:S(2)}) collective-permute-start(bf16[576,128]{1,0:T(8,128)(2,1)S(1)} %collective-permute-done.1.col.refs_1_), channel_id=1, source_target_pairs={{0,12},{4,8},{8,4},{12,0},{1,13},{5,9},{9,5},{13,1},{2,14},{6,10},... | collective-permute-start | bytes 442376 | tf_op jit(solution)/shard_map/ppermute | solution.py:252
  22.7 4.0 %copy-start = (bf16[2,128,128]{2,1,0:T(8,128)(2,1)S(1)}, bf16[2,128,128]{2,1,0:T(8,128)(2,1)}, u32[]{:S(2)}) copy-start(bf16[2,128,128]{2,1,0:T(8,128)(2,1)} %w_out.3) | copy-start | bytes 196612
  26.7 7.6 %copy-start.2 = (bf16[24,24,128]{2,1,0:T(8,128)(2,1)S(1)}, bf16[24,24,128]{2,1,0:T(8,128)(2,1)}, u32[]{:S(2)}) copy-start(bf16[24,24,128]{2,1,0:T(8,128)(2,1)} %param.10) | copy-start | bytes 442372
  29.7 10.8 %collective-permute-start.7 = (bf16[576,128]{1,0:T(8,128)(2,1)S(1)}, bf16[576,128]{1,0:T(8,128)(2,1)S(1)}, u32[]{:S(2)}, u32[]{:S(2)}) collective-permute-start(bf16[576,128]{1,0:T(8,128)(2,1)S(1)} %get-tuple-element.39.refs_0_), channel_id=1, source_target_pairs={{0,2},{1,3},{2,0},{3,1},{4,6},{5,7},{6,4},{7,5},{8,10},{9,11},{10,... | collective-permute-start | bytes 442376 | tf_op jit(solution)/shard_map/ppermute | solution.py:247
  32.8 8.4 %collective-permute-start.10 = (bf16[576,128]{1,0:T(8,128)(2,1)S(1)}, bf16[576,128]{1,0:T(8,128)(2,1)S(1)}, u32[]{:S(2)}, u32[]{:S(2)}) collective-permute-start(bf16[576,128]{1,0:T(8,128)(2,1)S(1)} %get-tuple-element.39.refs_0_), channel_id=1, source_target_pairs={{0,1},{1,0},{2,3},{3,2},{4,5},{5,4},{6,7},{7,6},{8,9},{9,8},{10,11... | collective-permute-start | bytes 442376 | tf_op jit(solution)/shard_map/ppermute | solution.py:247
  38.0 6.5 %collective-permute-start.12 = (bf16[576,128]{1,0:T(8,128)(2,1)S(1)}, bf16[576,128]{1,0:T(8,128)(2,1)S(1)}, u32[]{:S(2)}, u32[]{:S(2)}) collective-permute-start(bf16[576,128]{1,0:T(8,128)(2,1)S(1)} %get-tuple-element.43.refs_0_), channel_id=1, source_target_pairs={{0,4},{4,0},{8,12},{12,8},{1,5},{5,1},{9,13},{13,9},{2,6},{6,2},{1... | collective-permute-start | bytes 442376 | tf_op jit(solution)/shard_map/ppermute | solution.py:247
  38.0 6.5 %collective-permute-start.9 = (bf16[576,128]{1,0:T(8,128)(2,1)S(1)}, bf16[576,128]{1,0:T(8,128)(2,1)S(1)}, u32[]{:S(2)}, u32[]{:S(2)}) collective-permute-start(bf16[576,128]{1,0:T(8,128)(2,1)S(1)} %get-tuple-element.43.refs_0_), channel_id=1, source_target_pairs={{0,8},{4,12},{8,0},{12,4},{1,9},{5,13},{9,1},{13,5},{2,10},{6,14},... | collective-permute-start | bytes 442376 | tf_op jit(solution)/shard_map/ppermute | solution.py:247
  40.6 6.0 %collective-permute-start.8 = (bf16[576,128]{1,0:T(8,128)(2,1)S(1)}, bf16[576,128]{1,0:T(8,128)(2,1)S(1)}, u32[]{:S(2)}, u32[]{:S(2)}) collective-permute-start(bf16[576,128]{1,0:T(8,128)(2,1)S(1)} %collective-permute-done.7.refs_2_), channel_id=1, source_target_pairs={{0,1},{1,0},{2,3},{3,2},{4,5},{5,4},{6,7},{7,6},{8,9},{9,8},{10,11... | collective-permute-start | bytes 442376 | tf_op jit(solution)/shard_map/ppermute | solution.py:247
  44.5 2.1 %collective-permute-start.11 = (bf16[576,128]{1,0:T(8,128)(2,1)S(1)}, bf16[576,128]{1,0:T(8,128)(2,1)S(1)}, u32[]{:S(2)}, u32[]{:S(2)}) collective-permute-start(bf16[576,128]{1,0:T(8,128)(2,1)S(1)} %collective-permute-done.9.refs_2_), channel_id=1, source_target_pairs={{0,4},{4,0},{8,12},{12,8},{1,5},{5,1},{9,13},{13,9},{2,6},{6,2},{1... | collective-permute-start | bytes 442376 | tf_op jit(solution)/shard_map/ppermute | solution.py:247

commit v15 on v14

--- a/solution.py
+++ b/solution.py
@@ -151,16 +151,26 @@
     sides(col, wide, col_l.at[0], col_r.at[0], outer, inner, constants(wide.shape[1]), table, weights)
 
 
-def middle_sides_kernel(n, t, *refs):
-    rows, cols, (table, weights) = refs[: n - 2], refs[n - 2 : 2 * n - 4], refs[2 * n - 4 : 2 * n - 2]
-    row_l, row_r, col_l, col_r, mixed, wide = refs[2 * n + 2 :]
+def first_sides_kernel(n, t, *refs):
+    rows, (col, table, weights) = refs[: n - 2], refs[n - 2 : n + 1]
+    row_l, row_r, col_l, col_r, wide = refs[n + 5 :]
     r, c = lax.axis_index("row"), lax.axis_index("col")
     consts = constants(wide.shape[1])
     here, there = mask_of(table, r, t), mask_of(table, c, t)
     for s, block in enumerate(rows, 1):
         outer = mask_of(table, c ^ s, t)
         sides(block, wide, row_l.at[s], row_r.at[s], outer, here, consts, table, weights)
-    for s, block in enumerate(cols, 1):
+    outer = mask_of(table, placed_at(r ^ 1, n), t)
+    sides(col, wide, col_l.at[1], col_r.at[1], outer, there, consts, table, weights)
+
+
+def second_sides_kernel(n, t, *refs):
+    cols, (table, weights, row_r) = refs[: n - 3], refs[n - 3 : n]
+    col_l, col_r, mixed, wide = refs[n + 2 :]
+    r, c = lax.axis_index("row"), lax.axis_index("col")
+    consts = constants(wide.shape[1])
+    there = mask_of(table, c, t)
+    for s, block in enumerate(cols, 2):
         outer = mask_of(table, placed_at(r ^ s, n), t)
         sides(block, wide, col_l.at[s], col_r.at[s], outer, there, consts, table, weights)
     count, slot = early_pairs(c ^ placed_at(r ^ (n - 1), n), n)
@@ -217,13 +227,27 @@
     out[...] = block[...].astype(F32)
 
 
-def middle_kernel(n, t, *refs):
-    sources, (lefts, rights, mixed) = refs[: n - 1], refs[n - 1 :]
-    r, c = lax.axis_index("row"), lax.axis_index("col")
-    for s in range(n - 1):
-        rights[s] = sources[s][...].astype(F32)
-    count, slot = early_pairs(r ^ c ^ (n - 1), n)
-    mix(mixed, None, lefts, rights, 0, count, slot, lambda i: r ^ c ^ slot(i), t)
+def right_lot(late, first, last):
+    skips = (late >= first) & (late < last)
+    count = last - first - jnp.where(skips, 1, 0)
+    return count, lambda i: first + i + jnp.where(skips & (first + i >= late), 1, 0)
+
+
+def near_kernel(n, t, own, core, lefts, rights, mixed):
+    r, c = lax.axis_index("row"), lax.axis_index("col")
+    rights[0] = own[...].astype(F32)
+    rights[1] = core[...].astype(F32)
+    count, slot = right_lot(r ^ c ^ (n - 1), 0, 2)
+    mix(mixed, None, lefts, rights, 0, count, lambda i: r ^ c ^ slot(i), slot, t)
+
+
+def far_kernel(n, t, *refs):
+    sources, (lefts, _, old, rights, mixed) = refs[: n - 3], refs[n - 3 :]
+    r, c = lax.axis_index("row"), lax.axis_index("col")
+    for s, source in enumerate(sources, 2):
+        rights[s] = source[...].astype(F32)
+    count, slot = right_lot(r ^ c ^ (n - 1), 2, n - 1)
+    mix(mixed, old, lefts, rights, 0, count, lambda i: r ^ c ^ slot(i), slot, t)
 
 
 def end_kernel(n, t, left, right, old, pair, gating, table, w_out, left_in, right_in, out, lefts, rights, mixed):
@@ -248,8 +272,10 @@
             step //= 2
         return [held[s] for s in range(n)]
 
-    def direct(block):
-        return [block] + [lax.ppermute(block, "row", [(k, k ^ s) for k in range(n)]) for s in range(1, n)]
+    def direct(block, last):
+        return [block] + [
+            lax.ppermute(last if s == n - 1 else block, "row", [(k, k ^ s) for k in range(n)]) for s in range(1, n)
+        ]
 
     def mirrored(block):
         pairs = [(a * n + z, (z // 2 + z % 2 * (n // 2)) * n + a) for a in range(n) for z in range(n)]
@@ -295,21 +321,34 @@
             functools.partial(early_kernel, n, t), "early_sides", (slots,) * 2, [scratch], col_block, table, weights
         )
         rows = gather(pair, "col", lambda s, step: (own_l, col_l) if s else ())
-        cols = direct(lax.optimization_barrier((col_block, own_l))[0])
-        row_l, row_r, col_l, col_r, mixed = call(
-            functools.partial(middle_sides_kernel, n, t),
-            "middle_sides",
-            (slots,) * 4 + (broad,),
+        cols = direct(*(lax.optimization_barrier((col_block, after))[0] for after in (own_l, col_l)))
+        row_l, row_r, col_l, col_r = call(
+            functools.partial(first_sides_kernel, n, t),
+            "first_sides",
+            (slots,) * 4,
             [scratch],
             *rows[1:-1],
-            *cols[1:-1],
+            cols[1],
             table,
             weights,
             row_l,
             row_r,
             col_l,
             col_r,
-            alias={2 * n - 2: 0, 2 * n - 1: 1, 2 * n: 2, 2 * n + 1: 3},
+            alias={n + 1: 0, n + 2: 1, n + 3: 2, n + 4: 3},
+        )
+        col_l, col_r, mixed = call(
+            functools.partial(second_sides_kernel, n, t),
+            "second_sides",
+            (slots, slots, broad),
+            [scratch],
+            *cols[2:-1],
+            table,
+            weights,
+            row_r,
+            col_l,
+            col_r,
+            alias={n: 0, n + 1: 1},
         )
         left, row_l, _, _, col_r = call(
             functools.partial(mirror_kernel, n, t),
@@ -343,10 +382,23 @@
         )
         lefts = gather(left, "col", lambda s, step: ())
         left_slots = call(functools.partial(left_kernel, n), "left_slots", slots, [], *lefts[:-1], weight=20)
-        rights = gather(right, "row", lambda s, step: left_slots if s else ())
-        gating = call(gate_kernel, "gate", broad, [], pair, table, weights)
+        core = lax.ppermute(right, "row", [(k, k ^ 1) for k in range(n)])
         right_slots, mixed = call(
-            functools.partial(middle_kernel, n, t), "middle_slots", (slots, broad), [], *rights[:-1], left_slots
+            functools.partial(near_kernel, n, t), "near_slots", (slots, broad), [], right, core, left_slots
+        )
+        rights = gather(right, "row", lambda s, step: mixed if s else ())
+        settled = lax.optimization_barrier((pair, left_slots))[0]
+        gating = call(gate_kernel, "gate", broad, [], settled, table, weights)
+        right_slots, mixed = call(
+            functools.partial(far_kernel, n, t),
+            "far_slots",
+            (slots, broad),
+            [],
+            *rights[2:-1],
+            left_slots,
+            right_slots,
+            mixed,
+            alias={n - 2: 0, n - 1: 1},
         )
         left_last = call(widen_kernel, "left_last", broad, [], lefts[-1], weight=30)
         out, _, _ = call(

time: 48.9 us -> 47.1 us (0.963)
  waiting for transfers between devices: 6.56 us -> 4.65 us
    ppermute x3 -> x4, waiting for transfers between devices: 1.24 us -> 0.01 us  [the longest x3 0.01 us: direct(): lax.ppermute(last if s == n - 1 else block, 'row', [(k, k ^ s) for k in r...]
    ppermute x9 -> x8, waiting for transfers between devices: 5.32 us -> 4.64 us  [gather(): held[s ^ step] = lax.ppermute(part, axis, [(k, k ^ step) for k in range(n)])]
    ppermute x9 -> x8, starting transfers between devices: 14.3 us -> 13.9 us  [gather(): held[s ^ step] = lax.ppermute(part, axis, [(k, k ^ step) for k in range(n)])]
    ppermute x3 -> x4, starting transfers between devices: 4.43 us -> 4.78 us  [the longest x3 4.71 us: direct(): lax.ppermute(last if s == n - 1 else block, 'row', [(k, k ^ s) for k in r...]
    pallas_call x10 -> x12, Pallas kernels: 16.8 us -> 17 us  [call(): pl.pallas_call(kernel, out_shape=outs, scratch_shapes=scratches, input_ou...]
  transfers between devices with their start and end apart: 13 -> 13, of which waited for: 3 -> 4; matrix products, arithmetic and copies ran while one was open for 6% -> 6% of each run, Pallas kernels for 24% -> 26%
where the time goes in v15:
time: 47.1 us; the launch traced here: 46.9 us
  starting transfers between devices  20.2 us (43%)
  Pallas kernels  17 us (36%)
  waiting for transfers between devices  4.65 us (10%)
  local copies, waits for them, and re-layouts  4.17 us (9%)
  other arithmetic  0.66 us (1%)
    pallas_call x12, Pallas kernels, call(): pl.pallas_call(kernel, out_shape=outs, scratch_shapes=scratches, input_ou...  17 us
    ppermute x8, starting transfers between devices, gather(): held[s ^ step] = lax.ppermute(part, axis, [(k, k ^ step) for k in range(n)])  13.9 us
    ppermute x3, starting transfers between devices, direct(): lax.ppermute(last if s == n - 1 else block, 'row', [(k, k ^ s) for k in r...  4.71 us
    ppermute x8, waiting for transfers between devices, gather(): held[s ^ step] = lax.ppermute(part, axis, [(k, k ^ step) for k in range(n)])  4.64 us
    unnamed x8, local copies, waits for them, and re-layouts  1.89 us
    ppermute x1, starting transfers between devices, mirrored(): return lax.ppermute(block, ('row', 'col'), pairs)  1.56 us
    concatenate x1, local copies, waits for them, and re-layouts, per_device(): jnp.concatenate(vectors + [jnp.zeros((TABLE_MASK - 20, width), F32), mask])  1.51 us
  transfers between devices with their start and end apart: 13, of which 4 were waited for; matrix products, arithmetic and copies ran while one was open for 6% of the time, Pallas kernels for 26%

profile of v15, /device:TPU:0, one launch (start us, length us, event | category | flops | bytes accessed | tf_op | source)
XLA Modules:
  0.0 46.9 jit_solution(7581391867930586195)
XLA Ops:
  0.0 1.6 %collective-permute-start.1 = (bf16[576,128]{1,0:T(8,128)(2,1)}, bf16[576,128]{1,0:T(8,128)(2,1)S(1)}, u32[]{:S(2)}, u32[]{:S(2)}) collective-permute-start(bf16[576,128]{1,0:T(8,128)(2,1)} %bitcast.2), channel_id=1, source_target_pairs={{0,0},{1,8},{2,4},{3,12},{4,1},{5,9},{6,5},{7,13},{8,2},{9,10},{10... | collective-permute-start | bytes 442376 | tf_op jit(solution)/shard_map/ppermute | solution.py:282
  1.6 4.5 %collective-permute-start = (bf16[576,128]{1,0:T(8,128)(2,1)}, bf16[576,128]{1,0:T(8,128)(2,1)S(1)}, u32[]{:S(2)}, u32[]{:S(2)}) collective-permute-start(bf16[576,128]{1,0:T(8,128)(2,1)} %bitcast.3), channel_id=1, source_target_pairs={{0,2},{1,3},{2,0},{3,1},{4,6},{5,7},{6,4},{7,5},{8,10},{9,11},{10,... | collective-permute-start | bytes 442376 | tf_op jit(solution)/shard_map/ppermute | solution.py:271
  6.0 2.2 %collective-permute-start.6 = (bf16[576,128]{1,0:T(8,128)(2,1)}, bf16[576,128]{1,0:T(8,128)(2,1)S(1)}, u32[]{:S(2)}, u32[]{:S(2)}) collective-permute-start(bf16[576,128]{1,0:T(8,128)(2,1)} %bitcast.4), channel_id=1, source_target_pairs={{0,1},{1,0},{2,3},{3,2},{4,5},{5,4},{6,7},{7,6},{8,9},{9,8},{10,11... | collective-permute-start | bytes 442376 | tf_op jit(solution)/shard_map/ppermute | solution.py:271
  8.2 0.7 %convert_element_type.3 = f32[96]{0:T(128)S(1)} convert(s32[96]{0:T(128)} %param.11) | non-fusion elementwise | flops 96 | bytes 768 | tf_op jit(solution)/shard_map/convert_element_type | solution.py:307
  8.8 0.7 %reshape.11 = f32[10,128]{1,0:T(8,128)S(1)} reshape(f32[2,640]{1,0:T(2,128)} %param.15) | data formatting | bytes 10240 | tf_op jit(solution)/shard_map/reshape | solution.py:308
  9.5 0.1 broadcast_in_dim.10
  9.6 1.5 %concatenate.3.table.refs_3_.refs_1_.refs_5_ = f32[120,128]{1,0:T(8,128)S(1)} concatenate(f32[2,128]{1,0:T(2,128)} %param.12, f32[2,128]{1,0:T(2,128)} %param.13, f32[2,128]{1,0:T(2,128)} %param.16, f32[2,128]{1,0:T(2,128)} %param.17, f32[2,128]{1,0:T(2,128)} %param.19, f32[10,128]{1,0:T(8,128)S(1)} %reshape.11, f32[4,128]{1,0:T(4,128)S(1)} %broadcast_in_dim.4, ...), dimensions={0} | concatenate | bytes 122880 | tf_op jit(solution)/shard_map/concatenate | solution.py:309
  11.1 0.9 %copy-done.1 = bf16[24,24,128]{2,1,0:T(8,128)(2,1)S(1)} copy-done((bf16[24,24,128]{2,1,0:T(8,128)(2,1)S(1)}, bf16[24,24,128]{2,1,0:T(8,128)(2,1)}, u32[]{:S(2)}) %copy-start.1) | copy-done | bytes 147480
  12.0 0.0 copy-start.3
  12.0 1.0 %copy-done.3 = bf16[2,128,640]{2,1,0:T(8,128)(2,1)S(1)} copy-done((bf16[2,128,640]{2,1,0:T(8,128)(2,1)S(1)}, bf16[2,128,640]{2,1,0:T(8,128)(2,1)}, u32[]{:S(2)}) %copy-start.3) | copy-done | bytes 327704
  13.0 1.0 %own_sides.1 = (bf16[2,128,640]{2,1,0:T(8,128)(2,1)S(1)}, f32[4,576,128]{2,1,0:T(8,128)S(1)}, f32[4,576,128]{2,1,0:T(8,128)S(1)}, f32[576,128]{1,0:T(8,128)S(1)}) custom-call(bf16[576,128]{1,0:T(8,128)(2,1)S(1)} %bitcast.5, f32[120,128]{1,0:T(8,128)S(1)} %concatenate.3.table.refs_3_.refs_1_.refs_5_, bf16[2,128,640]{2,1,0:T(8,128)(2,1)S(1)} %copy-done.3), custom_call_target="tpu_custom_call" | custom-call | tf_op jit(solution)/shard_map/own_sides/pallas_call | solution.py:292
  14.0 0.0 collective-permute-done.1.col.refs_1_
  14.0 1.0 %collective-permute-start.4 = (bf16[576,128]{1,0:T(8,128)(2,1)S(1)}, bf16[576,128]{1,0:T(8,128)(2,1)S(1)}, u32[]{:S(2)}, u32[]{:S(2)}) collective-permute-start(bf16[576,128]{1,0:T(8,128)(2,1)S(1)} %collective-permute-done.1.col.refs_1_), channel_id=1, source_target_pairs={{0,8},{4,12},{8,0},{12,4},{1,9},{5,13},{9,1},{13,5},{2,10},{6,14},... | collective-permute-start | bytes 442376 | tf_op jit(solution)/shard_map/ppermute | solution.py:277
  15.0 2.0 %collective-permute-start.3 = (bf16[576,128]{1,0:T(8,128)(2,1)S(1)}, bf16[576,128]{1,0:T(8,128)(2,1)S(1)}, u32[]{:S(2)}, u32[]{:S(2)}) collective-permute-start(bf16[576,128]{1,0:T(8,128)(2,1)S(1)} %collective-permute-done.1.col.refs_1_), channel_id=1, source_target_pairs={{0,4},{4,0},{8,12},{12,8},{1,5},{5,1},{9,13},{13,9},{2,6},{6,2},{1... | collective-permute-start | bytes 442376 | tf_op jit(solution)/shard_map/ppermute | solution.py:277
  16.9 0.6 %early_sides.1 = (f32[4,576,128]{2,1,0:T(8,128)S(1)}, f32[4,576,128]{2,1,0:T(8,128)S(1)}) custom-call(bf16[576,128]{1,0:T(8,128)(2,1)S(1)} %collective-permute-done.1.col.refs_1_, f32[120,128]{1,0:T(8,128)S(1)} %concatenate.3.table.refs_3_.refs_1_.refs_5_, bf16[2,128,640]{2,1,0:T(8,128)(2,1)S(1)} %get-tuple-element.34.weights.refs_4_.refs_2_.refs_6_), custom_call_target="tpu_custom_call" | custom-call | tf_op jit(solution)/shard_map/early_sides/pallas_call | solution.py:292
  17.5 2.1 %collective-permute-done.refs_1_ = bf16[576,128]{1,0:T(8,128)(2,1)S(1)} collective-permute-done((bf16[576,128]{1,0:T(8,128)(2,1)}, bf16[576,128]{1,0:T(8,128)(2,1)S(1)}, u32[]{:S(2)}, u32[]{:S(2)}) %collective-permute-start) | collective-permute-done | bytes 147488 | tf_op jit(solution)/shard_map/ppermute | solution.py:271
  19.6 0.1 collective-permute-start.2
  19.7 1.8 %collective-permute-start.5 = (bf16[576,128]{1,0:T(8,128)(2,1)S(1)}, bf16[576,128]{1,0:T(8,128)(2,1)S(1)}, u32[]{:S(2)}, u32[]{:S(2)}) collective-permute-start(bf16[576,128]{1,0:T(8,128)(2,1)S(1)} %collective-permute-done.1.col.refs_1_), channel_id=1, source_target_pairs={{0,12},{4,8},{8,4},{12,0},{1,13},{5,9},{9,5},{13,1},{2,14},{6,10},... | collective-permute-start | bytes 442376 | tf_op jit(solution)/shard_map/ppermute | solution.py:277
  21.5 0.0 collective-permute-done.6.refs_0_
  21.5 0.0 collective-permute-done.3.refs_2_
  21.5 1.5 %first_sides.1 = (f32[4,576,128]{2,1,0:T(8,128)S(1)}, f32[4,576,128]{2,1,0:T(8,128)S(1)}, f32[4,576,128]{2,1,0:T(8,128)S(1)}, f32[4,576,128]{2,1,0:T(8,128)S(1)}) custom-call(bf16[576,128]{1,0:T(8,128)(2,1)S(1)} %collective-permute-done.6.refs_0_, ...), custom_call_target="tpu_custom_call", output_to_operand_aliasing={{0}: (5, {}), {1}: (6, {}), {2}: (7, {}), {3}: (8, {})} | custom-call | tf_op jit(solution)/shard_map/first_sides/pallas_call | solution.py:292
  22.9 0.0 collective-permute-done.4.refs_0_.refs_3_
  22.9 0.0 copy-start
  22.9 2.6 %second_sides.1 = (f32[4,576,128]{2,1,0:T(8,128)S(1)}, f32[4,576,128]{2,1,0:T(8,128)S(1)}, f32[576,128]{1,0:T(8,128)S(1)}) custom-call(bf16[576,128]{1,0:T(8,128)(2,1)S(1)} %collective-permute-done.4.refs_0_.refs_3_, f32[120,128]{1,0:T(8,128)S(1)} %concatenate.3.table.refs_3_.refs_1_.refs_5_, ...), custom_call_target="tpu_custom_call", output_to_operand_aliasing={{0}: (4, {}), {1}: (5, {})} | custom-call | tf_op jit(solution)/shard_map/second_sides/pallas_call | solution.py:292
  25.6 0.0 collective-permute-done.2.refs_0_
  25.6 0.0 collective-permute-done.5.refs_4_
  25.6 0.0 copy-done
  25.6 0.0 copy-start.2
  25.6 3.1 %mirror_end.1 = (bf16[576,128]{1,0:T(8,128)(2,1)S(1)}, f32[4,576,128]{2,1,0:T(8,128)S(1)}, f32[4,576,128]{2,1,0:T(8,128)S(1)}, f32[4,576,128]{2,1,0:T(8,128)S(1)}, f32[4,576,128]{2,1,0:T(8,128)S(1)}) custom-call(bf16[576,128]{1,0:T(8,128)(2,1)S(1)} %collective-permute-done.2.refs_0_, ...), custom_call_target="tpu_custom_call", output_to_operand_aliasing={{1}: (8, {}), {2}: (9, {}), {3}: (10, {}), {4}: (11, {})} | custom-call | tf_op jit(solution)/shard_map/mirror_end/pallas_call | solution.py:292
  28.7 4.1 %collective-permute-start.7 = (bf16[576,128]{1,0:T(8,128)(2,1)S(1)}, bf16[576,128]{1,0:T(8,128)(2,1)S(1)}, u32[]{:S(2)}, u32[]{:S(2)}) collective-permute-start(bf16[576,128]{1,0:T(8,128)(2,1)S(1)} %get-tuple-element.48.refs_0_), channel_id=1, source_target_pairs={{0,2},{1,3},{2,0},{3,1},{4,6},{5,7},{6,4},{7,5},{8,10},{9,11},{10,... | collective-permute-start | bytes 442376 | tf_op jit(solution)/shard_map/ppermute | solution.py:271
  32.8 0.4 collective-permute-start.11
  33.2 0.0 copy-done.2
  33.2 3.6 %own_end.1 = (bf16[576,128]{1,0:T(8,128)(2,1)S(1)}, bf16[576,128]{1,0:T(8,128)(2,1)S(1)}) custom-call(f32[4,576,128]{2,1,0:T(8,128)S(1)} %get-tuple-element.49.row_l, f32[4,576,128]{2,1,0:T(8,128)S(1)} %get-tuple-element.50.col_r, f32[120,128]{1,0:T(8,128)S(1)} %concatenate.3.table.refs_3_.refs_1_.refs_5_, ...), custom_call_target="tpu_custom_call" | custom-call | tf_op jit(solution)/shard_map/own_end/pallas_call | solution.py:292
  36.9 0.1 collective-permute-start.10
  36.9 1.7 %collective-permute-start.9 = (bf16[576,128]{1,0:T(8,128)(2,1)S(1)}, bf16[576,128]{1,0:T(8,128)(2,1)S(1)}, u32[]{:S(2)}, u32[]{:S(2)}) collective-permute-start(bf16[576,128]{1,0:T(8,128)(2,1)S(1)} %get-tuple-element.52.own), channel_id=1, source_target_pairs={{0,8},{4,12},{8,0},{12,4},{1,9},{5,13},{9,1},{13,5},{2,10},{6,14},... | collective-permute-start | bytes 442376 | tf_op jit(solution)/shard_map/ppermute | solution.py:271
  38.6 1.0 %collective-permute-done.7.refs_2_ = bf16[576,128]{1,0:T(8,128)(2,1)S(1)} collective-permute-done((bf16[576,128]{1,0:T(8,128)(2,1)S(1)}, bf16[576,128]{1,0:T(8,128)(2,1)S(1)}, u32[]{:S(2)}, u32[]{:S(2)}) %collective-permute-start.7) | collective-permute-done | bytes 147488 | tf_op jit(solution)/shard_map/ppermute | solution.py:271
  39.6 1.0 %collective-permute-start.8 = (bf16[576,128]{1,0:T(8,128)(2,1)S(1)}, bf16[576,128]{1,0:T(8,128)(2,1)S(1)}, u32[]{:S(2)}, u32[]{:S(2)}) collective-permute-start(bf16[576,128]{1,0:T(8,128)(2,1)S(1)} %collective-permute-done.7.refs_2_), channel_id=1, source_target_pairs={{0,1},{1,0},{2,3},{3,2},{4,5},{5,4},{6,7},{7,6},{8,9},{9,8},{10,11... | collective-permute-start | bytes 442376 | tf_op jit(solution)/shard_map/ppermute | solution.py:271
  40.6 0.0 collective-permute-done.11.refs_1_
  40.6 0.1 left_slots.1.lefts.refs_1_.left_in
  40.7 0.5 %gate.1.gating = f32[576,128]{1,0:T(8,128)S(1)} custom-call(bf16[576,128]{1,0:T(8,128)(2,1)S(1)} %get-tuple-element.58.pair, f32[120,128]{1,0:T(8,128)S(1)} %concatenate.3.table.refs_3_.refs_1_.refs_5_, bf16[2,128,640]{2,1,0:T(8,128)(2,1)S(1)} %get-tuple-element.34.weights.refs_4_.refs_2_.refs_6_), custom_call_target="tpu_custom_call" | custom-call | tf_op jit(solution)/shard_map/gate/pallas_call | solution.py:292
  41.2 0.0 collective-permute-done.10.core
  41.3 1.4 %near_slots.1 = (f32[4,576,128]{2,1,0:T(8,128)S(1)}, f32[576,128]{1,0:T(8,128)S(1)}) custom-call(bf16[576,128]{1,0:T(8,128)(2,1)S(1)} %get-tuple-element.52.own, bf16[576,128]{1,0:T(8,128)(2,1)S(1)} %collective-permute-done.10.core, f32[4,576,128]{2,1,0:T(8,128)S(1)} %left_slots.1.lefts.refs_1_.left_in), custom_call_target="tpu_custom_call" | custom-call | tf_op jit(solution)/shard_map/near_slots/pallas_call | solution.py:292
  42.6 0.6 %collective-permute-done.9.refs_0_ = bf16[576,128]{1,0:T(8,128)(2,1)S(1)} collective-permute-done((bf16[576,128]{1,0:T(8,128)(2,1)S(1)}, bf16[576,128]{1,0:T(8,128)(2,1)S(1)}, u32[]{:S(2)}, u32[]{:S(2)}) %collective-permute-start.9) | collective-permute-done | bytes 147488 | tf_op jit(solution)/shard_map/ppermute | solution.py:271
  43.2 0.0 collective-permute-start.12
  43.2 0.7 %far_slots.1 = (f32[4,576,128]{2,1,0:T(8,128)S(1)}, f32[576,128]{1,0:T(8,128)S(1)}) custom-call(bf16[576,128]{1,0:T(8,128)(2,1)S(1)} %collective-permute-done.9.refs_0_, f32[4,576,128]{2,1,0:T(8,128)S(1)} %left_slots.1.lefts.refs_1_.left_in, f32[4,576,128]{2,1,0:T(8,128)S(1)} %get-tuple-element.55.refs_2_, ...), custom_call_target="tpu_custom_call", output_to_operand_aliasing={{0}: (2, {}), {1}: (3, {})} | custom-call | tf_op jit(solution)/shard_map/far_slots/pallas_call | solution.py:292
  43.9 1.0 %collective-permute-done.8.block = bf16[576,128]{1,0:T(8,128)(2,1)S(1)} collective-permute-done((bf16[576,128]{1,0:T(8,128)(2,1)S(1)}, bf16[576,128]{1,0:T(8,128)(2,1)S(1)}, u32[]{:S(2)}, u32[]{:S(2)}) %collective-permute-start.8) | collective-permute-done | bytes 147488 | tf_op jit(solution)/shard_map/ppermute | solution.py:271
  44.9 0.0 collective-permute-done.12.right
  44.9 1.9 %end.1 = (bf16[576,128]{1,0:T(8,128)(2,1)}, f32[4,576,128]{2,1,0:T(8,128)S(1)}, f32[4,576,128]{2,1,0:T(8,128)S(1)}) custom-call(f32[576,128]{1,0:T(8,128)S(1)} %left_last.1.left, bf16[576,128]{1,0:T(8,128)(2,1)S(1)} %collective-permute-done.12.right, f32[576,128]{1,0:T(8,128)S(1)} %get-tuple-element.56.old, ...), custom_call_target="tpu_custom_call", output_to_operand_aliasing={{1}: (7, {}), {2}: (8, {})} | custom-call | tf_op jit(solution)/shard_map/end/pallas_call | solution.py:292
  (3 shorter events, 0.0 us)
Async XLA Ops:
  0.0 14.0 %collective-permute-start.1 = (bf16[576,128]{1,0:T(8,128)(2,1)}, bf16[576,128]{1,0:T(8,128)(2,1)S(1)}, u32[]{:S(2)}, u32[]{:S(2)}) collective-permute-start(bf16[576,128]{1,0:T(8,128)(2,1)} %bitcast.2), channel_id=1, source_target_pairs={{0,0},{1,8},{2,4},{3,12},{4,1},{5,9},{6,5},{7,13},{8,2},{9,10},{10... | collective-permute-start | bytes 442376 | tf_op jit(solution)/shard_map/ppermute | solution.py:282
  1.6 18.1 %collective-permute-start = (bf16[576,128]{1,0:T(8,128)(2,1)}, bf16[576,128]{1,0:T(8,128)(2,1)S(1)}, u32[]{:S(2)}, u32[]{:S(2)}) collective-permute-start(bf16[576,128]{1,0:T(8,128)(2,1)} %bitcast.3), channel_id=1, source_target_pairs={{0,2},{1,3},{2,0},{3,1},{4,6},{5,7},{6,4},{7,5},{8,10},{9,11},{10,... | collective-permute-start | bytes 442376 | tf_op jit(solution)/shard_map/ppermute | solution.py:271
  6.0 15.4 %collective-permute-start.6 = (bf16[576,128]{1,0:T(8,128)(2,1)}, bf16[576,128]{1,0:T(8,128)(2,1)S(1)}, u32[]{:S(2)}, u32[]{:S(2)}) collective-permute-start(bf16[576,128]{1,0:T(8,128)(2,1)} %bitcast.4), channel_id=1, source_target_pairs={{0,1},{1,0},{2,3},{3,2},{4,5},{5,4},{6,7},{7,6},{8,9},{9,8},{10,11... | collective-permute-start | bytes 442376 | tf_op jit(solution)/shard_map/ppermute | solution.py:271
  11.1 0.9 %copy-start.1 = (bf16[24,24,128]{2,1,0:T(8,128)(2,1)S(1)}, bf16[24,24,128]{2,1,0:T(8,128)(2,1)}, u32[]{:S(2)}) copy-start(bf16[24,24,128]{2,1,0:T(8,128)(2,1)} %param.10) | copy-start | bytes 442372
  12.0 1.0 %copy-start.3 = (bf16[2,128,640]{2,1,0:T(8,128)(2,1)S(1)}, bf16[2,128,640]{2,1,0:T(8,128)(2,1)}, u32[]{:S(2)}) copy-start(bf16[2,128,640]{2,1,0:T(8,128)(2,1)} %w_in.1) | copy-start | bytes 983044
  14.0 8.9 %collective-permute-start.4 = (bf16[576,128]{1,0:T(8,128)(2,1)S(1)}, bf16[576,128]{1,0:T(8,128)(2,1)S(1)}, u32[]{:S(2)}, u32[]{:S(2)}) collective-permute-start(bf16[576,128]{1,0:T(8,128)(2,1)S(1)} %collective-permute-done.1.col.refs_1_), channel_id=1, source_target_pairs={{0,8},{4,12},{8,0},{12,4},{1,9},{5,13},{9,1},{13,5},{2,10},{6,14},... | collective-permute-start | bytes 442376 | tf_op jit(solution)/shard_map/ppermute | solution.py:277
  15.0 6.5 %collective-permute-start.3 = (bf16[576,128]{1,0:T(8,128)(2,1)S(1)}, bf16[576,128]{1,0:T(8,128)(2,1)S(1)}, u32[]{:S(2)}, u32[]{:S(2)}) collective-permute-start(bf16[576,128]{1,0:T(8,128)(2,1)S(1)} %collective-permute-done.1.col.refs_1_), channel_id=1, source_target_pairs={{0,4},{4,0},{8,12},{12,8},{1,5},{5,1},{9,13},{13,9},{2,6},{6,2},{1... | collective-permute-start | bytes 442376 | tf_op jit(solution)/shard_map/ppermute | solution.py:277
  19.6 6.0 %collective-permute-start.2 = (bf16[576,128]{1,0:T(8,128)(2,1)S(1)}, bf16[576,128]{1,0:T(8,128)(2,1)S(1)}, u32[]{:S(2)}, u32[]{:S(2)}) collective-permute-start(bf16[576,128]{1,0:T(8,128)(2,1)S(1)} %collective-permute-done.refs_1_), channel_id=1, source_target_pairs={{0,1},{1,0},{2,3},{3,2},{4,5},{5,4},{6,7},{7,6},{8,9},{9,8},{10,11... | collective-permute-start | bytes 442376 | tf_op jit(solution)/shard_map/ppermute | solution.py:271
  19.7 5.9 %collective-permute-start.5 = (bf16[576,128]{1,0:T(8,128)(2,1)S(1)}, bf16[576,128]{1,0:T(8,128)(2,1)S(1)}, u32[]{:S(2)}, u32[]{:S(2)}) collective-permute-start(bf16[576,128]{1,0:T(8,128)(2,1)S(1)} %collective-permute-done.1.col.refs_1_), channel_id=1, source_target_pairs={{0,12},{4,8},{8,4},{12,0},{1,13},{5,9},{9,5},{13,1},{2,14},{6,10},... | collective-permute-start | bytes 442376 | tf_op jit(solution)/shard_map/ppermute | solution.py:277
  22.9 2.7 %copy-start = (bf16[2,128,128]{2,1,0:T(8,128)(2,1)S(1)}, bf16[2,128,128]{2,1,0:T(8,128)(2,1)}, u32[]{:S(2)}) copy-start(bf16[2,128,128]{2,1,0:T(8,128)(2,1)} %w_out.3) | copy-start | bytes 196612
  25.6 7.6 %copy-start.2 = (bf16[24,24,128]{2,1,0:T(8,128)(2,1)S(1)}, bf16[24,24,128]{2,1,0:T(8,128)(2,1)}, u32[]{:S(2)}) copy-start(bf16[24,24,128]{2,1,0:T(8,128)(2,1)} %param.10) | copy-start | bytes 442372
  28.7 10.9 %collective-permute-start.7 = (bf16[576,128]{1,0:T(8,128)(2,1)S(1)}, bf16[576,128]{1,0:T(8,128)(2,1)S(1)}, u32[]{:S(2)}, u32[]{:S(2)}) collective-permute-start(bf16[576,128]{1,0:T(8,128)(2,1)S(1)} %get-tuple-element.48.refs_0_), channel_id=1, source_target_pairs={{0,2},{1,3},{2,0},{3,1},{4,6},{5,7},{6,4},{7,5},{8,10},{9,11},{10,... | collective-permute-start | bytes 442376 | tf_op jit(solution)/shard_map/ppermute | solution.py:271
  32.8 7.9 %collective-permute-start.11 = (bf16[576,128]{1,0:T(8,128)(2,1)S(1)}, bf16[576,128]{1,0:T(8,128)(2,1)S(1)}, u32[]{:S(2)}, u32[]{:S(2)}) collective-permute-start(bf16[576,128]{1,0:T(8,128)(2,1)S(1)} %get-tuple-element.48.refs_0_), channel_id=1, source_target_pairs={{0,1},{1,0},{2,3},{3,2},{4,5},{5,4},{6,7},{7,6},{8,9},{9,8},{10,11... | collective-permute-start | bytes 442376 | tf_op jit(solution)/shard_map/ppermute | solution.py:271
  36.9 4.4 %collective-permute-start.10 = (bf16[576,128]{1,0:T(8,128)(2,1)S(1)}, bf16[576,128]{1,0:T(8,128)(2,1)S(1)}, u32[]{:S(2)}, u32[]{:S(2)}) collective-permute-start(bf16[576,128]{1,0:T(8,128)(2,1)S(1)} %get-tuple-element.52.own), channel_id=1, source_target_pairs={{0,4},{4,0},{8,12},{12,8},{1,5},{5,1},{9,13},{13,9},{2,6},{6,2},{1... | collective-permute-start | bytes 442376 | tf_op jit(solution)/shard_map/ppermute | solution.py:385
  36.9 6.3 %collective-permute-start.9 = (bf16[576,128]{1,0:T(8,128)(2,1)S(1)}, bf16[576,128]{1,0:T(8,128)(2,1)S(1)}, u32[]{:S(2)}, u32[]{:S(2)}) collective-permute-start(bf16[576,128]{1,0:T(8,128)(2,1)S(1)} %get-tuple-element.52.own), channel_id=1, source_target_pairs={{0,8},{4,12},{8,0},{12,4},{1,9},{5,13},{9,1},{13,5},{2,10},{6,14},... | collective-permute-start | bytes 442376 | tf_op jit(solution)/shard_map/ppermute | solution.py:271
  39.6 5.3 %collective-permute-start.8 = (bf16[576,128]{1,0:T(8,128)(2,1)S(1)}, bf16[576,128]{1,0:T(8,128)(2,1)S(1)}, u32[]{:S(2)}, u32[]{:S(2)}) collective-permute-start(bf16[576,128]{1,0:T(8,128)(2,1)S(1)} %collective-permute-done.7.refs_2_), channel_id=1, source_target_pairs={{0,1},{1,0},{2,3},{3,2},{4,5},{5,4},{6,7},{7,6},{8,9},{9,8},{10,11... | collective-permute-start | bytes 442376 | tf_op jit(solution)/shard_map/ppermute | solution.py:271
  43.2 1.7 %collective-permute-start.12 = (bf16[576,128]{1,0:T(8,128)(2,1)S(1)}, bf16[576,128]{1,0:T(8,128)(2,1)S(1)}, u32[]{:S(2)}, u32[]{:S(2)}) collective-permute-start(bf16[576,128]{1,0:T(8,128)(2,1)S(1)} %collective-permute-done.9.refs_0_), channel_id=1, source_target_pairs={{0,4},{4,0},{8,12},{12,8},{1,5},{5,1},{9,13},{13,9},{2,6},{6,2},{1... | collective-permute-start | bytes 442376 | tf_op jit(solution)/shard_map/ppermute | solution.py:271

commit v16 on v15

--- a/solution.py
+++ b/solution.py
@@ -177,20 +177,23 @@
     mix(mixed, None, col_l, row_r, 0, count, lambda i: r ^ place(c ^ slot(i), n), slot, t)
 
 
+def last_column_kernel(n, t, col, table, weights, left_in, right_in, col_l, col_r, wide):
+    r, c = lax.axis_index("row"), lax.axis_index("col")
+    outer, inner = mask_of(table, placed_at(r ^ (n - 1), n), t), mask_of(table, c, t)
+    consts = constants(wide.shape[1])
+    sides(col, wide, col_l.at[n - 1], col_r.at[n - 1], outer, inner, consts, table, weights)
+
+
 def mirror_kernel(n, t, *refs):
     row, cols, (table, weights, w_out) = refs[0], refs[1 : n + 1], refs[n + 1 : n + 4]
-    old = refs[n + 8]
-    left_ref, row_l, row_r, col_l, col_r, mixed, wide, held = refs[n + 9 :]
+    col_l, old = refs[n + 6 : n + 8]
+    left_ref, row_l, row_r, mixed, wide, held = refs[n + 8 :]
     width = wide.shape[1]
     r, c = lax.axis_index("row"), lax.axis_index("col")
     consts = constants(width)
     here, there = mask_of(table, r, t), mask_of(table, c, t)
-    for block, left, right, outer, inner in (
-        (row, row_l, row_r, c ^ (n - 1), here),
-        (cols[-1], col_l, col_r, placed_at(r ^ (n - 1), n), there),
-    ):
-        outer = mask_of(table, outer, t)
-        sides(block, wide, left.at[n - 1], right.at[n - 1], outer, inner, consts, table, weights)
+    outer = mask_of(table, c ^ (n - 1), t)
+    sides(row, wide, row_l.at[n - 1], row_r.at[n - 1], outer, here, consts, table, weights)
     count, slot = late_pairs(c ^ placed_at(r ^ (n - 1), n), n)
     mix(mixed, old, col_l, row_r, 0, count, lambda i: r ^ place(c ^ slot(i), n), slot, t)
     for s in range(n):
@@ -321,7 +324,7 @@
             functools.partial(early_kernel, n, t), "early_sides", (slots,) * 2, [scratch], col_block, table, weights
         )
         rows = gather(pair, "col", lambda s, step: (own_l, col_l) if s else ())
-        cols = direct(*(lax.optimization_barrier((col_block, after))[0] for after in (own_l, col_l)))
+        cols = direct(*(lax.optimization_barrier((col_block, after))[0] for after in (own_l, own_l)))
         row_l, row_r, col_l, col_r = call(
             functools.partial(first_sides_kernel, n, t),
             "first_sides",
@@ -350,10 +353,23 @@
             col_r,
             alias={n: 0, n + 1: 1},
         )
-        left, row_l, _, _, col_r = call(
+        col_l, col_r = call(
+            functools.partial(last_column_kernel, n, t),
+            "last_column",
+            (slots, slots),
+            [scratch],
+            cols[-1],
+            table,
+            weights,
+            col_l,
+            col_r,
+            alias={3: 0, 4: 1},
+            weight=30,
+        )
+        left, row_l, _ = call(
             functools.partial(mirror_kernel, n, t),
             "mirror_end",
-            (narrow, slots, slots, slots, slots),
+            (narrow, slots, slots),
             [scratch] * 2 + [pltpu.VMEM((n,) + area, BF16)],
             rows[-1],
             *cols,
@@ -363,9 +379,8 @@
             row_l,
             row_r,
             col_l,
-            col_r,
             mixed,
-            alias={n + 4: 1, n + 5: 2, n + 6: 3, n + 7: 4},
+            alias={n + 4: 1, n + 5: 2},
         )
         pair, right = call(
             functools.partial(own_end_kernel, n, t),

time: 47.1 us -> 48.2 us (1.023)
  waiting for transfers between devices: 4.65 us -> 6.25 us
  starting transfers between devices: 20.2 us -> 18.9 us
    ppermute x3, waiting for transfers between devices: 0.01 us -> 2.22 us  [direct(): lax.ppermute(last if s == n - 1 else block, 'row', [(k, k ^ s) for k in r...]
    ppermute x8, starting transfers between devices: 13.9 us -> 13 us  [gather(): held[s ^ step] = lax.ppermute(part, axis, [(k, k ^ step) for k in range(n)])]
    ppermute x8, waiting for transfers between devices: 4.64 us -> 4.03 us  [gather(): held[s ^ step] = lax.ppermute(part, axis, [(k, k ^ step) for k in range(n)])]
    pallas_call x12 -> x13, Pallas kernels: 17 us -> 17.1 us  [call(): pl.pallas_call(kernel, out_shape=outs, scratch_shapes=scratches, input_ou...]
  transfers between devices with their start and end apart: 13 -> 13, of which waited for: 4 -> 7; matrix products, arithmetic and copies ran while one was open for 6% -> 6% of each run, Pallas kernels for 26% -> 26%
where the time goes in v16:
time: 48.2 us; the launch traced here: 47.5 us
  starting transfers between devices  18.9 us (39%)
  Pallas kernels  17.1 us (35%)
  waiting for transfers between devices  6.25 us (13%)
  local copies, waits for them, and re-layouts  4.4 us (9%)
  other arithmetic  0.66 us (1%)
    pallas_call x13, Pallas kernels, call(): pl.pallas_call(kernel, out_shape=outs, scratch_shapes=scratches, input_ou...  17.1 us
    ppermute x8, starting transfers between devices, gather(): held[s ^ step] = lax.ppermute(part, axis, [(k, k ^ step) for k in range(n)])  13 us
    ppermute x3, starting transfers between devices, direct(): lax.ppermute(last if s == n - 1 else block, 'row', [(k, k ^ s) for k in r...  4.3 us
    ppermute x8, waiting for transfers between devices, gather(): held[s ^ step] = lax.ppermute(part, axis, [(k, k ^ step) for k in range(n)])  4.03 us
    ppermute x3, waiting for transfers between devices, direct(): lax.ppermute(last if s == n - 1 else block, 'row', [(k, k ^ s) for k in r...  2.22 us
    unnamed x8, local copies, waits for them, and re-layouts  2.12 us
    ppermute x1, starting transfers between devices, mirrored(): return lax.ppermute(block, ('row', 'col'), pairs)  1.56 us
    concatenate x1, local copies, waits for them, and re-layouts, per_device(): jnp.concatenate(vectors + [jnp.zeros((TABLE_MASK - 20, width), F32), mask])  1.51 us
  transfers between devices with their start and end apart: 13, of which 7 were waited for; matrix products, arithmetic and copies ran while one was open for 6% of the time, Pallas kernels for 26%

profile of v16, /device:TPU:0, one launch (start us, length us, event | category | flops | bytes accessed | tf_op | source)
XLA Modules:
  0.0 47.5 jit_solution(18288029774136668324)
XLA Ops:
  0.0 1.6 %collective-permute-start.1 = (bf16[576,128]{1,0:T(8,128)(2,1)}, bf16[576,128]{1,0:T(8,128)(2,1)S(1)}, u32[]{:S(2)}, u32[]{:S(2)}) collective-permute-start(bf16[576,128]{1,0:T(8,128)(2,1)} %bitcast.2), channel_id=1, source_target_pairs={{0,0},{1,8},{2,4},{3,12},{4,1},{5,9},{6,5},{7,13},{8,2},{9,10},{10... | collective-permute-start | bytes 442376 | tf_op jit(solution)/shard_map/ppermute | solution.py:285
  1.6 4.5 %collective-permute-start = (bf16[576,128]{1,0:T(8,128)(2,1)}, bf16[576,128]{1,0:T(8,128)(2,1)S(1)}, u32[]{:S(2)}, u32[]{:S(2)}) collective-permute-start(bf16[576,128]{1,0:T(8,128)(2,1)} %bitcast.3), channel_id=1, source_target_pairs={{0,2},{1,3},{2,0},{3,1},{4,6},{5,7},{6,4},{7,5},{8,10},{9,11},{10,... | collective-permute-start | bytes 442376 | tf_op jit(solution)/shard_map/ppermute | solution.py:274
  6.0 2.2 %collective-permute-start.6 = (bf16[576,128]{1,0:T(8,128)(2,1)}, bf16[576,128]{1,0:T(8,128)(2,1)S(1)}, u32[]{:S(2)}, u32[]{:S(2)}) collective-permute-start(bf16[576,128]{1,0:T(8,128)(2,1)} %bitcast.4), channel_id=1, source_target_pairs={{0,1},{1,0},{2,3},{3,2},{4,5},{5,4},{6,7},{7,6},{8,9},{9,8},{10,11... | collective-permute-start | bytes 442376 | tf_op jit(solution)/shard_map/ppermute | solution.py:274
  8.2 0.7 %convert_element_type.3 = f32[96]{0:T(128)S(1)} convert(s32[96]{0:T(128)} %param.11) | non-fusion elementwise | flops 96 | bytes 768 | tf_op jit(solution)/shard_map/convert_element_type | solution.py:310
  8.8 0.7 %reshape.11 = f32[10,128]{1,0:T(8,128)S(1)} reshape(f32[2,640]{1,0:T(2,128)} %param.15) | data formatting | bytes 10240 | tf_op jit(solution)/shard_map/reshape | solution.py:311
  9.5 0.1 broadcast_in_dim.10
  9.6 1.5 %concatenate.3.table.refs_3_.refs_1_.refs_5_ = f32[120,128]{1,0:T(8,128)S(1)} concatenate(f32[2,128]{1,0:T(2,128)} %param.12, f32[2,128]{1,0:T(2,128)} %param.13, f32[2,128]{1,0:T(2,128)} %param.16, f32[2,128]{1,0:T(2,128)} %param.17, f32[2,128]{1,0:T(2,128)} %param.19, f32[10,128]{1,0:T(8,128)S(1)} %reshape.11, f32[4,128]{1,0:T(4,128)S(1)} %broadcast_in_dim.4, ...), dimensions={0} | concatenate | bytes 122880 | tf_op jit(solution)/shard_map/concatenate | solution.py:312
  11.1 0.9 %copy-done.1 = bf16[24,24,128]{2,1,0:T(8,128)(2,1)S(1)} copy-done((bf16[24,24,128]{2,1,0:T(8,128)(2,1)S(1)}, bf16[24,24,128]{2,1,0:T(8,128)(2,1)}, u32[]{:S(2)}) %copy-start.1) | copy-done | bytes 147480
  12.0 0.0 copy-start.3
  12.0 1.0 %copy-done.3 = bf16[2,128,640]{2,1,0:T(8,128)(2,1)S(1)} copy-done((bf16[2,128,640]{2,1,0:T(8,128)(2,1)S(1)}, bf16[2,128,640]{2,1,0:T(8,128)(2,1)}, u32[]{:S(2)}) %copy-start.3) | copy-done | bytes 327704
  13.0 1.0 %own_sides.1 = (bf16[2,128,640]{2,1,0:T(8,128)(2,1)S(1)}, f32[4,576,128]{2,1,0:T(8,128)S(1)}, f32[4,576,128]{2,1,0:T(8,128)S(1)}, f32[576,128]{1,0:T(8,128)S(1)}) custom-call(bf16[576,128]{1,0:T(8,128)(2,1)S(1)} %bitcast.5, f32[120,128]{1,0:T(8,128)S(1)} %concatenate.3.table.refs_3_.refs_1_.refs_5_, bf16[2,128,640]{2,1,0:T(8,128)(2,1)S(1)} %copy-done.3), custom_call_target="tpu_custom_call" | custom-call | tf_op jit(solution)/shard_map/own_sides/pallas_call | solution.py:295
  14.0 0.0 collective-permute-done.1.col.refs_1_
  14.0 2.9 %collective-permute-start.3 = (bf16[576,128]{1,0:T(8,128)(2,1)S(1)}, bf16[576,128]{1,0:T(8,128)(2,1)S(1)}, u32[]{:S(2)}, u32[]{:S(2)}) collective-permute-start(bf16[576,128]{1,0:T(8,128)(2,1)S(1)} %collective-permute-done.1.col.refs_1_), channel_id=1, source_target_pairs={{0,4},{4,0},{8,12},{12,8},{1,5},{5,1},{9,13},{13,9},{2,6},{6,2},{1... | collective-permute-start | bytes 442376 | tf_op jit(solution)/shard_map/ppermute | solution.py:280
  16.9 0.0 collective-permute-start.4
  16.9 1.4 %collective-permute-start.5 = (bf16[576,128]{1,0:T(8,128)(2,1)S(1)}, bf16[576,128]{1,0:T(8,128)(2,1)S(1)}, u32[]{:S(2)}, u32[]{:S(2)}) collective-permute-start(bf16[576,128]{1,0:T(8,128)(2,1)S(1)} %collective-permute-done.1.col.refs_1_), channel_id=1, source_target_pairs={{0,12},{4,8},{8,4},{12,0},{1,13},{5,9},{9,5},{13,1},{2,14},{6,10},... | collective-permute-start | bytes 442376 | tf_op jit(solution)/shard_map/ppermute | solution.py:280
  18.3 0.6 %early_sides.1 = (f32[4,576,128]{2,1,0:T(8,128)S(1)}, f32[4,576,128]{2,1,0:T(8,128)S(1)}) custom-call(bf16[576,128]{1,0:T(8,128)(2,1)S(1)} %collective-permute-done.1.col.refs_1_, f32[120,128]{1,0:T(8,128)S(1)} %concatenate.3.table.refs_3_.refs_1_.refs_5_, bf16[2,128,640]{2,1,0:T(8,128)(2,1)S(1)} %get-tuple-element.34.weights.refs_4_.refs_2_.refs_6_), custom_call_target="tpu_custom_call" | custom-call | tf_op jit(solution)/shard_map/early_sides/pallas_call | solution.py:295
  18.9 0.8 %collective-permute-done.refs_1_ = bf16[576,128]{1,0:T(8,128)(2,1)S(1)} collective-permute-done((bf16[576,128]{1,0:T(8,128)(2,1)}, bf16[576,128]{1,0:T(8,128)(2,1)S(1)}, u32[]{:S(2)}, u32[]{:S(2)}) %collective-permute-start) | collective-permute-done | bytes 147488 | tf_op jit(solution)/shard_map/ppermute | solution.py:274
  19.6 0.4 collective-permute-start.2
  20.0 0.0 collective-permute-done.6.refs_0_
  20.0 0.0 collective-permute-done.3.refs_2_
  20.0 1.5 %first_sides.1 = (f32[4,576,128]{2,1,0:T(8,128)S(1)}, f32[4,576,128]{2,1,0:T(8,128)S(1)}, f32[4,576,128]{2,1,0:T(8,128)S(1)}, f32[4,576,128]{2,1,0:T(8,128)S(1)}) custom-call(bf16[576,128]{1,0:T(8,128)(2,1)S(1)} %collective-permute-done.6.refs_0_, ...), custom_call_target="tpu_custom_call", output_to_operand_aliasing={{0}: (5, {}), {1}: (6, {}), {2}: (7, {}), {3}: (8, {})} | custom-call | tf_op jit(solution)/shard_map/first_sides/pallas_call | solution.py:295
  21.4 2.2 %collective-permute-done.4.refs_0_.refs_3_ = bf16[576,128]{1,0:T(8,128)(2,1)S(1)} collective-permute-done((bf16[576,128]{1,0:T(8,128)(2,1)S(1)}, bf16[576,128]{1,0:T(8,128)(2,1)S(1)}, u32[]{:S(2)}, u32[]{:S(2)}) %collective-permute-start.4) | collective-permute-done | bytes 147488 | tf_op jit(solution)/shard_map/ppermute | solution.py:280
  23.7 2.6 %second_sides.1 = (f32[4,576,128]{2,1,0:T(8,128)S(1)}, f32[4,576,128]{2,1,0:T(8,128)S(1)}, f32[576,128]{1,0:T(8,128)S(1)}) custom-call(bf16[576,128]{1,0:T(8,128)(2,1)S(1)} %collective-permute-done.4.refs_0_.refs_3_, f32[120,128]{1,0:T(8,128)S(1)} %concatenate.3.table.refs_3_.refs_1_.refs_5_, ...), custom_call_target="tpu_custom_call", output_to_operand_aliasing={{0}: (4, {}), {1}: (5, {})} | custom-call | tf_op jit(solution)/shard_map/second_sides/pallas_call | solution.py:295
  26.3 0.0 collective-permute-done.5.col.refs_4_
  26.3 0.0 copy-start
  26.3 0.6 %last_column.1 = (f32[4,576,128]{2,1,0:T(8,128)S(1)}, f32[4,576,128]{2,1,0:T(8,128)S(1)}) custom-call(bf16[576,128]{1,0:T(8,128)(2,1)S(1)} %collective-permute-done.5.col.refs_4_, f32[120,128]{1,0:T(8,128)S(1)} %concatenate.3.table.refs_3_.refs_1_.refs_5_, ...), custom_call_target="tpu_custom_call", output_to_operand_aliasing={{0}: (3, {}), {1}: (4, {})} | custom-call | flops 30000001024 | bytes 30000000 | tf_op jit(solution)/shard_map/last_column/pallas_call | solution.py:295
  26.9 0.0 collective-permute-done.2.refs_0_
  26.9 0.2 copy-done
  27.1 2.6 %mirror_end.1 = (bf16[576,128]{1,0:T(8,128)(2,1)S(1)}, f32[4,576,128]{2,1,0:T(8,128)S(1)}, f32[4,576,128]{2,1,0:T(8,128)S(1)}) custom-call(bf16[576,128]{1,0:T(8,128)(2,1)S(1)} %collective-permute-done.2.refs_0_, bf16[576,128]{1,0:T(8,128)(2,1)S(1)} %collective-permute-done.1.col.refs_1_, ...), custom_call_target="tpu_custom_call", output_to_operand_aliasing={{1}: (8, {}), {2}: (9, {})} | custom-call | tf_op jit(solution)/shard_map/mirror_end/pallas_call | solution.py:295
  29.8 2.2 %collective-permute-start.7 = (bf16[576,128]{1,0:T(8,128)(2,1)S(1)}, bf16[576,128]{1,0:T(8,128)(2,1)S(1)}, u32[]{:S(2)}, u32[]{:S(2)}) collective-permute-start(bf16[576,128]{1,0:T(8,128)(2,1)S(1)} %get-tuple-element.48.refs_0_), channel_id=1, source_target_pairs={{0,2},{1,3},{2,0},{3,1},{4,6},{5,7},{6,4},{7,5},{8,10},{9,11},{10,... | collective-permute-start | bytes 442376 | tf_op jit(solution)/shard_map/ppermute | solution.py:274
  32.0 2.2 %collective-permute-start.11 = (bf16[576,128]{1,0:T(8,128)(2,1)S(1)}, bf16[576,128]{1,0:T(8,128)(2,1)S(1)}, u32[]{:S(2)}, u32[]{:S(2)}) collective-permute-start(bf16[576,128]{1,0:T(8,128)(2,1)S(1)} %get-tuple-element.48.refs_0_), channel_id=1, source_target_pairs={{0,1},{1,0},{2,3},{3,2},{4,5},{5,4},{6,7},{7,6},{8,9},{9,8},{10,11... | collective-permute-start | bytes 442376 | tf_op jit(solution)/shard_map/ppermute | solution.py:274
  34.2 0.0 copy-done.2
  34.2 3.6 %own_end.1 = (bf16[576,128]{1,0:T(8,128)(2,1)S(1)}, bf16[576,128]{1,0:T(8,128)(2,1)S(1)}) custom-call(f32[4,576,128]{2,1,0:T(8,128)S(1)} %get-tuple-element.49.row_l, f32[4,576,128]{2,1,0:T(8,128)S(1)} %get-tuple-element.50.col_r, f32[120,128]{1,0:T(8,128)S(1)} %concatenate.3.table.refs_3_.refs_1_.refs_5_, ...), custom_call_target="tpu_custom_call" | custom-call | tf_op jit(solution)/shard_map/own_end/pallas_call | solution.py:295
  37.8 0.1 collective-permute-start.10
  37.9 1.6 %collective-permute-start.9 = (bf16[576,128]{1,0:T(8,128)(2,1)S(1)}, bf16[576,128]{1,0:T(8,128)(2,1)S(1)}, u32[]{:S(2)}, u32[]{:S(2)}) collective-permute-start(bf16[576,128]{1,0:T(8,128)(2,1)S(1)} %get-tuple-element.52.own), channel_id=1, source_target_pairs={{0,8},{4,12},{8,0},{12,4},{1,9},{5,13},{9,1},{13,5},{2,10},{6,14},... | collective-permute-start | bytes 442376 | tf_op jit(solution)/shard_map/ppermute | solution.py:274
  39.5 0.3 collective-permute-done.7.refs_2_
  39.8 0.0 collective-permute-start.8
  39.8 0.1 collective-permute-done.11.refs_1_
  39.9 0.1 left_slots.1.lefts.refs_1_.left_in
  39.9 0.5 %gate.1.gating = f32[576,128]{1,0:T(8,128)S(1)} custom-call(bf16[576,128]{1,0:T(8,128)(2,1)S(1)} %get-tuple-element.58.pair, f32[120,128]{1,0:T(8,128)S(1)} %concatenate.3.table.refs_3_.refs_1_.refs_5_, bf16[2,128,640]{2,1,0:T(8,128)(2,1)S(1)} %get-tuple-element.34.weights.refs_4_.refs_2_.refs_6_), custom_call_target="tpu_custom_call" | custom-call | tf_op jit(solution)/shard_map/gate/pallas_call | solution.py:295
  40.5 0.0 collective-permute-done.10.core
  40.5 1.4 %near_slots.1 = (f32[4,576,128]{2,1,0:T(8,128)S(1)}, f32[576,128]{1,0:T(8,128)S(1)}) custom-call(bf16[576,128]{1,0:T(8,128)(2,1)S(1)} %get-tuple-element.52.own, bf16[576,128]{1,0:T(8,128)(2,1)S(1)} %collective-permute-done.10.core, f32[4,576,128]{2,1,0:T(8,128)S(1)} %left_slots.1.lefts.refs_1_.left_in), custom_call_target="tpu_custom_call" | custom-call | tf_op jit(solution)/shard_map/near_slots/pallas_call | solution.py:295
  41.9 2.3 %collective-permute-done.9.refs_0_ = bf16[576,128]{1,0:T(8,128)(2,1)S(1)} collective-permute-done((bf16[576,128]{1,0:T(8,128)(2,1)S(1)}, bf16[576,128]{1,0:T(8,128)(2,1)S(1)}, u32[]{:S(2)}, u32[]{:S(2)}) %collective-permute-start.9) | collective-permute-done | bytes 147488 | tf_op jit(solution)/shard_map/ppermute | solution.py:274
  44.2 0.0 collective-permute-start.12
  44.2 0.7 %far_slots.1 = (f32[4,576,128]{2,1,0:T(8,128)S(1)}, f32[576,128]{1,0:T(8,128)S(1)}) custom-call(bf16[576,128]{1,0:T(8,128)(2,1)S(1)} %collective-permute-done.9.refs_0_, f32[4,576,128]{2,1,0:T(8,128)S(1)} %left_slots.1.lefts.refs_1_.left_in, f32[4,576,128]{2,1,0:T(8,128)S(1)} %get-tuple-element.55.refs_2_, ...), custom_call_target="tpu_custom_call", output_to_operand_aliasing={{0}: (2, {}), {1}: (3, {})} | custom-call | tf_op jit(solution)/shard_map/far_slots/pallas_call | solution.py:295
  44.9 0.5 %collective-permute-done.8.block = bf16[576,128]{1,0:T(8,128)(2,1)S(1)} collective-permute-done((bf16[576,128]{1,0:T(8,128)(2,1)S(1)}, bf16[576,128]{1,0:T(8,128)(2,1)S(1)}, u32[]{:S(2)}, u32[]{:S(2)}) %collective-permute-start.8) | collective-permute-done | bytes 147488 | tf_op jit(solution)/shard_map/ppermute | solution.py:274
  45.5 0.1 collective-permute-done.12.right
  45.6 1.9 %end.1 = (bf16[576,128]{1,0:T(8,128)(2,1)}, f32[4,576,128]{2,1,0:T(8,128)S(1)}, f32[4,576,128]{2,1,0:T(8,128)S(1)}) custom-call(f32[576,128]{1,0:T(8,128)S(1)} %left_last.1.left, bf16[576,128]{1,0:T(8,128)(2,1)S(1)} %collective-permute-done.12.right, f32[576,128]{1,0:T(8,128)S(1)} %get-tuple-element.56.old, ...), custom_call_target="tpu_custom_call", output_to_operand_aliasing={{1}: (7, {}), {2}: (8, {})} | custom-call | tf_op jit(solution)/shard_map/end/pallas_call | solution.py:295
  (4 shorter events, 0.0 us)
Async XLA Ops:
  0.0 14.0 %collective-permute-start.1 = (bf16[576,128]{1,0:T(8,128)(2,1)}, bf16[576,128]{1,0:T(8,128)(2,1)S(1)}, u32[]{:S(2)}, u32[]{:S(2)}) collective-permute-start(bf16[576,128]{1,0:T(8,128)(2,1)} %bitcast.2), channel_id=1, source_target_pairs={{0,0},{1,8},{2,4},{3,12},{4,1},{5,9},{6,5},{7,13},{8,2},{9,10},{10... | collective-permute-start | bytes 442376 | tf_op jit(solution)/shard_map/ppermute | solution.py:285
  1.6 18.1 %collective-permute-start = (bf16[576,128]{1,0:T(8,128)(2,1)}, bf16[576,128]{1,0:T(8,128)(2,1)S(1)}, u32[]{:S(2)}, u32[]{:S(2)}) collective-permute-start(bf16[576,128]{1,0:T(8,128)(2,1)} %bitcast.3), channel_id=1, source_target_pairs={{0,2},{1,3},{2,0},{3,1},{4,6},{5,7},{6,4},{7,5},{8,10},{9,11},{10,... | collective-permute-start | bytes 442376 | tf_op jit(solution)/shard_map/ppermute | solution.py:274
  6.0 14.0 %collective-permute-start.6 = (bf16[576,128]{1,0:T(8,128)(2,1)}, bf16[576,128]{1,0:T(8,128)(2,1)S(1)}, u32[]{:S(2)}, u32[]{:S(2)}) collective-permute-start(bf16[576,128]{1,0:T(8,128)(2,1)} %bitcast.4), channel_id=1, source_target_pairs={{0,1},{1,0},{2,3},{3,2},{4,5},{5,4},{6,7},{7,6},{8,9},{9,8},{10,11... | collective-permute-start | bytes 442376 | tf_op jit(solution)/shard_map/ppermute | solution.py:274
  11.1 0.9 %copy-start.1 = (bf16[24,24,128]{2,1,0:T(8,128)(2,1)S(1)}, bf16[24,24,128]{2,1,0:T(8,128)(2,1)}, u32[]{:S(2)}) copy-start(bf16[24,24,128]{2,1,0:T(8,128)(2,1)} %param.10) | copy-start | bytes 442372
  12.0 1.0 %copy-start.3 = (bf16[2,128,640]{2,1,0:T(8,128)(2,1)S(1)}, bf16[2,128,640]{2,1,0:T(8,128)(2,1)}, u32[]{:S(2)}) copy-start(bf16[2,128,640]{2,1,0:T(8,128)(2,1)} %w_in.1) | copy-start | bytes 983044
  14.0 6.0 %collective-permute-start.3 = (bf16[576,128]{1,0:T(8,128)(2,1)S(1)}, bf16[576,128]{1,0:T(8,128)(2,1)S(1)}, u32[]{:S(2)}, u32[]{:S(2)}) collective-permute-start(bf16[576,128]{1,0:T(8,128)(2,1)S(1)} %collective-permute-done.1.col.refs_1_), channel_id=1, source_target_pairs={{0,4},{4,0},{8,12},{12,8},{1,5},{5,1},{9,13},{13,9},{2,6},{6,2},{1... | collective-permute-start | bytes 442376 | tf_op jit(solution)/shard_map/ppermute | solution.py:280
  16.9 6.7 %collective-permute-start.4 = (bf16[576,128]{1,0:T(8,128)(2,1)S(1)}, bf16[576,128]{1,0:T(8,128)(2,1)S(1)}, u32[]{:S(2)}, u32[]{:S(2)}) collective-permute-start(bf16[576,128]{1,0:T(8,128)(2,1)S(1)} %collective-permute-done.1.col.refs_1_), channel_id=1, source_target_pairs={{0,8},{4,12},{8,0},{12,4},{1,9},{5,13},{9,1},{13,5},{2,10},{6,14},... | collective-permute-start | bytes 442376 | tf_op jit(solution)/shard_map/ppermute | solution.py:280
  16.9 9.4 %collective-permute-start.5 = (bf16[576,128]{1,0:T(8,128)(2,1)S(1)}, bf16[576,128]{1,0:T(8,128)(2,1)S(1)}, u32[]{:S(2)}, u32[]{:S(2)}) collective-permute-start(bf16[576,128]{1,0:T(8,128)(2,1)S(1)} %collective-permute-done.1.col.refs_1_), channel_id=1, source_target_pairs={{0,12},{4,8},{8,4},{12,0},{1,13},{5,9},{9,5},{13,1},{2,14},{6,10},... | collective-permute-start | bytes 442376 | tf_op jit(solution)/shard_map/ppermute | solution.py:280
  19.6 7.3 %collective-permute-start.2 = (bf16[576,128]{1,0:T(8,128)(2,1)S(1)}, bf16[576,128]{1,0:T(8,128)(2,1)S(1)}, u32[]{:S(2)}, u32[]{:S(2)}) collective-permute-start(bf16[576,128]{1,0:T(8,128)(2,1)S(1)} %collective-permute-done.refs_1_), channel_id=1, source_target_pairs={{0,1},{1,0},{2,3},{3,2},{4,5},{5,4},{6,7},{7,6},{8,9},{9,8},{10,11... | collective-permute-start | bytes 442376 | tf_op jit(solution)/shard_map/ppermute | solution.py:274
  26.3 0.8 %copy-start = (bf16[2,128,128]{2,1,0:T(8,128)(2,1)S(1)}, bf16[2,128,128]{2,1,0:T(8,128)(2,1)}, u32[]{:S(2)}) copy-start(bf16[2,128,128]{2,1,0:T(8,128)(2,1)} %w_out.3) | copy-start | bytes 196612
  27.1 7.1 %copy-start.2 = (bf16[24,24,128]{2,1,0:T(8,128)(2,1)S(1)}, bf16[24,24,128]{2,1,0:T(8,128)(2,1)}, u32[]{:S(2)}) copy-start(bf16[24,24,128]{2,1,0:T(8,128)(2,1)} %param.10) | copy-start | bytes 442372
  29.8 10.0 %collective-permute-start.7 = (bf16[576,128]{1,0:T(8,128)(2,1)S(1)}, bf16[576,128]{1,0:T(8,128)(2,1)S(1)}, u32[]{:S(2)}, u32[]{:S(2)}) collective-permute-start(bf16[576,128]{1,0:T(8,128)(2,1)S(1)} %get-tuple-element.48.refs_0_), channel_id=1, source_target_pairs={{0,2},{1,3},{2,0},{3,1},{4,6},{5,7},{6,4},{7,5},{8,10},{9,11},{10,... | collective-permute-start | bytes 442376 | tf_op jit(solution)/shard_map/ppermute | solution.py:274
  32.0 7.9 %collective-permute-start.11 = (bf16[576,128]{1,0:T(8,128)(2,1)S(1)}, bf16[576,128]{1,0:T(8,128)(2,1)S(1)}, u32[]{:S(2)}, u32[]{:S(2)}) collective-permute-start(bf16[576,128]{1,0:T(8,128)(2,1)S(1)} %get-tuple-element.48.refs_0_), channel_id=1, source_target_pairs={{0,1},{1,0},{2,3},{3,2},{4,5},{5,4},{6,7},{7,6},{8,9},{9,8},{10,11... | collective-permute-start | bytes 442376 | tf_op jit(solution)/shard_map/ppermute | solution.py:274
  37.8 2.7 %collective-permute-start.10 = (bf16[576,128]{1,0:T(8,128)(2,1)S(1)}, bf16[576,128]{1,0:T(8,128)(2,1)S(1)}, u32[]{:S(2)}, u32[]{:S(2)}) collective-permute-start(bf16[576,128]{1,0:T(8,128)(2,1)S(1)} %get-tuple-element.52.own), channel_id=1, source_target_pairs={{0,4},{4,0},{8,12},{12,8},{1,5},{5,1},{9,13},{13,9},{2,6},{6,2},{1... | collective-permute-start | bytes 442376 | tf_op jit(solution)/shard_map/ppermute | solution.py:400
  37.9 6.3 %collective-permute-start.9 = (bf16[576,128]{1,0:T(8,128)(2,1)S(1)}, bf16[576,128]{1,0:T(8,128)(2,1)S(1)}, u32[]{:S(2)}, u32[]{:S(2)}) collective-permute-start(bf16[576,128]{1,0:T(8,128)(2,1)S(1)} %get-tuple-element.52.own), channel_id=1, source_target_pairs={{0,8},{4,12},{8,0},{12,4},{1,9},{5,13},{9,1},{13,5},{2,10},{6,14},... | collective-permute-start | bytes 442376 | tf_op jit(solution)/shard_map/ppermute | solution.py:274
  39.8 5.6 %collective-permute-start.8 = (bf16[576,128]{1,0:T(8,128)(2,1)S(1)}, bf16[576,128]{1,0:T(8,128)(2,1)S(1)}, u32[]{:S(2)}, u32[]{:S(2)}) collective-permute-start(bf16[576,128]{1,0:T(8,128)(2,1)S(1)} %collective-permute-done.7.refs_2_), channel_id=1, source_target_pairs={{0,1},{1,0},{2,3},{3,2},{4,5},{5,4},{6,7},{7,6},{8,9},{9,8},{10,11... | collective-permute-start | bytes 442376 | tf_op jit(solution)/shard_map/ppermute | solution.py:274
  44.2 1.4 %collective-permute-start.12 = (bf16[576,128]{1,0:T(8,128)(2,1)S(1)}, bf16[576,128]{1,0:T(8,128)(2,1)S(1)}, u32[]{:S(2)}, u32[]{:S(2)}) collective-permute-start(bf16[576,128]{1,0:T(8,128)(2,1)S(1)} %collective-permute-done.9.refs_0_), channel_id=1, source_target_pairs={{0,4},{4,0},{8,12},{12,8},{1,5},{5,1},{9,13},{13,9},{2,6},{6,2},{1... | collective-permute-start | bytes 442376 | tf_op jit(solution)/shard_map/ppermute | solution.py:274

commit v17 on v16

--- a/solution.py
+++ b/solution.py
@@ -177,23 +177,23 @@
     mix(mixed, None, col_l, row_r, 0, count, lambda i: r ^ place(c ^ slot(i), n), slot, t)
 
 
-def last_column_kernel(n, t, col, table, weights, left_in, right_in, col_l, col_r, wide):
-    r, c = lax.axis_index("row"), lax.axis_index("col")
-    outer, inner = mask_of(table, placed_at(r ^ (n - 1), n), t), mask_of(table, c, t)
+def last_row_kernel(n, t, row, table, weights, left_in, right_in, row_l, row_r, wide):
+    r, c = lax.axis_index("row"), lax.axis_index("col")
+    outer, inner = mask_of(table, c ^ (n - 1), t), mask_of(table, r, t)
     consts = constants(wide.shape[1])
-    sides(col, wide, col_l.at[n - 1], col_r.at[n - 1], outer, inner, consts, table, weights)
+    sides(row, wide, row_l.at[n - 1], row_r.at[n - 1], outer, inner, consts, table, weights)
 
 
 def mirror_kernel(n, t, *refs):
-    row, cols, (table, weights, w_out) = refs[0], refs[1 : n + 1], refs[n + 1 : n + 4]
-    col_l, old = refs[n + 6 : n + 8]
-    left_ref, row_l, row_r, mixed, wide, held = refs[n + 8 :]
+    cols, (table, weights, w_out, row_r) = refs[:n], refs[n : n + 4]
+    old = refs[n + 6]
+    left_ref, col_l, col_r, mixed, wide, held = refs[n + 7 :]
     width = wide.shape[1]
     r, c = lax.axis_index("row"), lax.axis_index("col")
     consts = constants(width)
     here, there = mask_of(table, r, t), mask_of(table, c, t)
-    outer = mask_of(table, c ^ (n - 1), t)
-    sides(row, wide, row_l.at[n - 1], row_r.at[n - 1], outer, here, consts, table, weights)
+    outer = mask_of(table, placed_at(r ^ (n - 1), n), t)
+    sides(cols[-1], wide, col_l.at[n - 1], col_r.at[n - 1], outer, there, consts, table, weights)
     count, slot = late_pairs(c ^ placed_at(r ^ (n - 1), n), n)
     mix(mixed, old, col_l, row_r, 0, count, lambda i: r ^ place(c ^ slot(i), n), slot, t)
     for s in range(n):
@@ -275,11 +275,6 @@
             step //= 2
         return [held[s] for s in range(n)]
 
-    def direct(block, last):
-        return [block] + [
-            lax.ppermute(last if s == n - 1 else block, "row", [(k, k ^ s) for k in range(n)]) for s in range(1, n)
-        ]
-
     def mirrored(block):
         pairs = [(a * n + z, (z // 2 + z % 2 * (n // 2)) * n + a) for a in range(n) for z in range(n)]
         return lax.ppermute(block, ("row", "col"), pairs)
@@ -324,14 +319,15 @@
             functools.partial(early_kernel, n, t), "early_sides", (slots,) * 2, [scratch], col_block, table, weights
         )
         rows = gather(pair, "col", lambda s, step: (own_l, col_l) if s else ())
-        cols = direct(*(lax.optimization_barrier((col_block, after))[0] for after in (own_l, own_l)))
+        ready = lax.optimization_barrier((col_block, own_l))[0]
+        core = lax.ppermute(ready, "row", [(k, k ^ 1) for k in range(n)])
         row_l, row_r, col_l, col_r = call(
             functools.partial(first_sides_kernel, n, t),
             "first_sides",
             (slots,) * 4,
             [scratch],
             *rows[1:-1],
-            cols[1],
+            core,
             table,
             weights,
             row_l,
@@ -340,6 +336,8 @@
             col_r,
             alias={n + 1: 0, n + 2: 1, n + 3: 2, n + 4: 3},
         )
+        cols = gather(ready, "row", lambda s, step: row_l if s else ())
+        cols[1] = core
         col_l, col_r, mixed = call(
             functools.partial(second_sides_kernel, n, t),
             "second_sides",
@@ -353,32 +351,31 @@
             col_r,
             alias={n: 0, n + 1: 1},
         )
-        col_l, col_r = call(
-            functools.partial(last_column_kernel, n, t),
-            "last_column",
+        row_l, row_r = call(
+            functools.partial(last_row_kernel, n, t),
+            "last_row",
             (slots, slots),
             [scratch],
-            cols[-1],
+            rows[-1],
             table,
             weights,
-            col_l,
-            col_r,
+            row_l,
+            lax.optimization_barrier((row_r, mixed))[0],
             alias={3: 0, 4: 1},
-            weight=30,
-        )
-        left, row_l, _ = call(
+            weight=1,
+        )
+        left, _, col_r = call(
             functools.partial(mirror_kernel, n, t),
             "mirror_end",
             (narrow, slots, slots),
             [scratch] * 2 + [pltpu.VMEM((n,) + area, BF16)],
-            rows[-1],
             *cols,
             table,
             weights,
             w_out,
-            row_l,
             row_r,
             col_l,
+            col_r,
             mixed,
             alias={n + 4: 1, n + 5: 2},
         )

time: 48.2 us -> 47.2 us (0.979)
  starting transfers between devices: 18.9 us -> 17.9 us
    ppermute x8 -> x10, waiting for transfers between devices: 4.03 us -> 6.49 us  [gather(): held[s ^ step] = lax.ppermute(part, axis, [(k, k ^ step) for k in range(n)])]
    ppermute x3 -> x1, waiting for transfers between devices: 2.22 us -> 0.01 us  [per_device(): core = lax.ppermute(ready, 'row', [(k, k ^ 1) for k in range(n)])]
    ppermute x3 -> x1, starting transfers between devices: 4.3 us -> 2.95 us  [per_device(): core = lax.ppermute(ready, 'row', [(k, k ^ 1) for k in range(n)])]
    ppermute x8 -> x10, starting transfers between devices: 13 us -> 13.3 us  [gather(): held[s ^ step] = lax.ppermute(part, axis, [(k, k ^ step) for k in range(n)])]
  transfers between devices with their start and end apart: 13 -> 13, of which waited for: 7 -> 5; matrix products, arithmetic and copies ran while one was open for 6% -> 6% of each run, Pallas kernels for 26% -> 27%
where the time goes in v17:
time: 47.2 us; the launch traced here: 46.7 us
  starting transfers between devices  17.9 us (38%)
  Pallas kernels  17.1 us (36%)
  waiting for transfers between devices  6.5 us (14%)
  local copies, waits for them, and re-layouts  4.39 us (9%)
  other arithmetic  0.66 us (1%)
    pallas_call x13, Pallas kernels, call(): pl.pallas_call(kernel, out_shape=outs, scratch_shapes=scratches, input_ou...  17.1 us
    ppermute x10, starting transfers between devices, gather(): held[s ^ step] = lax.ppermute(part, axis, [(k, k ^ step) for k in range(n)])  13.3 us
    ppermute x10, waiting for transfers between devices, gather(): held[s ^ step] = lax.ppermute(part, axis, [(k, k ^ step) for k in range(n)])  6.49 us
    ppermute x1, starting transfers between devices, per_device(): core = lax.ppermute(ready, 'row', [(k, k ^ 1) for k in range(n)])  2.95 us
    unnamed x8, local copies, waits for them, and re-layouts  2.11 us
    ppermute x1, starting transfers between devices, mirrored(): return lax.ppermute(block, ('row', 'col'), pairs)  1.56 us
    concatenate x1, local copies, waits for them, and re-layouts, per_device(): jnp.concatenate(vectors + [jnp.zeros((TABLE_MASK - 20, width), F32), mask])  1.51 us
  transfers between devices with their start and end apart: 13, of which 5 were waited for; matrix products, arithmetic and copies ran while one was open for 6% of the time, Pallas kernels for 27%

profile of v17, /device:TPU:0, one launch (start us, length us, event | category | flops | bytes accessed | tf_op | source)
XLA Modules:
  0.0 46.7 jit_solution(9999533928514849437)
XLA Ops:
  0.0 1.6 %collective-permute-start = (bf16[576,128]{1,0:T(8,128)(2,1)}, bf16[576,128]{1,0:T(8,128)(2,1)S(1)}, u32[]{:S(2)}, u32[]{:S(2)}) collective-permute-start(bf16[576,128]{1,0:T(8,128)(2,1)} %bitcast.2), channel_id=1, source_target_pairs={{0,0},{1,8},{2,4},{3,12},{4,1},{5,9},{6,5},{7,13},{8,2},{9,10},{10... | collective-permute-start | bytes 442376 | tf_op jit(solution)/shard_map/ppermute | solution.py:280
  1.6 4.5 %collective-permute-start.4 = (bf16[576,128]{1,0:T(8,128)(2,1)}, bf16[576,128]{1,0:T(8,128)(2,1)S(1)}, u32[]{:S(2)}, u32[]{:S(2)}) collective-permute-start(bf16[576,128]{1,0:T(8,128)(2,1)} %bitcast.3), channel_id=1, source_target_pairs={{0,2},{1,3},{2,0},{3,1},{4,6},{5,7},{6,4},{7,5},{8,10},{9,11},{10,... | collective-permute-start | bytes 442376 | tf_op jit(solution)/shard_map/ppermute | solution.py:274
  6.0 2.2 %collective-permute-start.3 = (bf16[576,128]{1,0:T(8,128)(2,1)}, bf16[576,128]{1,0:T(8,128)(2,1)S(1)}, u32[]{:S(2)}, u32[]{:S(2)}) collective-permute-start(bf16[576,128]{1,0:T(8,128)(2,1)} %bitcast.4), channel_id=1, source_target_pairs={{0,1},{1,0},{2,3},{3,2},{4,5},{5,4},{6,7},{7,6},{8,9},{9,8},{10,11... | collective-permute-start | bytes 442376 | tf_op jit(solution)/shard_map/ppermute | solution.py:274
  8.2 0.7 %convert_element_type.3 = f32[96]{0:T(128)S(1)} convert(s32[96]{0:T(128)} %param.11) | non-fusion elementwise | flops 96 | bytes 768 | tf_op jit(solution)/shard_map/convert_element_type | solution.py:305
  8.8 0.7 %reshape.11 = f32[10,128]{1,0:T(8,128)S(1)} reshape(f32[2,640]{1,0:T(2,128)} %param.15) | data formatting | bytes 10240 | tf_op jit(solution)/shard_map/reshape | solution.py:306
  9.5 0.1 broadcast_in_dim.10
  9.6 1.5 %concatenate.3.table.refs_3_.refs_1_.refs_4_ = f32[120,128]{1,0:T(8,128)S(1)} concatenate(f32[2,128]{1,0:T(2,128)} %param.12, f32[2,128]{1,0:T(2,128)} %param.13, f32[2,128]{1,0:T(2,128)} %param.16, f32[2,128]{1,0:T(2,128)} %param.17, f32[2,128]{1,0:T(2,128)} %param.19, f32[10,128]{1,0:T(8,128)S(1)} %reshape.11, f32[4,128]{1,0:T(4,128)S(1)} %broadcast_in_dim.4, ...), dimensions={0} | concatenate | bytes 122880 | tf_op jit(solution)/shard_map/concatenate | solution.py:307
  11.1 0.0 copy-start.1
  11.1 0.9 %copy-done.1 = bf16[24,24,128]{2,1,0:T(8,128)(2,1)S(1)} copy-done((bf16[24,24,128]{2,1,0:T(8,128)(2,1)S(1)}, bf16[24,24,128]{2,1,0:T(8,128)(2,1)}, u32[]{:S(2)}) %copy-start.1) | copy-done | bytes 147480
  12.0 1.0 %copy-done.3 = bf16[2,128,640]{2,1,0:T(8,128)(2,1)S(1)} copy-done((bf16[2,128,640]{2,1,0:T(8,128)(2,1)S(1)}, bf16[2,128,640]{2,1,0:T(8,128)(2,1)}, u32[]{:S(2)}) %copy-start.3) | copy-done | bytes 327704
  13.0 1.0 %own_sides.1 = (bf16[2,128,640]{2,1,0:T(8,128)(2,1)S(1)}, f32[4,576,128]{2,1,0:T(8,128)S(1)}, f32[4,576,128]{2,1,0:T(8,128)S(1)}, f32[576,128]{1,0:T(8,128)S(1)}) custom-call(bf16[576,128]{1,0:T(8,128)(2,1)S(1)} %bitcast.5, f32[120,128]{1,0:T(8,128)S(1)} %concatenate.3.table.refs_3_.refs_1_.refs_4_, bf16[2,128,640]{2,1,0:T(8,128)(2,1)S(1)} %copy-done.3), custom_call_target="tpu_custom_call" | custom-call | tf_op jit(solution)/shard_map/own_sides/pallas_call | solution.py:290
  14.0 0.0 collective-permute-done.col.refs_0_
  14.0 2.9 %collective-permute-start.1 = (bf16[576,128]{1,0:T(8,128)(2,1)S(1)}, bf16[576,128]{1,0:T(8,128)(2,1)S(1)}, u32[]{:S(2)}, u32[]{:S(2)}) collective-permute-start(bf16[576,128]{1,0:T(8,128)(2,1)S(1)} %collective-permute-done.col.refs_0_), channel_id=1, source_target_pairs={{0,4},{4,0},{8,12},{12,8},{1,5},{5,1},{9,13},{13,9},{2,6},{6,2},{1... | collective-permute-start | bytes 442376 | tf_op jit(solution)/shard_map/ppermute | solution.py:323
  16.9 0.0 collective-permute-start.2
  16.9 0.6 %early_sides.1 = (f32[4,576,128]{2,1,0:T(8,128)S(1)}, f32[4,576,128]{2,1,0:T(8,128)S(1)}) custom-call(bf16[576,128]{1,0:T(8,128)(2,1)S(1)} %collective-permute-done.col.refs_0_, f32[120,128]{1,0:T(8,128)S(1)} %concatenate.3.table.refs_3_.refs_1_.refs_4_, bf16[2,128,640]{2,1,0:T(8,128)(2,1)S(1)} %get-tuple-element.37.weights.refs_4_.refs_2_.refs_5_), custom_call_target="tpu_custom_call" | custom-call | tf_op jit(solution)/shard_map/early_sides/pallas_call | solution.py:290
  17.5 2.1 %collective-permute-done.4.refs_1_ = bf16[576,128]{1,0:T(8,128)(2,1)S(1)} collective-permute-done((bf16[576,128]{1,0:T(8,128)(2,1)}, bf16[576,128]{1,0:T(8,128)(2,1)S(1)}, u32[]{:S(2)}, u32[]{:S(2)}) %collective-permute-start.4) | collective-permute-done | bytes 147488 | tf_op jit(solution)/shard_map/ppermute | solution.py:274
  19.6 0.4 collective-permute-start.6
  20.0 0.0 collective-permute-done.3.refs_0_
  20.0 0.0 collective-permute-done.1.refs_2_.refs_1_
  20.0 1.5 %first_sides.1 = (f32[4,576,128]{2,1,0:T(8,128)S(1)}, f32[4,576,128]{2,1,0:T(8,128)S(1)}, f32[4,576,128]{2,1,0:T(8,128)S(1)}, f32[4,576,128]{2,1,0:T(8,128)S(1)}) custom-call(bf16[576,128]{1,0:T(8,128)(2,1)S(1)} %collective-permute-done.3.refs_0_, ...), custom_call_target="tpu_custom_call", output_to_operand_aliasing={{0}: (5, {}), {1}: (6, {}), {2}: (7, {}), {3}: (8, {})} | custom-call | tf_op jit(solution)/shard_map/first_sides/pallas_call | solution.py:290
  21.4 1.3 %collective-permute-done.2.refs_0_.refs_2_ = bf16[576,128]{1,0:T(8,128)(2,1)S(1)} collective-permute-done((bf16[576,128]{1,0:T(8,128)(2,1)S(1)}, bf16[576,128]{1,0:T(8,128)(2,1)S(1)}, u32[]{:S(2)}, u32[]{:S(2)}) %collective-permute-start.2) | collective-permute-done | bytes 147488 | tf_op jit(solution)/shard_map/ppermute | solution.py:274
  22.7 0.0 collective-permute-start.5
  22.7 2.6 %second_sides.1 = (f32[4,576,128]{2,1,0:T(8,128)S(1)}, f32[4,576,128]{2,1,0:T(8,128)S(1)}, f32[576,128]{1,0:T(8,128)S(1)}) custom-call(bf16[576,128]{1,0:T(8,128)(2,1)S(1)} %collective-permute-done.2.refs_0_.refs_2_, f32[120,128]{1,0:T(8,128)S(1)} %concatenate.3.table.refs_3_.refs_1_.refs_4_, ...), custom_call_target="tpu_custom_call", output_to_operand_aliasing={{0}: (4, {}), {1}: (5, {})} | custom-call | tf_op jit(solution)/shard_map/second_sides/pallas_call | solution.py:290
  25.3 0.0 copy-start
  25.3 0.0 collective-permute-done.6.row
  25.4 0.6 %last_row.1 = (f32[4,576,128]{2,1,0:T(8,128)S(1)}, f32[4,576,128]{2,1,0:T(8,128)S(1)}) custom-call(bf16[576,128]{1,0:T(8,128)(2,1)S(1)} %collective-permute-done.6.row, f32[120,128]{1,0:T(8,128)S(1)} %concatenate.3.table.refs_3_.refs_1_.refs_4_, ...), custom_call_target="tpu_custom_call", output_to_operand_aliasing={{0}: (3, {}), {1}: (4, {})} | custom-call | flops 1000000000 | bytes 1000000 | tf_op jit(solution)/shard_map/last_row/pallas_call | solution.py:290
  25.9 0.0 collective-permute-done.5.refs_3_
  26.0 0.2 copy-done
  26.2 2.6 %mirror_end.1 = (bf16[576,128]{1,0:T(8,128)(2,1)S(1)}, f32[4,576,128]{2,1,0:T(8,128)S(1)}, f32[4,576,128]{2,1,0:T(8,128)S(1)}) custom-call(bf16[576,128]{1,0:T(8,128)(2,1)S(1)} %collective-permute-done.col.refs_0_, bf16[576,128]{1,0:T(8,128)(2,1)S(1)} %collective-permute-done.1.refs_2_.refs_1_, ...), custom_call_target="tpu_custom_call", output_to_operand_aliasing={{1}: (8, {}), {2}: (9, {})} | custom-call | tf_op jit(solution)/shard_map/mirror_end/pallas_call | solution.py:290
  28.8 2.6 %collective-permute-start.7 = (bf16[576,128]{1,0:T(8,128)(2,1)S(1)}, bf16[576,128]{1,0:T(8,128)(2,1)S(1)}, u32[]{:S(2)}, u32[]{:S(2)}) collective-permute-start(bf16[576,128]{1,0:T(8,128)(2,1)S(1)} %get-tuple-element.52.refs_0_), channel_id=1, source_target_pairs={{0,2},{1,3},{2,0},{3,1},{4,6},{5,7},{6,4},{7,5},{8,10},{9,11},{10,... | collective-permute-start | bytes 442376 | tf_op jit(solution)/shard_map/ppermute | solution.py:274
  31.4 1.8 %collective-permute-start.11 = (bf16[576,128]{1,0:T(8,128)(2,1)S(1)}, bf16[576,128]{1,0:T(8,128)(2,1)S(1)}, u32[]{:S(2)}, u32[]{:S(2)}) collective-permute-start(bf16[576,128]{1,0:T(8,128)(2,1)S(1)} %get-tuple-element.52.refs_0_), channel_id=1, source_target_pairs={{0,1},{1,0},{2,3},{3,2},{4,5},{5,4},{6,7},{7,6},{8,9},{9,8},{10,11... | collective-permute-start | bytes 442376 | tf_op jit(solution)/shard_map/ppermute | solution.py:274
  33.2 0.0 copy-done.2
  33.2 3.6 %own_end.1 = (bf16[576,128]{1,0:T(8,128)(2,1)S(1)}, bf16[576,128]{1,0:T(8,128)(2,1)S(1)}) custom-call(f32[4,576,128]{2,1,0:T(8,128)S(1)} %get-tuple-element.53.row_l, f32[4,576,128]{2,1,0:T(8,128)S(1)} %get-tuple-element.54.col_r, f32[120,128]{1,0:T(8,128)S(1)} %concatenate.3.table.refs_3_.refs_1_.refs_4_, ...), custom_call_target="tpu_custom_call" | custom-call | tf_op jit(solution)/shard_map/own_end/pallas_call | solution.py:290
  36.8 0.1 collective-permute-start.10
  36.9 1.8 %collective-permute-start.9 = (bf16[576,128]{1,0:T(8,128)(2,1)S(1)}, bf16[576,128]{1,0:T(8,128)(2,1)S(1)}, u32[]{:S(2)}, u32[]{:S(2)}) collective-permute-start(bf16[576,128]{1,0:T(8,128)(2,1)S(1)} %get-tuple-element.56.own), channel_id=1, source_target_pairs={{0,8},{4,12},{8,0},{12,4},{1,9},{5,13},{9,1},{13,5},{2,10},{6,14},... | collective-permute-start | bytes 442376 | tf_op jit(solution)/shard_map/ppermute | solution.py:274
  38.7 0.6 %collective-permute-done.7.refs_2_ = bf16[576,128]{1,0:T(8,128)(2,1)S(1)} collective-permute-done((bf16[576,128]{1,0:T(8,128)(2,1)S(1)}, bf16[576,128]{1,0:T(8,128)(2,1)S(1)}, u32[]{:S(2)}, u32[]{:S(2)}) %collective-permute-start.7) | collective-permute-done | bytes 147488 | tf_op jit(solution)/shard_map/ppermute | solution.py:274
  39.3 0.1 collective-permute-start.8
  39.4 0.0 collective-permute-done.11.refs_1_
  39.4 0.1 left_slots.1.lefts.refs_1_.left_in
  39.5 0.5 %gate.1.gating = f32[576,128]{1,0:T(8,128)S(1)} custom-call(bf16[576,128]{1,0:T(8,128)(2,1)S(1)} %get-tuple-element.62.pair, f32[120,128]{1,0:T(8,128)S(1)} %concatenate.3.table.refs_3_.refs_1_.refs_4_, bf16[2,128,640]{2,1,0:T(8,128)(2,1)S(1)} %get-tuple-element.37.weights.refs_4_.refs_2_.refs_5_), custom_call_target="tpu_custom_call" | custom-call | tf_op jit(solution)/shard_map/gate/pallas_call | solution.py:290
  40.1 0.0 collective-permute-done.10.core
  40.1 1.4 %near_slots.1 = (f32[4,576,128]{2,1,0:T(8,128)S(1)}, f32[576,128]{1,0:T(8,128)S(1)}) custom-call(bf16[576,128]{1,0:T(8,128)(2,1)S(1)} %get-tuple-element.56.own, bf16[576,128]{1,0:T(8,128)(2,1)S(1)} %collective-permute-done.10.core, f32[4,576,128]{2,1,0:T(8,128)S(1)} %left_slots.1.lefts.refs_1_.left_in), custom_call_target="tpu_custom_call" | custom-call | tf_op jit(solution)/shard_map/near_slots/pallas_call | solution.py:290
  41.5 1.7 %collective-permute-done.9.refs_0_ = bf16[576,128]{1,0:T(8,128)(2,1)S(1)} collective-permute-done((bf16[576,128]{1,0:T(8,128)(2,1)S(1)}, bf16[576,128]{1,0:T(8,128)(2,1)S(1)}, u32[]{:S(2)}, u32[]{:S(2)}) %collective-permute-start.9) | collective-permute-done | bytes 147488 | tf_op jit(solution)/shard_map/ppermute | solution.py:274
  43.2 0.0 collective-permute-start.12
  43.2 0.7 %far_slots.1 = (f32[4,576,128]{2,1,0:T(8,128)S(1)}, f32[576,128]{1,0:T(8,128)S(1)}) custom-call(bf16[576,128]{1,0:T(8,128)(2,1)S(1)} %collective-permute-done.9.refs_0_, f32[4,576,128]{2,1,0:T(8,128)S(1)} %left_slots.1.lefts.refs_1_.left_in, f32[4,576,128]{2,1,0:T(8,128)S(1)} %get-tuple-element.59.refs_2_, ...), custom_call_target="tpu_custom_call", output_to_operand_aliasing={{0}: (2, {}), {1}: (3, {})} | custom-call | tf_op jit(solution)/shard_map/far_slots/pallas_call | solution.py:290
  43.9 0.8 %collective-permute-done.8.block = bf16[576,128]{1,0:T(8,128)(2,1)S(1)} collective-permute-done((bf16[576,128]{1,0:T(8,128)(2,1)S(1)}, bf16[576,128]{1,0:T(8,128)(2,1)S(1)}, u32[]{:S(2)}, u32[]{:S(2)}) %collective-permute-start.8) | collective-permute-done | bytes 147488 | tf_op jit(solution)/shard_map/ppermute | solution.py:274
  44.7 0.0 collective-permute-done.12.right
  44.7 1.9 %end.1 = (bf16[576,128]{1,0:T(8,128)(2,1)}, f32[4,576,128]{2,1,0:T(8,128)S(1)}, f32[4,576,128]{2,1,0:T(8,128)S(1)}) custom-call(f32[576,128]{1,0:T(8,128)S(1)} %left_last.1.left, bf16[576,128]{1,0:T(8,128)(2,1)S(1)} %collective-permute-done.12.right, f32[576,128]{1,0:T(8,128)S(1)} %get-tuple-element.60.old, ...), custom_call_target="tpu_custom_call", output_to_operand_aliasing={{1}: (7, {}), {2}: (8, {})} | custom-call | tf_op jit(solution)/shard_map/end/pallas_call | solution.py:290
  (4 shorter events, 0.0 us)
Async XLA Ops:
  0.0 14.0 %collective-permute-start = (bf16[576,128]{1,0:T(8,128)(2,1)}, bf16[576,128]{1,0:T(8,128)(2,1)S(1)}, u32[]{:S(2)}, u32[]{:S(2)}) collective-permute-start(bf16[576,128]{1,0:T(8,128)(2,1)} %bitcast.2), channel_id=1, source_target_pairs={{0,0},{1,8},{2,4},{3,12},{4,1},{5,9},{6,5},{7,13},{8,2},{9,10},{10... | collective-permute-start | bytes 442376 | tf_op jit(solution)/shard_map/ppermute | solution.py:280
  1.6 18.1 %collective-permute-start.4 = (bf16[576,128]{1,0:T(8,128)(2,1)}, bf16[576,128]{1,0:T(8,128)(2,1)S(1)}, u32[]{:S(2)}, u32[]{:S(2)}) collective-permute-start(bf16[576,128]{1,0:T(8,128)(2,1)} %bitcast.3), channel_id=1, source_target_pairs={{0,2},{1,3},{2,0},{3,1},{4,6},{5,7},{6,4},{7,5},{8,10},{9,11},{10,... | collective-permute-start | bytes 442376 | tf_op jit(solution)/shard_map/ppermute | solution.py:274
  6.0 14.0 %collective-permute-start.3 = (bf16[576,128]{1,0:T(8,128)(2,1)}, bf16[576,128]{1,0:T(8,128)(2,1)S(1)}, u32[]{:S(2)}, u32[]{:S(2)}) collective-permute-start(bf16[576,128]{1,0:T(8,128)(2,1)} %bitcast.4), channel_id=1, source_target_pairs={{0,1},{1,0},{2,3},{3,2},{4,5},{5,4},{6,7},{7,6},{8,9},{9,8},{10,11... | collective-permute-start | bytes 442376 | tf_op jit(solution)/shard_map/ppermute | solution.py:274
  11.1 0.9 %copy-start.1 = (bf16[24,24,128]{2,1,0:T(8,128)(2,1)S(1)}, bf16[24,24,128]{2,1,0:T(8,128)(2,1)}, u32[]{:S(2)}) copy-start(bf16[24,24,128]{2,1,0:T(8,128)(2,1)} %param.10) | copy-start | bytes 442372
  12.0 1.0 %copy-start.3 = (bf16[2,128,640]{2,1,0:T(8,128)(2,1)S(1)}, bf16[2,128,640]{2,1,0:T(8,128)(2,1)}, u32[]{:S(2)}) copy-start(bf16[2,128,640]{2,1,0:T(8,128)(2,1)} %w_in.1) | copy-start | bytes 983044
  14.0 6.0 %collective-permute-start.1 = (bf16[576,128]{1,0:T(8,128)(2,1)S(1)}, bf16[576,128]{1,0:T(8,128)(2,1)S(1)}, u32[]{:S(2)}, u32[]{:S(2)}) collective-permute-start(bf16[576,128]{1,0:T(8,128)(2,1)S(1)} %collective-permute-done.col.refs_0_), channel_id=1, source_target_pairs={{0,4},{4,0},{8,12},{12,8},{1,5},{5,1},{9,13},{13,9},{2,6},{6,2},{1... | collective-permute-start | bytes 442376 | tf_op jit(solution)/shard_map/ppermute | solution.py:323
  16.9 5.8 %collective-permute-start.2 = (bf16[576,128]{1,0:T(8,128)(2,1)S(1)}, bf16[576,128]{1,0:T(8,128)(2,1)S(1)}, u32[]{:S(2)}, u32[]{:S(2)}) collective-permute-start(bf16[576,128]{1,0:T(8,128)(2,1)S(1)} %collective-permute-done.col.refs_0_), channel_id=1, source_target_pairs={{0,8},{4,12},{8,0},{12,4},{1,9},{5,13},{9,1},{13,5},{2,10},{6,14},... | collective-permute-start | bytes 442376 | tf_op jit(solution)/shard_map/ppermute | solution.py:274
  19.6 5.7 %collective-permute-start.6 = (bf16[576,128]{1,0:T(8,128)(2,1)S(1)}, bf16[576,128]{1,0:T(8,128)(2,1)S(1)}, u32[]{:S(2)}, u32[]{:S(2)}) collective-permute-start(bf16[576,128]{1,0:T(8,128)(2,1)S(1)} %collective-permute-done.4.refs_1_), channel_id=1, source_target_pairs={{0,1},{1,0},{2,3},{3,2},{4,5},{5,4},{6,7},{7,6},{8,9},{9,8},{10,11... | collective-permute-start | bytes 442376 | tf_op jit(solution)/shard_map/ppermute | solution.py:274
  22.7 3.2 %collective-permute-start.5 = (bf16[576,128]{1,0:T(8,128)(2,1)S(1)}, bf16[576,128]{1,0:T(8,128)(2,1)S(1)}, u32[]{:S(2)}, u32[]{:S(2)}) collective-permute-start(bf16[576,128]{1,0:T(8,128)(2,1)S(1)} %collective-permute-done.2.refs_0_.refs_2_), channel_id=1, source_target_pairs={{0,4},{4,0},{8,12},{12,8},{1,5},{5,1},{9,13},{13,9},{2,6},{6,2},{1... | collective-permute-start | bytes 442376 | tf_op jit(solution)/shard_map/ppermute | solution.py:274
  25.3 0.8 %copy-start = (bf16[2,128,128]{2,1,0:T(8,128)(2,1)S(1)}, bf16[2,128,128]{2,1,0:T(8,128)(2,1)}, u32[]{:S(2)}) copy-start(bf16[2,128,128]{2,1,0:T(8,128)(2,1)} %w_out.3) | copy-start | bytes 196612
  26.2 7.0 %copy-start.2 = (bf16[24,24,128]{2,1,0:T(8,128)(2,1)S(1)}, bf16[24,24,128]{2,1,0:T(8,128)(2,1)}, u32[]{:S(2)}) copy-start(bf16[24,24,128]{2,1,0:T(8,128)(2,1)} %param.10) | copy-start | bytes 442372
  28.8 10.5 %collective-permute-start.7 = (bf16[576,128]{1,0:T(8,128)(2,1)S(1)}, bf16[576,128]{1,0:T(8,128)(2,1)S(1)}, u32[]{:S(2)}, u32[]{:S(2)}) collective-permute-start(bf16[576,128]{1,0:T(8,128)(2,1)S(1)} %get-tuple-element.52.refs_0_), channel_id=1, source_target_pairs={{0,2},{1,3},{2,0},{3,1},{4,6},{5,7},{6,4},{7,5},{8,10},{9,11},{10,... | collective-permute-start | bytes 442376 | tf_op jit(solution)/shard_map/ppermute | solution.py:274
  31.4 8.1 %collective-permute-start.11 = (bf16[576,128]{1,0:T(8,128)(2,1)S(1)}, bf16[576,128]{1,0:T(8,128)(2,1)S(1)}, u32[]{:S(2)}, u32[]{:S(2)}) collective-permute-start(bf16[576,128]{1,0:T(8,128)(2,1)S(1)} %get-tuple-element.52.refs_0_), channel_id=1, source_target_pairs={{0,1},{1,0},{2,3},{3,2},{4,5},{5,4},{6,7},{7,6},{8,9},{9,8},{10,11... | collective-permute-start | bytes 442376 | tf_op jit(solution)/shard_map/ppermute | solution.py:274
  36.8 3.2 %collective-permute-start.10 = (bf16[576,128]{1,0:T(8,128)(2,1)S(1)}, bf16[576,128]{1,0:T(8,128)(2,1)S(1)}, u32[]{:S(2)}, u32[]{:S(2)}) collective-permute-start(bf16[576,128]{1,0:T(8,128)(2,1)S(1)} %get-tuple-element.56.own), channel_id=1, source_target_pairs={{0,4},{4,0},{8,12},{12,8},{1,5},{5,1},{9,13},{13,9},{2,6},{6,2},{1... | collective-permute-start | bytes 442376 | tf_op jit(solution)/shard_map/ppermute | solution.py:397
  36.9 6.3 %collective-permute-start.9 = (bf16[576,128]{1,0:T(8,128)(2,1)S(1)}, bf16[576,128]{1,0:T(8,128)(2,1)S(1)}, u32[]{:S(2)}, u32[]{:S(2)}) collective-permute-start(bf16[576,128]{1,0:T(8,128)(2,1)S(1)} %get-tuple-element.56.own), channel_id=1, source_target_pairs={{0,8},{4,12},{8,0},{12,4},{1,9},{5,13},{9,1},{13,5},{2,10},{6,14},... | collective-permute-start | bytes 442376 | tf_op jit(solution)/shard_map/ppermute | solution.py:274
  39.3 5.4 %collective-permute-start.8 = (bf16[576,128]{1,0:T(8,128)(2,1)S(1)}, bf16[576,128]{1,0:T(8,128)(2,1)S(1)}, u32[]{:S(2)}, u32[]{:S(2)}) collective-permute-start(bf16[576,128]{1,0:T(8,128)(2,1)S(1)} %collective-permute-done.7.refs_2_), channel_id=1, source_target_pairs={{0,1},{1,0},{2,3},{3,2},{4,5},{5,4},{6,7},{7,6},{8,9},{9,8},{10,11... | collective-permute-start | bytes 442376 | tf_op jit(solution)/shard_map/ppermute | solution.py:274
  43.2 1.6 %collective-permute-start.12 = (bf16[576,128]{1,0:T(8,128)(2,1)S(1)}, bf16[576,128]{1,0:T(8,128)(2,1)S(1)}, u32[]{:S(2)}, u32[]{:S(2)}) collective-permute-start(bf16[576,128]{1,0:T(8,128)(2,1)S(1)} %collective-permute-done.9.refs_0_), channel_id=1, source_target_pairs={{0,4},{4,0},{8,12},{12,8},{1,5},{5,1},{9,13},{13,9},{2,6},{6,2},{1... | collective-permute-start | bytes 442376 | tf_op jit(solution)/shard_map/ppermute | solution.py:274

commit v18 on v17

--- a/solution.py
+++ b/solution.py
@@ -320,7 +320,8 @@
         )
         rows = gather(pair, "col", lambda s, step: (own_l, col_l) if s else ())
         ready = lax.optimization_barrier((col_block, own_l))[0]
-        core = lax.ppermute(ready, "row", [(k, k ^ 1) for k in range(n)])
+        core = lax.optimization_barrier((col_block, col_l))[0]
+        core = lax.ppermute(core, "row", [(k, k ^ 1) for k in range(n)])
         row_l, row_r, col_l, col_r = call(
             functools.partial(first_sides_kernel, n, t),
             "first_sides",

time: 47.2 us -> 47.8 us (1.013)
  waiting for transfers between devices: 6.5 us -> 7.31 us
    ppermute x10, waiting for transfers between devices: 6.49 us -> 7.3 us  [gather(): held[s ^ step] = lax.ppermute(part, axis, [(k, k ^ step) for k in range(n)])]
    unnamed x8 -> x6, local copies, waits for them, and re-layouts: 2.11 us -> 2.11 us
where the time goes in v18:
time: 47.8 us; the launch traced here: 47.4 us
  starting transfers between devices  17.8 us (37%)
  Pallas kernels  17.1 us (36%)
  waiting for transfers between devices  7.31 us (15%)
  local copies, waits for them, and re-layouts  4.39 us (9%)
  other arithmetic  0.66 us (1%)
    pallas_call x13, Pallas kernels, call(): pl.pallas_call(kernel, out_shape=outs, scratch_shapes=scratches, input_ou...  17.1 us
    ppermute x10, starting transfers between devices, gather(): held[s ^ step] = lax.ppermute(part, axis, [(k, k ^ step) for k in range(n)])  13.1 us
    ppermute x10, waiting for transfers between devices, gather(): held[s ^ step] = lax.ppermute(part, axis, [(k, k ^ step) for k in range(n)])  7.3 us
    ppermute x1, starting transfers between devices, per_device(): core = lax.ppermute(core, 'row', [(k, k ^ 1) for k in range(n)])  3.01 us
    unnamed x6, local copies, waits for them, and re-layouts  2.11 us
    ppermute x1, starting transfers between devices, mirrored(): return lax.ppermute(block, ('row', 'col'), pairs)  1.56 us
    concatenate x1, local copies, waits for them, and re-layouts, per_device(): jnp.concatenate(vectors + [jnp.zeros((TABLE_MASK - 20, width), F32), mask])  1.51 us
  transfers between devices with their start and end apart: 13, of which 5 were waited for; matrix products, arithmetic and copies ran while one was open for 6% of the time, Pallas kernels for 27%

profile of v18, /device:TPU:0, one launch (start us, length us, event | category | flops | bytes accessed | tf_op | source)
XLA Modules:
  0.0 47.4 jit_solution(13116288922233392661)
XLA Ops:
  0.0 1.6 %collective-permute-start = (bf16[576,128]{1,0:T(8,128)(2,1)}, bf16[576,128]{1,0:T(8,128)(2,1)S(1)}, u32[]{:S(2)}, u32[]{:S(2)}) collective-permute-start(bf16[576,128]{1,0:T(8,128)(2,1)} %bitcast.2), channel_id=1, source_target_pairs={{0,0},{1,8},{2,4},{3,12},{4,1},{5,9},{6,5},{7,13},{8,2},{9,10},{10... | collective-permute-start | bytes 442376 | tf_op jit(solution)/shard_map/ppermute | solution.py:280
  1.6 4.5 %collective-permute-start.4 = (bf16[576,128]{1,0:T(8,128)(2,1)}, bf16[576,128]{1,0:T(8,128)(2,1)S(1)}, u32[]{:S(2)}, u32[]{:S(2)}) collective-permute-start(bf16[576,128]{1,0:T(8,128)(2,1)} %bitcast.3), channel_id=1, source_target_pairs={{0,2},{1,3},{2,0},{3,1},{4,6},{5,7},{6,4},{7,5},{8,10},{9,11},{10,... | collective-permute-start | bytes 442376 | tf_op jit(solution)/shard_map/ppermute | solution.py:274
  6.0 2.2 %collective-permute-start.3 = (bf16[576,128]{1,0:T(8,128)(2,1)}, bf16[576,128]{1,0:T(8,128)(2,1)S(1)}, u32[]{:S(2)}, u32[]{:S(2)}) collective-permute-start(bf16[576,128]{1,0:T(8,128)(2,1)} %bitcast.4), channel_id=1, source_target_pairs={{0,1},{1,0},{2,3},{3,2},{4,5},{5,4},{6,7},{7,6},{8,9},{9,8},{10,11... | collective-permute-start | bytes 442376 | tf_op jit(solution)/shard_map/ppermute | solution.py:274
  8.2 0.7 %convert_element_type.3 = f32[96]{0:T(128)S(1)} convert(s32[96]{0:T(128)} %param.11) | non-fusion elementwise | flops 96 | bytes 768 | tf_op jit(solution)/shard_map/convert_element_type | solution.py:305
  8.8 0.7 %reshape.11 = f32[10,128]{1,0:T(8,128)S(1)} reshape(f32[2,640]{1,0:T(2,128)} %param.15) | data formatting | bytes 10240 | tf_op jit(solution)/shard_map/reshape | solution.py:306
  9.5 0.1 broadcast_in_dim.10
  9.6 1.5 %concatenate.3.table.refs_3_.refs_1_.refs_4_ = f32[120,128]{1,0:T(8,128)S(1)} concatenate(f32[2,128]{1,0:T(2,128)} %param.12, f32[2,128]{1,0:T(2,128)} %param.13, f32[2,128]{1,0:T(2,128)} %param.16, f32[2,128]{1,0:T(2,128)} %param.17, f32[2,128]{1,0:T(2,128)} %param.19, f32[10,128]{1,0:T(8,128)S(1)} %reshape.11, f32[4,128]{1,0:T(4,128)S(1)} %broadcast_in_dim.4, ...), dimensions={0} | concatenate | bytes 122880 | tf_op jit(solution)/shard_map/concatenate | solution.py:307
  11.1 0.0 copy-start.1
  11.1 0.9 %copy-done.1 = bf16[24,24,128]{2,1,0:T(8,128)(2,1)S(1)} copy-done((bf16[24,24,128]{2,1,0:T(8,128)(2,1)S(1)}, bf16[24,24,128]{2,1,0:T(8,128)(2,1)}, u32[]{:S(2)}) %copy-start.1) | copy-done | bytes 147480
  12.0 0.0 copy-start.2
  12.0 1.0 %copy-done.2 = bf16[2,128,640]{2,1,0:T(8,128)(2,1)S(1)} copy-done((bf16[2,128,640]{2,1,0:T(8,128)(2,1)S(1)}, bf16[2,128,640]{2,1,0:T(8,128)(2,1)}, u32[]{:S(2)}) %copy-start.2) | copy-done | bytes 327704
  13.0 1.0 %own_sides.1 = (bf16[2,128,640]{2,1,0:T(8,128)(2,1)S(1)}, f32[4,576,128]{2,1,0:T(8,128)S(1)}, f32[4,576,128]{2,1,0:T(8,128)S(1)}, f32[576,128]{1,0:T(8,128)S(1)}) custom-call(bf16[576,128]{1,0:T(8,128)(2,1)S(1)} %bitcast.5, f32[120,128]{1,0:T(8,128)S(1)} %concatenate.3.table.refs_3_.refs_1_.refs_4_, bf16[2,128,640]{2,1,0:T(8,128)(2,1)S(1)} %copy-done.2), custom_call_target="tpu_custom_call" | custom-call | tf_op jit(solution)/shard_map/own_sides/pallas_call | solution.py:290
  14.0 0.0 collective-permute-done.col.refs_0_
  14.0 0.6 %early_sides.1 = (f32[4,576,128]{2,1,0:T(8,128)S(1)}, f32[4,576,128]{2,1,0:T(8,128)S(1)}) custom-call(bf16[576,128]{1,0:T(8,128)(2,1)S(1)} %collective-permute-done.col.refs_0_, f32[120,128]{1,0:T(8,128)S(1)} %concatenate.3.table.refs_3_.refs_1_.refs_4_, bf16[2,128,640]{2,1,0:T(8,128)(2,1)S(1)} %get-tuple-element.38.weights.refs_4_.refs_2_.refs_5_), custom_call_target="tpu_custom_call" | custom-call | tf_op jit(solution)/shard_map/early_sides/pallas_call | solution.py:290
  14.6 3.0 %collective-permute-start.1 = (bf16[576,128]{1,0:T(8,128)(2,1)S(1)}, bf16[576,128]{1,0:T(8,128)(2,1)S(1)}, u32[]{:S(2)}, u32[]{:S(2)}) collective-permute-start(bf16[576,128]{1,0:T(8,128)(2,1)S(1)} %collective-permute-done.col.refs_0_), channel_id=1, source_target_pairs={{0,4},{4,0},{8,12},{12,8},{1,5},{5,1},{9,13},{13,9},{2,6},{6,2},{1... | collective-permute-start | bytes 442376 | tf_op jit(solution)/shard_map/ppermute | solution.py:324
  17.6 0.0 collective-permute-start.2
  17.6 2.0 %collective-permute-done.4.refs_1_ = bf16[576,128]{1,0:T(8,128)(2,1)S(1)} collective-permute-done((bf16[576,128]{1,0:T(8,128)(2,1)}, bf16[576,128]{1,0:T(8,128)(2,1)S(1)}, u32[]{:S(2)}, u32[]{:S(2)}) %collective-permute-start.4) | collective-permute-done | bytes 147488 | tf_op jit(solution)/shard_map/ppermute | solution.py:274
  19.6 0.3 collective-permute-start.6
  20.0 0.0 collective-permute-done.3.refs_0_
  20.0 0.0 collective-permute-done.1.refs_2_.refs_1_
  20.0 1.5 %first_sides.1 = (f32[4,576,128]{2,1,0:T(8,128)S(1)}, f32[4,576,128]{2,1,0:T(8,128)S(1)}, f32[4,576,128]{2,1,0:T(8,128)S(1)}, f32[4,576,128]{2,1,0:T(8,128)S(1)}) custom-call(bf16[576,128]{1,0:T(8,128)(2,1)S(1)} %collective-permute-done.3.refs_0_, ...), custom_call_target="tpu_custom_call", output_to_operand_aliasing={{0}: (5, {}), {1}: (6, {}), {2}: (7, {}), {3}: (8, {})} | custom-call | tf_op jit(solution)/shard_map/first_sides/pallas_call | solution.py:290
  21.4 2.0 %collective-permute-done.2.refs_0_.refs_2_ = bf16[576,128]{1,0:T(8,128)(2,1)S(1)} collective-permute-done((bf16[576,128]{1,0:T(8,128)(2,1)S(1)}, bf16[576,128]{1,0:T(8,128)(2,1)S(1)}, u32[]{:S(2)}, u32[]{:S(2)}) %collective-permute-start.2) | collective-permute-done | bytes 147488 | tf_op jit(solution)/shard_map/ppermute | solution.py:274
  23.4 0.0 collective-permute-start.5
  23.4 2.6 %second_sides.1 = (f32[4,576,128]{2,1,0:T(8,128)S(1)}, f32[4,576,128]{2,1,0:T(8,128)S(1)}, f32[576,128]{1,0:T(8,128)S(1)}) custom-call(bf16[576,128]{1,0:T(8,128)(2,1)S(1)} %collective-permute-done.2.refs_0_.refs_2_, f32[120,128]{1,0:T(8,128)S(1)} %concatenate.3.table.refs_3_.refs_1_.refs_4_, ...), custom_call_target="tpu_custom_call", output_to_operand_aliasing={{0}: (4, {}), {1}: (5, {})} | custom-call | tf_op jit(solution)/shard_map/second_sides/pallas_call | solution.py:290
  26.1 0.0 copy-start
  26.1 0.0 collective-permute-done.6.row
  26.1 0.6 %last_row.1 = (f32[4,576,128]{2,1,0:T(8,128)S(1)}, f32[4,576,128]{2,1,0:T(8,128)S(1)}) custom-call(bf16[576,128]{1,0:T(8,128)(2,1)S(1)} %collective-permute-done.6.row, f32[120,128]{1,0:T(8,128)S(1)} %concatenate.3.table.refs_3_.refs_1_.refs_4_, ...), custom_call_target="tpu_custom_call", output_to_operand_aliasing={{0}: (3, {}), {1}: (4, {})} | custom-call | flops 1000000000 | bytes 1000000 | tf_op jit(solution)/shard_map/last_row/pallas_call | solution.py:290
  26.7 0.0 collective-permute-done.5.refs_3_
  26.7 0.2 copy-done
  26.9 2.6 %mirror_end.1 = (bf16[576,128]{1,0:T(8,128)(2,1)S(1)}, f32[4,576,128]{2,1,0:T(8,128)S(1)}, f32[4,576,128]{2,1,0:T(8,128)S(1)}) custom-call(bf16[576,128]{1,0:T(8,128)(2,1)S(1)} %collective-permute-done.col.refs_0_, bf16[576,128]{1,0:T(8,128)(2,1)S(1)} %collective-permute-done.1.refs_2_.refs_1_, ...), custom_call_target="tpu_custom_call", output_to_operand_aliasing={{1}: (8, {}), {2}: (9, {})} | custom-call | tf_op jit(solution)/shard_map/mirror_end/pallas_call | solution.py:290
  29.5 2.1 %collective-permute-start.7 = (bf16[576,128]{1,0:T(8,128)(2,1)S(1)}, bf16[576,128]{1,0:T(8,128)(2,1)S(1)}, u32[]{:S(2)}, u32[]{:S(2)}) collective-permute-start(bf16[576,128]{1,0:T(8,128)(2,1)S(1)} %get-tuple-element.54.refs_0_), channel_id=1, source_target_pairs={{0,2},{1,3},{2,0},{3,1},{4,6},{5,7},{6,4},{7,5},{8,10},{9,11},{10,... | collective-permute-start | bytes 442376 | tf_op jit(solution)/shard_map/ppermute | solution.py:274
  31.7 2.2 %collective-permute-start.11 = (bf16[576,128]{1,0:T(8,128)(2,1)S(1)}, bf16[576,128]{1,0:T(8,128)(2,1)S(1)}, u32[]{:S(2)}, u32[]{:S(2)}) collective-permute-start(bf16[576,128]{1,0:T(8,128)(2,1)S(1)} %get-tuple-element.54.refs_0_), channel_id=1, source_target_pairs={{0,1},{1,0},{2,3},{3,2},{4,5},{5,4},{6,7},{7,6},{8,9},{9,8},{10,11... | collective-permute-start | bytes 442376 | tf_op jit(solution)/shard_map/ppermute | solution.py:274
  33.8 3.6 %own_end.1 = (bf16[576,128]{1,0:T(8,128)(2,1)S(1)}, bf16[576,128]{1,0:T(8,128)(2,1)S(1)}) custom-call(f32[4,576,128]{2,1,0:T(8,128)S(1)} %get-tuple-element.55.row_l, f32[4,576,128]{2,1,0:T(8,128)S(1)} %get-tuple-element.56.col_r, f32[120,128]{1,0:T(8,128)S(1)} %concatenate.3.table.refs_3_.refs_1_.refs_4_, ...), custom_call_target="tpu_custom_call" | custom-call | tf_op jit(solution)/shard_map/own_end/pallas_call | solution.py:290
  37.5 0.1 collective-permute-start.10
  37.6 1.8 %collective-permute-start.9 = (bf16[576,128]{1,0:T(8,128)(2,1)S(1)}, bf16[576,128]{1,0:T(8,128)(2,1)S(1)}, u32[]{:S(2)}, u32[]{:S(2)}) collective-permute-start(bf16[576,128]{1,0:T(8,128)(2,1)S(1)} %get-tuple-element.58.own), channel_id=1, source_target_pairs={{0,8},{4,12},{8,0},{12,4},{1,9},{5,13},{9,1},{13,5},{2,10},{6,14},... | collective-permute-start | bytes 442376 | tf_op jit(solution)/shard_map/ppermute | solution.py:274
  39.4 0.6 %collective-permute-done.7.refs_2_ = bf16[576,128]{1,0:T(8,128)(2,1)S(1)} collective-permute-done((bf16[576,128]{1,0:T(8,128)(2,1)S(1)}, bf16[576,128]{1,0:T(8,128)(2,1)S(1)}, u32[]{:S(2)}, u32[]{:S(2)}) %collective-permute-start.7) | collective-permute-done | bytes 147488 | tf_op jit(solution)/shard_map/ppermute | solution.py:274
  40.0 0.1 collective-permute-start.8
  40.1 0.0 collective-permute-done.11.refs_1_
  40.1 0.1 left_slots.1.lefts.refs_1_.left_in
  40.2 0.5 %gate.1.gating = f32[576,128]{1,0:T(8,128)S(1)} custom-call(bf16[576,128]{1,0:T(8,128)(2,1)S(1)} %get-tuple-element.64.pair, f32[120,128]{1,0:T(8,128)S(1)} %concatenate.3.table.refs_3_.refs_1_.refs_4_, bf16[2,128,640]{2,1,0:T(8,128)(2,1)S(1)} %get-tuple-element.38.weights.refs_4_.refs_2_.refs_5_), custom_call_target="tpu_custom_call" | custom-call | tf_op jit(solution)/shard_map/gate/pallas_call | solution.py:290
  40.7 0.0 collective-permute-done.10.core
  40.7 1.4 %near_slots.1 = (f32[4,576,128]{2,1,0:T(8,128)S(1)}, f32[576,128]{1,0:T(8,128)S(1)}) custom-call(bf16[576,128]{1,0:T(8,128)(2,1)S(1)} %get-tuple-element.58.own, bf16[576,128]{1,0:T(8,128)(2,1)S(1)} %collective-permute-done.10.core, f32[4,576,128]{2,1,0:T(8,128)S(1)} %left_slots.1.lefts.refs_1_.left_in), custom_call_target="tpu_custom_call" | custom-call | tf_op jit(solution)/shard_map/near_slots/pallas_call | solution.py:290
  42.1 1.7 %collective-permute-done.9.refs_0_ = bf16[576,128]{1,0:T(8,128)(2,1)S(1)} collective-permute-done((bf16[576,128]{1,0:T(8,128)(2,1)S(1)}, bf16[576,128]{1,0:T(8,128)(2,1)S(1)}, u32[]{:S(2)}, u32[]{:S(2)}) %collective-permute-start.9) | collective-permute-done | bytes 147488 | tf_op jit(solution)/shard_map/ppermute | solution.py:274
  43.8 0.0 collective-permute-start.12
  43.8 0.7 %far_slots.1 = (f32[4,576,128]{2,1,0:T(8,128)S(1)}, f32[576,128]{1,0:T(8,128)S(1)}) custom-call(bf16[576,128]{1,0:T(8,128)(2,1)S(1)} %collective-permute-done.9.refs_0_, f32[4,576,128]{2,1,0:T(8,128)S(1)} %left_slots.1.lefts.refs_1_.left_in, f32[4,576,128]{2,1,0:T(8,128)S(1)} %get-tuple-element.61.refs_2_, ...), custom_call_target="tpu_custom_call", output_to_operand_aliasing={{0}: (2, {}), {1}: (3, {})} | custom-call | tf_op jit(solution)/shard_map/far_slots/pallas_call | solution.py:290
  44.5 0.9 %collective-permute-done.8.block = bf16[576,128]{1,0:T(8,128)(2,1)S(1)} collective-permute-done((bf16[576,128]{1,0:T(8,128)(2,1)S(1)}, bf16[576,128]{1,0:T(8,128)(2,1)S(1)}, u32[]{:S(2)}, u32[]{:S(2)}) %collective-permute-start.8) | collective-permute-done | bytes 147488 | tf_op jit(solution)/shard_map/ppermute | solution.py:274
  45.5 0.0 collective-permute-done.12.right
  45.5 1.9 %end.1 = (bf16[576,128]{1,0:T(8,128)(2,1)}, f32[4,576,128]{2,1,0:T(8,128)S(1)}, f32[4,576,128]{2,1,0:T(8,128)S(1)}) custom-call(f32[576,128]{1,0:T(8,128)S(1)} %left_last.1.left, bf16[576,128]{1,0:T(8,128)(2,1)S(1)} %collective-permute-done.12.right, f32[576,128]{1,0:T(8,128)S(1)} %get-tuple-element.62.old, ...), custom_call_target="tpu_custom_call", output_to_operand_aliasing={{1}: (7, {}), {2}: (8, {})} | custom-call | tf_op jit(solution)/shard_map/end/pallas_call | solution.py:290
  (2 shorter events, 0.0 us)
Async XLA Ops:
  0.0 14.0 %collective-permute-start = (bf16[576,128]{1,0:T(8,128)(2,1)}, bf16[576,128]{1,0:T(8,128)(2,1)S(1)}, u32[]{:S(2)}, u32[]{:S(2)}) collective-permute-start(bf16[576,128]{1,0:T(8,128)(2,1)} %bitcast.2), channel_id=1, source_target_pairs={{0,0},{1,8},{2,4},{3,12},{4,1},{5,9},{6,5},{7,13},{8,2},{9,10},{10... | collective-permute-start | bytes 442376 | tf_op jit(solution)/shard_map/ppermute | solution.py:280
  1.6 18.1 %collective-permute-start.4 = (bf16[576,128]{1,0:T(8,128)(2,1)}, bf16[576,128]{1,0:T(8,128)(2,1)S(1)}, u32[]{:S(2)}, u32[]{:S(2)}) collective-permute-start(bf16[576,128]{1,0:T(8,128)(2,1)} %bitcast.3), channel_id=1, source_target_pairs={{0,2},{1,3},{2,0},{3,1},{4,6},{5,7},{6,4},{7,5},{8,10},{9,11},{10,... | collective-permute-start | bytes 442376 | tf_op jit(solution)/shard_map/ppermute | solution.py:274
  6.0 14.0 %collective-permute-start.3 = (bf16[576,128]{1,0:T(8,128)(2,1)}, bf16[576,128]{1,0:T(8,128)(2,1)S(1)}, u32[]{:S(2)}, u32[]{:S(2)}) collective-permute-start(bf16[576,128]{1,0:T(8,128)(2,1)} %bitcast.4), channel_id=1, source_target_pairs={{0,1},{1,0},{2,3},{3,2},{4,5},{5,4},{6,7},{7,6},{8,9},{9,8},{10,11... | collective-permute-start | bytes 442376 | tf_op jit(solution)/shard_map/ppermute | solution.py:274
  11.1 0.9 %copy-start.1 = (bf16[24,24,128]{2,1,0:T(8,128)(2,1)S(1)}, bf16[24,24,128]{2,1,0:T(8,128)(2,1)}, u32[]{:S(2)}) copy-start(bf16[24,24,128]{2,1,0:T(8,128)(2,1)} %param.10) | copy-start | bytes 442372
  12.0 1.0 %copy-start.2 = (bf16[2,128,640]{2,1,0:T(8,128)(2,1)S(1)}, bf16[2,128,640]{2,1,0:T(8,128)(2,1)}, u32[]{:S(2)}) copy-start(bf16[2,128,640]{2,1,0:T(8,128)(2,1)} %w_in.1) | copy-start | bytes 983044
  14.6 5.4 %collective-permute-start.1 = (bf16[576,128]{1,0:T(8,128)(2,1)S(1)}, bf16[576,128]{1,0:T(8,128)(2,1)S(1)}, u32[]{:S(2)}, u32[]{:S(2)}) collective-permute-start(bf16[576,128]{1,0:T(8,128)(2,1)S(1)} %collective-permute-done.col.refs_0_), channel_id=1, source_target_pairs={{0,4},{4,0},{8,12},{12,8},{1,5},{5,1},{9,13},{13,9},{2,6},{6,2},{1... | collective-permute-start | bytes 442376 | tf_op jit(solution)/shard_map/ppermute | solution.py:324
  17.6 5.8 %collective-permute-start.2 = (bf16[576,128]{1,0:T(8,128)(2,1)S(1)}, bf16[576,128]{1,0:T(8,128)(2,1)S(1)}, u32[]{:S(2)}, u32[]{:S(2)}) collective-permute-start(bf16[576,128]{1,0:T(8,128)(2,1)S(1)} %collective-permute-done.col.refs_0_), channel_id=1, source_target_pairs={{0,8},{4,12},{8,0},{12,4},{1,9},{5,13},{9,1},{13,5},{2,10},{6,14},... | collective-permute-start | bytes 442376 | tf_op jit(solution)/shard_map/ppermute | solution.py:274
  19.6 6.4 %collective-permute-start.6 = (bf16[576,128]{1,0:T(8,128)(2,1)S(1)}, bf16[576,128]{1,0:T(8,128)(2,1)S(1)}, u32[]{:S(2)}, u32[]{:S(2)}) collective-permute-start(bf16[576,128]{1,0:T(8,128)(2,1)S(1)} %collective-permute-done.4.refs_1_), channel_id=1, source_target_pairs={{0,1},{1,0},{2,3},{3,2},{4,5},{5,4},{6,7},{7,6},{8,9},{9,8},{10,11... | collective-permute-start | bytes 442376 | tf_op jit(solution)/shard_map/ppermute | solution.py:274
  23.4 3.2 %collective-permute-start.5 = (bf16[576,128]{1,0:T(8,128)(2,1)S(1)}, bf16[576,128]{1,0:T(8,128)(2,1)S(1)}, u32[]{:S(2)}, u32[]{:S(2)}) collective-permute-start(bf16[576,128]{1,0:T(8,128)(2,1)S(1)} %collective-permute-done.2.refs_0_.refs_2_), channel_id=1, source_target_pairs={{0,4},{4,0},{8,12},{12,8},{1,5},{5,1},{9,13},{13,9},{2,6},{6,2},{1... | collective-permute-start | bytes 442376 | tf_op jit(solution)/shard_map/ppermute | solution.py:274
  26.1 0.8 %copy-start = (bf16[2,128,128]{2,1,0:T(8,128)(2,1)S(1)}, bf16[2,128,128]{2,1,0:T(8,128)(2,1)}, u32[]{:S(2)}) copy-start(bf16[2,128,128]{2,1,0:T(8,128)(2,1)} %w_out.3) | copy-start | bytes 196612
  29.5 10.5 %collective-permute-start.7 = (bf16[576,128]{1,0:T(8,128)(2,1)S(1)}, bf16[576,128]{1,0:T(8,128)(2,1)S(1)}, u32[]{:S(2)}, u32[]{:S(2)}) collective-permute-start(bf16[576,128]{1,0:T(8,128)(2,1)S(1)} %get-tuple-element.54.refs_0_), channel_id=1, source_target_pairs={{0,2},{1,3},{2,0},{3,1},{4,6},{5,7},{6,4},{7,5},{8,10},{9,11},{10,... | collective-permute-start | bytes 442376 | tf_op jit(solution)/shard_map/ppermute | solution.py:274
  31.7 8.4 %collective-permute-start.11 = (bf16[576,128]{1,0:T(8,128)(2,1)S(1)}, bf16[576,128]{1,0:T(8,128)(2,1)S(1)}, u32[]{:S(2)}, u32[]{:S(2)}) collective-permute-start(bf16[576,128]{1,0:T(8,128)(2,1)S(1)} %get-tuple-element.54.refs_0_), channel_id=1, source_target_pairs={{0,1},{1,0},{2,3},{3,2},{4,5},{5,4},{6,7},{7,6},{8,9},{9,8},{10,11... | collective-permute-start | bytes 442376 | tf_op jit(solution)/shard_map/ppermute | solution.py:274
  37.5 3.2 %collective-permute-start.10 = (bf16[576,128]{1,0:T(8,128)(2,1)S(1)}, bf16[576,128]{1,0:T(8,128)(2,1)S(1)}, u32[]{:S(2)}, u32[]{:S(2)}) collective-permute-start(bf16[576,128]{1,0:T(8,128)(2,1)S(1)} %get-tuple-element.58.own), channel_id=1, source_target_pairs={{0,4},{4,0},{8,12},{12,8},{1,5},{5,1},{9,13},{13,9},{2,6},{6,2},{1... | collective-permute-start | bytes 442376 | tf_op jit(solution)/shard_map/ppermute | solution.py:398
  37.6 6.3 %collective-permute-start.9 = (bf16[576,128]{1,0:T(8,128)(2,1)S(1)}, bf16[576,128]{1,0:T(8,128)(2,1)S(1)}, u32[]{:S(2)}, u32[]{:S(2)}) collective-permute-start(bf16[576,128]{1,0:T(8,128)(2,1)S(1)} %get-tuple-element.58.own), channel_id=1, source_target_pairs={{0,8},{4,12},{8,0},{12,4},{1,9},{5,13},{9,1},{13,5},{2,10},{6,14},... | collective-permute-start | bytes 442376 | tf_op jit(solution)/shard_map/ppermute | solution.py:274
  40.0 5.4 %collective-permute-start.8 = (bf16[576,128]{1,0:T(8,128)(2,1)S(1)}, bf16[576,128]{1,0:T(8,128)(2,1)S(1)}, u32[]{:S(2)}, u32[]{:S(2)}) collective-permute-start(bf16[576,128]{1,0:T(8,128)(2,1)S(1)} %collective-permute-done.7.refs_2_), channel_id=1, source_target_pairs={{0,1},{1,0},{2,3},{3,2},{4,5},{5,4},{6,7},{7,6},{8,9},{9,8},{10,11... | collective-permute-start | bytes 442376 | tf_op jit(solution)/shard_map/ppermute | solution.py:274
  43.8 1.6 %collective-permute-start.12 = (bf16[576,128]{1,0:T(8,128)(2,1)S(1)}, bf16[576,128]{1,0:T(8,128)(2,1)S(1)}, u32[]{:S(2)}, u32[]{:S(2)}) collective-permute-start(bf16[576,128]{1,0:T(8,128)(2,1)S(1)} %collective-permute-done.9.refs_0_), channel_id=1, source_target_pairs={{0,4},{4,0},{8,12},{12,8},{1,5},{5,1},{9,13},{13,9},{2,6},{6,2},{1... | collective-permute-start | bytes 442376 | tf_op jit(solution)/shard_map/ppermute | solution.py:274
